TPU v7x, 32 devices: a whole 2x2x4 slice. The times are simulated.
32 devices in a mesh: blk: 16 (over z, y, core), head: 2 (over x).
Axes of the slice: x: 2, y: 2, z: 4, core: 2. Of those that a mesh axis runs over, the one named last changes fastest.
Arguments:
- queries: bfloat16 [16384, 2048], P(('blk', 'head')), may hold values from -20 to 20
- keys: bfloat16 [16384, 1024], P(('blk', 'head')), may hold values from -20 to 20
- values: bfloat16 [16384, 1024], P(('blk', 'head')), may hold values from -6 to 6
- outputs: bfloat16 [16384, 2048], P(('blk', 'head')), may hold values from -6 to 6
- out_grads: bfloat16 [16384, 2048], P(('blk', 'head')), may hold values from -6 to 6
- segment_ids: int32 [16384], replicated, may hold values from 0 to 63, never falling along the last dimension, each value on 1 to 512 neighbouring positions
- block_order: int32 [32], replicated, may hold values from 0 to 31, as said below
Outputs:
- query_grads: bfloat16 [16384, 2048], P(('blk', 'head'))
- key_grads: bfloat16 [16384, 1024], P(('blk', 'head'))
- value_grads: bfloat16 [16384, 1024], P(('blk', 'head'))
Inputs may be any that keep to these rules, and one draw needn't show every extreme that they name: `segment_ids`: never falling along the sequence; each document has 1 to 512 tokens, one exactly 512. `block_order`: slots 2 i and 2 i + 1 hold the half-blocks i and 31 - i, in either order.
All inputs are finite; a program needn't handle non-finite values.
Results may differ from a plain program's by a relative error of at most 0.008.
Values may be sent and summed in bfloat16 or wider, within the bound.
No kernel may reach another device: no remote copies, remote signals or barrier semaphores. Data moves between devices by JAX's collectives and lax.ppermute only.
A program may use at most 128 MiB of HBM per device.

v0:
```python
import jax
import jax.numpy as jnp
from jax import lax
from jax.sharding import PartitionSpec as P

HEAD_SIZE = 128


NEGATIVE = -1e30


def shifted(value, axis, steps):
    count = lax.axis_size(axis)
    initial, last = (max(0, -steps), min(count, count - steps))
    return lax.ppermute(value, axis, [(source, source + steps) for source in range(initial, last)])


def row_terms_of(output_rows, grad_rows, head_dim):
    count_rows = output_rows.shape[0]
    heads = output_rows.shape[1] // head_dim
    product = output_rows.astype(jnp.float32) * grad_rows.astype(jnp.float32)
    return jnp.sum(product.reshape(count_rows, heads, head_dim), axis=2)


def local(queries, keys, values, outputs, out_grads, segment_ids, block_order):
    cycle_size = lax.axis_size("blk")
    cycle_index = lax.axis_index("blk")
    query_rows, key_rows, value_rows, output_rows, grad_rows = (
        lax.all_to_all(queries, "head", split_axis=1, concat_axis=0, tiled=True),
        lax.all_to_all(keys, "head", split_axis=1, concat_axis=0, tiled=True),
        lax.all_to_all(values, "head", split_axis=1, concat_axis=0, tiled=True),
        lax.all_to_all(outputs, "head", split_axis=1, concat_axis=0, tiled=True),
        lax.all_to_all(out_grads, "head", split_axis=1, concat_axis=0, tiled=True),
    )
    row_delta = row_terms_of(output_rows, grad_rows, HEAD_SIZE)
    block_rows = query_rows.shape[0]
    half_rows = block_rows // 2
    q_local = query_rows.shape[1] // HEAD_SIZE
    kv_local = key_rows.shape[1] // HEAD_SIZE
    query_group_size = q_local // kv_local
    softmax_scale = HEAD_SIZE ** (-0.5)
    row_offsets = jnp.arange(half_rows, dtype=jnp.int32)

    def half_of(source, late):
        clamped = jnp.clip(source, 0, cycle_size - 1)
        slots = lax.dynamic_slice_in_dim(block_order, 2 * clamped, 2)
        early_slot = (slots[0] > slots[1]).astype(jnp.int32)
        slot = 1 - early_slot if late else early_slot
        which = jnp.where(slot == 0, slots[0], slots[1])
        positions = which * half_rows + row_offsets
        return (slot, positions, segment_ids[positions])

    def rows_at(array, slot):
        return lax.dynamic_slice_in_dim(array, slot * half_rows, half_rows, 0)

    def place_half(term, slot):
        empty = jnp.zeros((block_rows, term.shape[1]), term.dtype)
        return lax.dynamic_update_slice_in_dim(empty, term, slot * half_rows, 0)

    own_half = {False: half_of(cycle_index, False), True: half_of(cycle_index, True)}
    early_slot = own_half[False][0]
    query_half = {}
    grad_half = {}
    delta_half = {}
    for late in (False, True):
        slot = own_half[late][0]
        query_half[late] = rows_at(query_rows, slot).reshape(
            half_rows, kv_local, query_group_size, HEAD_SIZE
        )
        grad_half[late] = rows_at(grad_rows, slot).reshape(
            half_rows, kv_local, query_group_size, HEAD_SIZE
        )
        delta_half[late] = rows_at(row_delta, slot).T.reshape(kv_local, query_group_size, half_rows)
    neighbour = {}
    for offset, late in ((1, False), (-1, True)):
        moved = shifted((key_rows, value_rows), "blk", offset)
        source_slot = half_of(cycle_index - offset, late)[0]
        neighbour[offset] = (rows_at(moved[0], source_slot), rows_at(moved[1], source_slot))
    specs = [
        (0, False, False),
        (0, True, True),
        (0, True, False),
        (1, False, False),
        (-1, True, True),
    ]
    blocks = {}
    masks = {}
    for spec in specs:
        offset, q_late, k_late = spec
        if offset == 0:
            slot = own_half[k_late][0]
            blocks[spec] = (rows_at(key_rows, slot), rows_at(value_rows, slot))
        else:
            blocks[spec] = neighbour[offset]
        source = cycle_index - offset
        inside = (source >= 0) & (source < cycle_size)
        k_info = half_of(source, k_late)
        q_info = own_half[q_late]
        masks[spec] = (
            (q_info[2][:, None] == k_info[2][None, :])
            & (k_info[1][None, :] <= q_info[1][:, None])
            & inside
        )

    def scores_of(query_four, key_block, visible):
        key_three = key_block.reshape(half_rows, kv_local, HEAD_SIZE)
        raw = (
            jnp.einsum("tjgd,ujd->jgtu", query_four, key_three, preferred_element_type=jnp.float32)
            * softmax_scale
        )
        return jnp.where(visible[None, None], raw, NEGATIVE)

    log_sums = {}
    for late in (False, True):
        stats = (
            jnp.full((kv_local, query_group_size, half_rows), NEGATIVE, jnp.float32),
            jnp.zeros((kv_local, query_group_size, half_rows), jnp.float32),
        )
        for spec in specs:
            if spec[1] == late:
                update_visible = masks[spec]
                maxima, totals = stats
                update_scores = scores_of(query_half[late], blocks[spec][0], update_visible)
                new_max = jnp.maximum(maxima, jnp.max(update_scores, axis=3))
                update_terms = jnp.where(
                    update_visible[None, None], jnp.exp(update_scores - new_max[..., None]), 0.0
                )
                stats = (
                    new_max,
                    totals * jnp.exp(maxima - new_max) + jnp.sum(update_terms, axis=3),
                )
        log_sums[late] = stats[0] + jnp.log(stats[1])
    terms = {}
    for spec in specs:
        tile_q_late = spec[1]
        tile_key_block = blocks[spec][0]
        tile_visible = masks[spec]
        tile_query_four = query_half[tile_q_late]
        grad_four = grad_half[tile_q_late]
        tile_key_three = tile_key_block.reshape(half_rows, kv_local, HEAD_SIZE)
        value_three = blocks[spec][1].reshape(half_rows, kv_local, HEAD_SIZE)
        scores = scores_of(tile_query_four, tile_key_block, tile_visible)
        weights = jnp.where(
            tile_visible[None, None], jnp.exp(scores - log_sums[tile_q_late][..., None]), 0.0
        )
        weights_b = weights.astype(jnp.bfloat16)
        value_term = jnp.einsum(
            "jgtu,tjgd->ujd", weights_b, grad_four, preferred_element_type=jnp.float32
        )
        weight_grads = jnp.einsum(
            "tjgd,ujd->jgtu", grad_four, value_three, preferred_element_type=jnp.float32
        )
        score_grads = weights * (weight_grads - delta_half[tile_q_late][..., None])
        score_grads_b = score_grads.astype(jnp.bfloat16)
        query_term = jnp.einsum(
            "jgtu,ujd->tjgd", score_grads_b, tile_key_three, preferred_element_type=jnp.float32
        )
        key_term = jnp.einsum(
            "jgtu,tjgd->ujd", score_grads_b, tile_query_four, preferred_element_type=jnp.float32
        )
        terms[spec] = (
            query_term.reshape(half_rows, q_local * HEAD_SIZE),
            key_term.reshape(half_rows, kv_local * HEAD_SIZE),
            value_term.reshape(half_rows, kv_local * HEAD_SIZE),
        )
    query_early = terms[0, False, False][0] + terms[1, False, False][0]
    query_late = terms[0, True, True][0] + terms[0, True, False][0] + terms[-1, True, True][0]
    key_early = terms[0, False, False][1] + terms[0, True, False][1]
    value_early = terms[0, False, False][2] + terms[0, True, False][2]
    key_late = terms[0, True, True][1]
    value_late = terms[0, True, True][2]
    received = {}
    for offset, late in ((1, False), (-1, True)):
        spec = (offset, late, late)
        source_slot = half_of(cycle_index - offset, late)[0]
        back_key, back_value = (
            shifted(
                place_half(terms[spec][1], source_slot).astype(jnp.bfloat16), "blk", -offset
            ).astype(jnp.float32),
            shifted(
                place_half(terms[spec][2], source_slot).astype(jnp.bfloat16), "blk", -offset
            ).astype(jnp.float32),
        )
        slot = own_half[late][0]
        received[late] = (rows_at(back_key, slot), rows_at(back_value, slot))
    key_early = key_early + received[False][0]
    value_early = value_early + received[False][1]
    key_late = key_late + received[True][0]
    value_late = value_late + received[True][1]

    def join(early, late):
        first = jnp.where(early_slot == 0, early, late)
        second = jnp.where(early_slot == 0, late, early)
        return jnp.concatenate([first, second], axis=0)

    query_block_grads = (join(query_early, query_late) * softmax_scale).astype(jnp.bfloat16)
    key_block_grads = (join(key_early, key_late) * softmax_scale).astype(jnp.bfloat16)
    value_block_grads = join(value_early, value_late).astype(jnp.bfloat16)
    return (
        lax.all_to_all(query_block_grads, "head", split_axis=0, concat_axis=1, tiled=True),
        lax.all_to_all(key_block_grads, "head", split_axis=0, concat_axis=1, tiled=True),
        lax.all_to_all(value_block_grads, "head", split_axis=0, concat_axis=1, tiled=True),
    )


def solution(mesh):
    return jax.shard_map(
        local,
        mesh=mesh,
        in_specs=(
            P(("blk", "head"), None),
            P(("blk", "head"), None),
            P(("blk", "head"), None),
            P(("blk", "head"), None),
            P(("blk", "head"), None),
            P(),
            P(),
        ),
        out_specs=(P(("blk", "head"), None), P(("blk", "head"), None), P(("blk", "head"), None)),
        check_vma=False,
    )
```

profile of v0, /device:TPU:0, one launch (start us, length us, event | category | flops | bytes accessed | tf_op | source)
XLA Modules:
  0.0 383.3 jit_solution(18010425302518543107)
XLA Ops:
  3.0 4.2 %all-to-all-start = ((bf16[512,2,512]{0,2,1:T(8,128)(2,1)}), bf16[512,2,512]{0,2,1:T(8,128)(2,1)S(1)}, u32[]{:S(2)}, u32[]{:S(2)}) async-start(bf16[512,2,512]{0,2,1:T(8,128)(2,1)} %bitcast.2), calls=%async_computation | async-start | bytes 2097152 | tf_op jit(solution)/shard_map/all_to_all | solution.py:30
  9.4 12.2 %all-to-all-done = bf16[512,2,512]{0,2,1:T(8,128)(2,1)S(1)} async-done(((bf16[512,2,512]{0,2,1:T(8,128)(2,1)}), bf16[512,2,512]{0,2,1:T(8,128)(2,1)S(1)}, u32[]{:S(2)}, u32[]{:S(2)}) %all-to-all-start) | async-done | bytes 1048608 | tf_op jit(solution)/shard_map/all_to_all | solution.py:30
  21.6 3.6 all-to-all-start.2
  25.2 3.9 %copy.218 = bf16[512,2048]{0,1:T(8,128)(2,1)} copy(bf16[512,2048]{1,0:T(8,128)(2,1)} %param.7) | data formatting | bytes 4194304 | tf_op args[0]
  29.1 9.4 %all-to-all-done.2 = bf16[512,2,512]{0,2,1:T(8,128)(2,1)S(1)} async-done(((bf16[512,2,512]{0,2,1:T(8,128)(2,1)}), bf16[512,2,512]{0,2,1:T(8,128)(2,1)S(1)}, u32[]{:S(2)}, u32[]{:S(2)}) %all-to-all-start.2) | async-done | bytes 1048608 | tf_op jit(solution)/shard_map/all_to_all | solution.py:31
  39.5 3.8 all-to-all-start.1
  43.2 3.9 %copy.229 = bf16[512,2048]{0,1:T(8,128)(2,1)} copy(bf16[512,2048]{1,0:T(8,128)(2,1)} %param.11) | data formatting | bytes 4194304 | tf_op args[4]
  47.2 19.7 %all-to-all-done.1 = bf16[512,2,1024]{0,2,1:T(8,128)(2,1)S(1)} async-done(((bf16[512,2,1024]{0,2,1:T(8,128)(2,1)}), bf16[512,2,1024]{0,2,1:T(8,128)(2,1)S(1)}, u32[]{:S(2)}, u32[]{:S(2)}) %all-to-all-start.1) | async-done | bytes 2097184 | tf_op jit(solution)/shard_map/all_to_all | solution.py:29
  68.2 3.8 all-to-all-start.3
  82.7 3.9 %copy.234 = bf16[512,2048]{0,1:T(8,128)(2,1)} copy(bf16[512,2048]{1,0:T(8,128)(2,1)} %param.10) | data formatting | bytes 4194304 | tf_op args[3]
  86.7 7.9 %all-to-all-done.3 = bf16[512,2,1024]{0,2,1:T(8,128)(2,1)S(1)} async-done(((bf16[512,2,1024]{0,2,1:T(8,128)(2,1)}), bf16[512,2,1024]{0,2,1:T(8,128)(2,1)S(1)}, u32[]{:S(2)}, u32[]{:S(2)}) %all-to-all-start.3) | async-done | bytes 2097184 | tf_op jit(solution)/shard_map/all_to_all | solution.py:33
  94.7 4.8 %all-to-all-start.4 = ((bf16[512,2,1024]{0,2,1:T(8,128)(2,1)}), bf16[512,2,1024]{0,2,1:T(8,128)(2,1)}, u32[]{:S(2)}, u32[]{:S(2)}) async-start(bf16[512,2,1024]{0,2,1:T(8,128)(2,1)} %bitcast.356), calls=%async_computation.4 | async-start | bytes 4194304 | tf_op jit(solution)/shard_map/all_to_all | solution.py:32
  99.6 3.1 gather_fusion.2
  102.7 3.1 gather_fusion.3
  105.9 3.1 gather_fusion
  118.2 4.0 %collective-permute-start.1 = (bf16[1024,512]{1,0:T(8,128)(2,1)}, bf16[1024,512]{1,0:T(8,128)(2,1)}, u32[]{:S(2)}, u32[]{:S(2)}) collective-permute-start(bf16[1024,512]{1,0:T(8,128)(2,1)} %bitcast.372), channel_id=1, source_target_pairs={{0,2},{2,4},{4,6},{6,8},{8,10},{10,12},{12,14},{14,16},{16,18},{18... | collective-permute-start | bytes 3145736 | tf_op jit(solution)/shard_map/ppermute | solution.py:15
  124.9 4.0 %collective-permute-start = (bf16[1024,512]{1,0:T(8,128)(2,1)}, bf16[1024,512]{1,0:T(8,128)(2,1)}, u32[]{:S(2)}, u32[]{:S(2)}) collective-permute-start(bf16[1024,512]{1,0:T(8,128)(2,1)} %bitcast.375), channel_id=1, source_target_pairs={{0,2},{2,4},{4,6},{6,8},{8,10},{10,12},{12,14},{14,16},{16,18},{18... | collective-permute-start | bytes 3145736 | tf_op jit(solution)/shard_map/ppermute | solution.py:15
  135.7 4.2 %copy.219 = bf16[2,512,1024]{2,1,0:T(8,128)(2,1)} copy(bf16[2,512,1024]{1,2,0:T(8,128)(2,1)} %bitcast.355) | data formatting | bytes 4194304 | tf_op jit(solution)/shard_map/all_to_all | solution.py:29
  142.3 4.2 %constant_dynamic-slice_fusion.7 = (bf16[512,1024]{1,0:T(8,128)(2,1)}, bf16[512,1024]{1,0:T(8,128)(2,1)S(1)}, bf16[512,1024]{1,0:T(8,128)(2,1)S(1)}, bf16[512,1024]{1,0:T(8,128)(2,1)}) fusion(bf16[1024,1024]{1,0:T(8,128)(2,1)} %bitcast.354, s32[]{:T(128)S(6)} %mul.159, s32[]{:T(128)S(6)} %select_n.212, bf16[1024,1024]{1,0:T(8,128)(2,1)} %bitcast.353), kind=kLoop, calls=%fused_computation.104 | loop fusion | bytes 8388616 | tf_op jit(solution)/shard_map/dynamic_slice | solution.py:54
  152.1 4.9 %bitcast_multiply_fusion = f32[2,512,1024]{1,2,0:T(8,128)} fusion(bf16[512,2,1024]{0,2,1:T(8,128)(2,1)} %all-to-all-done.4, bf16[512,2,1024]{0,2,1:T(8,128)(2,1)} %copy-done.4), kind=kLoop, calls=%fused_computation.46 | loop fusion | flops 3145728 | bytes 8388608 | tf_op jit(solution)/shard_map/mul | solution.py:21
  157.0 5.4 %copy.235 = f32[2,512,1024]{2,1,0:T(8,128)} copy(f32[2,512,1024]{1,2,0:T(8,128)} %bitcast_multiply_fusion) | data formatting | bytes 8388608 | tf_op jit(solution)/shard_map/mul | solution.py:21
  162.4 5.2 %copy.352 = f32[128,8,8,128]{3,2,1,0:T(8,128)} copy(f32[128,8,8,128]{3,1,2,0:T(8,128)} %bitcast.345) | data formatting | bytes 8388608
  167.6 4.2 %reduce_sum.56 = f32[1024,8]{1,0:T(8,128)} reduce(f32[1024,8,128]{2,1,0:T(8,128)} %bitcast.346, f32[]{:T(128)} %constant.15.clone.1), dimensions={2}, to_apply=%region_4.5 | reduce | flops 1040384 | bytes 4227076 | tf_op jit(solution)/shard_map/reduce_sum | solution.py:22
  171.7 5.9 %fusion.15 = (f32[4,2,512]{2,1,0:T(2,128)S(1)}, f32[4,512,512,2]{2,1,3,0:T(8,128)}) fusion(pred[512,512]{0,1:T(8,128)(4,1)} %get-tuple-element.27, bf16[512,4,128,1]{0,2,3,1:T(8,128)(2,1)S(1)} %bitcast.347, bf16[512,4,2,128]{0,3,2,1:T(8,128)(2,1)S(1)} %bitcast.340), kind=kOutput, calls=%fused_computation.39 | convolution fusion | flops 543158272 | bytes 10240000 | tf_op jit(solution)/shard_map/tjgd,ujd->jgtu/dot_general | solution.py:108
  180.6 5.8 %fusion.18 = (f32[4,2,512]{2,1,0:T(2,128)S(1)}, f32[4,512,512,2]{2,1,3,0:T(8,128)}) fusion(pred[512,512]{0,1:T(8,128)(4,1)} %get-tuple-element.29, bf16[512,4,128,1]{0,2,3,1:T(8,128)(2,1)S(1)} %bitcast.348, bf16[512,4,2,128]{0,3,2,1:T(8,128)(2,1)S(1)} %bitcast.324), kind=kOutput, calls=%fused_computation.42 | convolution fusion | flops 543158272 | bytes 10240000 | tf_op jit(solution)/shard_map/tjgd,ujd->jgtu/dot_general | solution.py:108
  186.5 4.9 %fusion.17 = (f32[4,2,512]{2,1,0:T(2,128)S(1)}, f32[4,512,512,2]{2,1,3,0:T(8,128)}) fusion(pred[512,512]{0,1:T(8,128)(4,1)S(1)} %get-tuple-element.30, bf16[512,4,128,1]{0,2,3,1:T(8,128)(2,1)S(1)} %bitcast.363, bf16[512,4,2,128]{0,3,2,1:T(8,128)(2,1)S(1)} %bitcast.325), kind=kOutput, calls=%fused_computation.41 | convolution fusion | flops 543158272 | bytes 10240000 | tf_op jit(solution)/shard_map/tjgd,ujd->jgtu/dot_general | solution.py:108
  197.3 8.1 %select_reduce_fusion.4 = f32[4,2,512]{2,1,0:T(2,128)S(1)} fusion(f32[4,512,512,2]{2,1,3,0:T(8,128)} %get-tuple-element.42, f32[4,2,512]{2,1,0:T(2,128)S(1)} %get-tuple-element.24, pred[512,512]{0,1:T(8,128)(4,1)S(1)} %copy-done.22), kind=kLoop, calls=%fused_computation.33 | loop fusion | flops 10481664 | bytes 8683520 | tf_op jit(solution)/shard_map/reduce_sum | solution.py:130
  207.6 3.6 fusion.37
  215.1 6.9 %fusion.27 = bf16[4,128,512,1]{2,1,3,0:T(8,128)(2,1)} fusion(bf16[512,4,2,128]{0,3,2,1:T(8,128)(2,1)} %bitcast.385, f32[4,512,512,2]{2,1,3,0:T(8,128)} %copy-done.2, f32[4,2,512]{2,1,0:T(2,128)S(1)} %log_add_fusion.1, pred[512,512]{0,1:T(8,128)(4,1)} %get-tuple-element.28), kind=kOutput, calls=%fused_computation.50 | convolution fusion | flops 547356672 | bytes 10240000 | tf_op jit(solution)/shard_map/jgtu,tjgd->ujd/dot_general | solution.py:147
  228.8 7.5 %select_reduce_fusion.2 = f32[4,2,512]{2,1,0:T(2,128)S(1)} fusion(f32[4,512,512,2]{2,1,3,0:T(8,128)} %get-tuple-element.50, f32[4,2,512]{2,1,0:T(2,128)S(1)} %get-tuple-element.26, pred[512,512]{0,1:T(8,128)(4,1)S(1)} %get-tuple-element.30), kind=kLoop, calls=%fused_computation.29 | loop fusion | flops 10481664 | bytes 8683520 | tf_op jit(solution)/shard_map/reduce_sum | solution.py:130
  240.8 3.4 fusion.3
  248.7 3.5 fusion.21
  256.2 7.0 %fusion.9 = bf16[4,2,512,512]{2,3,1,0:T(8,128)(2,1)S(1)} fusion(f32[4,512,512,2]{2,1,3,0:T(8,128)} %get-tuple-element.42, f32[4,2,512]{2,1,0:T(2,128)S(1)} %sub.175, f32[4,2,512]{2,1,0:T(2,128)S(1)} %log_add_fusion.1, pred[512,512]{0,1:T(8,128)(4,1)} %get-tuple-element.27, bf16[512,4,128,1]{0,2,3,1:T(8,128)(2,1)} %bitcast.390, ...), kind=kOutput, calls=%fused_computation.21 | convolution fusion | flops 551550976 | bytes 14450688 | tf_op jit(solution)/shard_map/tjgd,ujd->jgtu/dot_general | solution.py:150
  263.2 6.9 %fusion.7 = bf16[4,2,512,512]{2,3,1,0:T(8,128)(2,1)S(1)} fusion(f32[4,512,512,2]{2,1,3,0:T(8,128)} %copy-done.2, f32[4,2,512]{2,1,0:T(2,128)S(1)} %sub.175, f32[4,2,512]{2,1,0:T(2,128)S(1)} %log_add_fusion.1, pred[512,512]{0,1:T(8,128)(4,1)S(1)} %copy-done.21, bf16[512,4,128,1]{0,2,3,1:T(8,128)(2,1)S(1)} %bitcast.393, bf16[512,4,2,128]{0,3,2,1:T(8,128)(2,1)S(1)} %bitcast.388), kind=kOutput, calls=%fused_computation.18 | convolution fusion | flops 551550976 | bytes 14450688 | tf_op jit(solution)/shard_map/tjgd,ujd->jgtu/dot_general | solution.py:150
  280.4 5.9 %fusion.43 = f32[4,128,512]{2,1,0:T(8,128)} fusion(f32[4,128,512]{2,1,0:T(8,128)} %fusion.37, bf16[512,4,2,128]{0,3,2,1:T(8,128)(2,1)} %bitcast.379, f32[4,512,512,2]{2,1,3,0:T(8,128)S(1)} %bitcast.335, f32[4,2,512]{2,1,0:T(2,128)S(1)} %log_add_fusion, pred[512,512]{0,1:T(8,128)(4,1)S(1)} %copy-done.19), kind=kOutput, calls=%fused_computation.65 | convolution fusion | flops 547618816 | bytes 11812864 | tf_op jit(solution)/shard_map/jgtu,tjgd->ujd/dot_general | solution.py:147
  286.4 4.6 %fusion.1 = bf16[4,2,512,512]{2,3,1,0:T(8,128)(2,1)S(1)} fusion(f32[4,512,512,2]{2,1,3,0:T(8,128)S(1)} %bitcast.339, f32[4,2,512]{2,1,0:T(2,128)S(1)} %sub.194, f32[4,2,512]{2,1,0:T(2,128)S(1)} %log_add_fusion, pred[512,512]{0,1:T(8,128)(4,1)S(1)} %copy-done.17, bf16[512,4,128,1]{0,2,3,1:T(8,128)(2,1)} %bitcast.392, bf16[512,4,2,128]{0,3,2,1:T(8,128)(2,1)} %bitcast.380), kind=kOutput, calls=%fused_computation.6 | convolution fusion | flops 551550976 | bytes 14450688 | tf_op jit(solution)/shard_map/tjgd,ujd->jgtu/dot_general | solution.py:150
  293.0 4.7 %fusion.5 = bf16[4,2,512,512]{2,3,1,0:T(8,128)(2,1)S(1)} fusion(f32[4,512,512,2]{2,1,3,0:T(8,128)S(1)} %bitcast.331, f32[4,2,512]{2,1,0:T(2,128)S(1)} %sub.194, f32[4,2,512]{2,1,0:T(2,128)S(1)} %log_add_fusion, pred[512,512]{0,1:T(8,128)(4,1)S(1)} %get-tuple-element.30, bf16[512,4,128,1]{0,2,3,1:T(8,128)(2,1)S(1)} %bitcast.389, ...), kind=kOutput, calls=%fused_computation.12 | convolution fusion | flops 551550976 | bytes 14450688 | tf_op jit(solution)/shard_map/tjgd,ujd->jgtu/dot_general | solution.py:150
  300.5 5.0 %collective-permute-start.5 = (bf16[1024,512]{0,1:T(8,128)(2,1)}, bf16[1024,512]{0,1:T(8,128)(2,1)}, u32[]{:S(2)}, u32[]{:S(2)}) collective-permute-start(bf16[1024,512]{0,1:T(8,128)(2,1)} %constant_dynamic-update-slice_fusion.2), channel_id=1, source_target_pairs={{0,2},{2,4},{4,6},{6,8},{8,10},{10,12},{12,14},{14,16},{16,18},{18... | collective-permute-start | bytes 3145736 | tf_op jit(solution)/shard_map/ppermute | solution.py:15
  309.1 4.0 %copy.264 = bf16[1024,1024]{1,0:T(8,128)(2,1)} copy(bf16[1024,1024]{0,1:T(8,128)(2,1)} %fusion.20) | data formatting | bytes 4194304 | tf_op jit(solution)/shard_map/convert_element_type | solution.py:196
  313.1 5.1 %all-to-all-start.5 = ((bf16[2,512,1024]{2,1,0:T(8,128)(2,1)}), bf16[2,512,1024]{2,1,0:T(8,128)(2,1)}, u32[]{:S(2)}, u32[]{:S(2)}) async-start(bf16[2,512,1024]{2,1,0:T(8,128)(2,1)} %bitcast.359), calls=%async_computation.5 | async-start | bytes 4194304 | tf_op jit(solution)/shard_map/all_to_all | solution.py:200
  318.2 3.8 fusion.76
  325.0 3.6 collective-permute-start.7
  333.3 11.2 %all-to-all-done.5 = bf16[2,512,1024]{2,1,0:T(8,128)(2,1)} async-done(((bf16[2,512,1024]{2,1,0:T(8,128)(2,1)}), bf16[2,512,1024]{2,1,0:T(8,128)(2,1)}, u32[]{:S(2)}, u32[]{:S(2)}) %all-to-all-start.5) | async-done | bytes 2097184 | tf_op jit(solution)/shard_map/all_to_all | solution.py:200
  344.5 3.6 all-to-all-start.6
  348.1 6.2 %fusion.25 = f32[4,128,512,1]{2,1,3,0:T(8,128)S(1)} fusion(bf16[512,4,2,128]{0,3,2,1:T(8,128)(2,1)} %bitcast.382, f32[4,512,512,2]{2,1,3,0:T(8,128)} %get-tuple-element.50, f32[4,2,512]{2,1,0:T(2,128)S(1)} %log_add_fusion, pred[512,512]{0,1:T(8,128)(4,1)S(1)} %get-tuple-element.30), kind=kOutput, calls=%fused_computation.49 | convolution fusion | flops 547356672 | bytes 10764288 | tf_op jit(solution)/shard_map/jgtu,tjgd->ujd/dot_general | solution.py:147
  357.5 4.7 %all-to-all-done.6 = bf16[2,512,512]{2,1,0:T(8,128)(2,1)S(1)} async-done(((bf16[2,512,512]{2,1,0:T(8,128)(2,1)}), bf16[2,512,512]{2,1,0:T(8,128)(2,1)S(1)}, u32[]{:S(2)}, u32[]{:S(2)}) %all-to-all-start.6) | async-done | bytes 1048608 | tf_op jit(solution)/shard_map/all_to_all | solution.py:201
  362.2 4.4 %all-to-all-start.7 = ((bf16[2,512,512]{2,1,0:T(8,128)(2,1)}), bf16[2,512,512]{2,1,0:T(8,128)(2,1)}, u32[]{:S(2)}, u32[]{:S(2)}) async-start(bf16[2,512,512]{2,1,0:T(8,128)(2,1)} %bitcast.114), calls=%async_computation.7 | async-start | bytes 2097152 | tf_op jit(solution)/shard_map/all_to_all | solution.py:202
  373.8 6.3 %all-to-all-done.7 = bf16[2,512,512]{2,1,0:T(8,128)(2,1)} async-done(((bf16[2,512,512]{2,1,0:T(8,128)(2,1)}), bf16[2,512,512]{2,1,0:T(8,128)(2,1)}, u32[]{:S(2)}, u32[]{:S(2)}) %all-to-all-start.7) | async-done | bytes 1048608 | tf_op jit(solution)/shard_map/all_to_all | solution.py:202
  (189 shorter events, 109.2 us)
Async XLA Ops:
  0.6 98.9 %copy-start = (s32[16384]{0:T(1024)S(1)}, s32[16384]{0:T(1024)}, u32[]{:S(2)}) copy-start(s32[16384]{0:T(1024)} %param.12) | copy-start | bytes 196612
  3.0 18.6 %all-to-all-start = ((bf16[512,2,512]{0,2,1:T(8,128)(2,1)}), bf16[512,2,512]{0,2,1:T(8,128)(2,1)S(1)}, u32[]{:S(2)}, u32[]{:S(2)}) async-start(bf16[512,2,512]{0,2,1:T(8,128)(2,1)} %bitcast.2), calls=%async_computation | async-start | bytes 2097152 | tf_op jit(solution)/shard_map/all_to_all | solution.py:30
  21.6 16.9 %all-to-all-start.2 = ((bf16[512,2,512]{0,2,1:T(8,128)(2,1)}), bf16[512,2,512]{0,2,1:T(8,128)(2,1)S(1)}, u32[]{:S(2)}, u32[]{:S(2)}) async-start(bf16[512,2,512]{0,2,1:T(8,128)(2,1)} %bitcast.21), calls=%async_computation.2 | async-start | bytes 2097152 | tf_op jit(solution)/shard_map/all_to_all | solution.py:31
  25.2 46.8 %copy-start.34 = (s32[32]{0:T(128)S(1)}, s32[32]{0:T(128)}, u32[]{:S(2)}) copy-start(s32[32]{0:T(128)} %param.13) | copy-start | bytes 388
  39.5 27.4 %all-to-all-start.1 = ((bf16[512,2,1024]{0,2,1:T(8,128)(2,1)}), bf16[512,2,1024]{0,2,1:T(8,128)(2,1)S(1)}, u32[]{:S(2)}, u32[]{:S(2)}) async-start(bf16[512,2,1024]{0,2,1:T(8,128)(2,1)} %bitcast.358), calls=%async_computation.1 | async-start | bytes 4194304 | tf_op jit(solution)/shard_map/all_to_all | solution.py:29
  68.2 26.5 %all-to-all-start.3 = ((bf16[512,2,1024]{0,2,1:T(8,128)(2,1)}), bf16[512,2,1024]{0,2,1:T(8,128)(2,1)S(1)}, u32[]{:S(2)}, u32[]{:S(2)}) async-start(bf16[512,2,1024]{0,2,1:T(8,128)(2,1)} %bitcast.357), calls=%async_computation.3 | async-start | bytes 4194304 | tf_op jit(solution)/shard_map/all_to_all | solution.py:33
  94.7 45.3 %copy-start.4 = (bf16[512,2,1024]{0,2,1:T(8,128)(2,1)}, bf16[512,2,1024]{0,2,1:T(8,128)(2,1)S(1)}, u32[]{:S(2)}) copy-start(bf16[512,2,1024]{0,2,1:T(8,128)(2,1)S(1)} %all-to-all-done.3) | copy-start | bytes 6291460
  94.7 57.5 %all-to-all-start.4 = ((bf16[512,2,1024]{0,2,1:T(8,128)(2,1)}), bf16[512,2,1024]{0,2,1:T(8,128)(2,1)}, u32[]{:S(2)}, u32[]{:S(2)}) async-start(bf16[512,2,1024]{0,2,1:T(8,128)(2,1)} %bitcast.356), calls=%async_computation.4 | async-start | bytes 4194304 | tf_op jit(solution)/shard_map/all_to_all | solution.py:32
  117.0 94.2 %collective-permute-start.3 = (bf16[1024,512]{1,0:T(8,128)(2,1)}, bf16[1024,512]{1,0:T(8,128)(2,1)}, u32[]{:S(2)}, u32[]{:S(2)}) collective-permute-start(bf16[1024,512]{1,0:T(8,128)(2,1)} %bitcast.371), channel_id=1, source_target_pairs={{2,0},{4,2},{6,4},{8,6},{10,8},{12,10},{14,12},{16,14},{18,16},{20... | collective-permute-start | bytes 3145736 | tf_op jit(solution)/shard_map/ppermute | solution.py:15
  118.2 134.0 %collective-permute-start.1 = (bf16[1024,512]{1,0:T(8,128)(2,1)}, bf16[1024,512]{1,0:T(8,128)(2,1)}, u32[]{:S(2)}, u32[]{:S(2)}) collective-permute-start(bf16[1024,512]{1,0:T(8,128)(2,1)} %bitcast.372), channel_id=1, source_target_pairs={{0,2},{2,4},{4,6},{6,8},{8,10},{10,12},{12,14},{14,16},{16,18},{18... | collective-permute-start | bytes 3145736 | tf_op jit(solution)/shard_map/ppermute | solution.py:15
  123.6 98.4 %collective-permute-start.2 = (bf16[1024,512]{1,0:T(8,128)(2,1)}, bf16[1024,512]{1,0:T(8,128)(2,1)}, u32[]{:S(2)}, u32[]{:S(2)}) collective-permute-start(bf16[1024,512]{1,0:T(8,128)(2,1)} %bitcast.374), channel_id=1, source_target_pairs={{2,0},{4,2},{6,4},{8,6},{10,8},{12,10},{14,12},{16,14},{18,16},{20... | collective-permute-start | bytes 3145736 | tf_op jit(solution)/shard_map/ppermute | solution.py:15
  124.9 66.5 %collective-permute-start = (bf16[1024,512]{1,0:T(8,128)(2,1)}, bf16[1024,512]{1,0:T(8,128)(2,1)}, u32[]{:S(2)}, u32[]{:S(2)}) collective-permute-start(bf16[1024,512]{1,0:T(8,128)(2,1)} %bitcast.375), channel_id=1, source_target_pairs={{0,2},{2,4},{4,6},{6,8},{8,10},{10,12},{12,14},{14,16},{16,18},{18... | collective-permute-start | bytes 3145736 | tf_op jit(solution)/shard_map/ppermute | solution.py:15
  135.7 50.7 %copy-start.13 = (bf16[512,512]{0,1:T(8,128)(2,1)}, bf16[512,512]{0,1:T(8,128)(2,1)S(1)}, u32[]{:S(2)}) copy-start(bf16[512,512]{0,1:T(8,128)(2,1)S(1)} %copy.242) | copy-start | bytes 1572868
  194.5 10.8 %copy-start.20 = (pred[512,512]{0,1:T(8,128)(4,1)S(1)}, pred[512,512]{0,1:T(8,128)(4,1)}, u32[]{:S(2)}) copy-start(pred[512,512]{0,1:T(8,128)(4,1)} %get-tuple-element.28) | copy-start | bytes 786436
  197.2 10.2 %copy-start.2 = (f32[4,512,512,2]{2,1,3,0:T(8,128)}, f32[4,512,512,2]{2,1,3,0:T(8,128)S(1)}, u32[]{:S(2)}) copy-start(f32[4,512,512,2]{2,1,3,0:T(8,128)S(1)} %get-tuple-element.44) | copy-start | bytes 25165828
  197.2 10.3 %slice-start.6 = ((s8[8388608]{0:T(1024)(128)(4,1)}), s8[4194304]{0:T(1024)(128)(4,1)S(1)}, s32[]{:S(2)}) async-start(s8[8388608]{0:T(1024)(128)(4,1)} %bitcast.336), calls=%async_computation.14 | async-start | bytes 8388608
  197.2 10.3 %copy-start.28 = (bf16[512,1024]{0,1:T(8,128)(2,1)S(1)}, bf16[512,1024]{0,1:T(8,128)(2,1)}, u32[]{:S(2)}) copy-start(bf16[512,1024]{0,1:T(8,128)(2,1)} %copy.231) | copy-start | bytes 3145732
  225.9 10.4 %copy-start.16 = (pred[512,512]{0,1:T(8,128)(4,1)S(1)}, pred[512,512]{0,1:T(8,128)(4,1)}, u32[]{:S(2)}) copy-start(pred[512,512]{0,1:T(8,128)(4,1)} %get-tuple-element.31) | copy-start | bytes 786436
  228.7 20.0 %copy-start.3 = (f32[4,512,512,2]{2,1,3,0:T(8,128)}, f32[4,512,512,2]{2,1,3,0:T(8,128)S(1)}, u32[]{:S(2)}) copy-start(f32[4,512,512,2]{2,1,3,0:T(8,128)S(1)} %get-tuple-element.46) | copy-start | bytes 25165828
  228.8 9.6 %slice-start.2 = ((s8[8388608]{0:T(1024)(128)(4,1)}), s8[4194304]{0:T(1024)(128)(4,1)S(1)}, s32[]{:S(2)}) async-start(s8[8388608]{0:T(1024)(128)(4,1)} %bitcast.332), calls=%async_computation.10 | async-start | bytes 8388608
  228.8 9.6 %copy-start.18 = (pred[512,512]{0,1:T(8,128)(4,1)S(1)}, pred[512,512]{0,1:T(8,128)(4,1)}, u32[]{:S(2)}) copy-start(pred[512,512]{0,1:T(8,128)(4,1)} %get-tuple-element.29) | copy-start | bytes 786436
  256.1 7.0 %copy-start.21 = (pred[512,512]{0,1:T(8,128)(4,1)S(1)}, pred[512,512]{0,1:T(8,128)(4,1)}, u32[]{:S(2)}) copy-start(pred[512,512]{0,1:T(8,128)(4,1)} %get-tuple-element.28) | copy-start | bytes 786436
  256.2 7.0 %copy-start.29 = (bf16[512,1024]{0,1:T(8,128)(2,1)S(1)}, bf16[512,1024]{0,1:T(8,128)(2,1)}, u32[]{:S(2)}) copy-start(bf16[512,1024]{0,1:T(8,128)(2,1)} %copy.231) | copy-start | bytes 3145732
  256.2 7.0 %copy-start.32 = (bf16[512,512]{0,1:T(8,128)(2,1)S(1)}, bf16[512,512]{0,1:T(8,128)(2,1)}, u32[]{:S(2)}) copy-start(bf16[512,512]{0,1:T(8,128)(2,1)} %copy.238) | copy-start | bytes 1572868
  263.1 15.2 %copy-start.5 = (bf16[4,2,512,512]{2,3,1,0:T(8,128)(2,1)}, bf16[4,2,512,512]{2,3,1,0:T(8,128)(2,1)S(1)}, u32[]{:S(2)}) copy-start(bf16[4,2,512,512]{2,3,1,0:T(8,128)(2,1)S(1)} %fusion.9) | copy-start | bytes 12582916
  270.1 10.3 %slice-start.4 = ((s8[8388608]{0:T(1024)(128)(4,1)}), s8[4194304]{0:T(1024)(128)(4,1)S(1)}, s32[]{:S(2)}) async-start(s8[8388608]{0:T(1024)(128)(4,1)} %bitcast.334), calls=%async_computation.12 | async-start | bytes 8388608
  270.1 10.3 %copy-start.19 = (pred[512,512]{0,1:T(8,128)(4,1)S(1)}, pred[512,512]{0,1:T(8,128)(4,1)}, u32[]{:S(2)}) copy-start(pred[512,512]{0,1:T(8,128)(4,1)} %get-tuple-element.29) | copy-start | bytes 786436
  273.5 56.6 %collective-permute-start.4 = (bf16[1024,512]{0,1:T(8,128)(2,1)}, bf16[1024,512]{0,1:T(8,128)(2,1)}, u32[]{:S(2)}, u32[]{:S(2)}) collective-permute-start(bf16[1024,512]{0,1:T(8,128)(2,1)} %constant_dynamic-update-slice_fusion.3), channel_id=1, source_target_pairs={{2,0},{4,2},{6,4},{8,6},{10,8},{12,10},{14,12},{16,14},{18,16},{20... | collective-permute-start | bytes 3145736 | tf_op jit(solution)/shard_map/ppermute | solution.py:15
  276.8 77.5 %collective-permute-start.6 = (bf16[1024,512]{0,1:T(8,128)(2,1)}, bf16[1024,512]{0,1:T(8,128)(2,1)}, u32[]{:S(2)}, u32[]{:S(2)}) collective-permute-start(bf16[1024,512]{0,1:T(8,128)(2,1)} %constant_dynamic-update-slice_fusion.1), channel_id=1, source_target_pairs={{2,0},{4,2},{6,4},{8,6},{10,8},{12,10},{14,12},{16,14},{18,16},{20... | collective-permute-start | bytes 3145736 | tf_op jit(solution)/shard_map/ppermute | solution.py:15
  278.3 8.1 %slice-start.8 = ((s8[8388608]{0:T(1024)(128)(4,1)}), s8[4194304]{0:T(1024)(128)(4,1)S(1)}, s32[]{:S(2)}) async-start(s8[8388608]{0:T(1024)(128)(4,1)} %bitcast.338), calls=%async_computation.16 | async-start | bytes 8388608
  278.3 14.7 %slice-start = ((s8[8388608]{0:T(1024)(128)(4,1)}), s8[4194304]{0:T(1024)(128)(4,1)S(1)}, s32[]{:S(2)}) async-start(s8[8388608]{0:T(1024)(128)(4,1)} %bitcast.330), calls=%async_computation.8 | async-start | bytes 8388608
  280.4 6.0 %slice-start.9 = ((s8[8388608]{0:T(1024)(128)(4,1)}), s8[4194304]{0:T(1024)(128)(4,1)S(1)}, s32[]{:S(2)}) async-start(s8[8388608]{0:T(1024)(128)(4,1)} %bitcast.338), calls=%async_computation.17 | async-start | bytes 8388608
  280.4 12.6 %slice-start.1 = ((s8[8388608]{0:T(1024)(128)(4,1)}), s8[4194304]{0:T(1024)(128)(4,1)S(1)}, s32[]{:S(2)}) async-start(s8[8388608]{0:T(1024)(128)(4,1)} %bitcast.330), calls=%async_computation.9 | async-start | bytes 8388608
  286.4 6.6 %copy-start.30 = (bf16[512,512]{0,1:T(8,128)(2,1)S(1)}, bf16[512,512]{0,1:T(8,128)(2,1)}, u32[]{:S(2)}) copy-start(bf16[512,512]{0,1:T(8,128)(2,1)} %copy.251) | copy-start | bytes 1572868
  297.7 8.6 %copy-start.7 = (bf16[4,2,512,512]{2,3,1,0:T(8,128)(2,1)}, bf16[4,2,512,512]{2,3,1,0:T(8,128)(2,1)S(1)}, u32[]{:S(2)}) copy-start(bf16[4,2,512,512]{2,3,1,0:T(8,128)(2,1)S(1)} %fusion.5) | copy-start | bytes 12582916
  297.7 7.8 %copy-start.9 = (bf16[4,2,512,512]{2,3,1,0:T(8,128)(2,1)S(1)}, bf16[4,2,512,512]{2,3,1,0:T(8,128)(2,1)}, u32[]{:S(2)}) copy-start(bf16[4,2,512,512]{2,3,1,0:T(8,128)(2,1)} %copy-done.8) | copy-start | bytes 12582916
  297.7 7.8 %copy-start.12 = (f32[4,128,2,512]{3,1,2,0:T(8,128)S(1)}, f32[4,128,2,512]{3,1,2,0:T(8,128)}, u32[]{:S(2)}) copy-start(f32[4,128,2,512]{3,1,2,0:T(8,128)} %fusion.74) | copy-start | bytes 6291460
  297.7 7.8 %copy-start.15 = (bf16[512,512]{0,1:T(8,128)(2,1)S(1)}, bf16[512,512]{0,1:T(8,128)(2,1)}, u32[]{:S(2)}) copy-start(bf16[512,512]{0,1:T(8,128)(2,1)} %copy.248) | copy-start | bytes 1572868
  297.7 8.6 %copy-start.10 = (f32[4,128,2,512]{3,1,2,0:T(8,128)S(1)}, f32[4,128,2,512]{3,1,2,0:T(8,128)}, u32[]{:S(2)}) copy-start(f32[4,128,2,512]{3,1,2,0:T(8,128)} %fusion.72) | copy-start | bytes 6291460
  300.5 29.7 %collective-permute-start.5 = (bf16[1024,512]{0,1:T(8,128)(2,1)}, bf16[1024,512]{0,1:T(8,128)(2,1)}, u32[]{:S(2)}, u32[]{:S(2)}) collective-permute-start(bf16[1024,512]{0,1:T(8,128)(2,1)} %constant_dynamic-update-slice_fusion.2), channel_id=1, source_target_pairs={{0,2},{2,4},{4,6},{6,8},{8,10},{10,12},{12,14},{14,16},{16,18},{18... | collective-permute-start | bytes 3145736 | tf_op jit(solution)/shard_map/ppermute | solution.py:15
  309.1 19.5 %copy-start.24 = (f32[4,128,512]{2,1,0:T(8,128)S(1)}, f32[4,128,512]{2,1,0:T(8,128)}, u32[]{:S(2)}) copy-start(f32[4,128,512]{2,1,0:T(8,128)} %convolution_bitcast_fusion) | copy-start | bytes 3145732
  313.1 31.3 %all-to-all-start.5 = ((bf16[2,512,1024]{2,1,0:T(8,128)(2,1)}), bf16[2,512,1024]{2,1,0:T(8,128)(2,1)}, u32[]{:S(2)}, u32[]{:S(2)}) async-start(bf16[2,512,1024]{2,1,0:T(8,128)(2,1)} %bitcast.359), calls=%async_computation.5 | async-start | bytes 4194304 | tf_op jit(solution)/shard_map/all_to_all | solution.py:200
  318.2 10.4 %copy-start.6 = (bf16[4,2,512,512]{2,3,1,0:T(8,128)(2,1)S(1)}, bf16[4,2,512,512]{2,3,1,0:T(8,128)(2,1)}, u32[]{:S(2)}) copy-start(bf16[4,2,512,512]{2,3,1,0:T(8,128)(2,1)} %copy-done.5) | copy-start | bytes 12582916
  325.0 29.3 %collective-permute-start.7 = (bf16[1024,512]{0,1:T(8,128)(2,1)}, bf16[1024,512]{0,1:T(8,128)(2,1)}, u32[]{:S(2)}, u32[]{:S(2)}) collective-permute-start(bf16[1024,512]{0,1:T(8,128)(2,1)} %constant_dynamic-update-slice_fusion), channel_id=1, source_target_pairs={{0,2},{2,4},{4,6},{6,8},{8,10},{10,12},{12,14},{14,16},{16,18},{18... | collective-permute-start | bytes 3145736 | tf_op jit(solution)/shard_map/ppermute | solution.py:15
  344.5 17.7 %all-to-all-start.6 = ((bf16[2,512,512]{2,1,0:T(8,128)(2,1)}), bf16[2,512,512]{2,1,0:T(8,128)(2,1)S(1)}, u32[]{:S(2)}, u32[]{:S(2)}) async-start(bf16[2,512,512]{2,1,0:T(8,128)(2,1)} %bitcast.93), calls=%async_computation.6 | async-start | bytes 2097152 | tf_op jit(solution)/shard_map/all_to_all | solution.py:201
  348.1 6.3 %copy-start.26 = (f32[4,128,512]{2,1,0:T(8,128)S(1)}, f32[4,128,512]{2,1,0:T(8,128)}, u32[]{:S(2)}) copy-start(f32[4,128,512]{2,1,0:T(8,128)} %fusion.43) | copy-start | bytes 3145732
  362.2 17.8 %all-to-all-start.7 = ((bf16[2,512,512]{2,1,0:T(8,128)(2,1)}), bf16[2,512,512]{2,1,0:T(8,128)(2,1)}, u32[]{:S(2)}, u32[]{:S(2)}) async-start(bf16[2,512,512]{2,1,0:T(8,128)(2,1)} %bitcast.114), calls=%async_computation.7 | async-start | bytes 2097152 | tf_op jit(solution)/shard_map/all_to_all | solution.py:202
  366.6 16.2 %copy-start.1 = (s32[16384]{0:T(1024)S(1)}, s32[16384]{0:T(1024)}, u32[]{:S(2)}) copy-start(s32[16384]{0:T(1024)} %param.12) | copy-start | bytes 196612
  (13 other events, 48.4 us)
where the time goes:
time: 391 us; the launch traced here: 383 us
  local copies, waits for them, and re-layouts  115 us (29%)
  matrix products  91.9 us (24%)
  waiting for transfers between devices  71.3 us (18%)
  starting transfers between devices  55.2 us (14%)
  other arithmetic  39.2 us (10%)
  between operations  11 us (3%)
    dynamic_slice x19, local copies, waits for them, and re-layouts, rows_at(): return lax.dynamic_slice_in_dim(array, slot * half_rows, half_rows, 0)  31.5 us
    unnamed x99, local copies, waits for them, and re-layouts  29.7 us
    dot_general x5, matrix products, local(): jnp.einsum('tjgd,ujd->jgtu', grad_four, value_three, preferred_element_ty...  26.5 us
    dot_general x5, matrix products, local(): jnp.einsum('jgtu,tjgd->ujd', weights_b, grad_four, preferred_element_type...  26.2 us
    dot_general x5, matrix products, scores_of(): jnp.einsum('tjgd,ujd->jgtu', query_four, key_three, preferred_element_typ...  22.1 us
    ppermute x8, starting transfers between devices, shifted(): lax.ppermute(value, axis, [(source, source + steps) for source in range(i...  22 us
    reduce_sum x5, other arithmetic, local(): jnp.sum(update_terms, axis=3)  21.9 us
    all_to_all x1, waiting for transfers between devices, local(): lax.all_to_all(queries, 'head', split_axis=1, concat_axis=0, tiled=True)  19.7 us
  transfers between devices with their start and end apart: 16, of which 7 were waited for; matrix products, arithmetic and copies ran while one was open for 56% of the time, Pallas kernels for 0%

commit v1 on v0

v1 whole, which is shorter than its diff:
```python
import functools

import jax
import jax.numpy as jnp
from jax import lax
from jax.experimental import pallas as pl
from jax.experimental.pallas import tpu as pltpu
from jax.sharding import PartitionSpec as P

HEAD_SIZE = 128
NEGATIVE = -1e30
LOG2_E = 1.4426950408889634
CHUNKS = 2
TILE = 128
VMEM_BYTES = 40 * 1024 * 1024


def dot(left, right, left_dim, right_dim):
    return lax.dot_general(
        left, right, (((left_dim,), (right_dim,)), ((), ())), preferred_element_type=jnp.float32
    )


def attention_body(carried, group_ref, low_ref, q_ref, k_ref, v_ref, o_ref, do_ref, past_ref, *refs):
    dq_ref, dk_ref, dv_ref, back_ref, k_all, v_all, k_turned, dk_sum, dv_sum = refs[carried:]
    rows, head = k_ref.shape
    window = past_ref.shape[1]
    members = q_ref.shape[1] // head
    span = window + TILE
    scale = head**-0.5
    k_all[:window] = past_ref[0]
    k_all[window:] = k_ref[...]
    v_all[:window] = past_ref[1]
    v_all[window:] = v_ref[...]
    k_turned[...] = k_all[...].T
    dk_sum[...] = jnp.zeros_like(dk_sum)
    dv_sum[...] = jnp.zeros_like(dv_sum)

    def stacked(ref, start):
        return jnp.concatenate(
            [ref[start : start + TILE, m * head : (m + 1) * head] for m in range(members)], axis=0
        )

    for start in range(0, rows, TILE):
        queries = stacked(q_ref, start)
        grads = stacked(do_ref, start)
        product = grads.astype(jnp.float32) * stacked(o_ref, start).astype(jnp.float32)
        delta = jnp.sum(product.T, axis=0, keepdims=True)
        low = jnp.concatenate([low_ref[:, start : start + TILE]] * members, axis=1)
        keys = k_all[start : start + span]
        scores = dot(keys, queries, 1, 1)
        key_index = lax.broadcasted_iota(jnp.int32, scores.shape, 0)
        lane = lax.broadcasted_iota(jnp.int32, (1, members * TILE), 1)
        visible = (key_index >= low - start) & (key_index <= window + lane % TILE)
        scores = jnp.where(visible, scores, NEGATIVE)
        top = jnp.max(scores, axis=0, keepdims=True)
        terms = jnp.exp2((scores - top) * (scale * LOG2_E))
        weights = terms * (1.0 / jnp.sum(terms, axis=0, keepdims=True))
        weight_grads = dot(v_all[start : start + span], grads, 1, 1)
        score_grads = (weights * (weight_grads - delta)).astype(jnp.bfloat16)
        dv_sum[start : start + span] += dot(weights.astype(jnp.bfloat16), grads, 1, 0)
        dk_sum[start : start + span] += dot(score_grads, queries, 1, 0)
        dq = (dot(k_turned[:, start : start + span], score_grads, 1, 0) * scale).T
        for m in range(members):
            dq_ref[start : start + TILE, m * head : (m + 1) * head] = dq[
                m * TILE : (m + 1) * TILE
            ].astype(dq_ref.dtype)
    back_ref[0] = dk_sum[:window].astype(back_ref.dtype)
    back_ref[1] = dv_sum[:window].astype(back_ref.dtype)
    dk_ref[...] = dk_sum[window:]
    dv_ref[...] = dv_sum[window:]


def attention(group, low, row_arrays, past, first_head, heads_per_group, carried):
    queries, keys, values, outputs, grads = row_arrays
    rows, window, count = keys.shape[0], past.shape[1], past.shape[2] // HEAD_SIZE
    wide = queries.shape[1] // keys.shape[1] * HEAD_SIZE

    def column(step, group_ref):
        return (0, group_ref[0] * heads_per_group + first_head + step)

    query_spec = pl.BlockSpec((rows, wide), column)
    key_spec = pl.BlockSpec((rows, HEAD_SIZE), column)
    past_spec = pl.BlockSpec((2, window, HEAD_SIZE), lambda step, group_ref: (0, 0, step))
    low_spec = pl.BlockSpec((1, rows), lambda step, group_ref: (0, 0))
    tiles = count * queries.shape[1] // keys.shape[1] * rows * (window + TILE)
    return pl.pallas_call(
        functools.partial(attention_body, len(carried)),
        grid_spec=pltpu.PrefetchScalarGridSpec(
            num_scalar_prefetch=1,
            grid=(count,),
            in_specs=[low_spec, query_spec, key_spec, key_spec, query_spec, query_spec, past_spec]
            + [pl.BlockSpec(memory_space=pl.ANY)] * len(carried),
            out_specs=[query_spec, key_spec, key_spec, past_spec],
            scratch_shapes=[
                pltpu.VMEM((window + rows, HEAD_SIZE), jnp.bfloat16),
                pltpu.VMEM((window + rows, HEAD_SIZE), jnp.bfloat16),
                pltpu.VMEM((HEAD_SIZE, window + rows), jnp.bfloat16),
                pltpu.VMEM((window + rows, HEAD_SIZE), jnp.float32),
                pltpu.VMEM((window + rows, HEAD_SIZE), jnp.float32),
            ],
        ),
        out_shape=[
            jax.ShapeDtypeStruct(queries.shape, jnp.bfloat16),
            jax.ShapeDtypeStruct(keys.shape, jnp.float32),
            jax.ShapeDtypeStruct(keys.shape, jnp.float32),
            jax.ShapeDtypeStruct(past.shape, jnp.bfloat16),
        ],
        input_output_aliases={8 + i: i for i in range(len(carried))},
        compiler_params=pltpu.CompilerParams(vmem_limit_bytes=VMEM_BYTES),
        cost_estimate=pl.CostEstimate(
            flops=10 * tiles * HEAD_SIZE, bytes_accessed=count * rows * 2400, transcendentals=tiles
        ),
        name="attention",
    )(group, low, *row_arrays, past, *carried)


def finish_body(carried, group_ref, dk_ref, dv_ref, back_ref, *refs):
    key_out, value_out = refs[carried:]
    scale = HEAD_SIZE**-0.5
    key_out[...] = ((dk_ref[...] + back_ref[0].astype(jnp.float32)) * scale).astype(key_out.dtype)
    value_out[...] = (dv_ref[...] + back_ref[1].astype(jnp.float32)).astype(value_out.dtype)


def finish(group, own, back, first_head, heads_per_group, carried):
    rows, count = back.shape[1], back.shape[2] // HEAD_SIZE

    def column(step, group_ref):
        return (0, group_ref[0] * heads_per_group + first_head + step)

    key_spec = pl.BlockSpec((rows, HEAD_SIZE), column)
    back_spec = pl.BlockSpec((2, rows, HEAD_SIZE), lambda step, group_ref: (0, 0, step))
    return pl.pallas_call(
        functools.partial(finish_body, len(carried)),
        grid_spec=pltpu.PrefetchScalarGridSpec(
            num_scalar_prefetch=1,
            grid=(count,),
            in_specs=[key_spec, key_spec, back_spec]
            + [pl.BlockSpec(memory_space=pl.ANY)] * len(carried),
            out_specs=[key_spec, key_spec],
        ),
        out_shape=[jax.ShapeDtypeStruct(own[0].shape, jnp.bfloat16)] * 2,
        input_output_aliases={4 + i: i for i in range(len(carried))},
        cost_estimate=pl.CostEstimate(
            flops=count * rows * 512, bytes_accessed=count * rows * 2048, transcendentals=0
        ),
        name="finish",
    )(group, *own, back, *carried)


def pick(items, index):
    result = items[-1]
    for place in range(len(items) - 2, -1, -1):
        result = jnp.where(index == place, items[place], result)
    return result


def local(queries, keys, values, outputs, out_grads, segment_ids, block_order):
    blocks, sharers = lax.axis_size("blk"), lax.axis_size("head")
    block, place = lax.axis_index("blk"), lax.axis_index("head")
    rows = keys.shape[0]
    window = rows * sharers // 2
    parts = sharers // 2
    key_heads = keys.shape[1] // HEAD_SIZE
    heads_per_group = key_heads // sharers
    chunks = min(CHUNKS, heads_per_group)
    per_piece = heads_per_group // chunks
    slots = lax.dynamic_slice_in_dim(block_order, 2 * block, 2)
    early_slot = (slots[0] > slots[1]).astype(jnp.int32)
    last_block = block == blocks - 1

    def other(turn):
        return lax.rem(place + turn + sharers, sharers)

    def turned(value, turn):
        pairs = [(source, (source + turn) % sharers) for source in range(sharers)]
        return lax.ppermute(value, "head", pairs)

    def shifted(value, step):
        first, end = max(0, -step), min(blocks, blocks - step)
        return lax.ppermute(value, "blk", [(source, source + step) for source in range(first, end)])

    def columns(array, group, chunk):
        pieces = []
        for g in range(sharers):
            start = (g * heads_per_group + chunk * per_piece) * HEAD_SIZE
            pieces.append(array[:, start : start + per_piece * HEAD_SIZE])
        return pick(pieces, group)

    def piece_of(group, chunk):
        return jnp.stack([columns(keys, group, chunk), columns(values, group, chunk)])

    def is_early(device):
        return device // parts == early_slot

    def part_rows(array, device, count):
        if parts == 1:
            return array[:, :count]
        return lax.dynamic_slice_in_dim(array, device % parts * rows, count, 1)

    my_half = pick([slots[0], slots[1]], place // parts)
    start = my_half * window + place % parts * rows
    padded = jnp.concatenate([jnp.full((window,), -1, jnp.int32), segment_ids])
    near = lax.dynamic_slice_in_dim(padded, start, window + rows)
    low = jnp.sum((near[None, :] < near[window:, None]).astype(jnp.int32), axis=1)[None, :]

    row_arrays = (queries, keys, values, outputs, out_grads)
    groups = [other(-turn) for turn in range(sharers)]

    def halves_of(pieces):
        return [
            jnp.concatenate(
                [
                    pick(pieces, lax.rem(place - (slot * parts + p) + sharers, sharers))
                    for p in range(parts)
                ],
                axis=1,
            )
            for slot in (early_slot, 1 - early_slot)
        ]

    pasts = []
    for chunk in range(chunks):
        pieces = [piece_of(place, chunk)]
        for turn in range(1, sharers):
            pieces.append(turned(piece_of(other(turn), chunk), turn))
        early, late = halves_of(pieces)
        before_early, before_late = shifted(early, 1), shifted(late, -1)
        before_late = jnp.where(last_block, early, before_late)

        def past_of(device):
            before = jnp.where(is_early(device), before_early, before_late)
            if parts == 1:
                return before
            own = jnp.where(is_early(device), early, late)
            return part_rows(jnp.concatenate([before, own], axis=1), device, window)

        pasts.append(
            [past_of(place)]
            + [turned(past_of(other(turn)), turn) for turn in range(1, sharers)]
        )

    carried = ()
    backs = []
    for chunk in range(chunks):
        backs.append([])
        for turn in range(sharers):
            *carried, back = attention(
                groups[turn].reshape(1),
                low,
                row_arrays,
                pasts[chunk][turn],
                chunk * per_piece,
                heads_per_group,
                tuple(carried),
            )
            backs[chunk].append(back)

    query_grads, *own = carried
    results = ()
    for chunk in range(chunks):
        terms = [backs[chunk][0]]
        for turn in range(1, sharers):
            terms.append(turned(backs[chunk][turn], -turn))
        to_before, to_own = [], []
        for slot in (early_slot, 1 - early_slot):
            if parts == 1:
                to_before.append(pick(terms, lax.rem(slot - place + sharers, sharers)))
                to_own.append(None)
            else:
                total = jnp.zeros((2, 2 * window, terms[0].shape[2]), jnp.float32)
                for turn in range(sharers):
                    device = other(turn)
                    mine = jnp.where(device // parts == slot, terms[turn].astype(jnp.float32), 0.0)
                    wide = jnp.pad(mine, ((0, 0), (window, window), (0, 0)))
                    total += lax.dynamic_slice_in_dim(
                        wide, window - device % parts * rows, 2 * window, 1
                    )
                to_before.append(total[:, :window].astype(jnp.bfloat16))
                to_own.append(total[:, window:])
        for_early, for_late = shifted(to_before[0], -1), shifted(to_before[1], 1)
        for_early = jnp.where(last_block, to_before[1], for_early)
        sums = [
            came if more is None else (came.astype(jnp.float32) + more).astype(jnp.bfloat16)
            for came, more in zip((for_early, for_late), to_own)
        ]

        def rows_of(device):
            return part_rows(jnp.where(is_early(device), sums[0], sums[1]), device, rows)

        for turn in range(sharers):
            back = rows_of(other(turn))
            if turn:
                back = turned(back, turn)
            results = finish(
                groups[turn].reshape(1),
                own,
                back,
                chunk * per_piece,
                heads_per_group,
                tuple(results),
            )
    return (query_grads, *results)


def solution(mesh):
    spread = P(("blk", "head"), None)
    return jax.shard_map(
        local,
        mesh=mesh,
        in_specs=(spread,) * 5 + (P(), P()),
        out_specs=(spread,) * 3,
        check_vma=False,
    )
```

time: 391 us -> 142 us (0.36)
  the two profiles are of different devices: /device:TPU:0 before, /device:TPU:11 now
where the time goes in v1:
time: 142 us; the launch traced here: 140 us
  Pallas kernels  40.9 us (29%)
  waiting for transfers between devices  38.2 us (27%)
  starting transfers between devices  31 us (22%)
  other arithmetic  15.3 us (11%)
  local copies, waits for them, and re-layouts  11.6 us (8%)
  between operations  3.45 us (2%)
    pallas_call x4, Pallas kernels, attention(): pl.pallas_call(functools.partial(attention_body, len(carried)), grid_spec...  32.5 us
    ppermute x8, starting transfers between devices, shifted(): lax.ppermute(value, 'blk', [(source, source + step) for source in range(f...  25.8 us
    ppermute x8, waiting for transfers between devices, turned(): return lax.ppermute(value, 'head', pairs)  19.6 us
    ppermute x8, waiting for transfers between devices, shifted(): lax.ppermute(value, 'blk', [(source, source + step) for source in range(f...  18.5 us
    unnamed x36, local copies, waits for them, and re-layouts  10.9 us
    pallas_call x4, Pallas kernels, finish(): pl.pallas_call(functools.partial(finish_body, len(carried)), grid_spec=pl...  8.43 us
    select_n x4, other arithmetic, pick(): result = jnp.where(index == place, items[place], result)  5.74 us
    ppermute x8, starting transfers between devices, turned(): return lax.ppermute(value, 'head', pairs)  5.26 us
  transfers between devices with their start and end apart: 16, of which 10 were waited for; matrix products, arithmetic and copies ran while one was open for 10% of the time, Pallas kernels for 28%

profile of v1, /device:TPU:11, one launch (start us, length us, event | category | flops | bytes accessed | tf_op | source)
XLA Modules:
  0.0 140.5 jit_solution(13121973697662098337)
XLA Ops:
  0.6 1.7 %select_bitcast_fusion.2 = (bf16[1,512,256]{2,1,0:T(8,128)(2,1)S(1)}, bf16[1,512,256]{2,1,0:T(8,128)(2,1)S(1)}, bf16[1,512,256]{2,1,0:T(8,128)(2,1)S(1)}, bf16[1...) fusion(pred[]{:T(512)S(6)} %eq.22, ...), kind=kLoop, calls=%fused_computation.27 | loop fusion | flops 1048576 | bytes 4194306 | tf_op jit(solution)/shard_map/stack | solution.py:191
  2.8 1.3 collective-permute-start
  4.1 0.6 fusion
  6.0 9.2 %collective-permute-done.4 = bf16[2,512,256]{2,1,0:T(8,128)(2,1)S(1)} collective-permute-done((bf16[2,512,256]{2,1,0:T(8,128)(2,1)S(1)}, bf16[2,512,256]{2,1,0:T(8,128)(2,1)S(1)}, u32[]{:S(2)}, u32[]{:S(2)}) %collective-permute-start.4) | collective-permute-done | bytes 524320 | tf_op jit(solution)/shard_map/ppermute | solution.py:177
  15.3 0.9 broadcast_select_fusion.8
  16.1 4.6 %collective-permute-start.6 = (bf16[2,512,256]{2,1,0:T(8,128)(2,1)}, bf16[2,512,256]{2,1,0:T(8,128)(2,1)}, u32[]{:S(2)}, u32[]{:S(2)}) collective-permute-start(bf16[2,512,256]{2,1,0:T(8,128)(2,1)} %get-tuple-element.63), channel_id=1, source_target_pairs={{2,0},{4,2},{6,4},{8,6},{10,8},{12,10},{14,12},{16,14},{18,16},{20... | collective-permute-start | bytes 1572872 | tf_op jit(solution)/shard_map/ppermute | solution.py:181
  20.7 3.0 %collective-permute-start.5 = (bf16[2,512,256]{2,1,0:T(8,128)(2,1)S(1)}, bf16[2,512,256]{2,1,0:T(8,128)(2,1)}, u32[]{:S(2)}, u32[]{:S(2)}) collective-permute-start(bf16[2,512,256]{2,1,0:T(8,128)(2,1)S(1)} %get-tuple-element.64), channel_id=1, source_target_pairs={{0,2},{2,4},{4,6},{6,8},{8,10},{10,12},{12,14},{14,16},{16,18},{18... | collective-permute-start | bytes 1572872 | tf_op jit(solution)/shard_map/ppermute | solution.py:181
  23.8 2.8 %collective-permute-done = bf16[2,512,256]{2,1,0:T(8,128)(2,1)S(1)} collective-permute-done((bf16[2,512,256]{2,1,0:T(8,128)(2,1)S(1)}, bf16[2,512,256]{2,1,0:T(8,128)(2,1)S(1)}, u32[]{:S(2)}, u32[]{:S(2)}) %collective-permute-start) | collective-permute-done | bytes 524320 | tf_op jit(solution)/shard_map/ppermute | solution.py:177
  26.7 3.4 %collective-permute-start.2 = (bf16[2,512,256]{2,1,0:T(8,128)(2,1)S(1)}, bf16[2,512,256]{2,1,0:T(8,128)(2,1)S(1)}, u32[]{:S(2)}, u32[]{:S(2)}) collective-permute-start(bf16[2,512,256]{2,1,0:T(8,128)(2,1)S(1)} %get-tuple-element.73), channel_id=1, source_target_pairs={{2,0},{4,2},{6,4},{8,6},{10,8},{12,10},{14,12},{16,14},{18,16},{20... | collective-permute-start | bytes 1572872 | tf_op jit(solution)/shard_map/ppermute | solution.py:181
  30.0 3.0 %collective-permute-start.1 = (bf16[2,512,256]{2,1,0:T(8,128)(2,1)S(1)}, bf16[2,512,256]{2,1,0:T(8,128)(2,1)}, u32[]{:S(2)}, u32[]{:S(2)}) collective-permute-start(bf16[2,512,256]{2,1,0:T(8,128)(2,1)S(1)} %get-tuple-element.74), channel_id=1, source_target_pairs={{0,2},{2,4},{4,6},{6,8},{8,10},{10,12},{12,14},{14,16},{16,18},{18... | collective-permute-start | bytes 1572872 | tf_op jit(solution)/shard_map/ppermute | solution.py:181
  34.6 4.8 %collective-permute-done.5 = bf16[2,512,256]{2,1,0:T(8,128)(2,1)} collective-permute-done((bf16[2,512,256]{2,1,0:T(8,128)(2,1)S(1)}, bf16[2,512,256]{2,1,0:T(8,128)(2,1)}, u32[]{:S(2)}, u32[]{:S(2)}) %collective-permute-start.5) | collective-permute-done | bytes 524320 | tf_op jit(solution)/shard_map/ppermute | solution.py:181
  39.5 2.3 %broadcast_select_fusion.6 = (bf16[2,512,256]{2,1,0:T(8,128)(2,1)}, bf16[2,512,256]{2,1,0:T(8,128)(2,1)}) fusion(bf16[2,512,256]{2,1,0:T(8,128)(2,1)} %collective-permute-done.5, pred[]{:T(512)S(6)} %eq.54, bf16[2,512,256]{2,1,0:T(8,128)(2,1)S(1)} %get-tuple-element.64, bf16[2,512,256]{2,1,0:T(8,128)(2,1)} %collective-permute-done.6, pred[]{:T(512)S(6)} %eq.26, ...), kind=kLoop, calls=%fused_computation.11 | loop fusion | flops 786432 | bytes 2621443 | tf_op jit(solution)/shard_map/jit(_where)/select_n | solution.py:232
  42.0 3.9 %collective-permute-done.2 = bf16[2,512,256]{2,1,0:T(8,128)(2,1)S(1)} collective-permute-done((bf16[2,512,256]{2,1,0:T(8,128)(2,1)S(1)}, bf16[2,512,256]{2,1,0:T(8,128)(2,1)S(1)}, u32[]{:S(2)}, u32[]{:S(2)}) %collective-permute-start.2) | collective-permute-done | bytes 524320 | tf_op jit(solution)/shard_map/ppermute | solution.py:181
  45.9 2.1 %broadcast_select_fusion.7 = (bf16[2,512,256]{2,1,0:T(8,128)(2,1)}, bf16[2,512,256]{2,1,0:T(8,128)(2,1)}) fusion(bf16[2,512,256]{2,1,0:T(8,128)(2,1)} %collective-permute-done.1, pred[]{:T(512)S(6)} %eq.54, bf16[2,512,256]{2,1,0:T(8,128)(2,1)S(1)} %get-tuple-element.74, bf16[2,512,256]{2,1,0:T(8,128)(2,1)S(1)} %collective-permute-done.2, pred[]{:T(512)S(6)} %eq.26, ...), kind=kLoop, calls=%fused_computation.12 | loop fusion | flops 786432 | bytes 2621443 | tf_op jit(solution)/shard_map/jit(_where)/select_n | solution.py:232
  48.2 0.4 convert_reduce_fusion
  48.6 1.6 %copy-done.2 = bf16[512,2048]{1,0:T(8,128)(2,1)S(1)} copy-done((bf16[512,2048]{1,0:T(8,128)(2,1)S(1)}, bf16[512,2048]{1,0:T(8,128)(2,1)}, u32[]{:S(2)}) %copy-start.2) | copy-done | bytes 2097176
  50.2 1.6 %copy-done.4 = bf16[512,2048]{1,0:T(8,128)(2,1)S(1)} copy-done((bf16[512,2048]{1,0:T(8,128)(2,1)S(1)}, bf16[512,2048]{1,0:T(8,128)(2,1)}, u32[]{:S(2)}) %copy-start.4) | copy-done | bytes 2097176
  51.8 1.6 %copy-done.6 = bf16[512,2048]{1,0:T(8,128)(2,1)S(1)} copy-done((bf16[512,2048]{1,0:T(8,128)(2,1)S(1)}, bf16[512,2048]{1,0:T(8,128)(2,1)}, u32[]{:S(2)}) %copy-start.6) | copy-done | bytes 2097176
  53.4 1.2 copy-done.8
  54.6 1.0 copy-done.10
  55.7 7.8 %attention.4 = (bf16[512,2048]{1,0:T(8,128)(2,1)}, f32[512,1024]{1,0:T(8,128)S(1)}, f32[512,1024]{1,0:T(8,128)S(1)}, bf16[2,512,256]{2,1,0:T(8,128)(2,1)S(1)}) custom-call(s32[1]{0:T(128)} %bitcast.8.group_ref, s32[1,512]{1,0:T(1,128)S(1)} %bitcast.21, bf16[512,2048]{1,0:T(8,128)(2,1)S(1)} %copy-done.2, bf16[512,1024]{1,0:T(8,128)(2,1)S(1)} %copy-done.7, ...), custom_call_target="tpu_custom_call" | custom-call | flops 1677721600 | bytes 2457600 | tf_op jit(solution)/shard_map/attention/pallas_call | solution.py:87
  63.5 8.6 %attention.5 = (bf16[512,2048]{1,0:T(8,128)(2,1)}, f32[512,1024]{1,0:T(8,128)S(1)}, f32[512,1024]{1,0:T(8,128)S(1)}, bf16[2,512,256]{2,1,0:T(8,128)(2,1)}) custom-call(s32[1]{0:T(128)} %bitcast.group_ref, s32[1,512]{1,0:T(1,128)S(1)} %bitcast.22, bf16[512,2048]{1,0:T(8,128)(2,1)S(1)} %copy-done.3, ...), custom_call_target="tpu_custom_call", output_to_operand_aliasing={{0}: (8, {}), {1}: (9, {}), {2}: (10, {})} | custom-call | flops 1677721600 | bytes 2457600 | tf_op jit(solution)/shard_map/attention/pallas_call | solution.py:87
  72.0 1.2 collective-permute-start.12
  73.2 7.8 %attention.6 = (bf16[512,2048]{1,0:T(8,128)(2,1)}, f32[512,1024]{1,0:T(8,128)S(1)}, f32[512,1024]{1,0:T(8,128)S(1)}, bf16[2,512,256]{2,1,0:T(8,128)(2,1)S(1)}) custom-call(s32[1]{0:T(128)} %bitcast.8.group_ref, s32[1,512]{1,0:T(1,128)S(1)} %bitcast.23, bf16[512,2048]{1,0:T(8,128)(2,1)S(1)} %copy-done.3, ...), custom_call_target="tpu_custom_call", output_to_operand_aliasing={{0}: (8, {}), {1}: (9, {}), {2}: (10, {})} | custom-call | flops 1677721600 | bytes 2457600 | tf_op jit(solution)/shard_map/attention/pallas_call | solution.py:87
  81.0 0.8 copy-done.12
  81.8 8.4 %attention.7 = (bf16[512,2048]{1,0:T(8,128)(2,1)}, f32[512,1024]{1,0:T(8,128)S(1)}, f32[512,1024]{1,0:T(8,128)S(1)}, bf16[2,512,256]{2,1,0:T(8,128)(2,1)}) custom-call(s32[1]{0:T(128)} %bitcast.group_ref, s32[1,512]{1,0:T(1,128)S(1)} %bitcast.24, bf16[512,2048]{1,0:T(8,128)(2,1)S(1)} %copy-done.3, ...), custom_call_target="tpu_custom_call", output_to_operand_aliasing={{0}: (8, {}), {1}: (9, {}), {2}: (10, {})} | custom-call | flops 1677721600 | bytes 2457600 | tf_op jit(solution)/shard_map/attention/pallas_call | solution.py:87
  90.3 1.3 copy-done.1
  91.9 2.7 %broadcast_select_fusion.2 = (bf16[2,512,256]{2,1,0:T(8,128)(2,1)}, bf16[2,512,256]{2,1,0:T(8,128)(2,1)S(1)}) fusion(bf16[2,512,256]{2,1,0:T(8,128)(2,1)} %copy-done.11, bf16[2,512,256]{2,1,0:T(8,128)(2,1)} %collective-permute-done.12, pred[]{:T(512)S(6)} %eq.56, pred[]{:T(512)S(6)} %eq.55), kind=kLoop, calls=%fused_computation.7 | loop fusion | flops 524288 | bytes 2097154 | tf_op jit(solution)/shard_map/jit(_where)/select_n | solution.py:154
  94.6 1.9 %collective-permute-start.13 = (bf16[2,512,256]{2,1,0:T(8,128)(2,1)}, bf16[2,512,256]{2,1,0:T(8,128)(2,1)}, u32[]{:S(2)}, u32[]{:S(2)}) collective-permute-start(bf16[2,512,256]{2,1,0:T(8,128)(2,1)} %get-tuple-element.59), channel_id=1, source_target_pairs={{2,0},{4,2},{6,4},{8,6},{10,8},{12,10},{14,12},{16,14},{18,16},{20... | collective-permute-start | bytes 1572872 | tf_op jit(solution)/shard_map/ppermute | solution.py:181
  96.5 4.3 %collective-permute-start.14 = (bf16[2,512,256]{2,1,0:T(8,128)(2,1)S(1)}, bf16[2,512,256]{2,1,0:T(8,128)(2,1)}, u32[]{:S(2)}, u32[]{:S(2)}) collective-permute-start(bf16[2,512,256]{2,1,0:T(8,128)(2,1)S(1)} %get-tuple-element.60), channel_id=1, source_target_pairs={{0,2},{2,4},{4,6},{6,8},{8,10},{10,12},{12,14},{14,16},{16,18},{18... | collective-permute-start | bytes 1572872 | tf_op jit(solution)/shard_map/ppermute | solution.py:181
  100.8 2.0 %collective-permute-done.8 = bf16[2,512,256]{2,1,0:T(8,128)(2,1)} collective-permute-done((bf16[2,512,256]{2,1,0:T(8,128)(2,1)}, bf16[2,512,256]{2,1,0:T(8,128)(2,1)}, u32[]{:S(2)}, u32[]{:S(2)}) %collective-permute-start.8) | collective-permute-done | bytes 524320 | tf_op jit(solution)/shard_map/ppermute | solution.py:177
  102.7 2.1 %broadcast_select_fusion.3 = (bf16[2,512,256]{2,1,0:T(8,128)(2,1)}, bf16[2,512,256]{2,1,0:T(8,128)(2,1)}) fusion(bf16[2,512,256]{2,1,0:T(8,128)(2,1)S(1)} %copy-done.13, bf16[2,512,256]{2,1,0:T(8,128)(2,1)} %collective-permute-done.8, pred[]{:T(512)S(6)} %eq.56, pred[]{:T(512)S(6)} %eq.55), kind=kLoop, calls=%fused_computation.8 | loop fusion | flops 524288 | bytes 2097154 | tf_op jit(solution)/shard_map/jit(_where)/select_n | solution.py:154
  104.8 1.9 %collective-permute-start.9 = (bf16[2,512,256]{2,1,0:T(8,128)(2,1)}, bf16[2,512,256]{2,1,0:T(8,128)(2,1)S(1)}, u32[]{:S(2)}, u32[]{:S(2)}) collective-permute-start(bf16[2,512,256]{2,1,0:T(8,128)(2,1)} %get-tuple-element.61), channel_id=1, source_target_pairs={{2,0},{4,2},{6,4},{8,6},{10,8},{12,10},{14,12},{16,14},{18,16},{20... | collective-permute-start | bytes 1572872 | tf_op jit(solution)/shard_map/ppermute | solution.py:181
  106.7 3.6 %collective-permute-start.10 = (bf16[2,512,256]{2,1,0:T(8,128)(2,1)}, bf16[2,512,256]{2,1,0:T(8,128)(2,1)S(1)}, u32[]{:S(2)}, u32[]{:S(2)}) collective-permute-start(bf16[2,512,256]{2,1,0:T(8,128)(2,1)} %get-tuple-element.62), channel_id=1, source_target_pairs={{0,2},{2,4},{4,6},{6,8},{8,10},{10,12},{12,14},{14,16},{16,18},{18... | collective-permute-start | bytes 1572872 | tf_op jit(solution)/shard_map/ppermute | solution.py:181
  110.4 7.0 %collective-permute-done.13 = bf16[2,512,256]{2,1,0:T(8,128)(2,1)} collective-permute-done((bf16[2,512,256]{2,1,0:T(8,128)(2,1)}, bf16[2,512,256]{2,1,0:T(8,128)(2,1)}, u32[]{:S(2)}, u32[]{:S(2)}) %collective-permute-start.13) | collective-permute-done | bytes 524320 | tf_op jit(solution)/shard_map/ppermute | solution.py:181
  117.4 2.1 %broadcast_select_fusion = (bf16[2,512,256]{2,1,0:T(8,128)(2,1)}, bf16[2,512,256]{2,1,0:T(8,128)(2,1)S(1)}) fusion(bf16[2,512,256]{2,1,0:T(8,128)(2,1)} %collective-permute-done.14, pred[]{:T(512)S(6)} %eq.57, bf16[2,512,256]{2,1,0:T(8,128)(2,1)S(1)} %get-tuple-element.60, bf16[2,512,256]{2,1,0:T(8,128)(2,1)} %collective-permute-done.13, pred[]{:T(512)S(6)} %eq.26, ...), kind=kLoop, calls=%fused_computation.5 | loop fusion | flops 786432 | bytes 2621443 | tf_op jit(solution)/shard_map/jit(_where)/select_n | solution.py:289
  119.6 0.8 collective-permute-start.15
  120.4 2.6 %collective-permute-done.9 = bf16[2,512,256]{2,1,0:T(8,128)(2,1)S(1)} collective-permute-done((bf16[2,512,256]{2,1,0:T(8,128)(2,1)}, bf16[2,512,256]{2,1,0:T(8,128)(2,1)S(1)}, u32[]{:S(2)}, u32[]{:S(2)}) %collective-permute-start.9) | collective-permute-done | bytes 524320 | tf_op jit(solution)/shard_map/ppermute | solution.py:181
  123.0 0.9 broadcast_select_fusion.1
  124.0 0.8 collective-permute-start.11
  124.8 2.1 %finish.4 = (bf16[512,1024]{1,0:T(8,128)(2,1)}, bf16[512,1024]{1,0:T(8,128)(2,1)}) custom-call(s32[1]{0:T(128)} %bitcast.8.group_ref, f32[512,1024]{1,0:T(8,128)} %copy-done, f32[512,1024]{1,0:T(8,128)} %copy-done.1, bf16[2,512,256]{2,1,0:T(8,128)(2,1)} %get-tuple-element.51.back_ref), custom_call_target="tpu_custom_call" | custom-call | flops 524288 | bytes 2097152 | tf_op jit(solution)/shard_map/finish/pallas_call | solution.py:133
  126.9 5.1 %collective-permute-done.15.back_ref = bf16[2,512,256]{2,1,0:T(8,128)(2,1)S(1)} collective-permute-done((bf16[2,512,256]{2,1,0:T(8,128)(2,1)S(1)}, bf16[2,512,256]{2,1,0:T(8,128)(2,1)S(1)}, u32[]{:S(2)}, u32[]{:S(2)}) %collective-permute-start.15) | collective-permute-done | bytes 524320 | tf_op jit(solution)/shard_map/ppermute | solution.py:177
  132.0 0.8 copy-done.15
  132.8 2.1 %finish.5 = (bf16[512,1024]{1,0:T(8,128)(2,1)}, bf16[512,1024]{1,0:T(8,128)(2,1)}) custom-call(s32[1]{0:T(128)} %bitcast.group_ref, f32[512,1024]{1,0:T(8,128)} %copy-done, f32[512,1024]{1,0:T(8,128)} %copy-done.1, bf16[2,512,256]{2,1,0:T(8,128)(2,1)} %copy-done.15, ...), custom_call_target="tpu_custom_call", output_to_operand_aliasing={{0}: (4, {}), {1}: (5, {})} | custom-call | flops 524288 | bytes 2097152 | tf_op jit(solution)/shard_map/finish/pallas_call | solution.py:133
  134.9 2.1 %finish.6 = (bf16[512,1024]{1,0:T(8,128)(2,1)}, bf16[512,1024]{1,0:T(8,128)(2,1)}) custom-call(s32[1]{0:T(128)} %bitcast.8.group_ref, f32[512,1024]{1,0:T(8,128)} %copy-done, f32[512,1024]{1,0:T(8,128)} %copy-done.1, bf16[2,512,256]{2,1,0:T(8,128)(2,1)} %get-tuple-element.53.back_ref, ...), custom_call_target="tpu_custom_call", output_to_operand_aliasing={{0}: (4, {}), {1}: (5, {})} | custom-call | flops 524288 | bytes 2097152 | tf_op jit(solution)/shard_map/finish/pallas_call | solution.py:133
  137.0 0.6 collective-permute-done.11.back_ref
  137.6 0.8 copy-done.14
  138.4 2.1 %finish.7 = (bf16[512,1024]{1,0:T(8,128)(2,1)}, bf16[512,1024]{1,0:T(8,128)(2,1)}) custom-call(s32[1]{0:T(128)} %bitcast.group_ref, f32[512,1024]{1,0:T(8,128)} %copy-done, f32[512,1024]{1,0:T(8,128)} %copy-done.1, bf16[2,512,256]{2,1,0:T(8,128)(2,1)} %copy-done.14, ...), custom_call_target="tpu_custom_call", output_to_operand_aliasing={{0}: (4, {}), {1}: (5, {})} | custom-call | flops 524288 | bytes 2097152 | tf_op jit(solution)/shard_map/finish/pallas_call | solution.py:133
  (44 shorter events, 1.6 us)
Async XLA Ops:
  2.3 1.7 %copy-start.17 = (s32[32]{0:T(128)S(1)}, s32[32]{0:T(128)}, u32[]{:S(2)}) copy-start(s32[32]{0:T(128)} %param.13) | copy-start | bytes 388
  2.4 12.9 %collective-permute-start.4 = (bf16[2,512,256]{2,1,0:T(8,128)(2,1)S(1)}, bf16[2,512,256]{2,1,0:T(8,128)(2,1)S(1)}, u32[]{:S(2)}, u32[]{:S(2)}) collective-permute-start(bf16[2,512,256]{2,1,0:T(8,128)(2,1)S(1)} %pad_maximum_fusion.3), channel_id=1, source_target_pairs={{0,1},{1,0},{2,3},{3,2},{4,5},{5,4},{6,7},{7,6},{8,9},{9,8},{10,11... | collective-permute-start | bytes 1572872 | tf_op jit(solution)/shard_map/ppermute | solution.py:177
  2.8 23.8 %collective-permute-start = (bf16[2,512,256]{2,1,0:T(8,128)(2,1)S(1)}, bf16[2,512,256]{2,1,0:T(8,128)(2,1)S(1)}, u32[]{:S(2)}, u32[]{:S(2)}) collective-permute-start(bf16[2,512,256]{2,1,0:T(8,128)(2,1)S(1)} %pad_maximum_fusion.1), channel_id=1, source_target_pairs={{0,1},{1,0},{2,3},{3,2},{4,5},{5,4},{6,7},{7,6},{8,9},{9,8},{10,11... | collective-permute-start | bytes 1572872 | tf_op jit(solution)/shard_map/ppermute | solution.py:177
  15.3 19.1 %copy-start.16 = (s32[16384]{0:T(1024)S(1)}, s32[16384]{0:T(1024)}, u32[]{:S(2)}) copy-start(s32[16384]{0:T(1024)} %param.12) | copy-start | bytes 196612
  16.1 18.5 %collective-permute-start.6 = (bf16[2,512,256]{2,1,0:T(8,128)(2,1)}, bf16[2,512,256]{2,1,0:T(8,128)(2,1)}, u32[]{:S(2)}, u32[]{:S(2)}) collective-permute-start(bf16[2,512,256]{2,1,0:T(8,128)(2,1)} %get-tuple-element.63), channel_id=1, source_target_pairs={{2,0},{4,2},{6,4},{8,6},{10,8},{12,10},{14,12},{16,14},{18,16},{20... | collective-permute-start | bytes 1572872 | tf_op jit(solution)/shard_map/ppermute | solution.py:181
  20.7 18.8 %collective-permute-start.5 = (bf16[2,512,256]{2,1,0:T(8,128)(2,1)S(1)}, bf16[2,512,256]{2,1,0:T(8,128)(2,1)}, u32[]{:S(2)}, u32[]{:S(2)}) collective-permute-start(bf16[2,512,256]{2,1,0:T(8,128)(2,1)S(1)} %get-tuple-element.64), channel_id=1, source_target_pairs={{0,2},{2,4},{4,6},{6,8},{8,10},{10,12},{12,14},{14,16},{16,18},{18... | collective-permute-start | bytes 1572872 | tf_op jit(solution)/shard_map/ppermute | solution.py:181
  26.7 19.2 %collective-permute-start.2 = (bf16[2,512,256]{2,1,0:T(8,128)(2,1)S(1)}, bf16[2,512,256]{2,1,0:T(8,128)(2,1)S(1)}, u32[]{:S(2)}, u32[]{:S(2)}) collective-permute-start(bf16[2,512,256]{2,1,0:T(8,128)(2,1)S(1)} %get-tuple-element.73), channel_id=1, source_target_pairs={{2,0},{4,2},{6,4},{8,6},{10,8},{12,10},{14,12},{16,14},{18,16},{20... | collective-permute-start | bytes 1572872 | tf_op jit(solution)/shard_map/ppermute | solution.py:181
  30.0 15.8 %collective-permute-start.1 = (bf16[2,512,256]{2,1,0:T(8,128)(2,1)S(1)}, bf16[2,512,256]{2,1,0:T(8,128)(2,1)}, u32[]{:S(2)}, u32[]{:S(2)}) collective-permute-start(bf16[2,512,256]{2,1,0:T(8,128)(2,1)S(1)} %get-tuple-element.74), channel_id=1, source_target_pairs={{0,2},{2,4},{4,6},{6,8},{8,10},{10,12},{12,14},{14,16},{16,18},{18... | collective-permute-start | bytes 1572872 | tf_op jit(solution)/shard_map/ppermute | solution.py:181
  34.5 14.1 %copy-start.7 = (bf16[512,1024]{1,0:T(8,128)(2,1)S(1)}, bf16[512,1024]{1,0:T(8,128)(2,1)}, u32[]{:S(2)}) copy-start(bf16[512,1024]{1,0:T(8,128)(2,1)} %k_ref.7) | copy-start | bytes 3145732
  41.8 21.7 %collective-permute-start.7 = (bf16[2,512,256]{2,1,0:T(8,128)(2,1)}, bf16[2,512,256]{2,1,0:T(8,128)(2,1)}, u32[]{:S(2)}, u32[]{:S(2)}) collective-permute-start(bf16[2,512,256]{2,1,0:T(8,128)(2,1)} %get-tuple-element.56), channel_id=1, source_target_pairs={{0,1},{1,0},{2,3},{3,2},{4,5},{5,4},{6,7},{7,6},{8,9},{9,8},{10,11... | collective-permute-start | bytes 1572872 | tf_op jit(solution)/shard_map/ppermute | solution.py:177
  48.0 33.8 %collective-permute-start.3 = (bf16[2,512,256]{2,1,0:T(8,128)(2,1)}, bf16[2,512,256]{2,1,0:T(8,128)(2,1)}, u32[]{:S(2)}, u32[]{:S(2)}) collective-permute-start(bf16[2,512,256]{2,1,0:T(8,128)(2,1)} %get-tuple-element.58), channel_id=1, source_target_pairs={{0,1},{1,0},{2,3},{3,2},{4,5},{5,4},{6,7},{7,6},{8,9},{9,8},{10,11... | collective-permute-start | bytes 1572872 | tf_op jit(solution)/shard_map/ppermute | solution.py:177
  48.6 1.6 %copy-start.2 = (bf16[512,2048]{1,0:T(8,128)(2,1)S(1)}, bf16[512,2048]{1,0:T(8,128)(2,1)}, u32[]{:S(2)}) copy-start(bf16[512,2048]{1,0:T(8,128)(2,1)} %q_ref.7) | copy-start | bytes 6291460
  50.2 1.6 %copy-start.4 = (bf16[512,2048]{1,0:T(8,128)(2,1)S(1)}, bf16[512,2048]{1,0:T(8,128)(2,1)}, u32[]{:S(2)}) copy-start(bf16[512,2048]{1,0:T(8,128)(2,1)} %o_ref.7) | copy-start | bytes 6291460
  51.8 1.6 %copy-start.6 = (bf16[512,2048]{1,0:T(8,128)(2,1)S(1)}, bf16[512,2048]{1,0:T(8,128)(2,1)}, u32[]{:S(2)}) copy-start(bf16[512,2048]{1,0:T(8,128)(2,1)} %do_ref.7) | copy-start | bytes 6291460
  53.4 1.2 copy-start.8
  54.6 1.0 copy-start.10
  55.7 7.8 %copy-start.3 = (bf16[512,2048]{1,0:T(8,128)(2,1)S(1)}, bf16[512,2048]{1,0:T(8,128)(2,1)}, u32[]{:S(2)}) copy-start(bf16[512,2048]{1,0:T(8,128)(2,1)} %q_ref.7) | copy-start | bytes 6291460
  55.7 7.8 %copy-start.5 = (bf16[512,2048]{1,0:T(8,128)(2,1)S(1)}, bf16[512,2048]{1,0:T(8,128)(2,1)}, u32[]{:S(2)}) copy-start(bf16[512,2048]{1,0:T(8,128)(2,1)} %o_ref.7) | copy-start | bytes 6291460
  63.4 8.6 %copy-start.11 = (bf16[2,512,256]{2,1,0:T(8,128)(2,1)}, bf16[2,512,256]{2,1,0:T(8,128)(2,1)S(1)}, u32[]{:S(2)}) copy-start(bf16[2,512,256]{2,1,0:T(8,128)(2,1)S(1)} %get-tuple-element.41) | copy-start | bytes 1572868
  63.4 9.8 %copy-start.9 = (bf16[2,512,256]{2,1,0:T(8,128)(2,1)S(1)}, bf16[2,512,256]{2,1,0:T(8,128)(2,1)}, u32[]{:S(2)}) copy-start(bf16[2,512,256]{2,1,0:T(8,128)(2,1)} %get-tuple-element.57.past_ref) | copy-start | bytes 1572868
  72.0 19.8 %collective-permute-start.12 = (bf16[2,512,256]{2,1,0:T(8,128)(2,1)}, bf16[2,512,256]{2,1,0:T(8,128)(2,1)}, u32[]{:S(2)}, u32[]{:S(2)}) collective-permute-start(bf16[2,512,256]{2,1,0:T(8,128)(2,1)} %get-tuple-element.42), channel_id=1, source_target_pairs={{0,1},{1,0},{2,3},{3,2},{4,5},{5,4},{6,7},{7,6},{8,9},{9,8},{10,11... | collective-permute-start | bytes 1572872 | tf_op jit(solution)/shard_map/ppermute | solution.py:177
  81.0 0.8 copy-start.12
  90.3 1.3 copy-start.1
  91.6 13.2 %copy-start = (f32[512,1024]{1,0:T(8,128)}, f32[512,1024]{1,0:T(8,128)S(1)}, u32[]{:S(2)}) copy-start(f32[512,1024]{1,0:T(8,128)S(1)} %get-tuple-element.37.dk_ref) | copy-start | bytes 6291460
  91.6 11.1 %copy-start.13 = (bf16[2,512,256]{2,1,0:T(8,128)(2,1)S(1)}, bf16[2,512,256]{2,1,0:T(8,128)(2,1)}, u32[]{:S(2)}) copy-start(bf16[2,512,256]{2,1,0:T(8,128)(2,1)} %copy-done.12) | copy-start | bytes 1572868
  91.6 11.1 %collective-permute-start.8 = (bf16[2,512,256]{2,1,0:T(8,128)(2,1)}, bf16[2,512,256]{2,1,0:T(8,128)(2,1)}, u32[]{:S(2)}, u32[]{:S(2)}) collective-permute-start(bf16[2,512,256]{2,1,0:T(8,128)(2,1)} %get-tuple-element.40), channel_id=1, source_target_pairs={{0,1},{1,0},{2,3},{3,2},{4,5},{5,4},{6,7},{7,6},{8,9},{9,8},{10,11... | collective-permute-start | bytes 1572872 | tf_op jit(solution)/shard_map/ppermute | solution.py:177
  94.6 22.9 %collective-permute-start.13 = (bf16[2,512,256]{2,1,0:T(8,128)(2,1)}, bf16[2,512,256]{2,1,0:T(8,128)(2,1)}, u32[]{:S(2)}, u32[]{:S(2)}) collective-permute-start(bf16[2,512,256]{2,1,0:T(8,128)(2,1)} %get-tuple-element.59), channel_id=1, source_target_pairs={{2,0},{4,2},{6,4},{8,6},{10,8},{12,10},{14,12},{16,14},{18,16},{20... | collective-permute-start | bytes 1572872 | tf_op jit(solution)/shard_map/ppermute | solution.py:181
  96.5 20.9 %collective-permute-start.14 = (bf16[2,512,256]{2,1,0:T(8,128)(2,1)S(1)}, bf16[2,512,256]{2,1,0:T(8,128)(2,1)}, u32[]{:S(2)}, u32[]{:S(2)}) collective-permute-start(bf16[2,512,256]{2,1,0:T(8,128)(2,1)S(1)} %get-tuple-element.60), channel_id=1, source_target_pairs={{0,2},{2,4},{4,6},{6,8},{8,10},{10,12},{12,14},{14,16},{16,18},{18... | collective-permute-start | bytes 1572872 | tf_op jit(solution)/shard_map/ppermute | solution.py:181
  104.8 18.2 %collective-permute-start.9 = (bf16[2,512,256]{2,1,0:T(8,128)(2,1)}, bf16[2,512,256]{2,1,0:T(8,128)(2,1)S(1)}, u32[]{:S(2)}, u32[]{:S(2)}) collective-permute-start(bf16[2,512,256]{2,1,0:T(8,128)(2,1)} %get-tuple-element.61), channel_id=1, source_target_pairs={{2,0},{4,2},{6,4},{8,6},{10,8},{12,10},{14,12},{16,14},{18,16},{20... | collective-permute-start | bytes 1572872 | tf_op jit(solution)/shard_map/ppermute | solution.py:181
  106.7 16.3 %collective-permute-start.10 = (bf16[2,512,256]{2,1,0:T(8,128)(2,1)}, bf16[2,512,256]{2,1,0:T(8,128)(2,1)S(1)}, u32[]{:S(2)}, u32[]{:S(2)}) collective-permute-start(bf16[2,512,256]{2,1,0:T(8,128)(2,1)} %get-tuple-element.62), channel_id=1, source_target_pairs={{0,2},{2,4},{4,6},{6,8},{8,10},{10,12},{12,14},{14,16},{16,18},{18... | collective-permute-start | bytes 1572872 | tf_op jit(solution)/shard_map/ppermute | solution.py:181
  119.6 12.4 %collective-permute-start.15 = (bf16[2,512,256]{2,1,0:T(8,128)(2,1)S(1)}, bf16[2,512,256]{2,1,0:T(8,128)(2,1)S(1)}, u32[]{:S(2)}, u32[]{:S(2)}) collective-permute-start(bf16[2,512,256]{2,1,0:T(8,128)(2,1)S(1)} %get-tuple-element.52), channel_id=1, source_target_pairs={{0,1},{1,0},{2,3},{3,2},{4,5},{5,4},{6,7},{7,6},{8,9},{9,8},{10,11... | collective-permute-start | bytes 1572872 | tf_op jit(solution)/shard_map/ppermute | solution.py:177
  124.0 13.6 %collective-permute-start.11 = (bf16[2,512,256]{2,1,0:T(8,128)(2,1)S(1)}, bf16[2,512,256]{2,1,0:T(8,128)(2,1)S(1)}, u32[]{:S(2)}, u32[]{:S(2)}) collective-permute-start(bf16[2,512,256]{2,1,0:T(8,128)(2,1)S(1)} %get-tuple-element.54), channel_id=1, source_target_pairs={{0,1},{1,0},{2,3},{3,2},{4,5},{5,4},{6,7},{7,6},{8,9},{9,8},{10,11... | collective-permute-start | bytes 1572872 | tf_op jit(solution)/shard_map/ppermute | solution.py:177
  131.9 0.8 copy-start.15
  137.6 0.8 copy-start.14

commit v2 on v1

--- a/solution.py
+++ b/solution.py
@@ -12,7 +12,7 @@
 LOG2_E = 1.4426950408889634
 CHUNKS = 2
 TILE = 128
-VMEM_BYTES = 40 * 1024 * 1024
+VMEM_BYTES = 60 * 1024 * 1024
 
 
 def dot(left, right, left_dim, right_dim):
@@ -141,6 +141,7 @@
         ),
         out_shape=[jax.ShapeDtypeStruct(own[0].shape, jnp.bfloat16)] * 2,
         input_output_aliases={4 + i: i for i in range(len(carried))},
+        compiler_params=pltpu.CompilerParams(vmem_limit_bytes=VMEM_BYTES),
         cost_estimate=pl.CostEstimate(
             flops=count * rows * 512, bytes_accessed=count * rows * 2048, transcendentals=0
         ),
@@ -241,10 +242,9 @@
         )
 
     carried = ()
-    backs = []
-    for chunk in range(chunks):
-        backs.append([])
-        for turn in range(sharers):
+    backs = [[] for chunk in range(chunks)]
+    for turn in range(sharers):
+        for chunk in range(chunks):
             *carried, back = attention(
                 groups[turn].reshape(1),
                 low,

time: 142 us -> 134 us (0.944)
  local copies, waits for them, and re-layouts: 11.6 us -> 4.76 us
  other arithmetic: 15.3 us -> 10.6 us
  starting transfers between devices: 31 us -> 35.5 us
  waiting for transfers between devices: 38.2 us -> 35.6 us
  Pallas kernels: 40.9 us -> 42.7 us
    unnamed x36 -> x18, local copies, waits for them, and re-layouts: 10.9 us -> 4.01 us
    ppermute x8, waiting for transfers between devices: 19.6 us -> 15.4 us  [turned(): return lax.ppermute(value, 'head', pairs)]
    select_n x4, other arithmetic: 5.74 us -> 2.16 us  [pick(): result = jnp.where(index == place, items[place], result)]
    ppermute x8, starting transfers between devices: 5.26 us -> 7.89 us  [turned(): return lax.ppermute(value, 'head', pairs)]
    ppermute x8, starting transfers between devices: 25.8 us -> 27.6 us  [shifted(): lax.ppermute(value, 'blk', [(source, source + step) for source in range(f...]
    pallas_call x4, Pallas kernels: 32.5 us -> 34.2 us  [attention(): pl.pallas_call(functools.partial(attention_body, len(carried)), grid_spec...]
    ppermute x8, waiting for transfers between devices: 18.5 us -> 20.2 us  [shifted(): lax.ppermute(value, 'blk', [(source, source + step) for source in range(f...]
    select_n x2, other arithmetic: 4.38 us -> 2.81 us  [past_of(): before = jnp.where(is_early(device), before_early, before_late)]
  transfers between devices with their start and end apart: 16 -> 16, of which waited for: 10 -> 9; matrix products, arithmetic and copies ran while one was open for 10% -> 7% of each run, Pallas kernels for 28% -> 31%
where the time goes in v2:
time: 134 us; the launch traced here: 133 us
  Pallas kernels  42.7 us (32%)
  waiting for transfers between devices  35.6 us (27%)
  starting transfers between devices  35.5 us (26%)
  other arithmetic  10.6 us (8%)
  local copies, waits for them, and re-layouts  4.76 us (4%)
  between operations  3.46 us (3%)
    pallas_call x4, Pallas kernels, attention(): pl.pallas_call(functools.partial(attention_body, len(carried)), grid_spec...  34.2 us
    ppermute x8, starting transfers between devices, shifted(): lax.ppermute(value, 'blk', [(source, source + step) for source in range(f...  27.6 us
    ppermute x8, waiting for transfers between devices, shifted(): lax.ppermute(value, 'blk', [(source, source + step) for source in range(f...  20.2 us
    ppermute x8, waiting for transfers between devices, turned(): return lax.ppermute(value, 'head', pairs)  15.4 us
    pallas_call x4, Pallas kernels, finish(): pl.pallas_call(functools.partial(finish_body, len(carried)), grid_spec=pl...  8.43 us
    ppermute x8, starting transfers between devices, turned(): return lax.ppermute(value, 'head', pairs)  7.89 us
    unnamed x18, local copies, waits for them, and re-layouts  4.01 us
    select_n x2, other arithmetic, rows_of(): jnp.where(is_early(device), sums[0], sums[1])  2.85 us
  transfers between devices with their start and end apart: 16, of which 9 were waited for; matrix products, arithmetic and copies ran while one was open for 7% of the time, Pallas kernels for 31%

profile of v2, /device:TPU:11, one launch (start us, length us, event | category | flops | bytes accessed | tf_op | source)
XLA Modules:
  0.0 132.6 jit_solution(1066395566686463826)
XLA Ops:
  0.6 1.7 %select_bitcast_fusion.2 = (bf16[1,512,256]{2,1,0:T(8,128)(2,1)S(1)}, bf16[1,512,256]{2,1,0:T(8,128)(2,1)S(1)}, bf16[1,512,256]{2,1,0:T(8,128)(2,1)S(1)}, bf16[1...) fusion(pred[]{:T(512)S(6)} %eq.22, ...), kind=kLoop, calls=%fused_computation.27 | loop fusion | flops 1048576 | bytes 4194306 | tf_op jit(solution)/shard_map/stack | solution.py:192
  2.4 0.3 collective-permute-start.4
  2.8 1.3 collective-permute-start
  4.2 0.6 fusion
  6.0 9.2 %collective-permute-done.4 = bf16[2,512,256]{2,1,0:T(8,128)(2,1)S(1)} collective-permute-done((bf16[2,512,256]{2,1,0:T(8,128)(2,1)S(1)}, bf16[2,512,256]{2,1,0:T(8,128)(2,1)S(1)}, u32[]{:S(2)}, u32[]{:S(2)}) %collective-permute-start.4) | collective-permute-done | bytes 524320 | tf_op jit(solution)/shard_map/ppermute | solution.py:178
  15.3 0.8 copy-done.4
  16.1 1.1 broadcast_select_fusion.8
  17.2 4.6 %collective-permute-start.6 = (bf16[2,512,256]{2,1,0:T(8,128)(2,1)S(1)}, bf16[2,512,256]{2,1,0:T(8,128)(2,1)S(1)}, u32[]{:S(2)}, u32[]{:S(2)}) collective-permute-start(bf16[2,512,256]{2,1,0:T(8,128)(2,1)S(1)} %get-tuple-element.63), channel_id=1, source_target_pairs={{2,0},{4,2},{6,4},{8,6},{10,8},{12,10},{14,12},{16,14},{18,16},{20... | collective-permute-start | bytes 1572872 | tf_op jit(solution)/shard_map/ppermute | solution.py:182
  21.8 3.0 %collective-permute-start.5 = (bf16[2,512,256]{2,1,0:T(8,128)(2,1)S(1)}, bf16[2,512,256]{2,1,0:T(8,128)(2,1)}, u32[]{:S(2)}, u32[]{:S(2)}) collective-permute-start(bf16[2,512,256]{2,1,0:T(8,128)(2,1)S(1)} %get-tuple-element.64), channel_id=1, source_target_pairs={{0,2},{2,4},{4,6},{6,8},{8,10},{10,12},{12,14},{14,16},{16,18},{18... | collective-permute-start | bytes 1572872 | tf_op jit(solution)/shard_map/ppermute | solution.py:182
  26.2 0.3 collective-permute-done
  26.6 3.5 %collective-permute-start.2 = (bf16[2,512,256]{2,1,0:T(8,128)(2,1)S(1)}, bf16[2,512,256]{2,1,0:T(8,128)(2,1)S(1)}, u32[]{:S(2)}, u32[]{:S(2)}) collective-permute-start(bf16[2,512,256]{2,1,0:T(8,128)(2,1)S(1)} %get-tuple-element.73), channel_id=1, source_target_pairs={{2,0},{4,2},{6,4},{8,6},{10,8},{12,10},{14,12},{16,14},{18,16},{20... | collective-permute-start | bytes 1572872 | tf_op jit(solution)/shard_map/ppermute | solution.py:182
  30.1 3.0 %collective-permute-start.1 = (bf16[2,512,256]{2,1,0:T(8,128)(2,1)S(1)}, bf16[2,512,256]{2,1,0:T(8,128)(2,1)S(1)}, u32[]{:S(2)}, u32[]{:S(2)}) collective-permute-start(bf16[2,512,256]{2,1,0:T(8,128)(2,1)S(1)} %get-tuple-element.74), channel_id=1, source_target_pairs={{0,2},{2,4},{4,6},{6,8},{8,10},{10,12},{12,14},{14,16},{16,18},{18... | collective-permute-start | bytes 1572872 | tf_op jit(solution)/shard_map/ppermute | solution.py:182
  33.1 0.1 pad_dynamic-slice_fusion
  33.2 1.0 convert_reduce_fusion
  34.2 7.2 %collective-permute-done.6 = bf16[2,512,256]{2,1,0:T(8,128)(2,1)S(1)} collective-permute-done((bf16[2,512,256]{2,1,0:T(8,128)(2,1)S(1)}, bf16[2,512,256]{2,1,0:T(8,128)(2,1)S(1)}, u32[]{:S(2)}, u32[]{:S(2)}) %collective-permute-start.6) | collective-permute-done | bytes 524320 | tf_op jit(solution)/shard_map/ppermute | solution.py:182
  41.3 1.9 %broadcast_select_fusion.6 = (bf16[2,512,256]{2,1,0:T(8,128)(2,1)}, bf16[2,512,256]{2,1,0:T(8,128)(2,1)S(1)}) fusion(bf16[2,512,256]{2,1,0:T(8,128)(2,1)} %collective-permute-done.5, pred[]{:T(512)S(6)} %eq.54, bf16[2,512,256]{2,1,0:T(8,128)(2,1)S(1)} %get-tuple-element.64, bf16[2,512,256]{2,1,0:T(8,128)(2,1)S(1)} %collective-permute-done.6, pred[]{:T(512)S(6)} %eq.26, ...), kind=kLoop, calls=%fused_computation.11 | loop fusion | flops 786432 | bytes 2621443 | tf_op jit(solution)/shard_map/jit(_where)/select_n | solution.py:233
  43.3 0.3 collective-permute-start.7
  43.5 3.4 %collective-permute-done.2 = bf16[2,512,256]{2,1,0:T(8,128)(2,1)S(1)} collective-permute-done((bf16[2,512,256]{2,1,0:T(8,128)(2,1)S(1)}, bf16[2,512,256]{2,1,0:T(8,128)(2,1)S(1)}, u32[]{:S(2)}, u32[]{:S(2)}) %collective-permute-start.2) | collective-permute-done | bytes 524320 | tf_op jit(solution)/shard_map/ppermute | solution.py:182
  47.0 0.9 broadcast_select_fusion.7
  47.8 0.3 collective-permute-start.3
  48.1 8.6 %attention.4 = (bf16[512,2048]{1,0:T(8,128)(2,1)}, f32[512,1024]{1,0:T(8,128)}, f32[512,1024]{1,0:T(8,128)}, bf16[2,512,256]{2,1,0:T(8,128)(2,1)}) custom-call(s32[1]{0:T(128)} %bitcast.12.group_ref, s32[1,512]{1,0:T(1,128)} %bitcast.21, bf16[512,2048]{1,0:T(8,128)(2,1)} %q_ref.7, bf16[512,1024]{1,0:T(8,128)(2,1)} %k_ref.7, bf16[512,1024]{1,0:T(8,128)(2,1)} %v_ref.7, ...), custom_call_target="tpu_custom_call" | custom-call | flops 1677721600 | bytes 2457600 | tf_op jit(solution)/shard_map/attention/pallas_call | solution.py:87
  56.7 8.5 %attention.5 = (bf16[512,2048]{1,0:T(8,128)(2,1)}, f32[512,1024]{1,0:T(8,128)}, f32[512,1024]{1,0:T(8,128)}, bf16[2,512,256]{2,1,0:T(8,128)(2,1)}) custom-call(s32[1]{0:T(128)} %bitcast.12.group_ref, s32[1,512]{1,0:T(1,128)} %bitcast.22, bf16[512,2048]{1,0:T(8,128)(2,1)} %q_ref.7, ...), custom_call_target="tpu_custom_call", output_to_operand_aliasing={{0}: (8, {}), {1}: (9, {}), {2}: (10, {})} | custom-call | flops 1677721600 | bytes 2457600 | tf_op jit(solution)/shard_map/attention/pallas_call | solution.py:87
  65.3 0.8 copy-done.1
  66.0 8.5 %attention.6 = (bf16[512,2048]{1,0:T(8,128)(2,1)}, f32[512,1024]{1,0:T(8,128)}, f32[512,1024]{1,0:T(8,128)}, bf16[2,512,256]{2,1,0:T(8,128)(2,1)}) custom-call(s32[1]{0:T(128)} %bitcast.group_ref, s32[1,512]{1,0:T(1,128)} %bitcast.23, bf16[512,2048]{1,0:T(8,128)(2,1)} %q_ref.7, ...), custom_call_target="tpu_custom_call", output_to_operand_aliasing={{0}: (8, {}), {1}: (9, {}), {2}: (10, {})} | custom-call | flops 1677721600 | bytes 2457600 | tf_op jit(solution)/shard_map/attention/pallas_call | solution.py:87
  74.6 1.3 collective-permute-start.12
  75.9 0.8 copy-done
  76.7 8.6 %attention.7 = (bf16[512,2048]{1,0:T(8,128)(2,1)}, f32[512,1024]{1,0:T(8,128)}, f32[512,1024]{1,0:T(8,128)}, bf16[2,512,256]{2,1,0:T(8,128)(2,1)}) custom-call(s32[1]{0:T(128)} %bitcast.group_ref, s32[1,512]{1,0:T(1,128)} %bitcast.24, bf16[512,2048]{1,0:T(8,128)(2,1)} %q_ref.7, ...), custom_call_target="tpu_custom_call", output_to_operand_aliasing={{0}: (8, {}), {1}: (9, {}), {2}: (10, {})} | custom-call | flops 1677721600 | bytes 2457600 | tf_op jit(solution)/shard_map/attention/pallas_call | solution.py:87
  85.3 0.3 collective-permute-start.8
  85.6 1.9 %collective-permute-start.13 = (bf16[2,512,256]{2,1,0:T(8,128)(2,1)S(1)}, bf16[2,512,256]{2,1,0:T(8,128)(2,1)S(1)}, u32[]{:S(2)}, u32[]{:S(2)}) collective-permute-start(bf16[2,512,256]{2,1,0:T(8,128)(2,1)S(1)} %get-tuple-element.59), channel_id=1, source_target_pairs={{2,0},{4,2},{6,4},{8,6},{10,8},{12,10},{14,12},{16,14},{18,16},{20... | collective-permute-start | bytes 1572872 | tf_op jit(solution)/shard_map/ppermute | solution.py:182
  87.6 6.0 %collective-permute-start.14 = (bf16[2,512,256]{2,1,0:T(8,128)(2,1)S(1)}, bf16[2,512,256]{2,1,0:T(8,128)(2,1)}, u32[]{:S(2)}, u32[]{:S(2)}) collective-permute-start(bf16[2,512,256]{2,1,0:T(8,128)(2,1)S(1)} %get-tuple-element.60), channel_id=1, source_target_pairs={{0,2},{2,4},{4,6},{6,8},{8,10},{10,12},{12,14},{14,16},{16,18},{18... | collective-permute-start | bytes 1572872 | tf_op jit(solution)/shard_map/ppermute | solution.py:182
  93.6 2.0 %collective-permute-done.8 = bf16[2,512,256]{2,1,0:T(8,128)(2,1)S(1)} collective-permute-done((bf16[2,512,256]{2,1,0:T(8,128)(2,1)}, bf16[2,512,256]{2,1,0:T(8,128)(2,1)S(1)}, u32[]{:S(2)}, u32[]{:S(2)}) %collective-permute-start.8) | collective-permute-done | bytes 524320 | tf_op jit(solution)/shard_map/ppermute | solution.py:178
  95.6 0.9 broadcast_select_fusion.3
  96.4 1.9 %collective-permute-start.9 = (bf16[2,512,256]{2,1,0:T(8,128)(2,1)}, bf16[2,512,256]{2,1,0:T(8,128)(2,1)S(1)}, u32[]{:S(2)}, u32[]{:S(2)}) collective-permute-start(bf16[2,512,256]{2,1,0:T(8,128)(2,1)} %get-tuple-element.61), channel_id=1, source_target_pairs={{2,0},{4,2},{6,4},{8,6},{10,8},{12,10},{14,12},{16,14},{18,16},{20... | collective-permute-start | bytes 1572872 | tf_op jit(solution)/shard_map/ppermute | solution.py:182
  98.3 3.6 %collective-permute-start.10 = (bf16[2,512,256]{2,1,0:T(8,128)(2,1)S(1)}, bf16[2,512,256]{2,1,0:T(8,128)(2,1)S(1)}, u32[]{:S(2)}, u32[]{:S(2)}) collective-permute-start(bf16[2,512,256]{2,1,0:T(8,128)(2,1)S(1)} %get-tuple-element.62), channel_id=1, source_target_pairs={{0,2},{2,4},{4,6},{6,8},{8,10},{10,12},{12,14},{14,16},{16,18},{18... | collective-permute-start | bytes 1572872 | tf_op jit(solution)/shard_map/ppermute | solution.py:182
  102.0 8.1 %collective-permute-done.13 = bf16[2,512,256]{2,1,0:T(8,128)(2,1)S(1)} collective-permute-done((bf16[2,512,256]{2,1,0:T(8,128)(2,1)S(1)}, bf16[2,512,256]{2,1,0:T(8,128)(2,1)S(1)}, u32[]{:S(2)}, u32[]{:S(2)}) %collective-permute-start.13) | collective-permute-done | bytes 524320 | tf_op jit(solution)/shard_map/ppermute | solution.py:182
  110.1 2.0 %broadcast_select_fusion = (bf16[2,512,256]{2,1,0:T(8,128)(2,1)}, bf16[2,512,256]{2,1,0:T(8,128)(2,1)S(1)}) fusion(bf16[2,512,256]{2,1,0:T(8,128)(2,1)} %collective-permute-done.14, pred[]{:T(512)S(6)} %eq.57, bf16[2,512,256]{2,1,0:T(8,128)(2,1)S(1)} %get-tuple-element.60, bf16[2,512,256]{2,1,0:T(8,128)(2,1)S(1)} %collective-permute-done.13, pred[]{:T(512)S(6)} %eq.26, ...), kind=kLoop, calls=%fused_computation.5 | loop fusion | flops 786432 | bytes 2621443 | tf_op jit(solution)/shard_map/jit(_where)/select_n | solution.py:289
  112.0 2.1 %collective-permute-start.15 = (bf16[2,512,256]{2,1,0:T(8,128)(2,1)S(1)}, bf16[2,512,256]{2,1,0:T(8,128)(2,1)S(1)}, u32[]{:S(2)}, u32[]{:S(2)}) collective-permute-start(bf16[2,512,256]{2,1,0:T(8,128)(2,1)S(1)} %get-tuple-element.52), channel_id=1, source_target_pairs={{0,1},{1,0},{2,3},{3,2},{4,5},{5,4},{6,7},{7,6},{8,9},{9,8},{10,11... | collective-permute-start | bytes 1572872 | tf_op jit(solution)/shard_map/ppermute | solution.py:178
  114.1 1.6 %collective-permute-done.9 = bf16[2,512,256]{2,1,0:T(8,128)(2,1)S(1)} collective-permute-done((bf16[2,512,256]{2,1,0:T(8,128)(2,1)}, bf16[2,512,256]{2,1,0:T(8,128)(2,1)S(1)}, u32[]{:S(2)}, u32[]{:S(2)}) %collective-permute-start.9) | collective-permute-done | bytes 524320 | tf_op jit(solution)/shard_map/ppermute | solution.py:182
  115.7 0.9 broadcast_select_fusion.1
  116.6 2.1 %collective-permute-start.11 = (bf16[2,512,256]{2,1,0:T(8,128)(2,1)S(1)}, bf16[2,512,256]{2,1,0:T(8,128)(2,1)S(1)}, u32[]{:S(2)}, u32[]{:S(2)}) collective-permute-start(bf16[2,512,256]{2,1,0:T(8,128)(2,1)S(1)} %get-tuple-element.54), channel_id=1, source_target_pairs={{0,1},{1,0},{2,3},{3,2},{4,5},{5,4},{6,7},{7,6},{8,9},{9,8},{10,11... | collective-permute-start | bytes 1572872 | tf_op jit(solution)/shard_map/ppermute | solution.py:178
  118.7 2.1 %finish.4 = (bf16[512,1024]{1,0:T(8,128)(2,1)}, bf16[512,1024]{1,0:T(8,128)(2,1)}) custom-call(s32[1]{0:T(128)} %bitcast.12.group_ref, f32[512,1024]{1,0:T(8,128)} %get-tuple-element.37.dk_ref, f32[512,1024]{1,0:T(8,128)} %get-tuple-element.38.dv_ref, bf16[2,512,256]{2,1,0:T(8,128)(2,1)} %get-tuple-element.51.back_ref), custom_call_target="tpu_custom_call" | custom-call | flops 524288 | bytes 2097152 | tf_op jit(solution)/shard_map/finish/pallas_call | solution.py:133
  120.8 3.3 %collective-permute-done.15.back_ref = bf16[2,512,256]{2,1,0:T(8,128)(2,1)S(1)} collective-permute-done((bf16[2,512,256]{2,1,0:T(8,128)(2,1)S(1)}, bf16[2,512,256]{2,1,0:T(8,128)(2,1)S(1)}, u32[]{:S(2)}, u32[]{:S(2)}) %collective-permute-start.15) | collective-permute-done | bytes 524320 | tf_op jit(solution)/shard_map/ppermute | solution.py:178
  124.1 0.8 copy-done.6
  124.9 2.1 %finish.5 = (bf16[512,1024]{1,0:T(8,128)(2,1)}, bf16[512,1024]{1,0:T(8,128)(2,1)}) custom-call(s32[1]{0:T(128)} %bitcast.group_ref, f32[512,1024]{1,0:T(8,128)} %get-tuple-element.37.dk_ref, f32[512,1024]{1,0:T(8,128)} %get-tuple-element.38.dv_ref, bf16[2,512,256]{2,1,0:T(8,128)(2,1)} %copy-done.6, ...), custom_call_target="tpu_custom_call", output_to_operand_aliasing={{0}: (4, {}), {1}: (5, {})} | custom-call | flops 524288 | bytes 2097152 | tf_op jit(solution)/shard_map/finish/pallas_call | solution.py:133
  127.0 2.1 %finish.6 = (bf16[512,1024]{1,0:T(8,128)(2,1)}, bf16[512,1024]{1,0:T(8,128)(2,1)}) custom-call(s32[1]{0:T(128)} %bitcast.12.group_ref, f32[512,1024]{1,0:T(8,128)} %get-tuple-element.37.dk_ref, f32[512,1024]{1,0:T(8,128)} %get-tuple-element.38.dv_ref, bf16[2,512,256]{2,1,0:T(8,128)(2,1)} %get-tuple-element.53.back_ref, ...), custom_call_target="tpu_custom_call", output_to_operand_aliasing={{0}: (4, {}), {1}: (5, {})} | custom-call | flops 524288 | bytes 2097152 | tf_op jit(solution)/shard_map/finish/pallas_call | solution.py:133
  129.2 0.6 collective-permute-done.11.back_ref
  129.7 0.8 copy-done.5
  130.5 2.1 %finish.7 = (bf16[512,1024]{1,0:T(8,128)(2,1)}, bf16[512,1024]{1,0:T(8,128)(2,1)}) custom-call(s32[1]{0:T(128)} %bitcast.group_ref, f32[512,1024]{1,0:T(8,128)} %get-tuple-element.37.dk_ref, f32[512,1024]{1,0:T(8,128)} %get-tuple-element.38.dv_ref, bf16[2,512,256]{2,1,0:T(8,128)(2,1)} %copy-done.5, ...), custom_call_target="tpu_custom_call", output_to_operand_aliasing={{0}: (4, {}), {1}: (5, {})} | custom-call | flops 524288 | bytes 2097152 | tf_op jit(solution)/shard_map/finish/pallas_call | solution.py:133
  (26 shorter events, 0.4 us)
Async XLA Ops:
  2.4 1.7 %copy-start.8 = (s32[32]{0:T(128)S(1)}, s32[32]{0:T(128)}, u32[]{:S(2)}) copy-start(s32[32]{0:T(128)} %param.13) | copy-start | bytes 388
  2.4 12.9 %collective-permute-start.4 = (bf16[2,512,256]{2,1,0:T(8,128)(2,1)S(1)}, bf16[2,512,256]{2,1,0:T(8,128)(2,1)S(1)}, u32[]{:S(2)}, u32[]{:S(2)}) collective-permute-start(bf16[2,512,256]{2,1,0:T(8,128)(2,1)S(1)} %pad_maximum_fusion.3), channel_id=1, source_target_pairs={{0,1},{1,0},{2,3},{3,2},{4,5},{5,4},{6,7},{7,6},{8,9},{9,8},{10,11... | collective-permute-start | bytes 1572872 | tf_op jit(solution)/shard_map/ppermute | solution.py:178
  2.8 23.7 %collective-permute-start = (bf16[2,512,256]{2,1,0:T(8,128)(2,1)S(1)}, bf16[2,512,256]{2,1,0:T(8,128)(2,1)S(1)}, u32[]{:S(2)}, u32[]{:S(2)}) collective-permute-start(bf16[2,512,256]{2,1,0:T(8,128)(2,1)S(1)} %pad_maximum_fusion.1), channel_id=1, source_target_pairs={{0,1},{1,0},{2,3},{3,2},{4,5},{5,4},{6,7},{7,6},{8,9},{9,8},{10,11... | collective-permute-start | bytes 1572872 | tf_op jit(solution)/shard_map/ppermute | solution.py:178
  15.3 0.8 copy-start.4
  16.1 17.0 %copy-start.7 = (s32[16384]{0:T(1024)S(1)}, s32[16384]{0:T(1024)}, u32[]{:S(2)}) copy-start(s32[16384]{0:T(1024)} %param.12) | copy-start | bytes 196612
  17.2 24.1 %collective-permute-start.6 = (bf16[2,512,256]{2,1,0:T(8,128)(2,1)S(1)}, bf16[2,512,256]{2,1,0:T(8,128)(2,1)S(1)}, u32[]{:S(2)}, u32[]{:S(2)}) collective-permute-start(bf16[2,512,256]{2,1,0:T(8,128)(2,1)S(1)} %get-tuple-element.63), channel_id=1, source_target_pairs={{2,0},{4,2},{6,4},{8,6},{10,8},{12,10},{14,12},{16,14},{18,16},{20... | collective-permute-start | bytes 1572872 | tf_op jit(solution)/shard_map/ppermute | solution.py:182
  21.8 19.5 %collective-permute-start.5 = (bf16[2,512,256]{2,1,0:T(8,128)(2,1)S(1)}, bf16[2,512,256]{2,1,0:T(8,128)(2,1)}, u32[]{:S(2)}, u32[]{:S(2)}) collective-permute-start(bf16[2,512,256]{2,1,0:T(8,128)(2,1)S(1)} %get-tuple-element.64), channel_id=1, source_target_pairs={{0,2},{2,4},{4,6},{6,8},{8,10},{10,12},{12,14},{14,16},{16,18},{18... | collective-permute-start | bytes 1572872 | tf_op jit(solution)/shard_map/ppermute | solution.py:182
  26.6 20.4 %collective-permute-start.2 = (bf16[2,512,256]{2,1,0:T(8,128)(2,1)S(1)}, bf16[2,512,256]{2,1,0:T(8,128)(2,1)S(1)}, u32[]{:S(2)}, u32[]{:S(2)}) collective-permute-start(bf16[2,512,256]{2,1,0:T(8,128)(2,1)S(1)} %get-tuple-element.73), channel_id=1, source_target_pairs={{2,0},{4,2},{6,4},{8,6},{10,8},{12,10},{14,12},{16,14},{18,16},{20... | collective-permute-start | bytes 1572872 | tf_op jit(solution)/shard_map/ppermute | solution.py:182
  30.1 16.9 %collective-permute-start.1 = (bf16[2,512,256]{2,1,0:T(8,128)(2,1)S(1)}, bf16[2,512,256]{2,1,0:T(8,128)(2,1)S(1)}, u32[]{:S(2)}, u32[]{:S(2)}) collective-permute-start(bf16[2,512,256]{2,1,0:T(8,128)(2,1)S(1)} %get-tuple-element.74), channel_id=1, source_target_pairs={{0,2},{2,4},{4,6},{6,8},{8,10},{10,12},{12,14},{14,16},{16,18},{18... | collective-permute-start | bytes 1572872 | tf_op jit(solution)/shard_map/ppermute | solution.py:182
  43.3 22.0 %collective-permute-start.7 = (bf16[2,512,256]{2,1,0:T(8,128)(2,1)S(1)}, bf16[2,512,256]{2,1,0:T(8,128)(2,1)S(1)}, u32[]{:S(2)}, u32[]{:S(2)}) collective-permute-start(bf16[2,512,256]{2,1,0:T(8,128)(2,1)S(1)} %get-tuple-element.56), channel_id=1, source_target_pairs={{0,1},{1,0},{2,3},{3,2},{4,5},{5,4},{6,7},{7,6},{8,9},{9,8},{10,11... | collective-permute-start | bytes 1572872 | tf_op jit(solution)/shard_map/ppermute | solution.py:178
  47.8 28.0 %collective-permute-start.3 = (bf16[2,512,256]{2,1,0:T(8,128)(2,1)S(1)}, bf16[2,512,256]{2,1,0:T(8,128)(2,1)S(1)}, u32[]{:S(2)}, u32[]{:S(2)}) collective-permute-start(bf16[2,512,256]{2,1,0:T(8,128)(2,1)S(1)} %get-tuple-element.58), channel_id=1, source_target_pairs={{0,1},{1,0},{2,3},{3,2},{4,5},{5,4},{6,7},{7,6},{8,9},{9,8},{10,11... | collective-permute-start | bytes 1572872 | tf_op jit(solution)/shard_map/ppermute | solution.py:178
  65.2 0.8 copy-start.1
  74.6 11.0 %collective-permute-start.12 = (bf16[2,512,256]{2,1,0:T(8,128)(2,1)}, bf16[2,512,256]{2,1,0:T(8,128)(2,1)S(1)}, u32[]{:S(2)}, u32[]{:S(2)}) collective-permute-start(bf16[2,512,256]{2,1,0:T(8,128)(2,1)} %get-tuple-element.42), channel_id=1, source_target_pairs={{0,1},{1,0},{2,3},{3,2},{4,5},{5,4},{6,7},{7,6},{8,9},{9,8},{10,11... | collective-permute-start | bytes 1572872 | tf_op jit(solution)/shard_map/ppermute | solution.py:178
  75.9 0.8 copy-start
  76.7 8.9 %copy-start.3 = (bf16[2,512,256]{2,1,0:T(8,128)(2,1)S(1)}, bf16[2,512,256]{2,1,0:T(8,128)(2,1)}, u32[]{:S(2)}) copy-start(bf16[2,512,256]{2,1,0:T(8,128)(2,1)} %get-tuple-element.41) | copy-start | bytes 1572868
  85.3 10.3 %copy-start.2 = (bf16[2,512,256]{2,1,0:T(8,128)(2,1)S(1)}, bf16[2,512,256]{2,1,0:T(8,128)(2,1)}, u32[]{:S(2)}) copy-start(bf16[2,512,256]{2,1,0:T(8,128)(2,1)} %get-tuple-element.39) | copy-start | bytes 1572868
  85.3 10.3 %collective-permute-start.8 = (bf16[2,512,256]{2,1,0:T(8,128)(2,1)}, bf16[2,512,256]{2,1,0:T(8,128)(2,1)S(1)}, u32[]{:S(2)}, u32[]{:S(2)}) collective-permute-start(bf16[2,512,256]{2,1,0:T(8,128)(2,1)} %get-tuple-element.40), channel_id=1, source_target_pairs={{0,1},{1,0},{2,3},{3,2},{4,5},{5,4},{6,7},{7,6},{8,9},{9,8},{10,11... | collective-permute-start | bytes 1572872 | tf_op jit(solution)/shard_map/ppermute | solution.py:178
  85.6 24.4 %collective-permute-start.13 = (bf16[2,512,256]{2,1,0:T(8,128)(2,1)S(1)}, bf16[2,512,256]{2,1,0:T(8,128)(2,1)S(1)}, u32[]{:S(2)}, u32[]{:S(2)}) collective-permute-start(bf16[2,512,256]{2,1,0:T(8,128)(2,1)S(1)} %get-tuple-element.59), channel_id=1, source_target_pairs={{2,0},{4,2},{6,4},{8,6},{10,8},{12,10},{14,12},{16,14},{18,16},{20... | collective-permute-start | bytes 1572872 | tf_op jit(solution)/shard_map/ppermute | solution.py:182
  87.6 22.5 %collective-permute-start.14 = (bf16[2,512,256]{2,1,0:T(8,128)(2,1)S(1)}, bf16[2,512,256]{2,1,0:T(8,128)(2,1)}, u32[]{:S(2)}, u32[]{:S(2)}) collective-permute-start(bf16[2,512,256]{2,1,0:T(8,128)(2,1)S(1)} %get-tuple-element.60), channel_id=1, source_target_pairs={{0,2},{2,4},{4,6},{6,8},{8,10},{10,12},{12,14},{14,16},{16,18},{18... | collective-permute-start | bytes 1572872 | tf_op jit(solution)/shard_map/ppermute | solution.py:182
  96.4 19.2 %collective-permute-start.9 = (bf16[2,512,256]{2,1,0:T(8,128)(2,1)}, bf16[2,512,256]{2,1,0:T(8,128)(2,1)S(1)}, u32[]{:S(2)}, u32[]{:S(2)}) collective-permute-start(bf16[2,512,256]{2,1,0:T(8,128)(2,1)} %get-tuple-element.61), channel_id=1, source_target_pairs={{2,0},{4,2},{6,4},{8,6},{10,8},{12,10},{14,12},{16,14},{18,16},{20... | collective-permute-start | bytes 1572872 | tf_op jit(solution)/shard_map/ppermute | solution.py:182
  98.3 17.3 %collective-permute-start.10 = (bf16[2,512,256]{2,1,0:T(8,128)(2,1)S(1)}, bf16[2,512,256]{2,1,0:T(8,128)(2,1)S(1)}, u32[]{:S(2)}, u32[]{:S(2)}) collective-permute-start(bf16[2,512,256]{2,1,0:T(8,128)(2,1)S(1)} %get-tuple-element.62), channel_id=1, source_target_pairs={{0,2},{2,4},{4,6},{6,8},{8,10},{10,12},{12,14},{14,16},{16,18},{18... | collective-permute-start | bytes 1572872 | tf_op jit(solution)/shard_map/ppermute | solution.py:182
  112.0 12.1 %collective-permute-start.15 = (bf16[2,512,256]{2,1,0:T(8,128)(2,1)S(1)}, bf16[2,512,256]{2,1,0:T(8,128)(2,1)S(1)}, u32[]{:S(2)}, u32[]{:S(2)}) collective-permute-start(bf16[2,512,256]{2,1,0:T(8,128)(2,1)S(1)} %get-tuple-element.52), channel_id=1, source_target_pairs={{0,1},{1,0},{2,3},{3,2},{4,5},{5,4},{6,7},{7,6},{8,9},{9,8},{10,11... | collective-permute-start | bytes 1572872 | tf_op jit(solution)/shard_map/ppermute | solution.py:178
  116.6 13.2 %collective-permute-start.11 = (bf16[2,512,256]{2,1,0:T(8,128)(2,1)S(1)}, bf16[2,512,256]{2,1,0:T(8,128)(2,1)S(1)}, u32[]{:S(2)}, u32[]{:S(2)}) collective-permute-start(bf16[2,512,256]{2,1,0:T(8,128)(2,1)S(1)} %get-tuple-element.54), channel_id=1, source_target_pairs={{0,1},{1,0},{2,3},{3,2},{4,5},{5,4},{6,7},{7,6},{8,9},{9,8},{10,11... | collective-permute-start | bytes 1572872 | tf_op jit(solution)/shard_map/ppermute | solution.py:178
  124.1 0.8 copy-start.6
  129.7 0.8 copy-start.5

commit v3 on v2

v3 whole, which is shorter than its diff:
```python
import functools

import jax
import jax.numpy as jnp
from jax import lax
from jax.experimental import pallas as pl
from jax.experimental.pallas import tpu as pltpu
from jax.sharding import PartitionSpec as P

HEAD_SIZE = 128
NEGATIVE = -1e30
LOG2_E = 1.4426950408889634
CHUNKS = 2
TILE = 128
OWN_STEP = 2
VMEM_BYTES = 60 * 1024 * 1024


def dot(left, right, left_dim, right_dim):
    return lax.dot_general(
        left, right, (((left_dim,), (right_dim,)), ((), ())), preferred_element_type=jnp.float32
    )


def stacked(ref, start, head):
    return jnp.concatenate(
        [
            ref[start : start + TILE, column : column + head]
            for column in range(0, ref.shape[1], head)
        ],
        axis=0,
    )


def seen_scores(keys, queries, low, first, causal):
    scores = dot(keys, queries, 1, 1)
    key_index = lax.broadcasted_iota(jnp.int32, scores.shape, 0)
    visible = key_index >= low - first
    if causal:
        lane = lax.broadcasted_iota(jnp.int32, (1, scores.shape[1]), 1)
        visible &= key_index <= keys.shape[0] - TILE + lane % TILE
    return jnp.where(visible, scores, NEGATIVE)


def low_of(low_ref, start, members):
    return jnp.concatenate([low_ref[:, start : start + TILE]] * members, axis=1)


def for_each_tile(first_ref, rows, blocks_of, body):
    for tile in range(rows // TILE):
        for block in blocks_of(tile):
            pl.when(first_ref[tile] == block)(functools.partial(body, tile, block))


def own_stats_body(first_ref, low_ref, q_ref, k_ref, o_ref, do_ref, stats_ref):
    rows, head = k_ref.shape
    members = q_ref.shape[1] // head

    def body(tile, block):
        start, begin = tile * TILE, block * TILE
        queries, grads = stacked(q_ref, start, head), stacked(do_ref, start, head)
        product = grads.astype(jnp.float32) * stacked(o_ref, start, head).astype(jnp.float32)
        scores = seen_scores(
            k_ref[begin : start + TILE], queries, low_of(low_ref, start, members), begin, True
        )
        top = jnp.max(scores, axis=0, keepdims=True)
        total = jnp.sum(jnp.exp2((scores - top) * (head**-0.5 * LOG2_E)), axis=0, keepdims=True)
        lanes = pl.ds(tile * members * TILE, members * TILE)
        stats_ref[0, 0:1, lanes] = top
        stats_ref[0, 1:2, lanes] = total
        stats_ref[0, 2:3, lanes] = jnp.sum(product.T, axis=0, keepdims=True)

    for_each_tile(first_ref, rows, lambda tile: range(tile + 1), body)


def window_body(
    carried, group_ref, first_ref, low_ref, q_ref, do_ref, past_ref, stats_ref, *refs
):
    merged_ref, turned_ref, back_ref, k_turned, dk_sum, dv_sum = refs[carried:]
    window, head = past_ref.shape[1:]
    rows = q_ref.shape[0]
    members = q_ref.shape[1] // head
    factor = head**-0.5 * LOG2_E
    dk_sum[...] = jnp.zeros_like(dk_sum)
    dv_sum[...] = jnp.zeros_like(dv_sum)
    turned_ref[...] = jnp.zeros_like(turned_ref)
    merged_ref[0, 0:1] = stats_ref[0, 0:1]
    merged_ref[0, 1:2] = 1.0 / stats_ref[0, 1:2]
    merged_ref[0, 2:3] = stats_ref[0, 2:3]
    k_turned[...] = past_ref[0].T

    def body(tile, block):
        start, begin = tile * TILE, block * TILE
        lanes = pl.ds(tile * members * TILE, members * TILE)
        queries, grads = stacked(q_ref, start, head), stacked(do_ref, start, head)
        scores = seen_scores(
            past_ref[0, begin:], queries, low_of(low_ref, start, members), begin, False
        )
        own_top, own_total = stats_ref[0, 0:1, lanes], stats_ref[0, 1:2, lanes]
        top = jnp.maximum(own_top, jnp.max(scores, axis=0, keepdims=True))
        terms = jnp.exp2((scores - top) * factor)
        total = own_total * jnp.exp2((own_top - top) * factor)
        inverse = 1.0 / (total + jnp.sum(terms, axis=0, keepdims=True))
        merged_ref[0, 0:1, lanes] = top
        merged_ref[0, 1:2, lanes] = inverse
        weights = terms * inverse
        weight_grads = dot(past_ref[1, begin:], grads, 1, 1)
        score_grads = weights * (weight_grads - stats_ref[0, 2:3, lanes])
        score_grads = score_grads.astype(jnp.bfloat16)
        dv_sum[begin:] += dot(weights.astype(jnp.bfloat16), grads, 1, 0)
        dk_sum[begin:] += dot(score_grads, queries, 1, 0)
        turned_ref[0, :, lanes] = dot(k_turned[:, begin:], score_grads, 1, 0)

    for_each_tile(first_ref, rows, lambda tile: range(tile, window // TILE), body)
    back_ref[0] = dk_sum[...].astype(back_ref.dtype)
    back_ref[1] = dv_sum[...].astype(back_ref.dtype)


def own_body(
    carried, first_ref, low_ref, q_ref, k_ref, v_ref, do_ref, merged_ref, turned_ref, *refs
):
    dq_ref, dk_ref, dv_ref, k_turned = refs[carried:]
    rows, head = k_ref.shape
    members = q_ref.shape[1] // head
    scale = head**-0.5
    dk_ref[...] = jnp.zeros_like(dk_ref)
    dv_ref[...] = jnp.zeros_like(dv_ref)
    k_turned[...] = k_ref[...].T

    def body(tile, block):
        start, begin = tile * TILE, block * TILE
        end = start + TILE
        lanes = pl.ds(tile * members * TILE, members * TILE)
        queries, grads = stacked(q_ref, start, head), stacked(do_ref, start, head)
        scores = seen_scores(
            k_ref[begin:end], queries, low_of(low_ref, start, members), begin, True
        )
        terms = jnp.exp2((scores - merged_ref[0, 0:1, lanes]) * (scale * LOG2_E))
        weights = terms * merged_ref[0, 1:2, lanes]
        weight_grads = dot(v_ref[begin:end], grads, 1, 1)
        score_grads = weights * (weight_grads - merged_ref[0, 2:3, lanes])
        score_grads = score_grads.astype(jnp.bfloat16)
        dv_ref[begin:end] += dot(weights.astype(jnp.bfloat16), grads, 1, 0)
        dk_ref[begin:end] += dot(score_grads, queries, 1, 0)
        turned = turned_ref[0, :, lanes] + dot(k_turned[:, begin:end], score_grads, 1, 0)
        dq = (turned * scale).T
        for m in range(members):
            dq_ref[start:end, m * head : (m + 1) * head] = dq[
                m * TILE : (m + 1) * TILE
            ].astype(dq_ref.dtype)

    for_each_tile(first_ref, rows, lambda tile: range(tile + 1), body)


def cost(count, rows, keys, members, products):
    tiles = count * members * rows * keys
    return pl.CostEstimate(
        flops=2 * products * tiles * HEAD_SIZE,
        bytes_accessed=count * rows * members * HEAD_SIZE * 16,
        transcendentals=tiles,
    )


def specs_of(row_arrays, head_index):
    queries, keys = row_arrays[:2]
    rows, members = keys.shape[0], queries.shape[1] // keys.shape[1]

    def column(*at):
        return (0, head_index(*at))

    def leading(*at):
        return (head_index(*at), 0, 0)

    return (
        pl.BlockSpec((rows, members * HEAD_SIZE), column),
        pl.BlockSpec((rows, HEAD_SIZE), column),
        pl.BlockSpec((1, 3, members * rows), leading),
        pl.BlockSpec((1, HEAD_SIZE, members * rows), leading),
    )


def whole_spec(array):
    return pl.BlockSpec(array.shape, lambda *at: (0,) * array.ndim)


def own_stats(first, low, row_arrays):
    queries, keys, values, outputs, grads = row_arrays
    rows, heads = keys.shape[0], keys.shape[1] // HEAD_SIZE
    members = queries.shape[1] // keys.shape[1]
    query_spec, key_spec, stats_spec, _ = specs_of(row_arrays, lambda step, first_ref: step)
    return pl.pallas_call(
        own_stats_body,
        grid_spec=pltpu.PrefetchScalarGridSpec(
            num_scalar_prefetch=1,
            grid=(heads,),
            in_specs=[whole_spec(low), query_spec, key_spec, query_spec, query_spec],
            out_specs=stats_spec,
        ),
        out_shape=jax.ShapeDtypeStruct((heads, 3, members * rows), jnp.float32),
        compiler_params=pltpu.CompilerParams(vmem_limit_bytes=VMEM_BYTES),
        cost_estimate=cost(heads, rows, rows // 2, members, 1),
        name="own_stats",
    )(first, low, queries, keys, outputs, grads)


def window_terms(group, first, low, row_arrays, past, stats, first_head, heads_per_group, carried):
    queries, keys, values, outputs, grads = row_arrays
    rows, heads = keys.shape[0], keys.shape[1] // HEAD_SIZE
    window, count = past.shape[1], past.shape[2] // HEAD_SIZE
    members = queries.shape[1] // keys.shape[1]
    query_spec, _, stats_spec, turned_spec = specs_of(
        row_arrays,
        lambda step, group_ref, first_ref: group_ref[0] * heads_per_group + first_head + step,
    )
    past_spec = pl.BlockSpec((2, window, HEAD_SIZE), lambda step, *refs: (0, 0, step))
    return pl.pallas_call(
        functools.partial(window_body, len(carried)),
        grid_spec=pltpu.PrefetchScalarGridSpec(
            num_scalar_prefetch=2,
            grid=(count,),
            in_specs=[whole_spec(low), query_spec, query_spec, past_spec, stats_spec]
            + [pl.BlockSpec(memory_space=pl.ANY)] * len(carried),
            out_specs=[stats_spec, turned_spec, past_spec],
            scratch_shapes=[
                pltpu.VMEM((HEAD_SIZE, window), jnp.bfloat16),
                pltpu.VMEM((window, HEAD_SIZE), jnp.float32),
                pltpu.VMEM((window, HEAD_SIZE), jnp.float32),
            ],
        ),
        out_shape=[
            jax.ShapeDtypeStruct(stats.shape, jnp.float32),
            jax.ShapeDtypeStruct((heads, HEAD_SIZE, members * rows), jnp.float32),
            jax.ShapeDtypeStruct(past.shape, jnp.bfloat16),
        ],
        input_output_aliases={7 + i: i for i in range(len(carried))},
        compiler_params=pltpu.CompilerParams(vmem_limit_bytes=VMEM_BYTES),
        cost_estimate=cost(count, rows, window // 4, members, 5),
        name="window_terms",
    )(group, first, low, queries, grads, past, stats, *carried)


def own_terms(first, low, row_arrays, merged, turned, first_head, count, carried):
    queries, keys, values, outputs, grads = row_arrays
    rows, members = keys.shape[0], queries.shape[1] // keys.shape[1]
    query_spec, key_spec, stats_spec, turned_spec = specs_of(
        row_arrays, lambda step, first_ref: first_head + step
    )
    return pl.pallas_call(
        functools.partial(own_body, len(carried)),
        grid_spec=pltpu.PrefetchScalarGridSpec(
            num_scalar_prefetch=1,
            grid=(count,),
            in_specs=[
                whole_spec(low), query_spec, key_spec, key_spec, query_spec, stats_spec, turned_spec
            ]
            + [pl.BlockSpec(memory_space=pl.ANY)] * len(carried),
            out_specs=[query_spec, key_spec, key_spec],
            scratch_shapes=[pltpu.VMEM((HEAD_SIZE, rows), jnp.bfloat16)],
        ),
        out_shape=[
            jax.ShapeDtypeStruct(queries.shape, jnp.bfloat16),
            jax.ShapeDtypeStruct(keys.shape, jnp.float32),
            jax.ShapeDtypeStruct(keys.shape, jnp.float32),
        ],
        input_output_aliases={8 + i: i for i in range(len(carried))},
        compiler_params=pltpu.CompilerParams(vmem_limit_bytes=VMEM_BYTES),
        cost_estimate=cost(count, rows, rows // 2, members, 5),
        name="own_terms",
    )(first, low, queries, keys, values, grads, merged, turned, *carried)


def finish_body(carried, group_ref, dk_ref, dv_ref, back_ref, *refs):
    key_out, value_out = refs[carried:]
    scale = HEAD_SIZE**-0.5
    key_out[...] = ((dk_ref[...] + back_ref[0].astype(jnp.float32)) * scale).astype(key_out.dtype)
    value_out[...] = (dv_ref[...] + back_ref[1].astype(jnp.float32)).astype(value_out.dtype)


def finish(group, own, back, first_head, heads_per_group, carried):
    rows, count = back.shape[1], back.shape[2] // HEAD_SIZE

    def column(step, group_ref):
        return (0, group_ref[0] * heads_per_group + first_head + step)

    key_spec = pl.BlockSpec((rows, HEAD_SIZE), column)
    back_spec = pl.BlockSpec((2, rows, HEAD_SIZE), lambda step, group_ref: (0, 0, step))
    return pl.pallas_call(
        functools.partial(finish_body, len(carried)),
        grid_spec=pltpu.PrefetchScalarGridSpec(
            num_scalar_prefetch=1,
            grid=(count,),
            in_specs=[key_spec, key_spec, back_spec]
            + [pl.BlockSpec(memory_space=pl.ANY)] * len(carried),
            out_specs=[key_spec, key_spec],
        ),
        out_shape=[jax.ShapeDtypeStruct(own[0].shape, jnp.bfloat16)] * 2,
        input_output_aliases={4 + i: i for i in range(len(carried))},
        compiler_params=pltpu.CompilerParams(vmem_limit_bytes=VMEM_BYTES),
        cost_estimate=pl.CostEstimate(
            flops=count * rows * 512, bytes_accessed=count * rows * 2048, transcendentals=0
        ),
        name="finish",
    )(group, *own, back, *carried)


def together(*values):
    return lax.optimization_barrier(values)


def pick(items, index):
    result = items[-1]
    for place in range(len(items) - 2, -1, -1):
        result = jnp.where(index == place, items[place], result)
    return result


def local(queries, keys, values, outputs, out_grads, segment_ids, block_order):
    blocks, sharers = lax.axis_size("blk"), lax.axis_size("head")
    block, place = lax.axis_index("blk"), lax.axis_index("head")
    rows = keys.shape[0]
    window = rows * sharers // 2
    parts = sharers // 2
    key_heads = keys.shape[1] // HEAD_SIZE
    heads_per_group = key_heads // sharers
    chunks = min(CHUNKS, heads_per_group)
    per_piece = heads_per_group // chunks
    slots = lax.dynamic_slice_in_dim(block_order, 2 * block, 2)
    early_slot = (slots[0] > slots[1]).astype(jnp.int32)
    last_block = block == blocks - 1

    def other(turn):
        return lax.rem(place + turn + sharers, sharers)

    def turned(value, turn):
        pairs = [(source, (source + turn) % sharers) for source in range(sharers)]
        return lax.ppermute(value, "head", pairs)

    def shifted(value, step):
        first, end = max(0, -step), min(blocks, blocks - step)
        return lax.ppermute(value, "blk", [(source, source + step) for source in range(first, end)])

    def columns(array, group, chunk):
        pieces = []
        for g in range(sharers):
            start = (g * heads_per_group + chunk * per_piece) * HEAD_SIZE
            pieces.append(array[:, start : start + per_piece * HEAD_SIZE])
        return pick(pieces, group)

    def piece_of(group, chunk):
        return jnp.stack([columns(keys, group, chunk), columns(values, group, chunk)])

    def is_early(device):
        return device // parts == early_slot

    def part_rows(array, device, count):
        if parts == 1:
            return array[:, :count]
        return lax.dynamic_slice_in_dim(array, device % parts * rows, count, 1)

    my_half = pick([slots[0], slots[1]], place // parts)
    start = my_half * window + place % parts * rows
    padded = jnp.concatenate([jnp.full((window,), -1, jnp.int32), segment_ids])
    near = lax.dynamic_slice_in_dim(padded, start, window + rows)
    low = jnp.sum((near[None, :] < near[window:, None]).astype(jnp.int32), axis=1)[None, :]

    tile_low = low[0, ::TILE]
    first_past = tile_low // TILE
    first_own = jnp.maximum(tile_low - window, 0) // TILE

    row_arrays = (queries, keys, values, outputs, out_grads)
    groups = [other(-turn) for turn in range(sharers)]

    def halves_of(pieces):
        return [
            jnp.concatenate(
                [
                    pick(pieces, lax.rem(place - (slot * parts + p) + sharers, sharers))
                    for p in range(parts)
                ],
                axis=1,
            )
            for slot in (early_slot, 1 - early_slot)
        ]

    pieces = [
        [piece_of(place, chunk)]
        + [turned(piece_of(other(turn), chunk), turn) for turn in range(1, sharers)]
        for chunk in range(chunks)
    ]
    stats = own_stats(first_own, low - window, row_arrays)
    stats, pieces[0][-1] = together(stats, pieces[0][-1])
    halves = [halves_of(pieces[chunk]) for chunk in range(chunks)]
    before = [(shifted(early, 1), shifted(late, -1)) for early, late in halves]

    merged, own_backs, pasts = (), [], []
    for chunk in range(chunks):
        (early, late), (before_early, before_late) = halves[chunk], before[chunk]
        if chunk:
            *merged, before_early, before_late = together(*merged, before_early, before_late)
        before_late = jnp.where(last_block, early, before_late)

        def past_of(device):
            before = jnp.where(is_early(device), before_early, before_late)
            if parts == 1:
                return before
            own = jnp.where(is_early(device), early, late)
            return part_rows(jnp.concatenate([before, own], axis=1), device, window)

        pasts.append([turned(past_of(other(turn)), turn) for turn in range(1, sharers)])
        *merged, back = window_terms(
            groups[0].reshape(1), first_past, low, row_arrays, past_of(place), stats,
            chunk * per_piece, heads_per_group, tuple(merged),
        )
        own_backs.append(back)

    terms = [[back] for back in own_backs]
    for chunk in range(chunks):
        for turn in range(1, sharers):
            *merged, back = window_terms(
                groups[turn].reshape(1), first_past, low, row_arrays, pasts[chunk][turn - 1], stats,
                chunk * per_piece, heads_per_group, tuple(merged),
            )
            terms[chunk].append(turned(back, -turn))

    carried = ()
    for head in range(0, key_heads, OWN_STEP):
        carried = own_terms(
            first_own, low - window, row_arrays, *merged, head, OWN_STEP, tuple(carried)
        )
        step = head // OWN_STEP
        if step % 2 and step // 2 < chunks:
            chunk = step // 2
            *carried, terms[chunk][-1] = together(*carried, terms[chunk][-1])
    query_grads, *own = carried
    results = ()
    for chunk in range(chunks):
        to_before, to_own = [], []
        for slot in (early_slot, 1 - early_slot):
            if parts == 1:
                to_before.append(pick(terms[chunk], lax.rem(slot - place + sharers, sharers)))
                to_own.append(None)
            else:
                total = jnp.zeros((2, 2 * window, terms[chunk][0].shape[2]), jnp.float32)
                for turn in range(sharers):
                    device = other(turn)
                    mine = jnp.where(device // parts == slot, terms[chunk][turn].astype(jnp.float32), 0.0)
                    wide = jnp.pad(mine, ((0, 0), (window, window), (0, 0)))
                    total += lax.dynamic_slice_in_dim(
                        wide, window - device % parts * rows, 2 * window, 1
                    )
                to_before.append(total[:, :window].astype(jnp.bfloat16))
                to_own.append(total[:, window:])
        for_early, for_late = shifted(to_before[0], -1), shifted(to_before[1], 1)
        for_early = jnp.where(last_block, to_before[1], for_early)
        sums = [
            came if more is None else (came.astype(jnp.float32) + more).astype(jnp.bfloat16)
            for came, more in zip((for_early, for_late), to_own)
        ]

        def rows_of(device):
            return part_rows(jnp.where(is_early(device), sums[0], sums[1]), device, rows)

        for turn in range(sharers):
            back = rows_of(other(turn))
            if turn:
                back = turned(back, turn)
            results = finish(
                groups[turn].reshape(1),
                own,
                back,
                chunk * per_piece,
                heads_per_group,
                tuple(results),
            )
    return (query_grads, *results)


def solution(mesh):
    spread = P(("blk", "head"), None)
    return jax.shard_map(
        local,
        mesh=mesh,
        in_specs=(spread,) * 5 + (P(), P()),
        out_specs=(spread,) * 3,
        check_vma=False,
    )
```

time: 134 us -> 150 us (1.12)
  Pallas kernels: 42.7 us -> 77.6 us
  starting transfers between devices: 35.5 us -> 25.4 us
  waiting for transfers between devices: 35.6 us -> 28.6 us
    pallas_call x4 -> x9, Pallas kernels: 34.2 us -> 69.2 us  [the longest x4 30.1 us: own_terms(): pl.pallas_call(functools.partial(own_body, len(carried)), grid_spec=pltpu...]
    ppermute x8, waiting for transfers between devices: 15.4 us -> 7.7 us  [turned(): return lax.ppermute(value, 'head', pairs)]
    ppermute x8, starting transfers between devices: 7.89 us -> 2.34 us  [turned(): return lax.ppermute(value, 'head', pairs)]
    ppermute x8, starting transfers between devices: 27.6 us -> 23 us  [shifted(): lax.ppermute(value, 'blk', [(source, source + step) for source in range(f...]
    unnamed x18 -> x16, local copies, waits for them, and re-layouts: 4.01 us -> 2.42 us
  transfers between devices with their start and end apart: 16 -> 16, of which waited for: 9 -> 4; matrix products, arithmetic and copies ran while one was open for 7% -> 7% of each run, Pallas kernels for 31% -> 51%
where the time goes in v3:
time: 150 us; the launch traced here: 149 us
  Pallas kernels  77.6 us (52%)
  waiting for transfers between devices  28.6 us (19%)
  starting transfers between devices  25.4 us (17%)
  other arithmetic  10.9 us (7%)
  between operations  3.52 us (2%)
  local copies, waits for them, and re-layouts  3.27 us (2%)
    pallas_call x4, Pallas kernels, own_terms(): pl.pallas_call(functools.partial(own_body, len(carried)), grid_spec=pltpu...  30.1 us
    pallas_call x4, Pallas kernels, window_terms(): pl.pallas_call(functools.partial(window_body, len(carried)), grid_spec=pl...  26.9 us
    ppermute x8, starting transfers between devices, shifted(): lax.ppermute(value, 'blk', [(source, source + step) for source in range(f...  23 us
    ppermute x8, waiting for transfers between devices, shifted(): lax.ppermute(value, 'blk', [(source, source + step) for source in range(f...  20.9 us
    pallas_call x1, Pallas kernels, own_stats(): pl.pallas_call(own_stats_body, grid_spec=pltpu.PrefetchScalarGridSpec(num...  12.2 us
    pallas_call x4, Pallas kernels, finish(): pl.pallas_call(functools.partial(finish_body, len(carried)), grid_spec=pl...  8.46 us
    ppermute x8, waiting for transfers between devices, turned(): return lax.ppermute(value, 'head', pairs)  7.7 us
  transfers between devices with their start and end apart: 16, of which 4 were waited for; matrix products, arithmetic and copies ran while one was open for 7% of the time, Pallas kernels for 51%

profile of v3, /device:TPU:11, one launch (start us, length us, event | category | flops | bytes accessed | tf_op | source)
XLA Modules:
  0.0 149.3 jit_solution(17416086736835449987)
XLA Ops:
  0.6 1.7 %select_bitcast_fusion.2 = (bf16[1,512,256]{2,1,0:T(8,128)(2,1)S(1)}, bf16[1,512,256]{2,1,0:T(8,128)(2,1)S(1)}, bf16[1,512,256]{2,1,0:T(8,128)(2,1)S(1)}, bf16[1...) fusion(pred[]{:T(512)S(6)} %eq.22, ...), kind=kLoop, calls=%fused_computation.27 | loop fusion | flops 1048576 | bytes 4194306 | tf_op jit(solution)/shard_map/stack | solution.py:350
  2.4 0.3 collective-permute-start
  2.8 1.3 collective-permute-start.3
  4.1 0.1 dynamic_slice.6
  4.1 0.6 fusion.1
  6.0 0.1 pad_dynamic-slice_fusion
  6.1 0.4 convert_reduce_fusion
  6.5 0.1 slice.49
  6.6 0.5 broadcast_add_fusion.low_ref
  7.2 0.5 and_select_fusion
  9.0 12.2 %own_stats.1.stats_ref = f32[8,3,1024]{2,1,0:T(4,128)} custom-call(s32[4]{0:T(128)} %get-tuple-element.120.first_ref, s32[1,512]{1,0:T(1,128)} %broadcast_add_fusion.low_ref, bf16[512,2048]{1,0:T(8,128)(2,1)} %q_ref.17, bf16[512,1024]{1,0:T(8,128)(2,1)} %k_ref.9, bf16[512,2048]{1,0:T(8,128)(2,1)} %o_ref.1, bf16[512,2048]{1,0:T(8,128)(2,1)} %do_ref.17), custom_call_target="tpu_custom_call" | custom-call | flops 536870912 | bytes 16777216 | tf_op jit(solution)/shard_map/own_stats/pallas_call | solution.py:191
  21.3 0.9 broadcast_select_fusion.7
  22.1 2.2 %collective-permute-start.2 = (bf16[2,512,256]{2,1,0:T(8,128)(2,1)}, bf16[2,512,256]{2,1,0:T(8,128)(2,1)}, u32[]{:S(2)}, u32[]{:S(2)}) collective-permute-start(bf16[2,512,256]{2,1,0:T(8,128)(2,1)} %get-tuple-element.117), channel_id=1, source_target_pairs={{2,0},{4,2},{6,4},{8,6},{10,8},{12,10},{14,12},{16,14},{18,16},{20... | collective-permute-start | bytes 1572872 | tf_op jit(solution)/shard_map/ppermute | solution.py:340
  24.3 4.0 %collective-permute-start.1 = (bf16[2,512,256]{2,1,0:T(8,128)(2,1)S(1)}, bf16[2,512,256]{2,1,0:T(8,128)(2,1)}, u32[]{:S(2)}, u32[]{:S(2)}) collective-permute-start(bf16[2,512,256]{2,1,0:T(8,128)(2,1)S(1)} %get-tuple-element.118), channel_id=1, source_target_pairs={{0,2},{2,4},{4,6},{6,8},{8,10},{10,12},{12,14},{14,16},{16,18},{18... | collective-permute-start | bytes 1572872 | tf_op jit(solution)/shard_map/ppermute | solution.py:340
  28.3 0.1 broadcast_select_fusion.6
  28.4 1.9 %collective-permute-start.5 = (bf16[2,512,256]{2,1,0:T(8,128)(2,1)S(1)}, bf16[2,512,256]{2,1,0:T(8,128)(2,1)S(1)}, u32[]{:S(2)}, u32[]{:S(2)}) collective-permute-start(bf16[2,512,256]{2,1,0:T(8,128)(2,1)S(1)} %get-tuple-element.107), channel_id=1, source_target_pairs={{2,0},{4,2},{6,4},{8,6},{10,8},{12,10},{14,12},{16,14},{18,16},{20... | collective-permute-start | bytes 1572872 | tf_op jit(solution)/shard_map/ppermute | solution.py:340
  30.3 3.8 %collective-permute-start.4 = (bf16[2,512,256]{2,1,0:T(8,128)(2,1)S(1)}, bf16[2,512,256]{2,1,0:T(8,128)(2,1)S(1)}, u32[]{:S(2)}, u32[]{:S(2)}) collective-permute-start(bf16[2,512,256]{2,1,0:T(8,128)(2,1)S(1)} %get-tuple-element.108), channel_id=1, source_target_pairs={{0,2},{2,4},{4,6},{6,8},{8,10},{10,12},{12,14},{14,16},{16,18},{18... | collective-permute-start | bytes 1572872 | tf_op jit(solution)/shard_map/ppermute | solution.py:340
  34.2 10.9 %collective-permute-done.2 = bf16[2,512,256]{2,1,0:T(8,128)(2,1)} collective-permute-done((bf16[2,512,256]{2,1,0:T(8,128)(2,1)}, bf16[2,512,256]{2,1,0:T(8,128)(2,1)}, u32[]{:S(2)}, u32[]{:S(2)}) %collective-permute-start.2) | collective-permute-done | bytes 524320 | tf_op jit(solution)/shard_map/ppermute | solution.py:340
  45.1 2.1 %broadcast_select_fusion.18 = (bf16[2,512,256]{2,1,0:T(8,128)(2,1)S(1)}, bf16[2,512,256]{2,1,0:T(8,128)(2,1)}) fusion(bf16[2,512,256]{2,1,0:T(8,128)(2,1)} %collective-permute-done.1, pred[]{:T(512)S(6)} %eq.23, bf16[2,512,256]{2,1,0:T(8,128)(2,1)S(1)} %get-tuple-element.118, bf16[2,512,256]{2,1,0:T(8,128)(2,1)} %collective-permute-done.2, pred[]{:T(512)S(6)} %eq.27, ...), kind=kLoop, calls=%fused_computation.23 | loop fusion | flops 786432 | bytes 2621443 | tf_op jit(solution)/shard_map/jit(_where)/select_n | solution.py:403
  47.2 6.6 %window_terms.4 = (f32[8,3,1024]{2,1,0:T(4,128)}, f32[8,128,1024]{2,1,0:T(8,128)}, bf16[2,512,256]{2,1,0:T(8,128)(2,1)}) custom-call(s32[1]{0:T(128)} %bitcast.5.group_ref, s32[4]{0:T(128)} %get-tuple-element.119.first_ref, s32[1,512]{1,0:T(1,128)} %bitcast.36, bf16[512,2048]{1,0:T(8,128)(2,1)} %q_ref.17, bf16[512,2048]{1,0:T(8,128)(2,1)} %do_ref.17, ...), custom_call_target="tpu_custom_call" | custom-call | flops 335544320 | bytes 4194304 | tf_op jit(solution)/shard_map/window_terms/pallas_call | solution.py:216
  53.8 0.9 broadcast_select_fusion.14
  54.7 0.7 collective-permute-start.6
  55.4 6.7 %window_terms.5 = (f32[8,3,1024]{2,1,0:T(4,128)}, f32[8,128,1024]{2,1,0:T(8,128)}, bf16[2,512,256]{2,1,0:T(8,128)(2,1)}) custom-call(s32[1]{0:T(128)} %bitcast.5.group_ref, s32[4]{0:T(128)} %get-tuple-element.119.first_ref, s32[1,512]{1,0:T(1,128)} %bitcast.37, bf16[512,2048]{1,0:T(8,128)(2,1)} %q_ref.17, ...), custom_call_target="tpu_custom_call", output_to_operand_aliasing={{0}: (7, {}), {1}: (8, {})} | custom-call | flops 335544320 | bytes 4194304 | tf_op jit(solution)/shard_map/window_terms/pallas_call | solution.py:216
  62.0 6.7 %window_terms.6 = (f32[8,3,1024]{2,1,0:T(4,128)}, f32[8,128,1024]{2,1,0:T(8,128)}, bf16[2,512,256]{2,1,0:T(8,128)(2,1)}) custom-call(s32[1]{0:T(128)} %bitcast.4.group_ref, s32[4]{0:T(128)} %get-tuple-element.119.first_ref, s32[1,512]{1,0:T(1,128)} %bitcast.38, bf16[512,2048]{1,0:T(8,128)(2,1)} %q_ref.17, ...), custom_call_target="tpu_custom_call", output_to_operand_aliasing={{0}: (7, {}), {1}: (8, {})} | custom-call | flops 335544320 | bytes 4194304 | tf_op jit(solution)/shard_map/window_terms/pallas_call | solution.py:216
  68.7 2.7 %collective-permute-done.6.past_ref = bf16[2,512,256]{2,1,0:T(8,128)(2,1)S(1)} collective-permute-done((bf16[2,512,256]{2,1,0:T(8,128)(2,1)S(1)}, bf16[2,512,256]{2,1,0:T(8,128)(2,1)S(1)}, u32[]{:S(2)}, u32[]{:S(2)}) %collective-permute-start.6) | collective-permute-done | bytes 524320 | tf_op jit(solution)/shard_map/ppermute | solution.py:336
  71.4 0.8 copy-done.4
  72.2 6.9 %window_terms.7 = (f32[8,3,1024]{2,1,0:T(4,128)}, f32[8,128,1024]{2,1,0:T(8,128)}, bf16[2,512,256]{2,1,0:T(8,128)(2,1)}) custom-call(s32[1]{0:T(128)} %bitcast.4.group_ref, s32[4]{0:T(128)} %get-tuple-element.119.first_ref, s32[1,512]{1,0:T(1,128)} %bitcast.39, bf16[512,2048]{1,0:T(8,128)(2,1)} %q_ref.17, ...), custom_call_target="tpu_custom_call", output_to_operand_aliasing={{0}: (7, {}), {1}: (8, {})} | custom-call | flops 335544320 | bytes 4194304 | tf_op jit(solution)/shard_map/window_terms/pallas_call | solution.py:216
  79.1 0.1 collective-permute-start.9
  79.2 7.3 %own_terms.4 = (bf16[512,2048]{1,0:T(8,128)(2,1)}, f32[512,1024]{1,0:T(8,128)}, f32[512,1024]{1,0:T(8,128)}) custom-call(s32[4]{0:T(128)} %get-tuple-element.120.first_ref, s32[1,512]{1,0:T(1,128)} %broadcast_add_fusion.low_ref, bf16[512,2048]{1,0:T(8,128)(2,1)} %q_ref.17, bf16[512,1024]{1,0:T(8,128)(2,1)} %k_ref.9, bf16[512,1024]{1,0:T(8,128)(2,1)} %v_ref.7, ...), custom_call_target="tpu_custom_call" | custom-call | flops 671088640 | bytes 4194304 | tf_op jit(solution)/shard_map/own_terms/pallas_call | solution.py:248
  86.5 7.5 %own_terms.5 = (bf16[512,2048]{1,0:T(8,128)(2,1)}, f32[512,1024]{1,0:T(8,128)}, f32[512,1024]{1,0:T(8,128)}) custom-call(s32[4]{0:T(128)} %get-tuple-element.120.first_ref, s32[1,512]{1,0:T(1,128)} %broadcast_add_fusion.low_ref, bf16[512,2048]{1,0:T(8,128)(2,1)} %q_ref.17, ...), custom_call_target="tpu_custom_call", output_to_operand_aliasing={{0}: (8, {}), {1}: (9, {}), {2}: (10, {})} | custom-call | flops 671088640 | bytes 4194304 | tf_op jit(solution)/shard_map/own_terms/pallas_call | solution.py:248
  94.0 0.1 broadcast_select_fusion.2
  94.1 1.9 %collective-permute-start.13 = (bf16[2,512,256]{2,1,0:T(8,128)(2,1)S(1)}, bf16[2,512,256]{2,1,0:T(8,128)(2,1)S(1)}, u32[]{:S(2)}, u32[]{:S(2)}) collective-permute-start(bf16[2,512,256]{2,1,0:T(8,128)(2,1)S(1)} %get-tuple-element.103), channel_id=1, source_target_pairs={{2,0},{4,2},{6,4},{8,6},{10,8},{12,10},{14,12},{16,14},{18,16},{20... | collective-permute-start | bytes 1572872 | tf_op jit(solution)/shard_map/ppermute | solution.py:340
  96.0 3.6 %collective-permute-start.14 = (bf16[2,512,256]{2,1,0:T(8,128)(2,1)S(1)}, bf16[2,512,256]{2,1,0:T(8,128)(2,1)S(1)}, u32[]{:S(2)}, u32[]{:S(2)}) collective-permute-start(bf16[2,512,256]{2,1,0:T(8,128)(2,1)S(1)} %get-tuple-element.104), channel_id=1, source_target_pairs={{0,2},{2,4},{4,6},{6,8},{8,10},{10,12},{12,14},{14,16},{16,18},{18... | collective-permute-start | bytes 1572872 | tf_op jit(solution)/shard_map/ppermute | solution.py:340
  99.7 7.6 %own_terms.6 = (bf16[512,2048]{1,0:T(8,128)(2,1)}, f32[512,1024]{1,0:T(8,128)}, f32[512,1024]{1,0:T(8,128)}) custom-call(s32[4]{0:T(128)} %get-tuple-element.120.first_ref, s32[1,512]{1,0:T(1,128)} %broadcast_add_fusion.low_ref, bf16[512,2048]{1,0:T(8,128)(2,1)} %q_ref.17, ...), custom_call_target="tpu_custom_call", output_to_operand_aliasing={{0}: (8, {}), {1}: (9, {}), {2}: (10, {})} | custom-call | flops 671088640 | bytes 4194304 | tf_op jit(solution)/shard_map/own_terms/pallas_call | solution.py:248
  107.3 7.6 %own_terms.7 = (bf16[512,2048]{1,0:T(8,128)(2,1)}, f32[512,1024]{1,0:T(8,128)}, f32[512,1024]{1,0:T(8,128)}) custom-call(s32[4]{0:T(128)} %get-tuple-element.120.first_ref, s32[1,512]{1,0:T(1,128)} %broadcast_add_fusion.low_ref, bf16[512,2048]{1,0:T(8,128)(2,1)} %q_ref.17, ...), custom_call_target="tpu_custom_call", output_to_operand_aliasing={{0}: (8, {}), {1}: (9, {}), {2}: (10, {})} | custom-call | flops 671088640 | bytes 4194304 | tf_op jit(solution)/shard_map/own_terms/pallas_call | solution.py:248
  115.0 0.9 broadcast_select_fusion.3
  115.8 1.9 %collective-permute-start.10 = (bf16[2,512,256]{2,1,0:T(8,128)(2,1)}, bf16[2,512,256]{2,1,0:T(8,128)(2,1)S(1)}, u32[]{:S(2)}, u32[]{:S(2)}) collective-permute-start(bf16[2,512,256]{2,1,0:T(8,128)(2,1)} %get-tuple-element.105), channel_id=1, source_target_pairs={{2,0},{4,2},{6,4},{8,6},{10,8},{12,10},{14,12},{16,14},{18,16},{20... | collective-permute-start | bytes 1572872 | tf_op jit(solution)/shard_map/ppermute | solution.py:340
  117.7 3.6 %collective-permute-start.11 = (bf16[2,512,256]{2,1,0:T(8,128)(2,1)S(1)}, bf16[2,512,256]{2,1,0:T(8,128)(2,1)}, u32[]{:S(2)}, u32[]{:S(2)}) collective-permute-start(bf16[2,512,256]{2,1,0:T(8,128)(2,1)S(1)} %get-tuple-element.106), channel_id=1, source_target_pairs={{0,2},{2,4},{4,6},{6,8},{8,10},{10,12},{12,14},{14,16},{16,18},{18... | collective-permute-start | bytes 1572872 | tf_op jit(solution)/shard_map/ppermute | solution.py:340
  121.4 0.9 broadcast_select_fusion
  122.3 10.0 %collective-permute-done.10 = bf16[2,512,256]{2,1,0:T(8,128)(2,1)S(1)} collective-permute-done((bf16[2,512,256]{2,1,0:T(8,128)(2,1)}, bf16[2,512,256]{2,1,0:T(8,128)(2,1)S(1)}, u32[]{:S(2)}, u32[]{:S(2)}) %collective-permute-start.10) | collective-permute-done | bytes 524320 | tf_op jit(solution)/shard_map/ppermute | solution.py:340
  132.3 1.9 %broadcast_select_fusion.1 = (bf16[2,512,256]{2,1,0:T(8,128)(2,1)}, bf16[2,512,256]{2,1,0:T(8,128)(2,1)S(1)}) fusion(bf16[2,512,256]{2,1,0:T(8,128)(2,1)} %collective-permute-done.11, pred[]{:T(512)S(6)} %eq.57, bf16[2,512,256]{2,1,0:T(8,128)(2,1)S(1)} %get-tuple-element.106, bf16[2,512,256]{2,1,0:T(8,128)(2,1)S(1)} %collective-permute-done.10, pred[]{:T(512)S(6)} %eq.27, ...), kind=kLoop, calls=%fused_computation.6 | loop fusion | flops 786432 | bytes 2621443 | tf_op jit(solution)/shard_map/jit(_where)/select_n | solution.py:461
  134.3 2.1 %finish.4 = (bf16[512,1024]{1,0:T(8,128)(2,1)}, bf16[512,1024]{1,0:T(8,128)(2,1)}) custom-call(s32[1]{0:T(128)} %bitcast.5.group_ref, f32[512,1024]{1,0:T(8,128)} %get-tuple-element.81.dk_ref, f32[512,1024]{1,0:T(8,128)} %get-tuple-element.82.dv_ref, bf16[2,512,256]{2,1,0:T(8,128)(2,1)} %get-tuple-element.95.back_ref), custom_call_target="tpu_custom_call" | custom-call | flops 524288 | bytes 2097152 | tf_op jit(solution)/shard_map/finish/pallas_call | solution.py:287
  136.4 0.8 copy-done.3
  137.2 2.1 %finish.5 = (bf16[512,1024]{1,0:T(8,128)(2,1)}, bf16[512,1024]{1,0:T(8,128)(2,1)}) custom-call(s32[1]{0:T(128)} %bitcast.4.group_ref, f32[512,1024]{1,0:T(8,128)} %get-tuple-element.81.dk_ref, f32[512,1024]{1,0:T(8,128)} %get-tuple-element.82.dv_ref, bf16[2,512,256]{2,1,0:T(8,128)(2,1)} %copy-done.3, ...), custom_call_target="tpu_custom_call", output_to_operand_aliasing={{0}: (4, {}), {1}: (5, {})} | custom-call | flops 524288 | bytes 2097152 | tf_op jit(solution)/shard_map/finish/pallas_call | solution.py:287
  139.3 2.1 %finish.6 = (bf16[512,1024]{1,0:T(8,128)(2,1)}, bf16[512,1024]{1,0:T(8,128)(2,1)}) custom-call(s32[1]{0:T(128)} %bitcast.5.group_ref, f32[512,1024]{1,0:T(8,128)} %get-tuple-element.81.dk_ref, f32[512,1024]{1,0:T(8,128)} %get-tuple-element.82.dv_ref, bf16[2,512,256]{2,1,0:T(8,128)(2,1)} %get-tuple-element.97.back_ref, ...), custom_call_target="tpu_custom_call", output_to_operand_aliasing={{0}: (4, {}), {1}: (5, {})} | custom-call | flops 524288 | bytes 2097152 | tf_op jit(solution)/shard_map/finish/pallas_call | solution.py:287
  141.4 5.0 %collective-permute-done.12.back_ref = bf16[2,512,256]{2,1,0:T(8,128)(2,1)S(1)} collective-permute-done((bf16[2,512,256]{2,1,0:T(8,128)(2,1)S(1)}, bf16[2,512,256]{2,1,0:T(8,128)(2,1)S(1)}, u32[]{:S(2)}, u32[]{:S(2)}) %collective-permute-start.12) | collective-permute-done | bytes 524320 | tf_op jit(solution)/shard_map/ppermute | solution.py:336
  146.4 0.8 copy-done.2
  147.2 2.1 %finish.7 = (bf16[512,1024]{1,0:T(8,128)(2,1)}, bf16[512,1024]{1,0:T(8,128)(2,1)}) custom-call(s32[1]{0:T(128)} %bitcast.4.group_ref, f32[512,1024]{1,0:T(8,128)} %get-tuple-element.81.dk_ref, f32[512,1024]{1,0:T(8,128)} %get-tuple-element.82.dv_ref, bf16[2,512,256]{2,1,0:T(8,128)(2,1)} %copy-done.2, ...), custom_call_target="tpu_custom_call", output_to_operand_aliasing={{0}: (4, {}), {1}: (5, {})} | custom-call | flops 524288 | bytes 2097152 | tf_op jit(solution)/shard_map/finish/pallas_call | solution.py:287
  (32 shorter events, 0.2 us)
Async XLA Ops:
  2.3 1.7 %copy-start.7 = (s32[32]{0:T(128)S(1)}, s32[32]{0:T(128)}, u32[]{:S(2)}) copy-start(s32[32]{0:T(128)} %param.13) | copy-start | bytes 388
  2.4 3.7 %copy-start.6 = (s32[16384]{0:T(1024)S(1)}, s32[16384]{0:T(1024)}, u32[]{:S(2)}) copy-start(s32[16384]{0:T(1024)} %param.12) | copy-start | bytes 196612
  2.4 18.8 %collective-permute-start = (bf16[2,512,256]{2,1,0:T(8,128)(2,1)S(1)}, bf16[2,512,256]{2,1,0:T(8,128)(2,1)S(1)}, u32[]{:S(2)}, u32[]{:S(2)}) collective-permute-start(bf16[2,512,256]{2,1,0:T(8,128)(2,1)S(1)} %pad_maximum_fusion.1), channel_id=1, source_target_pairs={{0,1},{1,0},{2,3},{3,2},{4,5},{5,4},{6,7},{7,6},{8,9},{9,8},{10,11... | collective-permute-start | bytes 1572872 | tf_op jit(solution)/shard_map/ppermute | solution.py:336
  2.8 25.5 %collective-permute-start.3 = (bf16[2,512,256]{2,1,0:T(8,128)(2,1)S(1)}, bf16[2,512,256]{2,1,0:T(8,128)(2,1)S(1)}, u32[]{:S(2)}, u32[]{:S(2)}) collective-permute-start(bf16[2,512,256]{2,1,0:T(8,128)(2,1)S(1)} %pad_maximum_fusion.3), channel_id=1, source_target_pairs={{0,1},{1,0},{2,3},{3,2},{4,5},{5,4},{6,7},{7,6},{8,9},{9,8},{10,11... | collective-permute-start | bytes 1572872 | tf_op jit(solution)/shard_map/ppermute | solution.py:336
  6.5 14.7 %copy-start.5 = (s32[512]{0:T(512)}, s32[512]{0:T(512)S(1)}, u32[]{:S(2)}) copy-start(s32[512]{0:T(512)S(1)} %convert_reduce_fusion) | copy-start | bytes 6148
  22.1 23.0 %collective-permute-start.2 = (bf16[2,512,256]{2,1,0:T(8,128)(2,1)}, bf16[2,512,256]{2,1,0:T(8,128)(2,1)}, u32[]{:S(2)}, u32[]{:S(2)}) collective-permute-start(bf16[2,512,256]{2,1,0:T(8,128)(2,1)} %get-tuple-element.117), channel_id=1, source_target_pairs={{2,0},{4,2},{6,4},{8,6},{10,8},{12,10},{14,12},{16,14},{18,16},{20... | collective-permute-start | bytes 1572872 | tf_op jit(solution)/shard_map/ppermute | solution.py:340
  24.3 20.8 %collective-permute-start.1 = (bf16[2,512,256]{2,1,0:T(8,128)(2,1)S(1)}, bf16[2,512,256]{2,1,0:T(8,128)(2,1)}, u32[]{:S(2)}, u32[]{:S(2)}) collective-permute-start(bf16[2,512,256]{2,1,0:T(8,128)(2,1)S(1)} %get-tuple-element.118), channel_id=1, source_target_pairs={{0,2},{2,4},{4,6},{6,8},{8,10},{10,12},{12,14},{14,16},{16,18},{18... | collective-permute-start | bytes 1572872 | tf_op jit(solution)/shard_map/ppermute | solution.py:340
  28.4 25.4 %collective-permute-start.5 = (bf16[2,512,256]{2,1,0:T(8,128)(2,1)S(1)}, bf16[2,512,256]{2,1,0:T(8,128)(2,1)S(1)}, u32[]{:S(2)}, u32[]{:S(2)}) collective-permute-start(bf16[2,512,256]{2,1,0:T(8,128)(2,1)S(1)} %get-tuple-element.107), channel_id=1, source_target_pairs={{2,0},{4,2},{6,4},{8,6},{10,8},{12,10},{14,12},{16,14},{18,16},{20... | collective-permute-start | bytes 1572872 | tf_op jit(solution)/shard_map/ppermute | solution.py:340
  30.3 23.5 %collective-permute-start.4 = (bf16[2,512,256]{2,1,0:T(8,128)(2,1)S(1)}, bf16[2,512,256]{2,1,0:T(8,128)(2,1)S(1)}, u32[]{:S(2)}, u32[]{:S(2)}) collective-permute-start(bf16[2,512,256]{2,1,0:T(8,128)(2,1)S(1)} %get-tuple-element.108), channel_id=1, source_target_pairs={{0,2},{2,4},{4,6},{6,8},{8,10},{10,12},{12,14},{14,16},{16,18},{18... | collective-permute-start | bytes 1572872 | tf_op jit(solution)/shard_map/ppermute | solution.py:340
  47.2 14.9 %collective-permute-start.7 = (bf16[2,512,256]{2,1,0:T(8,128)(2,1)S(1)}, bf16[2,512,256]{2,1,0:T(8,128)(2,1)}, u32[]{:S(2)}, u32[]{:S(2)}) collective-permute-start(bf16[2,512,256]{2,1,0:T(8,128)(2,1)S(1)} %get-tuple-element.101), channel_id=1, source_target_pairs={{0,1},{1,0},{2,3},{3,2},{4,5},{5,4},{6,7},{7,6},{8,9},{9,8},{10,11... | collective-permute-start | bytes 1572872 | tf_op jit(solution)/shard_map/ppermute | solution.py:336
  54.7 16.7 %collective-permute-start.6 = (bf16[2,512,256]{2,1,0:T(8,128)(2,1)S(1)}, bf16[2,512,256]{2,1,0:T(8,128)(2,1)S(1)}, u32[]{:S(2)}, u32[]{:S(2)}) collective-permute-start(bf16[2,512,256]{2,1,0:T(8,128)(2,1)S(1)} %get-tuple-element.100), channel_id=1, source_target_pairs={{0,1},{1,0},{2,3},{3,2},{4,5},{5,4},{6,7},{7,6},{8,9},{9,8},{10,11... | collective-permute-start | bytes 1572872 | tf_op jit(solution)/shard_map/ppermute | solution.py:336
  68.7 25.3 %collective-permute-start.8 = (bf16[2,512,256]{2,1,0:T(8,128)(2,1)}, bf16[2,512,256]{2,1,0:T(8,128)(2,1)S(1)}, u32[]{:S(2)}, u32[]{:S(2)}) collective-permute-start(bf16[2,512,256]{2,1,0:T(8,128)(2,1)} %get-tuple-element.69), channel_id=1, source_target_pairs={{0,1},{1,0},{2,3},{3,2},{4,5},{5,4},{6,7},{7,6},{8,9},{9,8},{10,11... | collective-permute-start | bytes 1572872 | tf_op jit(solution)/shard_map/ppermute | solution.py:336
  71.4 0.8 copy-start.4
  79.1 35.9 %collective-permute-start.9 = (bf16[2,512,256]{2,1,0:T(8,128)(2,1)}, bf16[2,512,256]{2,1,0:T(8,128)(2,1)S(1)}, u32[]{:S(2)}, u32[]{:S(2)}) collective-permute-start(bf16[2,512,256]{2,1,0:T(8,128)(2,1)} %get-tuple-element.79), channel_id=1, source_target_pairs={{0,1},{1,0},{2,3},{3,2},{4,5},{5,4},{6,7},{7,6},{8,9},{9,8},{10,11... | collective-permute-start | bytes 1572872 | tf_op jit(solution)/shard_map/ppermute | solution.py:336
  86.5 7.5 %copy-start.1 = (bf16[2,512,256]{2,1,0:T(8,128)(2,1)S(1)}, bf16[2,512,256]{2,1,0:T(8,128)(2,1)}, u32[]{:S(2)}) copy-start(bf16[2,512,256]{2,1,0:T(8,128)(2,1)} %get-tuple-element.85) | copy-start | bytes 1572868
  94.1 27.3 %collective-permute-start.13 = (bf16[2,512,256]{2,1,0:T(8,128)(2,1)S(1)}, bf16[2,512,256]{2,1,0:T(8,128)(2,1)S(1)}, u32[]{:S(2)}, u32[]{:S(2)}) collective-permute-start(bf16[2,512,256]{2,1,0:T(8,128)(2,1)S(1)} %get-tuple-element.103), channel_id=1, source_target_pairs={{2,0},{4,2},{6,4},{8,6},{10,8},{12,10},{14,12},{16,14},{18,16},{20... | collective-permute-start | bytes 1572872 | tf_op jit(solution)/shard_map/ppermute | solution.py:340
  96.0 25.4 %collective-permute-start.14 = (bf16[2,512,256]{2,1,0:T(8,128)(2,1)S(1)}, bf16[2,512,256]{2,1,0:T(8,128)(2,1)S(1)}, u32[]{:S(2)}, u32[]{:S(2)}) collective-permute-start(bf16[2,512,256]{2,1,0:T(8,128)(2,1)S(1)} %get-tuple-element.104), channel_id=1, source_target_pairs={{0,2},{2,4},{4,6},{6,8},{8,10},{10,12},{12,14},{14,16},{16,18},{18... | collective-permute-start | bytes 1572872 | tf_op jit(solution)/shard_map/ppermute | solution.py:340
  107.3 7.6 %copy-start = (bf16[2,512,256]{2,1,0:T(8,128)(2,1)S(1)}, bf16[2,512,256]{2,1,0:T(8,128)(2,1)}, u32[]{:S(2)}) copy-start(bf16[2,512,256]{2,1,0:T(8,128)(2,1)} %get-tuple-element.83) | copy-start | bytes 1572868
  115.8 16.5 %collective-permute-start.10 = (bf16[2,512,256]{2,1,0:T(8,128)(2,1)}, bf16[2,512,256]{2,1,0:T(8,128)(2,1)S(1)}, u32[]{:S(2)}, u32[]{:S(2)}) collective-permute-start(bf16[2,512,256]{2,1,0:T(8,128)(2,1)} %get-tuple-element.105), channel_id=1, source_target_pairs={{2,0},{4,2},{6,4},{8,6},{10,8},{12,10},{14,12},{16,14},{18,16},{20... | collective-permute-start | bytes 1572872 | tf_op jit(solution)/shard_map/ppermute | solution.py:340
  117.7 14.6 %collective-permute-start.11 = (bf16[2,512,256]{2,1,0:T(8,128)(2,1)S(1)}, bf16[2,512,256]{2,1,0:T(8,128)(2,1)}, u32[]{:S(2)}, u32[]{:S(2)}) collective-permute-start(bf16[2,512,256]{2,1,0:T(8,128)(2,1)S(1)} %get-tuple-element.106), channel_id=1, source_target_pairs={{0,2},{2,4},{4,6},{6,8},{8,10},{10,12},{12,14},{14,16},{16,18},{18... | collective-permute-start | bytes 1572872 | tf_op jit(solution)/shard_map/ppermute | solution.py:340
  122.3 14.1 %collective-permute-start.15 = (bf16[2,512,256]{2,1,0:T(8,128)(2,1)S(1)}, bf16[2,512,256]{2,1,0:T(8,128)(2,1)S(1)}, u32[]{:S(2)}, u32[]{:S(2)}) collective-permute-start(bf16[2,512,256]{2,1,0:T(8,128)(2,1)S(1)} %get-tuple-element.96), channel_id=1, source_target_pairs={{0,1},{1,0},{2,3},{3,2},{4,5},{5,4},{6,7},{7,6},{8,9},{9,8},{10,11... | collective-permute-start | bytes 1572872 | tf_op jit(solution)/shard_map/ppermute | solution.py:336
  134.3 12.2 %collective-permute-start.12 = (bf16[2,512,256]{2,1,0:T(8,128)(2,1)S(1)}, bf16[2,512,256]{2,1,0:T(8,128)(2,1)S(1)}, u32[]{:S(2)}, u32[]{:S(2)}) collective-permute-start(bf16[2,512,256]{2,1,0:T(8,128)(2,1)S(1)} %get-tuple-element.98), channel_id=1, source_target_pairs={{0,1},{1,0},{2,3},{3,2},{4,5},{5,4},{6,7},{7,6},{8,9},{9,8},{10,11... | collective-permute-start | bytes 1572872 | tf_op jit(solution)/shard_map/ppermute | solution.py:336
  136.4 0.8 copy-start.3
  146.4 0.8 copy-start.2

commit v4 on v2

--- a/solution.py
+++ b/solution.py
@@ -12,6 +12,7 @@
 LOG2_E = 1.4426950408889634
 CHUNKS = 2
 TILE = 128
+STRIP = 64
 VMEM_BYTES = 60 * 1024 * 1024
 
 
@@ -21,12 +22,21 @@
     )
 
 
+def strips(count):
+    return [slice(start, start + STRIP) for start in range(0, count, STRIP)]
+
+
+def folded(strip, reduce):
+    return reduce(strip.reshape(strip.shape[0] // 8, 8, strip.shape[1]), axis=0)
+
+
 def attention_body(carried, group_ref, low_ref, q_ref, k_ref, v_ref, o_ref, do_ref, past_ref, *refs):
-    dq_ref, dk_ref, dv_ref, back_ref, k_all, v_all, k_turned, dk_sum, dv_sum = refs[carried:]
+    dq_ref, dk_ref, dv_ref, back_ref = refs[carried : carried + 4]
+    k_all, v_all, k_turned, dk_sum, dv_sum, scores, slopes, weights_b, slopes_b = refs[carried + 4 :]
     rows, head = k_ref.shape
     window = past_ref.shape[1]
     members = q_ref.shape[1] // head
-    span = window + TILE
+    span, lanes = window + TILE, members * TILE
     scale = head**-0.5
     k_all[:window] = past_ref[0]
     k_all[window:] = k_ref[...]
@@ -35,36 +45,66 @@
     k_turned[...] = k_all[...].T
     dk_sum[...] = jnp.zeros_like(dk_sum)
     dv_sum[...] = jnp.zeros_like(dv_sum)
+    lane = lax.broadcasted_iota(jnp.int32, (1, lanes), 1) % TILE
+    tiles = range(rows // TILE)
 
     def stacked(ref, start):
         return jnp.concatenate(
             [ref[start : start + TILE, m * head : (m + 1) * head] for m in range(members)], axis=0
         )
 
-    for start in range(0, rows, TILE):
-        queries = stacked(q_ref, start)
-        grads = stacked(do_ref, start)
+    def enter(tile):
+        keys = pl.ds(tile * TILE, span)
+        queries, grads = stacked(q_ref, tile * TILE), stacked(do_ref, tile * TILE)
+        scores[tile] = dot(k_all[keys], queries, 1, 1)
+        slopes[tile] = dot(v_all[keys], grads, 1, 1)
+        return queries, grads
+
+    def weigh(tile, grads):
+        start = tile * TILE
         product = grads.astype(jnp.float32) * stacked(o_ref, start).astype(jnp.float32)
         delta = jnp.sum(product.T, axis=0, keepdims=True)
-        low = jnp.concatenate([low_ref[:, start : start + TILE]] * members, axis=1)
-        keys = k_all[start : start + span]
-        scores = dot(keys, queries, 1, 1)
-        key_index = lax.broadcasted_iota(jnp.int32, scores.shape, 0)
-        lane = lax.broadcasted_iota(jnp.int32, (1, members * TILE), 1)
-        visible = (key_index >= low - start) & (key_index <= window + lane % TILE)
-        scores = jnp.where(visible, scores, NEGATIVE)
-        top = jnp.max(scores, axis=0, keepdims=True)
-        terms = jnp.exp2((scores - top) * (scale * LOG2_E))
-        weights = terms * (1.0 / jnp.sum(terms, axis=0, keepdims=True))
-        weight_grads = dot(v_all[start : start + span], grads, 1, 1)
-        score_grads = (weights * (weight_grads - delta)).astype(jnp.bfloat16)
-        dv_sum[start : start + span] += dot(weights.astype(jnp.bfloat16), grads, 1, 0)
-        dk_sum[start : start + span] += dot(score_grads, queries, 1, 0)
-        dq = (dot(k_turned[:, start : start + span], score_grads, 1, 0) * scale).T
+        low = jnp.concatenate([low_ref[:, start : start + TILE]] * members, axis=1) - start
+
+        def visible(strip):
+            index = strip.start + lax.broadcasted_iota(jnp.int32, (STRIP, lanes), 0)
+            seen = index >= low
+            return seen & (index <= window + lane) if strip.stop > window else seen
+
+        top = jnp.full((8, lanes), NEGATIVE, jnp.float32)
+        for strip in strips(span):
+            masked = jnp.where(visible(strip), scores[tile, strip], NEGATIVE)
+            top = jnp.maximum(top, folded(masked, jnp.max))
+        top = jnp.max(top, axis=0, keepdims=True)
+        total = jnp.zeros((8, lanes), jnp.float32)
+        for strip in strips(span):
+            terms = jnp.exp2((scores[tile, strip] - top) * (scale * LOG2_E))
+            terms = jnp.where(visible(strip), terms, 0.0)
+            total = total + folded(terms, jnp.sum)
+            scores[tile, strip] = terms
+        inverse = 1.0 / jnp.sum(total, axis=0, keepdims=True)
+        for strip in strips(span):
+            weights = scores[tile, strip] * inverse
+            weights_b[tile, strip] = weights.astype(jnp.bfloat16)
+            slopes_b[tile, strip] = (weights * (slopes[tile, strip] - delta)).astype(jnp.bfloat16)
+
+    def leave(tile, queries, grads):
+        start = tile * TILE
+        keys = pl.ds(start, span)
+        dv_sum[keys] += dot(weights_b[tile], grads, 1, 0)
+        dk_sum[keys] += dot(slopes_b[tile], queries, 1, 0)
+        dq = (dot(k_turned[:, keys], slopes_b[tile], 1, 0) * scale).T
         for m in range(members):
             dq_ref[start : start + TILE, m * head : (m + 1) * head] = dq[
                 m * TILE : (m + 1) * TILE
             ].astype(dq_ref.dtype)
+
+    entered = {0: enter(0)}
+    for tile in tiles:
+        if tile + 1 in tiles:
+            entered[tile + 1] = enter(tile + 1)
+        weigh(tile, entered[tile][1])
+        leave(tile, *entered[tile])
     back_ref[0] = dk_sum[:window].astype(back_ref.dtype)
     back_ref[1] = dv_sum[:window].astype(back_ref.dtype)
     dk_ref[...] = dk_sum[window:]
@@ -83,6 +123,7 @@
     key_spec = pl.BlockSpec((rows, HEAD_SIZE), column)
     past_spec = pl.BlockSpec((2, window, HEAD_SIZE), lambda step, group_ref: (0, 0, step))
     low_spec = pl.BlockSpec((1, rows), lambda step, group_ref: (0, 0))
+    square = (rows // TILE, window + TILE, wide // HEAD_SIZE * TILE)
     tiles = count * queries.shape[1] // keys.shape[1] * rows * (window + TILE)
     return pl.pallas_call(
         functools.partial(attention_body, len(carried)),
@@ -98,6 +139,10 @@
                 pltpu.VMEM((HEAD_SIZE, window + rows), jnp.bfloat16),
                 pltpu.VMEM((window + rows, HEAD_SIZE), jnp.float32),
                 pltpu.VMEM((window + rows, HEAD_SIZE), jnp.float32),
+                pltpu.VMEM(square, jnp.float32),
+                pltpu.VMEM(square, jnp.float32),
+                pltpu.VMEM(square, jnp.bfloat16),
+                pltpu.VMEM(square, jnp.bfloat16),
             ],
         ),
         out_shape=[
@@ -149,6 +194,10 @@
     )(group, *own, back, *carried)
 
 
+def together(*values):
+    return lax.optimization_barrier(values)
+
+
 def pick(items, index):
     result = items[-1]
     for place in range(len(items) - 2, -1, -1):
@@ -220,13 +269,25 @@
             for slot in (early_slot, 1 - early_slot)
         ]
 
-    pasts = []
+    halves = []
     for chunk in range(chunks):
         pieces = [piece_of(place, chunk)]
-        for turn in range(1, sharers):
-            pieces.append(turned(piece_of(other(turn), chunk), turn))
-        early, late = halves_of(pieces)
-        before_early, before_late = shifted(early, 1), shifted(late, -1)
+        pieces += [turned(piece_of(other(turn), chunk), turn) for turn in range(1, sharers)]
+        halves.append(halves_of(pieces))
+    before = [(shifted(early, 1), shifted(late, -1)) for early, late in halves]
+
+    def run(turn, chunk, past, carried):
+        *carried, back = attention(
+            groups[turn].reshape(1), low, row_arrays, past,
+            chunk * per_piece, heads_per_group, tuple(carried),
+        )
+        return carried, back
+
+    carried, terms, pasts = (), [], []
+    for chunk in range(chunks):
+        (early, late), (before_early, before_late) = halves[chunk], before[chunk]
+        if chunk:
+            *carried, before_early, before_late = together(*carried, before_early, before_late)
         before_late = jnp.where(last_block, early, before_late)
 
         def past_of(device):
@@ -236,42 +297,28 @@
             own = jnp.where(is_early(device), early, late)
             return part_rows(jnp.concatenate([before, own], axis=1), device, window)
 
-        pasts.append(
-            [past_of(place)]
-            + [turned(past_of(other(turn)), turn) for turn in range(1, sharers)]
-        )
-
-    carried = ()
-    backs = [[] for chunk in range(chunks)]
-    for turn in range(sharers):
-        for chunk in range(chunks):
-            *carried, back = attention(
-                groups[turn].reshape(1),
-                low,
-                row_arrays,
-                pasts[chunk][turn],
-                chunk * per_piece,
-                heads_per_group,
-                tuple(carried),
-            )
-            backs[chunk].append(back)
+        pasts.append([turned(past_of(other(turn)), turn) for turn in range(1, sharers)])
+        carried, back = run(0, chunk, past_of(place), carried)
+        terms.append([back])
+
+    for chunk in range(chunks):
+        for turn in range(1, sharers):
+            carried, back = run(turn, chunk, pasts[chunk][turn - 1], carried)
+            terms[chunk].append(turned(back, -turn))
 
     query_grads, *own = carried
     results = ()
     for chunk in range(chunks):
-        terms = [backs[chunk][0]]
-        for turn in range(1, sharers):
-            terms.append(turned(backs[chunk][turn], -turn))
         to_before, to_own = [], []
         for slot in (early_slot, 1 - early_slot):
             if parts == 1:
-                to_before.append(pick(terms, lax.rem(slot - place + sharers, sharers)))
+                to_before.append(pick(terms[chunk], lax.rem(slot - place + sharers, sharers)))
                 to_own.append(None)
             else:
-                total = jnp.zeros((2, 2 * window, terms[0].shape[2]), jnp.float32)
+                total = jnp.zeros((2, 2 * window, terms[chunk][0].shape[2]), jnp.float32)
                 for turn in range(sharers):
                     device = other(turn)
-                    mine = jnp.where(device // parts == slot, terms[turn].astype(jnp.float32), 0.0)
+                    mine = jnp.where(device // parts == slot, terms[chunk][turn].astype(jnp.float32), 0.0)
                     wide = jnp.pad(mine, ((0, 0), (window, window), (0, 0)))
                     total += lax.dynamic_slice_in_dim(
                         wide, window - device % parts * rows, 2 * window, 1

time: 134 us -> 126 us (0.940)
  Pallas kernels: 42.7 us -> 38 us
  starting transfers between devices: 35.5 us -> 33.2 us
    pallas_call x4, Pallas kernels: 34.2 us -> 29.5 us  [attention(): pl.pallas_call(functools.partial(attention_body, len(carried)), grid_spec...]
    ppermute x8, starting transfers between devices: 7.89 us -> 4.67 us  [turned(): return lax.ppermute(value, 'head', pairs)]
    ppermute x8, waiting for transfers between devices: 15.4 us -> 17.9 us  [turned(): return lax.ppermute(value, 'head', pairs)]
    ppermute x8, waiting for transfers between devices: 20.2 us -> 18.8 us  [shifted(): lax.ppermute(value, 'blk', [(source, source + step) for source in range(f...]
    unnamed x18 -> x16, local copies, waits for them, and re-layouts: 4.01 us -> 3.21 us
  transfers between devices with their start and end apart: 16 -> 16, of which waited for: 9 -> 8; matrix products, arithmetic and copies ran while one was open for 7% -> 7% of each run, Pallas kernels for 31% -> 29%
where the time goes in v4:
time: 126 us; the launch traced here: 125 us
  Pallas kernels  38 us (30%)
  waiting for transfers between devices  36.7 us (29%)
  starting transfers between devices  33.2 us (26%)
  other arithmetic  9.77 us (8%)
  local copies, waits for them, and re-layouts  3.96 us (3%)
  between operations  3.48 us (3%)
    pallas_call x4, Pallas kernels, attention(): pl.pallas_call(functools.partial(attention_body, len(carried)), grid_spec...  29.5 us
    ppermute x8, starting transfers between devices, shifted(): lax.ppermute(value, 'blk', [(source, source + step) for source in range(f...  28.5 us
    ppermute x8, waiting for transfers between devices, shifted(): lax.ppermute(value, 'blk', [(source, source + step) for source in range(f...  18.8 us
    ppermute x8, waiting for transfers between devices, turned(): return lax.ppermute(value, 'head', pairs)  17.9 us
    pallas_call x4, Pallas kernels, finish(): pl.pallas_call(functools.partial(finish_body, len(carried)), grid_spec=pl...  8.44 us
    ppermute x8, starting transfers between devices, turned(): return lax.ppermute(value, 'head', pairs)  4.67 us
    select_n x4, other arithmetic, pick(): result = jnp.where(index == place, items[place], result)  3.47 us
    unnamed x16, local copies, waits for them, and re-layouts  3.21 us
  transfers between devices with their start and end apart: 16, of which 8 were waited for; matrix products, arithmetic and copies ran while one was open for 7% of the time, Pallas kernels for 29%

profile of v4, /device:TPU:11, one launch (start us, length us, event | category | flops | bytes accessed | tf_op | source)
XLA Modules:
  0.0 125.1 jit_solution(1159991465424187639)
XLA Ops:
  0.6 1.7 %select_bitcast_fusion.2 = (bf16[1,512,256]{2,1,0:T(8,128)(2,1)S(1)}, bf16[1,512,256]{2,1,0:T(8,128)(2,1)S(1)}, bf16[1,512,256]{2,1,0:T(8,128)(2,1)S(1)}, bf16[1...) fusion(pred[]{:T(512)S(6)} %eq.22, ...), kind=kLoop, calls=%fused_computation.27 | loop fusion | flops 1048576 | bytes 4194306 | tf_op jit(solution)/shard_map/stack | solution.py:241
  2.4 0.1 pad_maximum_fusion.1
  2.4 0.3 collective-permute-start
  2.8 1.3 %collective-permute-start.3 = (bf16[2,512,256]{2,1,0:T(8,128)(2,1)S(1)}, bf16[2,512,256]{2,1,0:T(8,128)(2,1)S(1)}, u32[]{:S(2)}, u32[]{:S(2)}) collective-permute-start(bf16[2,512,256]{2,1,0:T(8,128)(2,1)S(1)} %pad_maximum_fusion.3), channel_id=1, source_target_pairs={{0,1},{1,0},{2,3},{3,2},{4,5},{5,4},{6,7},{7,6},{8,9},{9,8},{10,11... | collective-permute-start | bytes 1572872 | tf_op jit(solution)/shard_map/ppermute | solution.py:227
  4.1 0.1 dynamic_slice.6
  4.1 0.6 fusion
  6.0 9.2 %collective-permute-done = bf16[2,512,256]{2,1,0:T(8,128)(2,1)S(1)} collective-permute-done((bf16[2,512,256]{2,1,0:T(8,128)(2,1)S(1)}, bf16[2,512,256]{2,1,0:T(8,128)(2,1)S(1)}, u32[]{:S(2)}, u32[]{:S(2)}) %collective-permute-start) | collective-permute-done | bytes 524320 | tf_op jit(solution)/shard_map/ppermute | solution.py:227
  15.3 0.9 broadcast_select_fusion.7
  16.1 4.6 %collective-permute-start.2 = (bf16[2,512,256]{2,1,0:T(8,128)(2,1)}, bf16[2,512,256]{2,1,0:T(8,128)(2,1)S(1)}, u32[]{:S(2)}, u32[]{:S(2)}) collective-permute-start(bf16[2,512,256]{2,1,0:T(8,128)(2,1)} %get-tuple-element.83), channel_id=1, source_target_pairs={{2,0},{4,2},{6,4},{8,6},{10,8},{12,10},{14,12},{16,14},{18,16},{20... | collective-permute-start | bytes 1572872 | tf_op jit(solution)/shard_map/ppermute | solution.py:231
  20.7 3.0 %collective-permute-start.1 = (bf16[2,512,256]{2,1,0:T(8,128)(2,1)S(1)}, bf16[2,512,256]{2,1,0:T(8,128)(2,1)S(1)}, u32[]{:S(2)}, u32[]{:S(2)}) collective-permute-start(bf16[2,512,256]{2,1,0:T(8,128)(2,1)S(1)} %get-tuple-element.84), channel_id=1, source_target_pairs={{0,2},{2,4},{4,6},{6,8},{8,10},{10,12},{12,14},{14,16},{16,18},{18... | collective-permute-start | bytes 1572872 | tf_op jit(solution)/shard_map/ppermute | solution.py:231
  25.1 0.1 pad_dynamic-slice_fusion
  25.2 1.3 %collective-permute-done.3 = bf16[2,512,256]{2,1,0:T(8,128)(2,1)S(1)} collective-permute-done((bf16[2,512,256]{2,1,0:T(8,128)(2,1)S(1)}, bf16[2,512,256]{2,1,0:T(8,128)(2,1)S(1)}, u32[]{:S(2)}, u32[]{:S(2)}) %collective-permute-start.3) | collective-permute-done | bytes 524320 | tf_op jit(solution)/shard_map/ppermute | solution.py:227
  26.5 0.9 broadcast_select_fusion.6
  27.4 3.4 %collective-permute-start.5 = (bf16[2,512,256]{2,1,0:T(8,128)(2,1)}, bf16[2,512,256]{2,1,0:T(8,128)(2,1)S(1)}, u32[]{:S(2)}, u32[]{:S(2)}) collective-permute-start(bf16[2,512,256]{2,1,0:T(8,128)(2,1)} %get-tuple-element.73), channel_id=1, source_target_pairs={{2,0},{4,2},{6,4},{8,6},{10,8},{12,10},{14,12},{16,14},{18,16},{20... | collective-permute-start | bytes 1572872 | tf_op jit(solution)/shard_map/ppermute | solution.py:231
  30.8 3.0 %collective-permute-start.4 = (bf16[2,512,256]{2,1,0:T(8,128)(2,1)S(1)}, bf16[2,512,256]{2,1,0:T(8,128)(2,1)S(1)}, u32[]{:S(2)}, u32[]{:S(2)}) collective-permute-start(bf16[2,512,256]{2,1,0:T(8,128)(2,1)S(1)} %get-tuple-element.74), channel_id=1, source_target_pairs={{0,2},{2,4},{4,6},{6,8},{8,10},{10,12},{12,14},{14,16},{16,18},{18... | collective-permute-start | bytes 1572872 | tf_op jit(solution)/shard_map/ppermute | solution.py:231
  33.9 0.9 convert_reduce_fusion
  34.8 4.7 %collective-permute-done.1 = bf16[2,512,256]{2,1,0:T(8,128)(2,1)S(1)} collective-permute-done((bf16[2,512,256]{2,1,0:T(8,128)(2,1)S(1)}, bf16[2,512,256]{2,1,0:T(8,128)(2,1)S(1)}, u32[]{:S(2)}, u32[]{:S(2)}) %collective-permute-start.1) | collective-permute-done | bytes 524320 | tf_op jit(solution)/shard_map/ppermute | solution.py:231
  39.5 0.9 broadcast_select_fusion.18
  40.4 0.3 collective-permute-start.7
  40.6 7.4 %attention.4 = (bf16[512,2048]{1,0:T(8,128)(2,1)}, f32[512,1024]{1,0:T(8,128)}, f32[512,1024]{1,0:T(8,128)}, bf16[2,512,256]{2,1,0:T(8,128)(2,1)}) custom-call(s32[1]{0:T(128)} %bitcast.4.group_ref, s32[1,512]{1,0:T(1,128)} %bitcast.21, bf16[512,2048]{1,0:T(8,128)(2,1)} %q_ref.7, bf16[512,1024]{1,0:T(8,128)(2,1)} %k_ref.7, bf16[512,1024]{1,0:T(8,128)(2,1)} %v_ref.7, ...), custom_call_target="tpu_custom_call" | custom-call | flops 1677721600 | bytes 2457600 | tf_op jit(solution)/shard_map/attention/pallas_call | solution.py:128
  48.0 0.9 broadcast_select_fusion.14
  48.9 1.2 collective-permute-start.6
  50.1 7.4 %attention.5 = (bf16[512,2048]{1,0:T(8,128)(2,1)}, f32[512,1024]{1,0:T(8,128)}, f32[512,1024]{1,0:T(8,128)}, bf16[2,512,256]{2,1,0:T(8,128)(2,1)}) custom-call(s32[1]{0:T(128)} %bitcast.4.group_ref, s32[1,512]{1,0:T(1,128)} %bitcast.22, bf16[512,2048]{1,0:T(8,128)(2,1)} %q_ref.7, ...), custom_call_target="tpu_custom_call", output_to_operand_aliasing={{0}: (8, {}), {1}: (9, {}), {2}: (10, {})} | custom-call | flops 1677721600 | bytes 2457600 | tf_op jit(solution)/shard_map/attention/pallas_call | solution.py:128
  57.5 0.8 copy-done
  58.3 7.4 %attention.6 = (bf16[512,2048]{1,0:T(8,128)(2,1)}, f32[512,1024]{1,0:T(8,128)}, f32[512,1024]{1,0:T(8,128)}, bf16[2,512,256]{2,1,0:T(8,128)(2,1)}) custom-call(s32[1]{0:T(128)} %bitcast.group_ref, s32[1,512]{1,0:T(1,128)} %bitcast.23, bf16[512,2048]{1,0:T(8,128)(2,1)} %q_ref.7, ...), custom_call_target="tpu_custom_call", output_to_operand_aliasing={{0}: (8, {}), {1}: (9, {}), {2}: (10, {})} | custom-call | flops 1677721600 | bytes 2457600 | tf_op jit(solution)/shard_map/attention/pallas_call | solution.py:128
  65.7 0.3 collective-permute-start.12
  66.0 0.8 copy-done.1
  66.8 7.4 %attention.7 = (bf16[512,2048]{1,0:T(8,128)(2,1)}, f32[512,1024]{1,0:T(8,128)}, f32[512,1024]{1,0:T(8,128)}, bf16[2,512,256]{2,1,0:T(8,128)(2,1)}) custom-call(s32[1]{0:T(128)} %bitcast.group_ref, s32[1,512]{1,0:T(1,128)} %bitcast.24, bf16[512,2048]{1,0:T(8,128)(2,1)} %q_ref.7, ...), custom_call_target="tpu_custom_call", output_to_operand_aliasing={{0}: (8, {}), {1}: (9, {}), {2}: (10, {})} | custom-call | flops 1677721600 | bytes 2457600 | tf_op jit(solution)/shard_map/attention/pallas_call | solution.py:128
  74.3 1.3 %collective-permute-start.8 = (bf16[2,512,256]{2,1,0:T(8,128)(2,1)}, bf16[2,512,256]{2,1,0:T(8,128)(2,1)S(1)}, u32[]{:S(2)}, u32[]{:S(2)}) collective-permute-start(bf16[2,512,256]{2,1,0:T(8,128)(2,1)} %get-tuple-element.50), channel_id=1, source_target_pairs={{0,1},{1,0},{2,3},{3,2},{4,5},{5,4},{6,7},{7,6},{8,9},{9,8},{10,11... | collective-permute-start | bytes 1572872 | tf_op jit(solution)/shard_map/ppermute | solution.py:227
  75.5 2.4 %collective-permute-done.12 = bf16[2,512,256]{2,1,0:T(8,128)(2,1)S(1)} collective-permute-done((bf16[2,512,256]{2,1,0:T(8,128)(2,1)}, bf16[2,512,256]{2,1,0:T(8,128)(2,1)S(1)}, u32[]{:S(2)}, u32[]{:S(2)}) %collective-permute-start.12) | collective-permute-done | bytes 524320 | tf_op jit(solution)/shard_map/ppermute | solution.py:227
  78.0 0.9 broadcast_select_fusion.2
  78.8 1.9 %collective-permute-start.13 = (bf16[2,512,256]{2,1,0:T(8,128)(2,1)}, bf16[2,512,256]{2,1,0:T(8,128)(2,1)S(1)}, u32[]{:S(2)}, u32[]{:S(2)}) collective-permute-start(bf16[2,512,256]{2,1,0:T(8,128)(2,1)} %get-tuple-element.69), channel_id=1, source_target_pairs={{2,0},{4,2},{6,4},{8,6},{10,8},{12,10},{14,12},{16,14},{18,16},{20... | collective-permute-start | bytes 1572872 | tf_op jit(solution)/shard_map/ppermute | solution.py:231
  80.7 6.1 %collective-permute-start.14 = (bf16[2,512,256]{2,1,0:T(8,128)(2,1)S(1)}, bf16[2,512,256]{2,1,0:T(8,128)(2,1)S(1)}, u32[]{:S(2)}, u32[]{:S(2)}) collective-permute-start(bf16[2,512,256]{2,1,0:T(8,128)(2,1)S(1)} %get-tuple-element.70), channel_id=1, source_target_pairs={{0,2},{2,4},{4,6},{6,8},{8,10},{10,12},{12,14},{14,16},{16,18},{18... | collective-permute-start | bytes 1572872 | tf_op jit(solution)/shard_map/ppermute | solution.py:231
  86.9 0.9 broadcast_select_fusion.3
  87.8 1.9 %collective-permute-start.9 = (bf16[2,512,256]{2,1,0:T(8,128)(2,1)}, bf16[2,512,256]{2,1,0:T(8,128)(2,1)S(1)}, u32[]{:S(2)}, u32[]{:S(2)}) collective-permute-start(bf16[2,512,256]{2,1,0:T(8,128)(2,1)} %get-tuple-element.71), channel_id=1, source_target_pairs={{2,0},{4,2},{6,4},{8,6},{10,8},{12,10},{14,12},{16,14},{18,16},{20... | collective-permute-start | bytes 1572872 | tf_op jit(solution)/shard_map/ppermute | solution.py:231
  89.7 4.4 %collective-permute-start.10 = (bf16[2,512,256]{2,1,0:T(8,128)(2,1)S(1)}, bf16[2,512,256]{2,1,0:T(8,128)(2,1)S(1)}, u32[]{:S(2)}, u32[]{:S(2)}) collective-permute-start(bf16[2,512,256]{2,1,0:T(8,128)(2,1)S(1)} %get-tuple-element.72), channel_id=1, source_target_pairs={{0,2},{2,4},{4,6},{6,8},{8,10},{10,12},{12,14},{14,16},{16,18},{18... | collective-permute-start | bytes 1572872 | tf_op jit(solution)/shard_map/ppermute | solution.py:231
  94.1 9.4 %collective-permute-done.13 = bf16[2,512,256]{2,1,0:T(8,128)(2,1)S(1)} collective-permute-done((bf16[2,512,256]{2,1,0:T(8,128)(2,1)}, bf16[2,512,256]{2,1,0:T(8,128)(2,1)S(1)}, u32[]{:S(2)}, u32[]{:S(2)}) %collective-permute-start.13) | collective-permute-done | bytes 524320 | tf_op jit(solution)/shard_map/ppermute | solution.py:231
  103.5 0.9 broadcast_select_fusion
  104.5 4.7 %collective-permute-done.9 = bf16[2,512,256]{2,1,0:T(8,128)(2,1)S(1)} collective-permute-done((bf16[2,512,256]{2,1,0:T(8,128)(2,1)}, bf16[2,512,256]{2,1,0:T(8,128)(2,1)S(1)}, u32[]{:S(2)}, u32[]{:S(2)}) %collective-permute-start.9) | collective-permute-done | bytes 524320 | tf_op jit(solution)/shard_map/ppermute | solution.py:231
  109.2 0.9 broadcast_select_fusion.1
  110.1 2.1 %finish.4 = (bf16[512,1024]{1,0:T(8,128)(2,1)}, bf16[512,1024]{1,0:T(8,128)(2,1)}) custom-call(s32[1]{0:T(128)} %bitcast.4.group_ref, f32[512,1024]{1,0:T(8,128)} %get-tuple-element.47.dk_ref, f32[512,1024]{1,0:T(8,128)} %get-tuple-element.48.dv_ref, bf16[2,512,256]{2,1,0:T(8,128)(2,1)} %get-tuple-element.61.back_ref), custom_call_target="tpu_custom_call" | custom-call | flops 524288 | bytes 2097152 | tf_op jit(solution)/shard_map/finish/pallas_call | solution.py:178
  112.2 4.4 %collective-permute-done.15.back_ref = bf16[2,512,256]{2,1,0:T(8,128)(2,1)S(1)} collective-permute-done((bf16[2,512,256]{2,1,0:T(8,128)(2,1)S(1)}, bf16[2,512,256]{2,1,0:T(8,128)(2,1)S(1)}, u32[]{:S(2)}, u32[]{:S(2)}) %collective-permute-start.15) | collective-permute-done | bytes 524320 | tf_op jit(solution)/shard_map/ppermute | solution.py:227
  116.6 0.8 copy-done.5
  117.4 2.1 %finish.5 = (bf16[512,1024]{1,0:T(8,128)(2,1)}, bf16[512,1024]{1,0:T(8,128)(2,1)}) custom-call(s32[1]{0:T(128)} %bitcast.group_ref, f32[512,1024]{1,0:T(8,128)} %get-tuple-element.47.dk_ref, f32[512,1024]{1,0:T(8,128)} %get-tuple-element.48.dv_ref, bf16[2,512,256]{2,1,0:T(8,128)(2,1)} %copy-done.5, ...), custom_call_target="tpu_custom_call", output_to_operand_aliasing={{0}: (4, {}), {1}: (5, {})} | custom-call | flops 524288 | bytes 2097152 | tf_op jit(solution)/shard_map/finish/pallas_call | solution.py:178
  119.5 2.1 %finish.6 = (bf16[512,1024]{1,0:T(8,128)(2,1)}, bf16[512,1024]{1,0:T(8,128)(2,1)}) custom-call(s32[1]{0:T(128)} %bitcast.4.group_ref, f32[512,1024]{1,0:T(8,128)} %get-tuple-element.47.dk_ref, f32[512,1024]{1,0:T(8,128)} %get-tuple-element.48.dv_ref, bf16[2,512,256]{2,1,0:T(8,128)(2,1)} %get-tuple-element.63.back_ref, ...), custom_call_target="tpu_custom_call", output_to_operand_aliasing={{0}: (4, {}), {1}: (5, {})} | custom-call | flops 524288 | bytes 2097152 | tf_op jit(solution)/shard_map/finish/pallas_call | solution.py:178
  121.6 0.6 collective-permute-done.11.back_ref
  122.2 0.8 copy-done.4
  123.0 2.1 %finish.7 = (bf16[512,1024]{1,0:T(8,128)(2,1)}, bf16[512,1024]{1,0:T(8,128)(2,1)}) custom-call(s32[1]{0:T(128)} %bitcast.group_ref, f32[512,1024]{1,0:T(8,128)} %get-tuple-element.47.dk_ref, f32[512,1024]{1,0:T(8,128)} %get-tuple-element.48.dv_ref, bf16[2,512,256]{2,1,0:T(8,128)(2,1)} %copy-done.4, ...), custom_call_target="tpu_custom_call", output_to_operand_aliasing={{0}: (4, {}), {1}: (5, {})} | custom-call | flops 524288 | bytes 2097152 | tf_op jit(solution)/shard_map/finish/pallas_call | solution.py:178
  (24 shorter events, 0.1 us)
Async XLA Ops:
  2.3 1.7 %copy-start.7 = (s32[32]{0:T(128)S(1)}, s32[32]{0:T(128)}, u32[]{:S(2)}) copy-start(s32[32]{0:T(128)} %param.13) | copy-start | bytes 388
  2.4 22.8 %copy-start.6 = (s32[16384]{0:T(1024)S(1)}, s32[16384]{0:T(1024)}, u32[]{:S(2)}) copy-start(s32[16384]{0:T(1024)} %param.12) | copy-start | bytes 196612
  2.4 12.9 %collective-permute-start = (bf16[2,512,256]{2,1,0:T(8,128)(2,1)S(1)}, bf16[2,512,256]{2,1,0:T(8,128)(2,1)S(1)}, u32[]{:S(2)}, u32[]{:S(2)}) collective-permute-start(bf16[2,512,256]{2,1,0:T(8,128)(2,1)S(1)} %pad_maximum_fusion.1), channel_id=1, source_target_pairs={{0,1},{1,0},{2,3},{3,2},{4,5},{5,4},{6,7},{7,6},{8,9},{9,8},{10,11... | collective-permute-start | bytes 1572872 | tf_op jit(solution)/shard_map/ppermute | solution.py:227
  2.8 23.7 %collective-permute-start.3 = (bf16[2,512,256]{2,1,0:T(8,128)(2,1)S(1)}, bf16[2,512,256]{2,1,0:T(8,128)(2,1)S(1)}, u32[]{:S(2)}, u32[]{:S(2)}) collective-permute-start(bf16[2,512,256]{2,1,0:T(8,128)(2,1)S(1)} %pad_maximum_fusion.3), channel_id=1, source_target_pairs={{0,1},{1,0},{2,3},{3,2},{4,5},{5,4},{6,7},{7,6},{8,9},{9,8},{10,11... | collective-permute-start | bytes 1572872 | tf_op jit(solution)/shard_map/ppermute | solution.py:227
  16.1 18.7 %collective-permute-start.2 = (bf16[2,512,256]{2,1,0:T(8,128)(2,1)}, bf16[2,512,256]{2,1,0:T(8,128)(2,1)S(1)}, u32[]{:S(2)}, u32[]{:S(2)}) collective-permute-start(bf16[2,512,256]{2,1,0:T(8,128)(2,1)} %get-tuple-element.83), channel_id=1, source_target_pairs={{2,0},{4,2},{6,4},{8,6},{10,8},{12,10},{14,12},{16,14},{18,16},{20... | collective-permute-start | bytes 1572872 | tf_op jit(solution)/shard_map/ppermute | solution.py:231
  20.7 18.8 %collective-permute-start.1 = (bf16[2,512,256]{2,1,0:T(8,128)(2,1)S(1)}, bf16[2,512,256]{2,1,0:T(8,128)(2,1)S(1)}, u32[]{:S(2)}, u32[]{:S(2)}) collective-permute-start(bf16[2,512,256]{2,1,0:T(8,128)(2,1)S(1)} %get-tuple-element.84), channel_id=1, source_target_pairs={{0,2},{2,4},{4,6},{6,8},{8,10},{10,12},{12,14},{14,16},{16,18},{18... | collective-permute-start | bytes 1572872 | tf_op jit(solution)/shard_map/ppermute | solution.py:231
  27.4 20.6 %collective-permute-start.5 = (bf16[2,512,256]{2,1,0:T(8,128)(2,1)}, bf16[2,512,256]{2,1,0:T(8,128)(2,1)S(1)}, u32[]{:S(2)}, u32[]{:S(2)}) collective-permute-start(bf16[2,512,256]{2,1,0:T(8,128)(2,1)} %get-tuple-element.73), channel_id=1, source_target_pairs={{2,0},{4,2},{6,4},{8,6},{10,8},{12,10},{14,12},{16,14},{18,16},{20... | collective-permute-start | bytes 1572872 | tf_op jit(solution)/shard_map/ppermute | solution.py:231
  30.8 17.2 %collective-permute-start.4 = (bf16[2,512,256]{2,1,0:T(8,128)(2,1)S(1)}, bf16[2,512,256]{2,1,0:T(8,128)(2,1)S(1)}, u32[]{:S(2)}, u32[]{:S(2)}) collective-permute-start(bf16[2,512,256]{2,1,0:T(8,128)(2,1)S(1)} %get-tuple-element.74), channel_id=1, source_target_pairs={{0,2},{2,4},{4,6},{6,8},{8,10},{10,12},{12,14},{14,16},{16,18},{18... | collective-permute-start | bytes 1572872 | tf_op jit(solution)/shard_map/ppermute | solution.py:231
  40.4 17.1 %collective-permute-start.7 = (bf16[2,512,256]{2,1,0:T(8,128)(2,1)S(1)}, bf16[2,512,256]{2,1,0:T(8,128)(2,1)S(1)}, u32[]{:S(2)}, u32[]{:S(2)}) collective-permute-start(bf16[2,512,256]{2,1,0:T(8,128)(2,1)S(1)} %get-tuple-element.67), channel_id=1, source_target_pairs={{0,1},{1,0},{2,3},{3,2},{4,5},{5,4},{6,7},{7,6},{8,9},{9,8},{10,11... | collective-permute-start | bytes 1572872 | tf_op jit(solution)/shard_map/ppermute | solution.py:227
  48.9 17.1 %collective-permute-start.6 = (bf16[2,512,256]{2,1,0:T(8,128)(2,1)S(1)}, bf16[2,512,256]{2,1,0:T(8,128)(2,1)S(1)}, u32[]{:S(2)}, u32[]{:S(2)}) collective-permute-start(bf16[2,512,256]{2,1,0:T(8,128)(2,1)S(1)} %get-tuple-element.66), channel_id=1, source_target_pairs={{0,1},{1,0},{2,3},{3,2},{4,5},{5,4},{6,7},{7,6},{8,9},{9,8},{10,11... | collective-permute-start | bytes 1572872 | tf_op jit(solution)/shard_map/ppermute | solution.py:227
  57.5 0.8 copy-start
  65.7 12.3 %collective-permute-start.12 = (bf16[2,512,256]{2,1,0:T(8,128)(2,1)}, bf16[2,512,256]{2,1,0:T(8,128)(2,1)S(1)}, u32[]{:S(2)}, u32[]{:S(2)}) collective-permute-start(bf16[2,512,256]{2,1,0:T(8,128)(2,1)} %get-tuple-element.52), channel_id=1, source_target_pairs={{0,1},{1,0},{2,3},{3,2},{4,5},{5,4},{6,7},{7,6},{8,9},{9,8},{10,11... | collective-permute-start | bytes 1572872 | tf_op jit(solution)/shard_map/ppermute | solution.py:227
  66.0 0.8 copy-start.1
  66.8 11.2 %copy-start.2 = (bf16[2,512,256]{2,1,0:T(8,128)(2,1)S(1)}, bf16[2,512,256]{2,1,0:T(8,128)(2,1)}, u32[]{:S(2)}) copy-start(bf16[2,512,256]{2,1,0:T(8,128)(2,1)} %get-tuple-element.51) | copy-start | bytes 1572868
  74.2 12.6 %copy-start.3 = (bf16[2,512,256]{2,1,0:T(8,128)(2,1)S(1)}, bf16[2,512,256]{2,1,0:T(8,128)(2,1)}, u32[]{:S(2)}) copy-start(bf16[2,512,256]{2,1,0:T(8,128)(2,1)} %get-tuple-element.49) | copy-start | bytes 1572868
  74.3 12.6 %collective-permute-start.8 = (bf16[2,512,256]{2,1,0:T(8,128)(2,1)}, bf16[2,512,256]{2,1,0:T(8,128)(2,1)S(1)}, u32[]{:S(2)}, u32[]{:S(2)}) collective-permute-start(bf16[2,512,256]{2,1,0:T(8,128)(2,1)} %get-tuple-element.50), channel_id=1, source_target_pairs={{0,1},{1,0},{2,3},{3,2},{4,5},{5,4},{6,7},{7,6},{8,9},{9,8},{10,11... | collective-permute-start | bytes 1572872 | tf_op jit(solution)/shard_map/ppermute | solution.py:227
  78.8 24.7 %collective-permute-start.13 = (bf16[2,512,256]{2,1,0:T(8,128)(2,1)}, bf16[2,512,256]{2,1,0:T(8,128)(2,1)S(1)}, u32[]{:S(2)}, u32[]{:S(2)}) collective-permute-start(bf16[2,512,256]{2,1,0:T(8,128)(2,1)} %get-tuple-element.69), channel_id=1, source_target_pairs={{2,0},{4,2},{6,4},{8,6},{10,8},{12,10},{14,12},{16,14},{18,16},{20... | collective-permute-start | bytes 1572872 | tf_op jit(solution)/shard_map/ppermute | solution.py:231
  80.7 22.8 %collective-permute-start.14 = (bf16[2,512,256]{2,1,0:T(8,128)(2,1)S(1)}, bf16[2,512,256]{2,1,0:T(8,128)(2,1)S(1)}, u32[]{:S(2)}, u32[]{:S(2)}) collective-permute-start(bf16[2,512,256]{2,1,0:T(8,128)(2,1)S(1)} %get-tuple-element.70), channel_id=1, source_target_pairs={{0,2},{2,4},{4,6},{6,8},{8,10},{10,12},{12,14},{14,16},{16,18},{18... | collective-permute-start | bytes 1572872 | tf_op jit(solution)/shard_map/ppermute | solution.py:231
  87.8 21.4 %collective-permute-start.9 = (bf16[2,512,256]{2,1,0:T(8,128)(2,1)}, bf16[2,512,256]{2,1,0:T(8,128)(2,1)S(1)}, u32[]{:S(2)}, u32[]{:S(2)}) collective-permute-start(bf16[2,512,256]{2,1,0:T(8,128)(2,1)} %get-tuple-element.71), channel_id=1, source_target_pairs={{2,0},{4,2},{6,4},{8,6},{10,8},{12,10},{14,12},{16,14},{18,16},{20... | collective-permute-start | bytes 1572872 | tf_op jit(solution)/shard_map/ppermute | solution.py:231
  89.7 19.5 %collective-permute-start.10 = (bf16[2,512,256]{2,1,0:T(8,128)(2,1)S(1)}, bf16[2,512,256]{2,1,0:T(8,128)(2,1)S(1)}, u32[]{:S(2)}, u32[]{:S(2)}) collective-permute-start(bf16[2,512,256]{2,1,0:T(8,128)(2,1)S(1)} %get-tuple-element.72), channel_id=1, source_target_pairs={{0,2},{2,4},{4,6},{6,8},{8,10},{10,12},{12,14},{14,16},{16,18},{18... | collective-permute-start | bytes 1572872 | tf_op jit(solution)/shard_map/ppermute | solution.py:231
  104.5 12.1 %collective-permute-start.15 = (bf16[2,512,256]{2,1,0:T(8,128)(2,1)S(1)}, bf16[2,512,256]{2,1,0:T(8,128)(2,1)S(1)}, u32[]{:S(2)}, u32[]{:S(2)}) collective-permute-start(bf16[2,512,256]{2,1,0:T(8,128)(2,1)S(1)} %get-tuple-element.62), channel_id=1, source_target_pairs={{0,1},{1,0},{2,3},{3,2},{4,5},{5,4},{6,7},{7,6},{8,9},{9,8},{10,11... | collective-permute-start | bytes 1572872 | tf_op jit(solution)/shard_map/ppermute | solution.py:227
  110.1 12.1 %collective-permute-start.11 = (bf16[2,512,256]{2,1,0:T(8,128)(2,1)S(1)}, bf16[2,512,256]{2,1,0:T(8,128)(2,1)S(1)}, u32[]{:S(2)}, u32[]{:S(2)}) collective-permute-start(bf16[2,512,256]{2,1,0:T(8,128)(2,1)S(1)} %get-tuple-element.64), channel_id=1, source_target_pairs={{0,1},{1,0},{2,3},{3,2},{4,5},{5,4},{6,7},{7,6},{8,9},{9,8},{10,11... | collective-permute-start | bytes 1572872 | tf_op jit(solution)/shard_map/ppermute | solution.py:227
  116.6 0.8 copy-start.5
  122.2 0.8 copy-start.4

commit v5 on v4

--- a/solution.py
+++ b/solution.py
@@ -13,6 +13,7 @@
 CHUNKS = 2
 TILE = 128
 STRIP = 64
+TOGETHER = 2
 VMEM_BYTES = 60 * 1024 * 1024
 
 
@@ -46,25 +47,24 @@
     dk_sum[...] = jnp.zeros_like(dk_sum)
     dv_sum[...] = jnp.zeros_like(dv_sum)
     lane = lax.broadcasted_iota(jnp.int32, (1, lanes), 1) % TILE
-    tiles = range(rows // TILE)
+    together = scores.shape[0]
 
     def stacked(ref, start):
         return jnp.concatenate(
-            [ref[start : start + TILE, m * head : (m + 1) * head] for m in range(members)], axis=0
+            [ref[pl.ds(start, TILE), m * head : (m + 1) * head] for m in range(members)], axis=0
         )
 
-    def enter(tile):
-        keys = pl.ds(tile * TILE, span)
-        queries, grads = stacked(q_ref, tile * TILE), stacked(do_ref, tile * TILE)
+    def enter(start, tile):
+        keys = pl.ds(start, span)
+        queries, grads = stacked(q_ref, start), stacked(do_ref, start)
         scores[tile] = dot(k_all[keys], queries, 1, 1)
         slopes[tile] = dot(v_all[keys], grads, 1, 1)
         return queries, grads
 
-    def weigh(tile, grads):
-        start = tile * TILE
+    def weigh(start, tile, grads):
         product = grads.astype(jnp.float32) * stacked(o_ref, start).astype(jnp.float32)
         delta = jnp.sum(product.T, axis=0, keepdims=True)
-        low = jnp.concatenate([low_ref[:, start : start + TILE]] * members, axis=1) - start
+        low = jnp.concatenate([low_ref[:, pl.ds(start, TILE)]] * members, axis=1) - start
 
         def visible(strip):
             index = strip.start + lax.broadcasted_iota(jnp.int32, (STRIP, lanes), 0)
@@ -88,23 +88,25 @@
             weights_b[tile, strip] = weights.astype(jnp.bfloat16)
             slopes_b[tile, strip] = (weights * (slopes[tile, strip] - delta)).astype(jnp.bfloat16)
 
-    def leave(tile, queries, grads):
-        start = tile * TILE
+    def leave(start, tile, queries, grads):
         keys = pl.ds(start, span)
         dv_sum[keys] += dot(weights_b[tile], grads, 1, 0)
         dk_sum[keys] += dot(slopes_b[tile], queries, 1, 0)
         dq = (dot(k_turned[:, keys], slopes_b[tile], 1, 0) * scale).T
         for m in range(members):
-            dq_ref[start : start + TILE, m * head : (m + 1) * head] = dq[
+            dq_ref[pl.ds(start, TILE), m * head : (m + 1) * head] = dq[
                 m * TILE : (m + 1) * TILE
             ].astype(dq_ref.dtype)
 
-    entered = {0: enter(0)}
-    for tile in tiles:
-        if tile + 1 in tiles:
-            entered[tile + 1] = enter(tile + 1)
-        weigh(tile, entered[tile][1])
-        leave(tile, *entered[tile])
+    @pl.loop(0, rows // TILE, step=together)
+    def _(first):
+        starts = [pl.multiple_of((first + tile) * TILE, TILE) for tile in range(together)]
+        entered = [enter(start, tile) for tile, start in enumerate(starts)]
+        for tile, start in enumerate(starts):
+            weigh(start, tile, entered[tile][1])
+        for tile, start in enumerate(starts):
+            leave(start, tile, *entered[tile])
+
     back_ref[0] = dk_sum[:window].astype(back_ref.dtype)
     back_ref[1] = dv_sum[:window].astype(back_ref.dtype)
     dk_ref[...] = dk_sum[window:]
@@ -123,7 +125,7 @@
     key_spec = pl.BlockSpec((rows, HEAD_SIZE), column)
     past_spec = pl.BlockSpec((2, window, HEAD_SIZE), lambda step, group_ref: (0, 0, step))
     low_spec = pl.BlockSpec((1, rows), lambda step, group_ref: (0, 0))
-    square = (rows // TILE, window + TILE, wide // HEAD_SIZE * TILE)
+    square = (min(TOGETHER, rows // TILE), window + TILE, wide // HEAD_SIZE * TILE)
     tiles = count * queries.shape[1] // keys.shape[1] * rows * (window + TILE)
     return pl.pallas_call(
         functools.partial(attention_body, len(carried)),

time: 126 us -> 130 us (1.032)
  Pallas kernels: 38 us -> 43.4 us
    pallas_call x4, Pallas kernels: 29.5 us -> 34.9 us  [attention(): pl.pallas_call(functools.partial(attention_body, len(carried)), grid_spec...]
    ppermute x8, waiting for transfers between devices: 18.8 us -> 17.5 us  [shifted(): lax.ppermute(value, 'blk', [(source, source + step) for source in range(f...]
  transfers between devices with their start and end apart: 16 -> 16, of which waited for: 8 -> 8; matrix products, arithmetic and copies ran while one was open for 7% -> 7% of each run, Pallas kernels for 29% -> 32%
where the time goes in v5:
time: 130 us; the launch traced here: 129 us
  Pallas kernels  43.4 us (33%)
  waiting for transfers between devices  35.5 us (27%)
  starting transfers between devices  33 us (25%)
  other arithmetic  9.77 us (8%)
  local copies, waits for them, and re-layouts  3.96 us (3%)
  between operations  3.46 us (3%)
    pallas_call x4, Pallas kernels, attention(): pl.pallas_call(functools.partial(attention_body, len(carried)), grid_spec...  34.9 us
    ppermute x8, starting transfers between devices, shifted(): lax.ppermute(value, 'blk', [(source, source + step) for source in range(f...  28.3 us
    ppermute x8, waiting for transfers between devices, turned(): return lax.ppermute(value, 'head', pairs)  18 us
    ppermute x8, waiting for transfers between devices, shifted(): lax.ppermute(value, 'blk', [(source, source + step) for source in range(f...  17.5 us
    pallas_call x4, Pallas kernels, finish(): pl.pallas_call(functools.partial(finish_body, len(carried)), grid_spec=pl...  8.44 us
    ppermute x8, starting transfers between devices, turned(): return lax.ppermute(value, 'head', pairs)  4.67 us
    select_n x4, other arithmetic, pick(): result = jnp.where(index == place, items[place], result)  3.46 us
    unnamed x16, local copies, waits for them, and re-layouts  3.21 us
  transfers between devices with their start and end apart: 16, of which 8 were waited for; matrix products, arithmetic and copies ran while one was open for 7% of the time, Pallas kernels for 32%

profile of v5, /device:TPU:11, one launch (start us, length us, event | category | flops | bytes accessed | tf_op | source)
XLA Modules:
  0.0 129.0 jit_solution(15343672397056379138)
XLA Ops:
  0.6 1.7 %select_bitcast_fusion.2 = (bf16[1,512,256]{2,1,0:T(8,128)(2,1)S(1)}, bf16[1,512,256]{2,1,0:T(8,128)(2,1)S(1)}, bf16[1,512,256]{2,1,0:T(8,128)(2,1)S(1)}, bf16[1...) fusion(pred[]{:T(512)S(6)} %eq.22, ...), kind=kLoop, calls=%fused_computation.27 | loop fusion | flops 1048576 | bytes 4194306 | tf_op jit(solution)/shard_map/stack | solution.py:243
  2.4 0.1 pad_maximum_fusion.1
  2.4 0.3 collective-permute-start
  2.8 1.3 collective-permute-start.3
  4.1 0.1 dynamic_slice.6
  4.1 0.6 fusion
  6.0 9.2 %collective-permute-done = bf16[2,512,256]{2,1,0:T(8,128)(2,1)S(1)} collective-permute-done((bf16[2,512,256]{2,1,0:T(8,128)(2,1)S(1)}, bf16[2,512,256]{2,1,0:T(8,128)(2,1)S(1)}, u32[]{:S(2)}, u32[]{:S(2)}) %collective-permute-start) | collective-permute-done | bytes 524320 | tf_op jit(solution)/shard_map/ppermute | solution.py:229
  15.3 0.9 broadcast_select_fusion.7
  16.1 4.6 %collective-permute-start.2 = (bf16[2,512,256]{2,1,0:T(8,128)(2,1)}, bf16[2,512,256]{2,1,0:T(8,128)(2,1)S(1)}, u32[]{:S(2)}, u32[]{:S(2)}) collective-permute-start(bf16[2,512,256]{2,1,0:T(8,128)(2,1)} %get-tuple-element.83), channel_id=1, source_target_pairs={{2,0},{4,2},{6,4},{8,6},{10,8},{12,10},{14,12},{16,14},{18,16},{20... | collective-permute-start | bytes 1572872 | tf_op jit(solution)/shard_map/ppermute | solution.py:233
  20.7 3.0 %collective-permute-start.1 = (bf16[2,512,256]{2,1,0:T(8,128)(2,1)S(1)}, bf16[2,512,256]{2,1,0:T(8,128)(2,1)S(1)}, u32[]{:S(2)}, u32[]{:S(2)}) collective-permute-start(bf16[2,512,256]{2,1,0:T(8,128)(2,1)S(1)} %get-tuple-element.84), channel_id=1, source_target_pairs={{0,2},{2,4},{4,6},{6,8},{8,10},{10,12},{12,14},{14,16},{16,18},{18... | collective-permute-start | bytes 1572872 | tf_op jit(solution)/shard_map/ppermute | solution.py:233
  25.1 0.1 pad_dynamic-slice_fusion
  25.2 1.3 %collective-permute-done.3 = bf16[2,512,256]{2,1,0:T(8,128)(2,1)S(1)} collective-permute-done((bf16[2,512,256]{2,1,0:T(8,128)(2,1)S(1)}, bf16[2,512,256]{2,1,0:T(8,128)(2,1)S(1)}, u32[]{:S(2)}, u32[]{:S(2)}) %collective-permute-start.3) | collective-permute-done | bytes 524320 | tf_op jit(solution)/shard_map/ppermute | solution.py:229
  26.5 0.9 broadcast_select_fusion.6
  27.4 3.4 %collective-permute-start.5 = (bf16[2,512,256]{2,1,0:T(8,128)(2,1)}, bf16[2,512,256]{2,1,0:T(8,128)(2,1)S(1)}, u32[]{:S(2)}, u32[]{:S(2)}) collective-permute-start(bf16[2,512,256]{2,1,0:T(8,128)(2,1)} %get-tuple-element.73), channel_id=1, source_target_pairs={{2,0},{4,2},{6,4},{8,6},{10,8},{12,10},{14,12},{16,14},{18,16},{20... | collective-permute-start | bytes 1572872 | tf_op jit(solution)/shard_map/ppermute | solution.py:233
  30.8 3.0 %collective-permute-start.4 = (bf16[2,512,256]{2,1,0:T(8,128)(2,1)S(1)}, bf16[2,512,256]{2,1,0:T(8,128)(2,1)S(1)}, u32[]{:S(2)}, u32[]{:S(2)}) collective-permute-start(bf16[2,512,256]{2,1,0:T(8,128)(2,1)S(1)} %get-tuple-element.74), channel_id=1, source_target_pairs={{0,2},{2,4},{4,6},{6,8},{8,10},{10,12},{12,14},{14,16},{16,18},{18... | collective-permute-start | bytes 1572872 | tf_op jit(solution)/shard_map/ppermute | solution.py:233
  33.9 0.9 convert_reduce_fusion
  34.8 4.7 %collective-permute-done.1 = bf16[2,512,256]{2,1,0:T(8,128)(2,1)S(1)} collective-permute-done((bf16[2,512,256]{2,1,0:T(8,128)(2,1)S(1)}, bf16[2,512,256]{2,1,0:T(8,128)(2,1)S(1)}, u32[]{:S(2)}, u32[]{:S(2)}) %collective-permute-start.1) | collective-permute-done | bytes 524320 | tf_op jit(solution)/shard_map/ppermute | solution.py:233
  39.5 0.9 broadcast_select_fusion.18
  40.4 0.3 collective-permute-start.7
  40.6 8.7 %attention.4 = (bf16[512,2048]{1,0:T(8,128)(2,1)}, f32[512,1024]{1,0:T(8,128)}, f32[512,1024]{1,0:T(8,128)}, bf16[2,512,256]{2,1,0:T(8,128)(2,1)}) custom-call(s32[1]{0:T(128)} %bitcast.4.group_ref, s32[1,512]{1,0:T(1,128)} %bitcast.21, bf16[512,2048]{1,0:T(8,128)(2,1)} %q_ref.7, bf16[512,1024]{1,0:T(8,128)(2,1)} %k_ref.7, bf16[512,1024]{1,0:T(8,128)(2,1)} %v_ref.7, ...), custom_call_target="tpu_custom_call" | custom-call | flops 1677721600 | bytes 2457600 | tf_op jit(solution)/shard_map/attention/pallas_call | solution.py:130
  49.4 0.9 broadcast_select_fusion.14
  50.3 1.2 collective-permute-start.6
  51.5 8.7 %attention.5 = (bf16[512,2048]{1,0:T(8,128)(2,1)}, f32[512,1024]{1,0:T(8,128)}, f32[512,1024]{1,0:T(8,128)}, bf16[2,512,256]{2,1,0:T(8,128)(2,1)}) custom-call(s32[1]{0:T(128)} %bitcast.4.group_ref, s32[1,512]{1,0:T(1,128)} %bitcast.22, bf16[512,2048]{1,0:T(8,128)(2,1)} %q_ref.7, ...), custom_call_target="tpu_custom_call", output_to_operand_aliasing={{0}: (8, {}), {1}: (9, {}), {2}: (10, {})} | custom-call | flops 1677721600 | bytes 2457600 | tf_op jit(solution)/shard_map/attention/pallas_call | solution.py:130
  60.2 0.8 copy-done
  61.0 8.7 %attention.6 = (bf16[512,2048]{1,0:T(8,128)(2,1)}, f32[512,1024]{1,0:T(8,128)}, f32[512,1024]{1,0:T(8,128)}, bf16[2,512,256]{2,1,0:T(8,128)(2,1)}) custom-call(s32[1]{0:T(128)} %bitcast.group_ref, s32[1,512]{1,0:T(1,128)} %bitcast.23, bf16[512,2048]{1,0:T(8,128)(2,1)} %q_ref.7, ...), custom_call_target="tpu_custom_call", output_to_operand_aliasing={{0}: (8, {}), {1}: (9, {}), {2}: (10, {})} | custom-call | flops 1677721600 | bytes 2457600 | tf_op jit(solution)/shard_map/attention/pallas_call | solution.py:130
  69.7 0.3 collective-permute-start.12
  70.1 0.8 copy-done.1
  70.9 8.8 %attention.7 = (bf16[512,2048]{1,0:T(8,128)(2,1)}, f32[512,1024]{1,0:T(8,128)}, f32[512,1024]{1,0:T(8,128)}, bf16[2,512,256]{2,1,0:T(8,128)(2,1)}) custom-call(s32[1]{0:T(128)} %bitcast.group_ref, s32[1,512]{1,0:T(1,128)} %bitcast.24, bf16[512,2048]{1,0:T(8,128)(2,1)} %q_ref.7, ...), custom_call_target="tpu_custom_call", output_to_operand_aliasing={{0}: (8, {}), {1}: (9, {}), {2}: (10, {})} | custom-call | flops 1677721600 | bytes 2457600 | tf_op jit(solution)/shard_map/attention/pallas_call | solution.py:130
  79.6 1.3 collective-permute-start.8
  80.9 0.9 broadcast_select_fusion.2
  81.8 1.9 %collective-permute-start.13 = (bf16[2,512,256]{2,1,0:T(8,128)(2,1)}, bf16[2,512,256]{2,1,0:T(8,128)(2,1)S(1)}, u32[]{:S(2)}, u32[]{:S(2)}) collective-permute-start(bf16[2,512,256]{2,1,0:T(8,128)(2,1)} %get-tuple-element.69), channel_id=1, source_target_pairs={{2,0},{4,2},{6,4},{8,6},{10,8},{12,10},{14,12},{16,14},{18,16},{20... | collective-permute-start | bytes 1572872 | tf_op jit(solution)/shard_map/ppermute | solution.py:233
  83.7 5.9 %collective-permute-start.14 = (bf16[2,512,256]{2,1,0:T(8,128)(2,1)S(1)}, bf16[2,512,256]{2,1,0:T(8,128)(2,1)S(1)}, u32[]{:S(2)}, u32[]{:S(2)}) collective-permute-start(bf16[2,512,256]{2,1,0:T(8,128)(2,1)S(1)} %get-tuple-element.70), channel_id=1, source_target_pairs={{0,2},{2,4},{4,6},{6,8},{8,10},{10,12},{12,14},{14,16},{16,18},{18... | collective-permute-start | bytes 1572872 | tf_op jit(solution)/shard_map/ppermute | solution.py:233
  89.6 1.3 %collective-permute-done.8 = bf16[2,512,256]{2,1,0:T(8,128)(2,1)S(1)} collective-permute-done((bf16[2,512,256]{2,1,0:T(8,128)(2,1)}, bf16[2,512,256]{2,1,0:T(8,128)(2,1)S(1)}, u32[]{:S(2)}, u32[]{:S(2)}) %collective-permute-start.8) | collective-permute-done | bytes 524320 | tf_op jit(solution)/shard_map/ppermute | solution.py:229
  90.9 0.9 broadcast_select_fusion.3
  91.8 1.9 %collective-permute-start.9 = (bf16[2,512,256]{2,1,0:T(8,128)(2,1)}, bf16[2,512,256]{2,1,0:T(8,128)(2,1)S(1)}, u32[]{:S(2)}, u32[]{:S(2)}) collective-permute-start(bf16[2,512,256]{2,1,0:T(8,128)(2,1)} %get-tuple-element.71), channel_id=1, source_target_pairs={{2,0},{4,2},{6,4},{8,6},{10,8},{12,10},{14,12},{16,14},{18,16},{20... | collective-permute-start | bytes 1572872 | tf_op jit(solution)/shard_map/ppermute | solution.py:233
  93.7 4.5 %collective-permute-start.10 = (bf16[2,512,256]{2,1,0:T(8,128)(2,1)S(1)}, bf16[2,512,256]{2,1,0:T(8,128)(2,1)S(1)}, u32[]{:S(2)}, u32[]{:S(2)}) collective-permute-start(bf16[2,512,256]{2,1,0:T(8,128)(2,1)S(1)} %get-tuple-element.72), channel_id=1, source_target_pairs={{0,2},{2,4},{4,6},{6,8},{8,10},{10,12},{12,14},{14,16},{16,18},{18... | collective-permute-start | bytes 1572872 | tf_op jit(solution)/shard_map/ppermute | solution.py:233
  98.2 8.1 %collective-permute-done.13 = bf16[2,512,256]{2,1,0:T(8,128)(2,1)S(1)} collective-permute-done((bf16[2,512,256]{2,1,0:T(8,128)(2,1)}, bf16[2,512,256]{2,1,0:T(8,128)(2,1)S(1)}, u32[]{:S(2)}, u32[]{:S(2)}) %collective-permute-start.13) | collective-permute-done | bytes 524320 | tf_op jit(solution)/shard_map/ppermute | solution.py:233
  106.3 0.9 broadcast_select_fusion
  107.2 4.7 %collective-permute-done.9 = bf16[2,512,256]{2,1,0:T(8,128)(2,1)S(1)} collective-permute-done((bf16[2,512,256]{2,1,0:T(8,128)(2,1)}, bf16[2,512,256]{2,1,0:T(8,128)(2,1)S(1)}, u32[]{:S(2)}, u32[]{:S(2)}) %collective-permute-start.9) | collective-permute-done | bytes 524320 | tf_op jit(solution)/shard_map/ppermute | solution.py:233
  111.9 0.9 broadcast_select_fusion.1
  112.8 2.1 %finish.4 = (bf16[512,1024]{1,0:T(8,128)(2,1)}, bf16[512,1024]{1,0:T(8,128)(2,1)}) custom-call(s32[1]{0:T(128)} %bitcast.4.group_ref, f32[512,1024]{1,0:T(8,128)} %get-tuple-element.47.dk_ref, f32[512,1024]{1,0:T(8,128)} %get-tuple-element.48.dv_ref, bf16[2,512,256]{2,1,0:T(8,128)(2,1)} %get-tuple-element.61.back_ref), custom_call_target="tpu_custom_call" | custom-call | flops 524288 | bytes 2097152 | tf_op jit(solution)/shard_map/finish/pallas_call | solution.py:180
  114.9 5.6 %collective-permute-done.15.back_ref = bf16[2,512,256]{2,1,0:T(8,128)(2,1)S(1)} collective-permute-done((bf16[2,512,256]{2,1,0:T(8,128)(2,1)S(1)}, bf16[2,512,256]{2,1,0:T(8,128)(2,1)S(1)}, u32[]{:S(2)}, u32[]{:S(2)}) %collective-permute-start.15) | collective-permute-done | bytes 524320 | tf_op jit(solution)/shard_map/ppermute | solution.py:229
  120.6 0.8 copy-done.5
  121.4 2.1 %finish.5 = (bf16[512,1024]{1,0:T(8,128)(2,1)}, bf16[512,1024]{1,0:T(8,128)(2,1)}) custom-call(s32[1]{0:T(128)} %bitcast.group_ref, f32[512,1024]{1,0:T(8,128)} %get-tuple-element.47.dk_ref, f32[512,1024]{1,0:T(8,128)} %get-tuple-element.48.dv_ref, bf16[2,512,256]{2,1,0:T(8,128)(2,1)} %copy-done.5, ...), custom_call_target="tpu_custom_call", output_to_operand_aliasing={{0}: (4, {}), {1}: (5, {})} | custom-call | flops 524288 | bytes 2097152 | tf_op jit(solution)/shard_map/finish/pallas_call | solution.py:180
  123.5 2.1 %finish.6 = (bf16[512,1024]{1,0:T(8,128)(2,1)}, bf16[512,1024]{1,0:T(8,128)(2,1)}) custom-call(s32[1]{0:T(128)} %bitcast.4.group_ref, f32[512,1024]{1,0:T(8,128)} %get-tuple-element.47.dk_ref, f32[512,1024]{1,0:T(8,128)} %get-tuple-element.48.dv_ref, bf16[2,512,256]{2,1,0:T(8,128)(2,1)} %get-tuple-element.63.back_ref, ...), custom_call_target="tpu_custom_call", output_to_operand_aliasing={{0}: (4, {}), {1}: (5, {})} | custom-call | flops 524288 | bytes 2097152 | tf_op jit(solution)/shard_map/finish/pallas_call | solution.py:180
  125.6 0.5 collective-permute-done.11.back_ref
  126.1 0.8 copy-done.4
  126.9 2.1 %finish.7 = (bf16[512,1024]{1,0:T(8,128)(2,1)}, bf16[512,1024]{1,0:T(8,128)(2,1)}) custom-call(s32[1]{0:T(128)} %bitcast.group_ref, f32[512,1024]{1,0:T(8,128)} %get-tuple-element.47.dk_ref, f32[512,1024]{1,0:T(8,128)} %get-tuple-element.48.dv_ref, bf16[2,512,256]{2,1,0:T(8,128)(2,1)} %copy-done.4, ...), custom_call_target="tpu_custom_call", output_to_operand_aliasing={{0}: (4, {}), {1}: (5, {})} | custom-call | flops 524288 | bytes 2097152 | tf_op jit(solution)/shard_map/finish/pallas_call | solution.py:180
  (24 shorter events, 0.1 us)
Async XLA Ops:
  2.3 1.7 %copy-start.7 = (s32[32]{0:T(128)S(1)}, s32[32]{0:T(128)}, u32[]{:S(2)}) copy-start(s32[32]{0:T(128)} %param.13) | copy-start | bytes 388
  2.4 22.8 %copy-start.6 = (s32[16384]{0:T(1024)S(1)}, s32[16384]{0:T(1024)}, u32[]{:S(2)}) copy-start(s32[16384]{0:T(1024)} %param.12) | copy-start | bytes 196612
  2.4 12.9 %collective-permute-start = (bf16[2,512,256]{2,1,0:T(8,128)(2,1)S(1)}, bf16[2,512,256]{2,1,0:T(8,128)(2,1)S(1)}, u32[]{:S(2)}, u32[]{:S(2)}) collective-permute-start(bf16[2,512,256]{2,1,0:T(8,128)(2,1)S(1)} %pad_maximum_fusion.1), channel_id=1, source_target_pairs={{0,1},{1,0},{2,3},{3,2},{4,5},{5,4},{6,7},{7,6},{8,9},{9,8},{10,11... | collective-permute-start | bytes 1572872 | tf_op jit(solution)/shard_map/ppermute | solution.py:229
  2.8 23.7 %collective-permute-start.3 = (bf16[2,512,256]{2,1,0:T(8,128)(2,1)S(1)}, bf16[2,512,256]{2,1,0:T(8,128)(2,1)S(1)}, u32[]{:S(2)}, u32[]{:S(2)}) collective-permute-start(bf16[2,512,256]{2,1,0:T(8,128)(2,1)S(1)} %pad_maximum_fusion.3), channel_id=1, source_target_pairs={{0,1},{1,0},{2,3},{3,2},{4,5},{5,4},{6,7},{7,6},{8,9},{9,8},{10,11... | collective-permute-start | bytes 1572872 | tf_op jit(solution)/shard_map/ppermute | solution.py:229
  16.1 18.7 %collective-permute-start.2 = (bf16[2,512,256]{2,1,0:T(8,128)(2,1)}, bf16[2,512,256]{2,1,0:T(8,128)(2,1)S(1)}, u32[]{:S(2)}, u32[]{:S(2)}) collective-permute-start(bf16[2,512,256]{2,1,0:T(8,128)(2,1)} %get-tuple-element.83), channel_id=1, source_target_pairs={{2,0},{4,2},{6,4},{8,6},{10,8},{12,10},{14,12},{16,14},{18,16},{20... | collective-permute-start | bytes 1572872 | tf_op jit(solution)/shard_map/ppermute | solution.py:233
  20.7 18.8 %collective-permute-start.1 = (bf16[2,512,256]{2,1,0:T(8,128)(2,1)S(1)}, bf16[2,512,256]{2,1,0:T(8,128)(2,1)S(1)}, u32[]{:S(2)}, u32[]{:S(2)}) collective-permute-start(bf16[2,512,256]{2,1,0:T(8,128)(2,1)S(1)} %get-tuple-element.84), channel_id=1, source_target_pairs={{0,2},{2,4},{4,6},{6,8},{8,10},{10,12},{12,14},{14,16},{16,18},{18... | collective-permute-start | bytes 1572872 | tf_op jit(solution)/shard_map/ppermute | solution.py:233
  27.4 22.0 %collective-permute-start.5 = (bf16[2,512,256]{2,1,0:T(8,128)(2,1)}, bf16[2,512,256]{2,1,0:T(8,128)(2,1)S(1)}, u32[]{:S(2)}, u32[]{:S(2)}) collective-permute-start(bf16[2,512,256]{2,1,0:T(8,128)(2,1)} %get-tuple-element.73), channel_id=1, source_target_pairs={{2,0},{4,2},{6,4},{8,6},{10,8},{12,10},{14,12},{16,14},{18,16},{20... | collective-permute-start | bytes 1572872 | tf_op jit(solution)/shard_map/ppermute | solution.py:233
  30.8 18.6 %collective-permute-start.4 = (bf16[2,512,256]{2,1,0:T(8,128)(2,1)S(1)}, bf16[2,512,256]{2,1,0:T(8,128)(2,1)S(1)}, u32[]{:S(2)}, u32[]{:S(2)}) collective-permute-start(bf16[2,512,256]{2,1,0:T(8,128)(2,1)S(1)} %get-tuple-element.74), channel_id=1, source_target_pairs={{0,2},{2,4},{4,6},{6,8},{8,10},{10,12},{12,14},{14,16},{16,18},{18... | collective-permute-start | bytes 1572872 | tf_op jit(solution)/shard_map/ppermute | solution.py:233
  40.4 19.8 %collective-permute-start.7 = (bf16[2,512,256]{2,1,0:T(8,128)(2,1)S(1)}, bf16[2,512,256]{2,1,0:T(8,128)(2,1)S(1)}, u32[]{:S(2)}, u32[]{:S(2)}) collective-permute-start(bf16[2,512,256]{2,1,0:T(8,128)(2,1)S(1)} %get-tuple-element.67), channel_id=1, source_target_pairs={{0,1},{1,0},{2,3},{3,2},{4,5},{5,4},{6,7},{7,6},{8,9},{9,8},{10,11... | collective-permute-start | bytes 1572872 | tf_op jit(solution)/shard_map/ppermute | solution.py:229
  50.3 19.8 %collective-permute-start.6 = (bf16[2,512,256]{2,1,0:T(8,128)(2,1)S(1)}, bf16[2,512,256]{2,1,0:T(8,128)(2,1)S(1)}, u32[]{:S(2)}, u32[]{:S(2)}) collective-permute-start(bf16[2,512,256]{2,1,0:T(8,128)(2,1)S(1)} %get-tuple-element.66), channel_id=1, source_target_pairs={{0,1},{1,0},{2,3},{3,2},{4,5},{5,4},{6,7},{7,6},{8,9},{9,8},{10,11... | collective-permute-start | bytes 1572872 | tf_op jit(solution)/shard_map/ppermute | solution.py:229
  60.2 0.8 copy-start
  69.7 11.2 %collective-permute-start.12 = (bf16[2,512,256]{2,1,0:T(8,128)(2,1)}, bf16[2,512,256]{2,1,0:T(8,128)(2,1)S(1)}, u32[]{:S(2)}, u32[]{:S(2)}) collective-permute-start(bf16[2,512,256]{2,1,0:T(8,128)(2,1)} %get-tuple-element.52), channel_id=1, source_target_pairs={{0,1},{1,0},{2,3},{3,2},{4,5},{5,4},{6,7},{7,6},{8,9},{9,8},{10,11... | collective-permute-start | bytes 1572872 | tf_op jit(solution)/shard_map/ppermute | solution.py:229
  70.1 0.8 copy-start.1
  70.9 10.1 %copy-start.2 = (bf16[2,512,256]{2,1,0:T(8,128)(2,1)S(1)}, bf16[2,512,256]{2,1,0:T(8,128)(2,1)}, u32[]{:S(2)}) copy-start(bf16[2,512,256]{2,1,0:T(8,128)(2,1)} %get-tuple-element.51) | copy-start | bytes 1572868
  79.6 11.3 %copy-start.3 = (bf16[2,512,256]{2,1,0:T(8,128)(2,1)S(1)}, bf16[2,512,256]{2,1,0:T(8,128)(2,1)}, u32[]{:S(2)}) copy-start(bf16[2,512,256]{2,1,0:T(8,128)(2,1)} %get-tuple-element.49) | copy-start | bytes 1572868
  79.6 11.3 %collective-permute-start.8 = (bf16[2,512,256]{2,1,0:T(8,128)(2,1)}, bf16[2,512,256]{2,1,0:T(8,128)(2,1)S(1)}, u32[]{:S(2)}, u32[]{:S(2)}) collective-permute-start(bf16[2,512,256]{2,1,0:T(8,128)(2,1)} %get-tuple-element.50), channel_id=1, source_target_pairs={{0,1},{1,0},{2,3},{3,2},{4,5},{5,4},{6,7},{7,6},{8,9},{9,8},{10,11... | collective-permute-start | bytes 1572872 | tf_op jit(solution)/shard_map/ppermute | solution.py:229
  81.8 24.5 %collective-permute-start.13 = (bf16[2,512,256]{2,1,0:T(8,128)(2,1)}, bf16[2,512,256]{2,1,0:T(8,128)(2,1)S(1)}, u32[]{:S(2)}, u32[]{:S(2)}) collective-permute-start(bf16[2,512,256]{2,1,0:T(8,128)(2,1)} %get-tuple-element.69), channel_id=1, source_target_pairs={{2,0},{4,2},{6,4},{8,6},{10,8},{12,10},{14,12},{16,14},{18,16},{20... | collective-permute-start | bytes 1572872 | tf_op jit(solution)/shard_map/ppermute | solution.py:233
  83.7 22.6 %collective-permute-start.14 = (bf16[2,512,256]{2,1,0:T(8,128)(2,1)S(1)}, bf16[2,512,256]{2,1,0:T(8,128)(2,1)S(1)}, u32[]{:S(2)}, u32[]{:S(2)}) collective-permute-start(bf16[2,512,256]{2,1,0:T(8,128)(2,1)S(1)} %get-tuple-element.70), channel_id=1, source_target_pairs={{0,2},{2,4},{4,6},{6,8},{8,10},{10,12},{12,14},{14,16},{16,18},{18... | collective-permute-start | bytes 1572872 | tf_op jit(solution)/shard_map/ppermute | solution.py:233
  91.8 20.1 %collective-permute-start.9 = (bf16[2,512,256]{2,1,0:T(8,128)(2,1)}, bf16[2,512,256]{2,1,0:T(8,128)(2,1)S(1)}, u32[]{:S(2)}, u32[]{:S(2)}) collective-permute-start(bf16[2,512,256]{2,1,0:T(8,128)(2,1)} %get-tuple-element.71), channel_id=1, source_target_pairs={{2,0},{4,2},{6,4},{8,6},{10,8},{12,10},{14,12},{16,14},{18,16},{20... | collective-permute-start | bytes 1572872 | tf_op jit(solution)/shard_map/ppermute | solution.py:233
  93.7 18.2 %collective-permute-start.10 = (bf16[2,512,256]{2,1,0:T(8,128)(2,1)S(1)}, bf16[2,512,256]{2,1,0:T(8,128)(2,1)S(1)}, u32[]{:S(2)}, u32[]{:S(2)}) collective-permute-start(bf16[2,512,256]{2,1,0:T(8,128)(2,1)S(1)} %get-tuple-element.72), channel_id=1, source_target_pairs={{0,2},{2,4},{4,6},{6,8},{8,10},{10,12},{12,14},{14,16},{16,18},{18... | collective-permute-start | bytes 1572872 | tf_op jit(solution)/shard_map/ppermute | solution.py:233
  107.2 13.3 %collective-permute-start.15 = (bf16[2,512,256]{2,1,0:T(8,128)(2,1)S(1)}, bf16[2,512,256]{2,1,0:T(8,128)(2,1)S(1)}, u32[]{:S(2)}, u32[]{:S(2)}) collective-permute-start(bf16[2,512,256]{2,1,0:T(8,128)(2,1)S(1)} %get-tuple-element.62), channel_id=1, source_target_pairs={{0,1},{1,0},{2,3},{3,2},{4,5},{5,4},{6,7},{7,6},{8,9},{9,8},{10,11... | collective-permute-start | bytes 1572872 | tf_op jit(solution)/shard_map/ppermute | solution.py:229
  112.8 13.3 %collective-permute-start.11 = (bf16[2,512,256]{2,1,0:T(8,128)(2,1)S(1)}, bf16[2,512,256]{2,1,0:T(8,128)(2,1)S(1)}, u32[]{:S(2)}, u32[]{:S(2)}) collective-permute-start(bf16[2,512,256]{2,1,0:T(8,128)(2,1)S(1)} %get-tuple-element.64), channel_id=1, source_target_pairs={{0,1},{1,0},{2,3},{3,2},{4,5},{5,4},{6,7},{7,6},{8,9},{9,8},{10,11... | collective-permute-start | bytes 1572872 | tf_op jit(solution)/shard_map/ppermute | solution.py:229
  120.6 0.8 copy-start.5
  126.1 0.8 copy-start.4

commit v6 on v4

--- a/solution.py
+++ b/solution.py
@@ -30,40 +30,91 @@
     return reduce(strip.reshape(strip.shape[0] // 8, 8, strip.shape[1]), axis=0)
 
 
-def attention_body(carried, group_ref, low_ref, q_ref, k_ref, v_ref, o_ref, do_ref, past_ref, *refs):
+def arrange_body(q_ref, k_ref, v_ref, o_ref, do_ref, q_out, do_out, delta_out, k_out, k_turned_out, v_out):
+    rows, head = k_ref.shape
+    members = q_ref.shape[1] // head
+    for tile in range(rows // TILE):
+        own = slice(tile * TILE, (tile + 1) * TILE)
+        for m in range(members):
+            place = slice((tile * members + m) * TILE, (tile * members + m + 1) * TILE)
+            columns = slice(m * head, (m + 1) * head)
+            q_out[0, place] = q_ref[own, columns]
+            do_out[0, place] = do_ref[own, columns]
+            product = do_ref[own, columns].astype(jnp.float32) * o_ref[own, columns].astype(jnp.float32)
+            delta_out[0, :, place] = jnp.sum(product.T, axis=0, keepdims=True)
+    k_out[0] = k_ref[...]
+    k_turned_out[0] = k_ref[...].T
+    v_out[0] = v_ref[...]
+
+
+def arrange(row_arrays, first_head, heads_per_group, per_piece):
+    queries, keys, values, outputs, grads = row_arrays
+    rows, members = keys.shape[0], queries.shape[1] // keys.shape[1]
+    groups = keys.shape[1] // HEAD_SIZE // heads_per_group
+    count = groups * per_piece
+
+    def column(group, step):
+        return (0, group * heads_per_group + first_head + step)
+
+    def leading(group, step):
+        return (group * per_piece + step, 0, 0)
+
+    query_spec = pl.BlockSpec((rows, members * HEAD_SIZE), column)
+    key_spec = pl.BlockSpec((rows, HEAD_SIZE), column)
+    shapes = [
+        ((members * rows, HEAD_SIZE), jnp.bfloat16),
+        ((members * rows, HEAD_SIZE), jnp.bfloat16),
+        ((1, members * rows), jnp.float32),
+        ((rows, HEAD_SIZE), jnp.bfloat16),
+        ((HEAD_SIZE, rows), jnp.bfloat16),
+        ((rows, HEAD_SIZE), jnp.bfloat16),
+    ]
+    return pl.pallas_call(
+        arrange_body,
+        grid=(groups, per_piece),
+        in_specs=[query_spec, key_spec, key_spec, query_spec, query_spec],
+        out_specs=[pl.BlockSpec((1, *shape), leading) for shape, _ in shapes],
+        out_shape=[jax.ShapeDtypeStruct((count, *shape), dtype) for shape, dtype in shapes],
+        compiler_params=pltpu.CompilerParams(vmem_limit_bytes=VMEM_BYTES),
+        cost_estimate=pl.CostEstimate(
+            flops=count * rows * 1024, bytes_accessed=count * rows * 4096, transcendentals=0
+        ),
+        name="arrange",
+    )(queries, keys, values, outputs, grads)
+
+
+def attention_body(
+    carried, group_ref, low_ref, q_ref, do_ref, delta_ref, k_ref, k_turned_ref, v_ref, past_ref, *refs
+):
     dq_ref, dk_ref, dv_ref, back_ref = refs[carried : carried + 4]
     k_all, v_all, k_turned, dk_sum, dv_sum, scores, slopes, weights_b, slopes_b = refs[carried + 4 :]
-    rows, head = k_ref.shape
+    rows, head = k_ref.shape[1:]
     window = past_ref.shape[1]
-    members = q_ref.shape[1] // head
+    members = q_ref.shape[1] // rows
     span, lanes = window + TILE, members * TILE
     scale = head**-0.5
     k_all[:window] = past_ref[0]
-    k_all[window:] = k_ref[...]
+    k_all[window:] = k_ref[0]
     v_all[:window] = past_ref[1]
-    v_all[window:] = v_ref[...]
-    k_turned[...] = k_all[...].T
+    v_all[window:] = v_ref[0]
+    k_turned[:, :window] = past_ref[0].T
+    k_turned[:, window:] = k_turned_ref[0]
     dk_sum[...] = jnp.zeros_like(dk_sum)
     dv_sum[...] = jnp.zeros_like(dv_sum)
     lane = lax.broadcasted_iota(jnp.int32, (1, lanes), 1) % TILE
     tiles = range(rows // TILE)
 
-    def stacked(ref, start):
-        return jnp.concatenate(
-            [ref[start : start + TILE, m * head : (m + 1) * head] for m in range(members)], axis=0
-        )
-
     def enter(tile):
         keys = pl.ds(tile * TILE, span)
-        queries, grads = stacked(q_ref, tile * TILE), stacked(do_ref, tile * TILE)
+        place = pl.ds(tile * lanes, lanes)
+        queries, grads = q_ref[0, place], do_ref[0, place]
         scores[tile] = dot(k_all[keys], queries, 1, 1)
         slopes[tile] = dot(v_all[keys], grads, 1, 1)
         return queries, grads
 
-    def weigh(tile, grads):
+    def weigh(tile):
         start = tile * TILE
-        product = grads.astype(jnp.float32) * stacked(o_ref, start).astype(jnp.float32)
-        delta = jnp.sum(product.T, axis=0, keepdims=True)
+        delta = delta_ref[0, :, pl.ds(tile * lanes, lanes)]
         low = jnp.concatenate([low_ref[:, start : start + TILE]] * members, axis=1) - start
 
         def visible(strip):
@@ -103,36 +154,42 @@
     for tile in tiles:
         if tile + 1 in tiles:
             entered[tile + 1] = enter(tile + 1)
-        weigh(tile, entered[tile][1])
-        leave(tile, *entered[tile])
+        if tile:
+            leave(tile - 1, *entered[tile - 1])
+        weigh(tile)
+    leave(tiles[-1], *entered[tiles[-1]])
     back_ref[0] = dk_sum[:window].astype(back_ref.dtype)
     back_ref[1] = dv_sum[:window].astype(back_ref.dtype)
-    dk_ref[...] = dk_sum[window:]
-    dv_ref[...] = dv_sum[window:]
-
-
-def attention(group, low, row_arrays, past, first_head, heads_per_group, carried):
-    queries, keys, values, outputs, grads = row_arrays
-    rows, window, count = keys.shape[0], past.shape[1], past.shape[2] // HEAD_SIZE
-    wide = queries.shape[1] // keys.shape[1] * HEAD_SIZE
+    dk_ref[0] = dk_sum[window:].astype(dk_ref.dtype)
+    dv_ref[0] = dv_sum[window:].astype(dv_ref.dtype)
+
+
+def attention(group, low, arranged, past, first_head, heads_per_group, heads, carried):
+    rows, window, count = arranged[3].shape[1], past.shape[1], past.shape[2] // HEAD_SIZE
+    members = arranged[0].shape[1] // rows
+
+    def leading(step, group_ref):
+        return (group_ref[0] * count + step, 0, 0)
 
     def column(step, group_ref):
         return (0, group_ref[0] * heads_per_group + first_head + step)
 
-    query_spec = pl.BlockSpec((rows, wide), column)
-    key_spec = pl.BlockSpec((rows, HEAD_SIZE), column)
     past_spec = pl.BlockSpec((2, window, HEAD_SIZE), lambda step, group_ref: (0, 0, step))
     low_spec = pl.BlockSpec((1, rows), lambda step, group_ref: (0, 0))
-    square = (rows // TILE, window + TILE, wide // HEAD_SIZE * TILE)
-    tiles = count * queries.shape[1] // keys.shape[1] * rows * (window + TILE)
+    own_spec = pl.BlockSpec((1, rows, HEAD_SIZE), lambda step, group_ref: (step, 0, 0))
+    own_shape = jax.ShapeDtypeStruct((count, rows, HEAD_SIZE), jnp.bfloat16)
+    square = (rows // TILE, window + TILE, members * TILE)
+    tiles = count * members * rows * (window + TILE)
     return pl.pallas_call(
         functools.partial(attention_body, len(carried)),
         grid_spec=pltpu.PrefetchScalarGridSpec(
             num_scalar_prefetch=1,
             grid=(count,),
-            in_specs=[low_spec, query_spec, key_spec, key_spec, query_spec, query_spec, past_spec]
+            in_specs=[low_spec]
+            + [pl.BlockSpec((1, *array.shape[1:]), leading) for array in arranged]
+            + [past_spec]
             + [pl.BlockSpec(memory_space=pl.ANY)] * len(carried),
-            out_specs=[query_spec, key_spec, key_spec, past_spec],
+            out_specs=[pl.BlockSpec((rows, members * HEAD_SIZE), column), own_spec, own_spec, past_spec],
             scratch_shapes=[
                 pltpu.VMEM((window + rows, HEAD_SIZE), jnp.bfloat16),
                 pltpu.VMEM((window + rows, HEAD_SIZE), jnp.bfloat16),
@@ -146,45 +203,49 @@
             ],
         ),
         out_shape=[
-            jax.ShapeDtypeStruct(queries.shape, jnp.bfloat16),
-            jax.ShapeDtypeStruct(keys.shape, jnp.float32),
-            jax.ShapeDtypeStruct(keys.shape, jnp.float32),
+            jax.ShapeDtypeStruct((rows, heads * members * HEAD_SIZE), jnp.bfloat16),
+            own_shape,
+            own_shape,
             jax.ShapeDtypeStruct(past.shape, jnp.bfloat16),
         ],
-        input_output_aliases={8 + i: i for i in range(len(carried))},
+        input_output_aliases={9 + i: i for i in range(len(carried))},
         compiler_params=pltpu.CompilerParams(vmem_limit_bytes=VMEM_BYTES),
         cost_estimate=pl.CostEstimate(
             flops=10 * tiles * HEAD_SIZE, bytes_accessed=count * rows * 2400, transcendentals=tiles
         ),
         name="attention",
-    )(group, low, *row_arrays, past, *carried)
+    )(group, low, *arranged, past, *carried)
 
 
 def finish_body(carried, group_ref, dk_ref, dv_ref, back_ref, *refs):
     key_out, value_out = refs[carried:]
-    scale = HEAD_SIZE**-0.5
-    key_out[...] = ((dk_ref[...] + back_ref[0].astype(jnp.float32)) * scale).astype(key_out.dtype)
-    value_out[...] = (dv_ref[...] + back_ref[1].astype(jnp.float32)).astype(value_out.dtype)
-
-
-def finish(group, own, back, first_head, heads_per_group, carried):
+    sums = [
+        own[0].astype(jnp.float32) + back_ref[i].astype(jnp.float32)
+        for i, own in enumerate((dk_ref, dv_ref))
+    ]
+    key_out[...] = (sums[0] * HEAD_SIZE**-0.5).astype(key_out.dtype)
+    value_out[...] = sums[1].astype(value_out.dtype)
+
+
+def finish(group, own, back, first_head, heads_per_group, heads, carried):
     rows, count = back.shape[1], back.shape[2] // HEAD_SIZE
 
     def column(step, group_ref):
         return (0, group_ref[0] * heads_per_group + first_head + step)
 
     key_spec = pl.BlockSpec((rows, HEAD_SIZE), column)
+    own_spec = pl.BlockSpec((1, rows, HEAD_SIZE), lambda step, group_ref: (step, 0, 0))
     back_spec = pl.BlockSpec((2, rows, HEAD_SIZE), lambda step, group_ref: (0, 0, step))
     return pl.pallas_call(
         functools.partial(finish_body, len(carried)),
         grid_spec=pltpu.PrefetchScalarGridSpec(
             num_scalar_prefetch=1,
             grid=(count,),
-            in_specs=[key_spec, key_spec, back_spec]
+            in_specs=[own_spec, own_spec, back_spec]
             + [pl.BlockSpec(memory_space=pl.ANY)] * len(carried),
             out_specs=[key_spec, key_spec],
         ),
-        out_shape=[jax.ShapeDtypeStruct(own[0].shape, jnp.bfloat16)] * 2,
+        out_shape=[jax.ShapeDtypeStruct((rows, heads * HEAD_SIZE), jnp.bfloat16)] * 2,
         input_output_aliases={4 + i: i for i in range(len(carried))},
         compiler_params=pltpu.CompilerParams(vmem_limit_bytes=VMEM_BYTES),
         cost_estimate=pl.CostEstimate(
@@ -269,21 +330,24 @@
             for slot in (early_slot, 1 - early_slot)
         ]
 
-    halves = []
+    arranged, halves = [], []
     for chunk in range(chunks):
         pieces = [piece_of(place, chunk)]
         pieces += [turned(piece_of(other(turn), chunk), turn) for turn in range(1, sharers)]
+        arrays = arrange(row_arrays, chunk * per_piece, heads_per_group, per_piece)
+        *arrays, pieces[-1] = together(*arrays, pieces[-1])
+        arranged.append(arrays)
         halves.append(halves_of(pieces))
     before = [(shifted(early, 1), shifted(late, -1)) for early, late in halves]
 
     def run(turn, chunk, past, carried):
-        *carried, back = attention(
-            groups[turn].reshape(1), low, row_arrays, past,
-            chunk * per_piece, heads_per_group, tuple(carried),
+        query_grads, *own[chunk, turn], back = attention(
+            groups[turn].reshape(1), low, arranged[chunk], past,
+            chunk * per_piece, heads_per_group, key_heads, carried,
         )
-        return carried, back
-
-    carried, terms, pasts = (), [], []
+        return (query_grads,), back
+
+    carried, own, terms, pasts = (), {}, [], []
     for chunk in range(chunks):
         (early, late), (before_early, before_late) = halves[chunk], before[chunk]
         if chunk:
@@ -306,7 +370,7 @@
             carried, back = run(turn, chunk, pasts[chunk][turn - 1], carried)
             terms[chunk].append(turned(back, -turn))
 
-    query_grads, *own = carried
+    (query_grads,) = carried
     results = ()
     for chunk in range(chunks):
         to_before, to_own = [], []
@@ -340,12 +404,8 @@
             if turn:
                 back = turned(back, turn)
             results = finish(
-                groups[turn].reshape(1),
-                own,
-                back,
-                chunk * per_piece,
-                heads_per_group,
-                tuple(results),
+                groups[turn].reshape(1), own[chunk, turn], back,
+                chunk * per_piece, heads_per_group, key_heads, tuple(results),
             )
     return (query_grads, *results)
 

time: 126 us -> 126 us (level)
  Pallas kernels: 38 us -> 46.1 us
  waiting for transfers between devices: 36.7 us -> 30 us
  starting transfers between devices: 33.2 us -> 30.1 us
  other arithmetic: 9.77 us -> 11.1 us
    pallas_call x0 -> x2, Pallas kernels: none -> 9.73 us  [arrange(): pl.pallas_call(arrange_body, grid=(groups, per_piece), in_specs=[query_sp...]
    ppermute x8, waiting for transfers between devices: 18.8 us -> 11.6 us  [shifted(): lax.ppermute(value, 'blk', [(source, source + step) for source in range(f...]
    ppermute x8, starting transfers between devices: 28.5 us -> 26.2 us  [shifted(): lax.ppermute(value, 'blk', [(source, source + step) for source in range(f...]
    select_n x2, other arithmetic: 1.8 us -> 3.87 us  [rows_of(): jnp.where(is_early(device), sums[0], sums[1])]
  transfers between devices with their start and end apart: 16 -> 16, of which waited for: 8 -> 8; matrix products, arithmetic and copies ran while one was open for 7% -> 8% of each run, Pallas kernels for 29% -> 35%
where the time goes in v6:
time: 126 us; the launch traced here: 125 us
  Pallas kernels  46.1 us (37%)
  starting transfers between devices  30.1 us (24%)
  waiting for transfers between devices  30 us (24%)
  other arithmetic  11.1 us (9%)
  local copies, waits for them, and re-layouts  3.97 us (3%)
  between operations  3.46 us (3%)
    pallas_call x4, Pallas kernels, attention(): pl.pallas_call(functools.partial(attention_body, len(carried)), grid_spec...  28.4 us
    ppermute x8, starting transfers between devices, shifted(): lax.ppermute(value, 'blk', [(source, source + step) for source in range(f...  26.2 us
    ppermute x8, waiting for transfers between devices, turned(): return lax.ppermute(value, 'head', pairs)  18.4 us
    ppermute x8, waiting for transfers between devices, shifted(): lax.ppermute(value, 'blk', [(source, source + step) for source in range(f...  11.6 us
    pallas_call x2, Pallas kernels, arrange(): pl.pallas_call(arrange_body, grid=(groups, per_piece), in_specs=[query_sp...  9.73 us
    pallas_call x4, Pallas kernels, finish(): pl.pallas_call(functools.partial(finish_body, len(carried)), grid_spec=pl...  7.96 us
    ppermute x8, starting transfers between devices, turned(): return lax.ppermute(value, 'head', pairs)  3.92 us
    select_n x2, other arithmetic, rows_of(): jnp.where(is_early(device), sums[0], sums[1])  3.87 us
  transfers between devices with their start and end apart: 16, of which 8 were waited for; matrix products, arithmetic and copies ran while one was open for 8% of the time, Pallas kernels for 35%

profile of v6, /device:TPU:11, one launch (start us, length us, event | category | flops | bytes accessed | tf_op | source)
XLA Modules:
  0.0 124.8 jit_solution(14328175060592685998)
XLA Ops:
  0.6 1.7 %select_bitcast_fusion = (bf16[1,512,256]{2,1,0:T(8,128)(2,1)S(1)}, bf16[1,512,256]{2,1,0:T(8,128)(2,1)S(1)}, bf16[1,512,256]{2,1,0:T(8,128)(2,1)S(1)}, bf16[1,5...) fusion(pred[]{:T(512)S(6)} %eq.22, ...), kind=kLoop, calls=%fused_computation.25 | loop fusion | flops 1048576 | bytes 4194306 | tf_op jit(solution)/shard_map/stack | solution.py:302
  2.4 0.3 collective-permute-start.1
  2.8 1.3 %collective-permute-start = (bf16[2,512,256]{2,1,0:T(8,128)(2,1)S(1)}, bf16[2,512,256]{2,1,0:T(8,128)(2,1)S(1)}, u32[]{:S(2)}, u32[]{:S(2)}) collective-permute-start(bf16[2,512,256]{2,1,0:T(8,128)(2,1)S(1)} %pad_maximum_fusion), channel_id=1, source_target_pairs={{0,1},{1,0},{2,3},{3,2},{4,5},{5,4},{6,7},{7,6},{8,9},{9,8},{10,11... | collective-permute-start | bytes 1572872 | tf_op jit(solution)/shard_map/ppermute | solution.py:288
  4.1 0.6 fusion
  6.0 4.9 %arrange.3 = (bf16[4,1024,128]{2,1,0:T(8,128)(2,1)}, bf16[4,1024,128]{2,1,0:T(8,128)(2,1)}, f32[4,1,1024]{2,1,0:T(1,128)}, bf16[4,512,128]{2,1,0:T(8,128)(2,1)},...) custom-call(bf16[512,2048]{1,0:T(8,128)(2,1)} %q_ref.3, bf16[512,1024]{1,0:T(8,128)(2,1)} %k_ref.3, ...), custom_call_target="tpu_custom_call" | custom-call | flops 2097152 | bytes 8388608 | tf_op jit(solution)/shard_map/arrange/pallas_call | solution.py:72
  10.9 4.3 %collective-permute-done.1 = bf16[2,512,256]{2,1,0:T(8,128)(2,1)S(1)} collective-permute-done((bf16[2,512,256]{2,1,0:T(8,128)(2,1)S(1)}, bf16[2,512,256]{2,1,0:T(8,128)(2,1)S(1)}, u32[]{:S(2)}, u32[]{:S(2)}) %collective-permute-start.1) | collective-permute-done | bytes 524320 | tf_op jit(solution)/shard_map/ppermute | solution.py:288
  15.3 0.9 broadcast_select_fusion.7
  16.1 4.6 %collective-permute-start.3 = (bf16[2,512,256]{2,1,0:T(8,128)(2,1)}, bf16[2,512,256]{2,1,0:T(8,128)(2,1)S(1)}, u32[]{:S(2)}, u32[]{:S(2)}) collective-permute-start(bf16[2,512,256]{2,1,0:T(8,128)(2,1)} %get-tuple-element.131), channel_id=1, source_target_pairs={{2,0},{4,2},{6,4},{8,6},{10,8},{12,10},{14,12},{16,14},{18,16},{20... | collective-permute-start | bytes 1572872 | tf_op jit(solution)/shard_map/ppermute | solution.py:292
  20.7 3.0 %collective-permute-start.2 = (bf16[2,512,256]{2,1,0:T(8,128)(2,1)S(1)}, bf16[2,512,256]{2,1,0:T(8,128)(2,1)S(1)}, u32[]{:S(2)}, u32[]{:S(2)}) collective-permute-start(bf16[2,512,256]{2,1,0:T(8,128)(2,1)S(1)} %get-tuple-element.132), channel_id=1, source_target_pairs={{0,2},{2,4},{4,6},{6,8},{8,10},{10,12},{12,14},{14,16},{16,18},{18... | collective-permute-start | bytes 1572872 | tf_op jit(solution)/shard_map/ppermute | solution.py:292
  25.2 4.9 %arrange.2 = (bf16[4,1024,128]{2,1,0:T(8,128)(2,1)}, bf16[4,1024,128]{2,1,0:T(8,128)(2,1)}, f32[4,1,1024]{2,1,0:T(1,128)}, bf16[4,512,128]{2,1,0:T(8,128)(2,1)},...) custom-call(bf16[512,2048]{1,0:T(8,128)(2,1)} %q_ref.3, bf16[512,1024]{1,0:T(8,128)(2,1)} %k_ref.3, ...), custom_call_target="tpu_custom_call" | custom-call | flops 2097152 | bytes 8388608 | tf_op jit(solution)/shard_map/arrange/pallas_call | solution.py:72
  30.1 0.9 broadcast_select_fusion.6
  31.0 1.9 %collective-permute-start.5 = (bf16[2,512,256]{2,1,0:T(8,128)(2,1)}, bf16[2,512,256]{2,1,0:T(8,128)(2,1)S(1)}, u32[]{:S(2)}, u32[]{:S(2)}) collective-permute-start(bf16[2,512,256]{2,1,0:T(8,128)(2,1)} %get-tuple-element.121), channel_id=1, source_target_pairs={{2,0},{4,2},{6,4},{8,6},{10,8},{12,10},{14,12},{16,14},{18,16},{20... | collective-permute-start | bytes 1572872 | tf_op jit(solution)/shard_map/ppermute | solution.py:292
  32.9 3.6 %collective-permute-start.4 = (bf16[2,512,256]{2,1,0:T(8,128)(2,1)S(1)}, bf16[2,512,256]{2,1,0:T(8,128)(2,1)S(1)}, u32[]{:S(2)}, u32[]{:S(2)}) collective-permute-start(bf16[2,512,256]{2,1,0:T(8,128)(2,1)S(1)} %get-tuple-element.122), channel_id=1, source_target_pairs={{0,2},{2,4},{4,6},{6,8},{8,10},{10,12},{12,14},{14,16},{16,18},{18... | collective-permute-start | bytes 1572872 | tf_op jit(solution)/shard_map/ppermute | solution.py:292
  36.5 1.0 convert_reduce_fusion
  37.5 0.9 broadcast_select_fusion.18
  38.4 0.3 collective-permute-start.7
  38.6 7.1 %attention.4 = (bf16[512,2048]{1,0:T(8,128)(2,1)}, bf16[2,512,128]{2,1,0:T(8,128)(2,1)}, bf16[2,512,128]{2,1,0:T(8,128)(2,1)}, bf16[2,512,256]{2,1,0:T(8,128)(2,1)}) custom-call(s32[1]{0:T(128)} %bitcast.6.group_ref, s32[1,512]{1,0:T(1,128)} %bitcast.21, bf16[4,1024,128]{2,1,0:T(8,128)(2,1)} %get-tuple-element.74.q_ref, ...), custom_call_target="tpu_custom_call" | custom-call | flops 1677721600 | bytes 2457600 | tf_op jit(solution)/shard_map/attention/pallas_call | solution.py:183
  45.7 1.8 %collective-permute-done.5 = bf16[2,512,256]{2,1,0:T(8,128)(2,1)S(1)} collective-permute-done((bf16[2,512,256]{2,1,0:T(8,128)(2,1)}, bf16[2,512,256]{2,1,0:T(8,128)(2,1)S(1)}, u32[]{:S(2)}, u32[]{:S(2)}) %collective-permute-start.5) | collective-permute-done | bytes 524320 | tf_op jit(solution)/shard_map/ppermute | solution.py:292
  47.6 0.9 broadcast_select_fusion.14
  48.5 0.3 collective-permute-start.6
  48.7 7.1 %attention.5 = (bf16[512,2048]{1,0:T(8,128)(2,1)}, bf16[2,512,128]{2,1,0:T(8,128)(2,1)}, bf16[2,512,128]{2,1,0:T(8,128)(2,1)}, bf16[2,512,256]{2,1,0:T(8,128)(2,1)}) custom-call(s32[1]{0:T(128)} %bitcast.6.group_ref, s32[1,512]{1,0:T(1,128)} %bitcast.22, bf16[4,1024,128]{2,1,0:T(8,128)(2,1)} %get-tuple-element.62.q_ref, ...), custom_call_target="tpu_custom_call", output_to_operand_aliasing={{0}: (9, {})} | custom-call | flops 1677721600 | bytes 2457600 | tf_op jit(solution)/shard_map/attention/pallas_call | solution.py:183
  55.8 0.8 copy-done
  56.6 7.1 %attention.6 = (bf16[512,2048]{1,0:T(8,128)(2,1)}, bf16[2,512,128]{2,1,0:T(8,128)(2,1)}, bf16[2,512,128]{2,1,0:T(8,128)(2,1)}, bf16[2,512,256]{2,1,0:T(8,128)(2,1)}) custom-call(s32[1]{0:T(128)} %bitcast.group_ref, s32[1,512]{1,0:T(1,128)} %bitcast.23, bf16[4,1024,128]{2,1,0:T(8,128)(2,1)} %get-tuple-element.74.q_ref, ...), custom_call_target="tpu_custom_call", output_to_operand_aliasing={{0}: (9, {})} | custom-call | flops 1677721600 | bytes 2457600 | tf_op jit(solution)/shard_map/attention/pallas_call | solution.py:183
  63.7 1.3 %collective-permute-start.12 = (bf16[2,512,256]{2,1,0:T(8,128)(2,1)}, bf16[2,512,256]{2,1,0:T(8,128)(2,1)S(1)}, u32[]{:S(2)}, u32[]{:S(2)}) collective-permute-start(bf16[2,512,256]{2,1,0:T(8,128)(2,1)} %get-tuple-element.98), channel_id=1, source_target_pairs={{0,1},{1,0},{2,3},{3,2},{4,5},{5,4},{6,7},{7,6},{8,9},{9,8},{10,11... | collective-permute-start | bytes 1572872 | tf_op jit(solution)/shard_map/ppermute | solution.py:288
  65.0 0.8 copy-done.1
  65.8 7.1 %attention.7 = (bf16[512,2048]{1,0:T(8,128)(2,1)}, bf16[2,512,128]{2,1,0:T(8,128)(2,1)}, bf16[2,512,128]{2,1,0:T(8,128)(2,1)}, bf16[2,512,256]{2,1,0:T(8,128)(2,1)}) custom-call(s32[1]{0:T(128)} %bitcast.group_ref, s32[1,512]{1,0:T(1,128)} %bitcast.24, bf16[4,1024,128]{2,1,0:T(8,128)(2,1)} %get-tuple-element.62.q_ref, ...), custom_call_target="tpu_custom_call", output_to_operand_aliasing={{0}: (9, {})} | custom-call | flops 1677721600 | bytes 2457600 | tf_op jit(solution)/shard_map/attention/pallas_call | solution.py:183
  73.0 0.3 collective-permute-start.8
  73.3 4.6 %collective-permute-done.12 = bf16[2,512,256]{2,1,0:T(8,128)(2,1)S(1)} collective-permute-done((bf16[2,512,256]{2,1,0:T(8,128)(2,1)}, bf16[2,512,256]{2,1,0:T(8,128)(2,1)S(1)}, u32[]{:S(2)}, u32[]{:S(2)}) %collective-permute-start.12) | collective-permute-done | bytes 524320 | tf_op jit(solution)/shard_map/ppermute | solution.py:288
  78.0 2.2 %collective-permute-start.13 = (bf16[2,512,256]{2,1,0:T(8,128)(2,1)S(1)}, bf16[2,512,256]{2,1,0:T(8,128)(2,1)S(1)}, u32[]{:S(2)}, u32[]{:S(2)}) collective-permute-start(bf16[2,512,256]{2,1,0:T(8,128)(2,1)S(1)} %get-tuple-element.117), channel_id=1, source_target_pairs={{2,0},{4,2},{6,4},{8,6},{10,8},{12,10},{14,12},{16,14},{18,16},{20... | collective-permute-start | bytes 1572872 | tf_op jit(solution)/shard_map/ppermute | solution.py:292
  80.2 5.2 %collective-permute-start.14 = (bf16[2,512,256]{2,1,0:T(8,128)(2,1)S(1)}, bf16[2,512,256]{2,1,0:T(8,128)(2,1)}, u32[]{:S(2)}, u32[]{:S(2)}) collective-permute-start(bf16[2,512,256]{2,1,0:T(8,128)(2,1)S(1)} %get-tuple-element.118), channel_id=1, source_target_pairs={{0,2},{2,4},{4,6},{6,8},{8,10},{10,12},{12,14},{14,16},{16,18},{18... | collective-permute-start | bytes 1572872 | tf_op jit(solution)/shard_map/ppermute | solution.py:292
  85.5 3.8 %collective-permute-done.8 = bf16[2,512,256]{2,1,0:T(8,128)(2,1)S(1)} collective-permute-done((bf16[2,512,256]{2,1,0:T(8,128)(2,1)}, bf16[2,512,256]{2,1,0:T(8,128)(2,1)S(1)}, u32[]{:S(2)}, u32[]{:S(2)}) %collective-permute-start.8) | collective-permute-done | bytes 524320 | tf_op jit(solution)/shard_map/ppermute | solution.py:288
  89.2 0.9 broadcast_select_fusion.3
  90.1 2.1 %collective-permute-start.9 = (bf16[2,512,256]{2,1,0:T(8,128)(2,1)}, bf16[2,512,256]{2,1,0:T(8,128)(2,1)S(1)}, u32[]{:S(2)}, u32[]{:S(2)}) collective-permute-start(bf16[2,512,256]{2,1,0:T(8,128)(2,1)} %get-tuple-element.119), channel_id=1, source_target_pairs={{2,0},{4,2},{6,4},{8,6},{10,8},{12,10},{14,12},{16,14},{18,16},{20... | collective-permute-start | bytes 1572872 | tf_op jit(solution)/shard_map/ppermute | solution.py:292
  92.3 3.4 %collective-permute-start.10 = (bf16[2,512,256]{2,1,0:T(8,128)(2,1)S(1)}, bf16[2,512,256]{2,1,0:T(8,128)(2,1)}, u32[]{:S(2)}, u32[]{:S(2)}) collective-permute-start(bf16[2,512,256]{2,1,0:T(8,128)(2,1)S(1)} %get-tuple-element.120), channel_id=1, source_target_pairs={{0,2},{2,4},{4,6},{6,8},{8,10},{10,12},{12,14},{14,16},{16,18},{18... | collective-permute-start | bytes 1572872 | tf_op jit(solution)/shard_map/ppermute | solution.py:292
  95.7 0.3 collective-permute-done.13
  96.0 2.0 %broadcast_select_fusion = (bf16[2,512,256]{2,1,0:T(8,128)(2,1)}, bf16[2,512,256]{2,1,0:T(8,128)(2,1)S(1)}) fusion(bf16[2,512,256]{2,1,0:T(8,128)(2,1)} %collective-permute-done.14, pred[]{:T(512)S(6)} %eq.57, bf16[2,512,256]{2,1,0:T(8,128)(2,1)S(1)} %get-tuple-element.118, bf16[2,512,256]{2,1,0:T(8,128)(2,1)S(1)} %collective-permute-done.13, pred[]{:T(512)S(6)} %eq.27, ...), kind=kLoop, calls=%fused_computation.5 | loop fusion | flops 786432 | bytes 2621443 | tf_op jit(solution)/shard_map/jit(_where)/select_n | solution.py:400
  98.0 0.1 collective-permute-start.15
  98.1 9.5 %collective-permute-done.9 = bf16[2,512,256]{2,1,0:T(8,128)(2,1)S(1)} collective-permute-done((bf16[2,512,256]{2,1,0:T(8,128)(2,1)}, bf16[2,512,256]{2,1,0:T(8,128)(2,1)S(1)}, u32[]{:S(2)}, u32[]{:S(2)}) %collective-permute-start.9) | collective-permute-done | bytes 524320 | tf_op jit(solution)/shard_map/ppermute | solution.py:292
  107.6 1.9 %broadcast_select_fusion.1 = (bf16[2,512,256]{2,1,0:T(8,128)(2,1)}, bf16[2,512,256]{2,1,0:T(8,128)(2,1)S(1)}) fusion(bf16[2,512,256]{2,1,0:T(8,128)(2,1)} %collective-permute-done.10, pred[]{:T(512)S(6)} %eq.57, bf16[2,512,256]{2,1,0:T(8,128)(2,1)S(1)} %get-tuple-element.120, bf16[2,512,256]{2,1,0:T(8,128)(2,1)S(1)} %collective-permute-done.9, pred[]{:T(512)S(6)} %eq.27, ...), kind=kLoop, calls=%fused_computation.6 | loop fusion | flops 786432 | bytes 2621443 | tf_op jit(solution)/shard_map/jit(_where)/select_n | solution.py:400
  109.5 0.1 collective-permute-start.11
  109.6 2.0 %finish.4 = (bf16[512,1024]{1,0:T(8,128)(2,1)}, bf16[512,1024]{1,0:T(8,128)(2,1)}) custom-call(s32[1]{0:T(128)} %bitcast.6.group_ref, bf16[2,512,128]{2,1,0:T(8,128)(2,1)} %get-tuple-element.99.dk_ref, bf16[2,512,128]{2,1,0:T(8,128)(2,1)} %get-tuple-element.100.dv_ref, bf16[2,512,256]{2,1,0:T(8,128)(2,1)} %get-tuple-element.109.back_ref), custom_call_target="tpu_custom_call" | custom-call | flops 524288 | bytes 2097152 | tf_op jit(solution)/shard_map/finish/pallas_call | solution.py:239
  111.6 0.3 collective-permute-done.15.back_ref
  111.9 0.8 copy-done.5
  112.7 2.0 %finish.5 = (bf16[512,1024]{1,0:T(8,128)(2,1)}, bf16[512,1024]{1,0:T(8,128)(2,1)}) custom-call(s32[1]{0:T(128)} %bitcast.group_ref, bf16[2,512,128]{2,1,0:T(8,128)(2,1)} %get-tuple-element.95.dk_ref, bf16[2,512,128]{2,1,0:T(8,128)(2,1)} %get-tuple-element.96.dv_ref, bf16[2,512,256]{2,1,0:T(8,128)(2,1)} %copy-done.5, ...), custom_call_target="tpu_custom_call", output_to_operand_aliasing={{0}: (4, {}), {1}: (5, {})} | custom-call | flops 524288 | bytes 2097152 | tf_op jit(solution)/shard_map/finish/pallas_call | solution.py:239
  114.7 2.0 %finish.6 = (bf16[512,1024]{1,0:T(8,128)(2,1)}, bf16[512,1024]{1,0:T(8,128)(2,1)}) custom-call(s32[1]{0:T(128)} %bitcast.6.group_ref, bf16[2,512,128]{2,1,0:T(8,128)(2,1)} %get-tuple-element.93.dk_ref, bf16[2,512,128]{2,1,0:T(8,128)(2,1)} %get-tuple-element.94.dv_ref, ...), custom_call_target="tpu_custom_call", output_to_operand_aliasing={{0}: (4, {}), {1}: (5, {})} | custom-call | flops 524288 | bytes 2097152 | tf_op jit(solution)/shard_map/finish/pallas_call | solution.py:239
  116.7 5.3 %collective-permute-done.11.back_ref = bf16[2,512,256]{2,1,0:T(8,128)(2,1)S(1)} collective-permute-done((bf16[2,512,256]{2,1,0:T(8,128)(2,1)S(1)}, bf16[2,512,256]{2,1,0:T(8,128)(2,1)S(1)}, u32[]{:S(2)}, u32[]{:S(2)}) %collective-permute-start.11) | collective-permute-done | bytes 524320 | tf_op jit(solution)/shard_map/ppermute | solution.py:288
  122.0 0.8 copy-done.4
  122.8 2.0 %finish.7 = (bf16[512,1024]{1,0:T(8,128)(2,1)}, bf16[512,1024]{1,0:T(8,128)(2,1)}) custom-call(s32[1]{0:T(128)} %bitcast.group_ref, bf16[2,512,128]{2,1,0:T(8,128)(2,1)} %get-tuple-element.89.dk_ref, bf16[2,512,128]{2,1,0:T(8,128)(2,1)} %get-tuple-element.90.dv_ref, bf16[2,512,256]{2,1,0:T(8,128)(2,1)} %copy-done.4, ...), custom_call_target="tpu_custom_call", output_to_operand_aliasing={{0}: (4, {}), {1}: (5, {})} | custom-call | flops 524288 | bytes 2097152 | tf_op jit(solution)/shard_map/finish/pallas_call | solution.py:239
  (26 shorter events, 0.4 us)
Async XLA Ops:
  2.3 1.7 %copy-start.7 = (s32[32]{0:T(128)S(1)}, s32[32]{0:T(128)}, u32[]{:S(2)}) copy-start(s32[32]{0:T(128)} %param.13) | copy-start | bytes 388
  2.4 12.9 %collective-permute-start.1 = (bf16[2,512,256]{2,1,0:T(8,128)(2,1)S(1)}, bf16[2,512,256]{2,1,0:T(8,128)(2,1)S(1)}, u32[]{:S(2)}, u32[]{:S(2)}) collective-permute-start(bf16[2,512,256]{2,1,0:T(8,128)(2,1)S(1)} %pad_maximum_fusion.1), channel_id=1, source_target_pairs={{0,1},{1,0},{2,3},{3,2},{4,5},{5,4},{6,7},{7,6},{8,9},{9,8},{10,11... | collective-permute-start | bytes 1572872 | tf_op jit(solution)/shard_map/ppermute | solution.py:288
  2.8 27.3 %collective-permute-start = (bf16[2,512,256]{2,1,0:T(8,128)(2,1)S(1)}, bf16[2,512,256]{2,1,0:T(8,128)(2,1)S(1)}, u32[]{:S(2)}, u32[]{:S(2)}) collective-permute-start(bf16[2,512,256]{2,1,0:T(8,128)(2,1)S(1)} %pad_maximum_fusion), channel_id=1, source_target_pairs={{0,1},{1,0},{2,3},{3,2},{4,5},{5,4},{6,7},{7,6},{8,9},{9,8},{10,11... | collective-permute-start | bytes 1572872 | tf_op jit(solution)/shard_map/ppermute | solution.py:288
  10.9 14.2 %copy-start.6 = (s32[16384]{0:T(1024)S(1)}, s32[16384]{0:T(1024)}, u32[]{:S(2)}) copy-start(s32[16384]{0:T(1024)} %param.12) | copy-start | bytes 196612
  16.1 21.4 %collective-permute-start.3 = (bf16[2,512,256]{2,1,0:T(8,128)(2,1)}, bf16[2,512,256]{2,1,0:T(8,128)(2,1)S(1)}, u32[]{:S(2)}, u32[]{:S(2)}) collective-permute-start(bf16[2,512,256]{2,1,0:T(8,128)(2,1)} %get-tuple-element.131), channel_id=1, source_target_pairs={{2,0},{4,2},{6,4},{8,6},{10,8},{12,10},{14,12},{16,14},{18,16},{20... | collective-permute-start | bytes 1572872 | tf_op jit(solution)/shard_map/ppermute | solution.py:292
  20.7 16.8 %collective-permute-start.2 = (bf16[2,512,256]{2,1,0:T(8,128)(2,1)S(1)}, bf16[2,512,256]{2,1,0:T(8,128)(2,1)S(1)}, u32[]{:S(2)}, u32[]{:S(2)}) collective-permute-start(bf16[2,512,256]{2,1,0:T(8,128)(2,1)S(1)} %get-tuple-element.132), channel_id=1, source_target_pairs={{0,2},{2,4},{4,6},{6,8},{8,10},{10,12},{12,14},{14,16},{16,18},{18... | collective-permute-start | bytes 1572872 | tf_op jit(solution)/shard_map/ppermute | solution.py:292
  31.0 16.6 %collective-permute-start.5 = (bf16[2,512,256]{2,1,0:T(8,128)(2,1)}, bf16[2,512,256]{2,1,0:T(8,128)(2,1)S(1)}, u32[]{:S(2)}, u32[]{:S(2)}) collective-permute-start(bf16[2,512,256]{2,1,0:T(8,128)(2,1)} %get-tuple-element.121), channel_id=1, source_target_pairs={{2,0},{4,2},{6,4},{8,6},{10,8},{12,10},{14,12},{16,14},{18,16},{20... | collective-permute-start | bytes 1572872 | tf_op jit(solution)/shard_map/ppermute | solution.py:292
  32.9 14.7 %collective-permute-start.4 = (bf16[2,512,256]{2,1,0:T(8,128)(2,1)S(1)}, bf16[2,512,256]{2,1,0:T(8,128)(2,1)S(1)}, u32[]{:S(2)}, u32[]{:S(2)}) collective-permute-start(bf16[2,512,256]{2,1,0:T(8,128)(2,1)S(1)} %get-tuple-element.122), channel_id=1, source_target_pairs={{0,2},{2,4},{4,6},{6,8},{8,10},{10,12},{12,14},{14,16},{16,18},{18... | collective-permute-start | bytes 1572872 | tf_op jit(solution)/shard_map/ppermute | solution.py:292
  38.4 17.4 %collective-permute-start.7 = (bf16[2,512,256]{2,1,0:T(8,128)(2,1)S(1)}, bf16[2,512,256]{2,1,0:T(8,128)(2,1)S(1)}, u32[]{:S(2)}, u32[]{:S(2)}) collective-permute-start(bf16[2,512,256]{2,1,0:T(8,128)(2,1)S(1)} %get-tuple-element.115), channel_id=1, source_target_pairs={{0,1},{1,0},{2,3},{3,2},{4,5},{5,4},{6,7},{7,6},{8,9},{9,8},{10,11... | collective-permute-start | bytes 1572872 | tf_op jit(solution)/shard_map/ppermute | solution.py:288
  48.5 16.5 %collective-permute-start.6 = (bf16[2,512,256]{2,1,0:T(8,128)(2,1)S(1)}, bf16[2,512,256]{2,1,0:T(8,128)(2,1)S(1)}, u32[]{:S(2)}, u32[]{:S(2)}) collective-permute-start(bf16[2,512,256]{2,1,0:T(8,128)(2,1)S(1)} %get-tuple-element.114), channel_id=1, source_target_pairs={{0,1},{1,0},{2,3},{3,2},{4,5},{5,4},{6,7},{7,6},{8,9},{9,8},{10,11... | collective-permute-start | bytes 1572872 | tf_op jit(solution)/shard_map/ppermute | solution.py:288
  55.8 0.8 copy-start
  63.7 14.2 %collective-permute-start.12 = (bf16[2,512,256]{2,1,0:T(8,128)(2,1)}, bf16[2,512,256]{2,1,0:T(8,128)(2,1)S(1)}, u32[]{:S(2)}, u32[]{:S(2)}) collective-permute-start(bf16[2,512,256]{2,1,0:T(8,128)(2,1)} %get-tuple-element.98), channel_id=1, source_target_pairs={{0,1},{1,0},{2,3},{3,2},{4,5},{5,4},{6,7},{7,6},{8,9},{9,8},{10,11... | collective-permute-start | bytes 1572872 | tf_op jit(solution)/shard_map/ppermute | solution.py:288
  65.0 0.8 copy-start.1
  65.8 12.1 %copy-start.2 = (bf16[2,512,256]{2,1,0:T(8,128)(2,1)S(1)}, bf16[2,512,256]{2,1,0:T(8,128)(2,1)}, u32[]{:S(2)}) copy-start(bf16[2,512,256]{2,1,0:T(8,128)(2,1)} %get-tuple-element.97) | copy-start | bytes 1572868
  73.0 16.3 %copy-start.3 = (bf16[2,512,256]{2,1,0:T(8,128)(2,1)S(1)}, bf16[2,512,256]{2,1,0:T(8,128)(2,1)}, u32[]{:S(2)}) copy-start(bf16[2,512,256]{2,1,0:T(8,128)(2,1)} %get-tuple-element.91) | copy-start | bytes 1572868
  73.0 16.3 %collective-permute-start.8 = (bf16[2,512,256]{2,1,0:T(8,128)(2,1)}, bf16[2,512,256]{2,1,0:T(8,128)(2,1)S(1)}, u32[]{:S(2)}, u32[]{:S(2)}) collective-permute-start(bf16[2,512,256]{2,1,0:T(8,128)(2,1)} %get-tuple-element.92), channel_id=1, source_target_pairs={{0,1},{1,0},{2,3},{3,2},{4,5},{5,4},{6,7},{7,6},{8,9},{9,8},{10,11... | collective-permute-start | bytes 1572872 | tf_op jit(solution)/shard_map/ppermute | solution.py:288
  78.0 18.0 %collective-permute-start.13 = (bf16[2,512,256]{2,1,0:T(8,128)(2,1)S(1)}, bf16[2,512,256]{2,1,0:T(8,128)(2,1)S(1)}, u32[]{:S(2)}, u32[]{:S(2)}) collective-permute-start(bf16[2,512,256]{2,1,0:T(8,128)(2,1)S(1)} %get-tuple-element.117), channel_id=1, source_target_pairs={{2,0},{4,2},{6,4},{8,6},{10,8},{12,10},{14,12},{16,14},{18,16},{20... | collective-permute-start | bytes 1572872 | tf_op jit(solution)/shard_map/ppermute | solution.py:292
  80.2 15.8 %collective-permute-start.14 = (bf16[2,512,256]{2,1,0:T(8,128)(2,1)S(1)}, bf16[2,512,256]{2,1,0:T(8,128)(2,1)}, u32[]{:S(2)}, u32[]{:S(2)}) collective-permute-start(bf16[2,512,256]{2,1,0:T(8,128)(2,1)S(1)} %get-tuple-element.118), channel_id=1, source_target_pairs={{0,2},{2,4},{4,6},{6,8},{8,10},{10,12},{12,14},{14,16},{16,18},{18... | collective-permute-start | bytes 1572872 | tf_op jit(solution)/shard_map/ppermute | solution.py:292
  90.1 17.4 %collective-permute-start.9 = (bf16[2,512,256]{2,1,0:T(8,128)(2,1)}, bf16[2,512,256]{2,1,0:T(8,128)(2,1)S(1)}, u32[]{:S(2)}, u32[]{:S(2)}) collective-permute-start(bf16[2,512,256]{2,1,0:T(8,128)(2,1)} %get-tuple-element.119), channel_id=1, source_target_pairs={{2,0},{4,2},{6,4},{8,6},{10,8},{12,10},{14,12},{16,14},{18,16},{20... | collective-permute-start | bytes 1572872 | tf_op jit(solution)/shard_map/ppermute | solution.py:292
  92.3 15.3 %collective-permute-start.10 = (bf16[2,512,256]{2,1,0:T(8,128)(2,1)S(1)}, bf16[2,512,256]{2,1,0:T(8,128)(2,1)}, u32[]{:S(2)}, u32[]{:S(2)}) collective-permute-start(bf16[2,512,256]{2,1,0:T(8,128)(2,1)S(1)} %get-tuple-element.120), channel_id=1, source_target_pairs={{0,2},{2,4},{4,6},{6,8},{8,10},{10,12},{12,14},{14,16},{16,18},{18... | collective-permute-start | bytes 1572872 | tf_op jit(solution)/shard_map/ppermute | solution.py:292
  98.0 13.9 %collective-permute-start.15 = (bf16[2,512,256]{2,1,0:T(8,128)(2,1)S(1)}, bf16[2,512,256]{2,1,0:T(8,128)(2,1)S(1)}, u32[]{:S(2)}, u32[]{:S(2)}) collective-permute-start(bf16[2,512,256]{2,1,0:T(8,128)(2,1)S(1)} %get-tuple-element.110), channel_id=1, source_target_pairs={{0,1},{1,0},{2,3},{3,2},{4,5},{5,4},{6,7},{7,6},{8,9},{9,8},{10,11... | collective-permute-start | bytes 1572872 | tf_op jit(solution)/shard_map/ppermute | solution.py:288
  109.5 12.5 %collective-permute-start.11 = (bf16[2,512,256]{2,1,0:T(8,128)(2,1)S(1)}, bf16[2,512,256]{2,1,0:T(8,128)(2,1)S(1)}, u32[]{:S(2)}, u32[]{:S(2)}) collective-permute-start(bf16[2,512,256]{2,1,0:T(8,128)(2,1)S(1)} %get-tuple-element.112), channel_id=1, source_target_pairs={{0,1},{1,0},{2,3},{3,2},{4,5},{5,4},{6,7},{7,6},{8,9},{9,8},{10,11... | collective-permute-start | bytes 1572872 | tf_op jit(solution)/shard_map/ppermute | solution.py:288
  111.9 0.8 copy-start.5
  122.0 0.8 copy-start.4

commit v7 on v6

--- a/solution.py
+++ b/solution.py
@@ -10,7 +10,6 @@
 HEAD_SIZE = 128
 NEGATIVE = -1e30
 LOG2_E = 1.4426950408889634
-CHUNKS = 2
 TILE = 128
 STRIP = 64
 VMEM_BYTES = 60 * 1024 * 1024
@@ -76,9 +75,6 @@
         out_specs=[pl.BlockSpec((1, *shape), leading) for shape, _ in shapes],
         out_shape=[jax.ShapeDtypeStruct((count, *shape), dtype) for shape, dtype in shapes],
         compiler_params=pltpu.CompilerParams(vmem_limit_bytes=VMEM_BYTES),
-        cost_estimate=pl.CostEstimate(
-            flops=count * rows * 1024, bytes_accessed=count * rows * 4096, transcendentals=0
-        ),
         name="arrange",
     )(queries, keys, values, outputs, grads)
 
@@ -164,22 +160,22 @@
     dv_ref[0] = dv_sum[window:].astype(dv_ref.dtype)
 
 
-def attention(group, low, arranged, past, first_head, heads_per_group, heads, carried):
+def attention(group, low, arranged, past, first_head, per_group, heads_per_group, heads, carried):
     rows, window, count = arranged[3].shape[1], past.shape[1], past.shape[2] // HEAD_SIZE
     members = arranged[0].shape[1] // rows
 
     def leading(step, group_ref):
-        return (group_ref[0] * count + step, 0, 0)
+        return (group_ref[0] * per_group + step, 0, 0)
 
     def column(step, group_ref):
-        return (0, group_ref[0] * heads_per_group + first_head + step)
+        group = group_ref[0] + step // per_group
+        return (0, group * heads_per_group + first_head + step % per_group)
 
     past_spec = pl.BlockSpec((2, window, HEAD_SIZE), lambda step, group_ref: (0, 0, step))
     low_spec = pl.BlockSpec((1, rows), lambda step, group_ref: (0, 0))
     own_spec = pl.BlockSpec((1, rows, HEAD_SIZE), lambda step, group_ref: (step, 0, 0))
     own_shape = jax.ShapeDtypeStruct((count, rows, HEAD_SIZE), jnp.bfloat16)
     square = (rows // TILE, window + TILE, members * TILE)
-    tiles = count * members * rows * (window + TILE)
     return pl.pallas_call(
         functools.partial(attention_body, len(carried)),
         grid_spec=pltpu.PrefetchScalarGridSpec(
@@ -210,9 +206,6 @@
         ],
         input_output_aliases={9 + i: i for i in range(len(carried))},
         compiler_params=pltpu.CompilerParams(vmem_limit_bytes=VMEM_BYTES),
-        cost_estimate=pl.CostEstimate(
-            flops=10 * tiles * HEAD_SIZE, bytes_accessed=count * rows * 2400, transcendentals=tiles
-        ),
         name="attention",
     )(group, low, *arranged, past, *carried)
 
@@ -227,11 +220,12 @@
     value_out[...] = sums[1].astype(value_out.dtype)
 
 
-def finish(group, own, back, first_head, heads_per_group, heads, carried):
+def finish(group, own, back, first_head, per_group, heads_per_group, heads, carried):
     rows, count = back.shape[1], back.shape[2] // HEAD_SIZE
 
     def column(step, group_ref):
-        return (0, group_ref[0] * heads_per_group + first_head + step)
+        group = group_ref[0] + step // per_group
+        return (0, group * heads_per_group + first_head + step % per_group)
 
     key_spec = pl.BlockSpec((rows, HEAD_SIZE), column)
     own_spec = pl.BlockSpec((1, rows, HEAD_SIZE), lambda step, group_ref: (step, 0, 0))
@@ -248,9 +242,6 @@
         out_shape=[jax.ShapeDtypeStruct((rows, heads * HEAD_SIZE), jnp.bfloat16)] * 2,
         input_output_aliases={4 + i: i for i in range(len(carried))},
         compiler_params=pltpu.CompilerParams(vmem_limit_bytes=VMEM_BYTES),
-        cost_estimate=pl.CostEstimate(
-            flops=count * rows * 512, bytes_accessed=count * rows * 2048, transcendentals=0
-        ),
         name="finish",
     )(group, *own, back, *carried)
 
@@ -264,6 +255,14 @@
     for place in range(len(items) - 2, -1, -1):
         result = jnp.where(index == place, items[place], result)
     return result
+
+
+def plan(heads_per_group, sharers):
+    direct = heads_per_group // 4 if sharers == 2 else 0
+    rest = heads_per_group - direct
+    large = (2 * rest + 2) // 3
+    chunks = [(direct, large), (direct + large, rest - large)]
+    return direct, [chunk for chunk in chunks if chunk[1]]
 
 
 def local(queries, keys, values, outputs, out_grads, segment_ids, block_order):
@@ -274,11 +273,14 @@
     parts = sharers // 2
     key_heads = keys.shape[1] // HEAD_SIZE
     heads_per_group = key_heads // sharers
-    chunks = min(CHUNKS, heads_per_group)
-    per_piece = heads_per_group // chunks
-    slots = lax.dynamic_slice_in_dim(block_order, 2 * block, 2)
-    early_slot = (slots[0] > slots[1]).astype(jnp.int32)
+    direct, chunks = plan(heads_per_group, sharers)
     last_block = block == blocks - 1
+
+    def early_slot_of(block):
+        slots = lax.dynamic_slice_in_dim(block_order, 2 * jnp.clip(block, 0, blocks - 1), 2)
+        return (slots[0] > slots[1]).astype(jnp.int32)
+
+    early_slot = early_slot_of(block)
 
     def other(turn):
         return lax.rem(place + turn + sharers, sharers)
@@ -291,15 +293,17 @@
         first, end = max(0, -step), min(blocks, blocks - step)
         return lax.ppermute(value, "blk", [(source, source + step) for source in range(first, end)])
 
-    def columns(array, group, chunk):
-        pieces = []
-        for g in range(sharers):
-            start = (g * heads_per_group + chunk * per_piece) * HEAD_SIZE
-            pieces.append(array[:, start : start + per_piece * HEAD_SIZE])
-        return pick(pieces, group)
-
-    def piece_of(group, chunk):
-        return jnp.stack([columns(keys, group, chunk), columns(values, group, chunk)])
+    def columns(array, group, first, count):
+        start = (group * heads_per_group + first) * HEAD_SIZE
+        return array[:, start : start + count * HEAD_SIZE]
+
+    def piece_of(group, first, count):
+        return jnp.stack(
+            [
+                pick([columns(array, g, first, count) for g in range(sharers)], group)
+                for array in (keys, values)
+            ]
+        )
 
     def is_early(device):
         return device // parts == early_slot
@@ -309,7 +313,8 @@
             return array[:, :count]
         return lax.dynamic_slice_in_dim(array, device % parts * rows, count, 1)
 
-    my_half = pick([slots[0], slots[1]], place // parts)
+    my_slots = lax.dynamic_slice_in_dim(block_order, 2 * block, 2)
+    my_half = pick([my_slots[0], my_slots[1]], place // parts)
     start = my_half * window + place % parts * rows
     padded = jnp.concatenate([jnp.full((window,), -1, jnp.int32), segment_ids])
     near = lax.dynamic_slice_in_dim(padded, start, window + rows)
@@ -317,6 +322,7 @@
 
     row_arrays = (queries, keys, values, outputs, out_grads)
     groups = [other(-turn) for turn in range(sharers)]
+    early = is_early(place)
 
     def halves_of(pieces):
         return [
@@ -330,59 +336,101 @@
             for slot in (early_slot, 1 - early_slot)
         ]
 
-    arranged, halves = [], []
-    for chunk in range(chunks):
-        pieces = [piece_of(place, chunk)]
-        pieces += [turned(piece_of(other(turn), chunk), turn) for turn in range(1, sharers)]
-        arrays = arrange(row_arrays, chunk * per_piece, heads_per_group, per_piece)
-        *arrays, pieces[-1] = together(*arrays, pieces[-1])
+    pieces = []
+    for first, count in chunks:
+        sent = [piece_of(other(turn), first, count) for turn in range(1, sharers)]
+        if not pieces:
+            key_rows, value_rows, _ = together(keys, values, sent[0])
+        pieces.append(
+            [piece_of(place, first, count)]
+            + [turned(piece, turn) for turn, piece in enumerate(sent, 1)]
+        )
+    arranged = []
+    for chunk, (first, count) in enumerate(chunks):
+        arrays = arrange(row_arrays, first, heads_per_group, count)
+        *arrays, pieces[chunk][-1] = together(*arrays, pieces[chunk][-1])
         arranged.append(arrays)
-        halves.append(halves_of(pieces))
-    before = [(shifted(early, 1), shifted(late, -1)) for early, late in halves]
-
-    def run(turn, chunk, past, carried):
-        query_grads, *own[chunk, turn], back = attention(
-            groups[turn].reshape(1), low, arranged[chunk], past,
-            chunk * per_piece, heads_per_group, key_heads, carried,
-        )
-        return (query_grads,), back
-
-    carried, own, terms, pasts = (), {}, [], []
-    for chunk in range(chunks):
-        (early, late), (before_early, before_late) = halves[chunk], before[chunk]
+    if direct:
+        straight = jnp.stack(
+            [
+                jnp.concatenate([columns(array, g, 0, direct) for g in range(sharers)], axis=1)
+                for array in (key_rows, value_rows)
+            ]
+        )
+        from_left, from_right = shifted(straight, 1), shifted(straight, -1)
+        same_left = early_slot_of(block - 1) == early_slot
+        same_right = (early_slot_of(block + 1) == early_slot) & ~last_block
+        mine = jnp.where(early, from_left, from_right)
+        theirs = jnp.where(early, jnp.where(last_block, straight, from_right), from_left)
+        direct_past = jnp.where(jnp.where(early, same_left, same_right), mine, turned(theirs, 1))
+        direct_arranged = arrange(row_arrays, 0, heads_per_group, direct)
+    halves = [halves_of(chunk_pieces) for chunk_pieces in pieces]
+    before = [(shifted(early_half, 1), shifted(late_half, -1)) for early_half, late_half in halves]
+
+    carried, own, terms, pasts = (), {}, {}, []
+
+    def run(key, group, arrays, past, first, per_group, carried):
+        query_grads, *own[key], terms[key] = attention(
+            group.reshape(1), low, arrays, past, first, per_group, heads_per_group, key_heads, carried
+        )
+        return (query_grads,)
+
+    for chunk, (first, count) in enumerate(chunks):
+        (early_half, late_half), (before_early, before_late) = halves[chunk], before[chunk]
         if chunk:
             *carried, before_early, before_late = together(*carried, before_early, before_late)
-        before_late = jnp.where(last_block, early, before_late)
+            carried = tuple(carried)
+        before_late = jnp.where(last_block, early_half, before_late)
 
         def past_of(device):
             before = jnp.where(is_early(device), before_early, before_late)
             if parts == 1:
                 return before
-            own = jnp.where(is_early(device), early, late)
-            return part_rows(jnp.concatenate([before, own], axis=1), device, window)
-
-        pasts.append([turned(past_of(other(turn)), turn) for turn in range(1, sharers)])
-        carried, back = run(0, chunk, past_of(place), carried)
-        terms.append([back])
-
-    for chunk in range(chunks):
-        for turn in range(1, sharers):
-            carried, back = run(turn, chunk, pasts[chunk][turn - 1], carried)
-            terms[chunk].append(turned(back, -turn))
-
+            half = jnp.where(is_early(device), early_half, late_half)
+            return part_rows(jnp.concatenate([before, half], axis=1), device, window)
+
+        pasts.append(
+            [past_of(place)] + [turned(past_of(other(turn)), turn) for turn in range(1, sharers)]
+        )
+        if chunk == 0:
+            carried = run((0, 0), groups[0], arranged[0], pasts[0][0], first, count, carried)
+
+    if direct:
+        carried = run(
+            "direct", jnp.zeros((), jnp.int32), direct_arranged, direct_past, 0, direct, carried
+        )
+    if len(chunks) > 1:
+        pasts[0][1], _ = together(pasts[0][1], pasts[1][0])
+    for chunk, (first, count) in enumerate(chunks):
+        for turn in range(sharers):
+            if (chunk, turn) != (0, 0):
+                carried = run(
+                    (chunk, turn), groups[turn], arranged[chunk], pasts[chunk][turn],
+                    first, count, carried,
+                )
     (query_grads,) = carried
+
     results = ()
-    for chunk in range(chunks):
+    if direct:
+        term = terms["direct"]
+        from_right, from_left = shifted(term, -1), shifted(term, 1)
+        mine = jnp.where(early, from_right, from_left)
+        theirs = jnp.where(early, from_left, jnp.where(last_block, term, from_right))
+        direct_back = jnp.where(jnp.where(early, same_right, same_left), mine, turned(theirs, 1))
+
+    for chunk, (first, count) in enumerate(chunks):
+        came = [terms[chunk, 0]]
+        came += [turned(terms[chunk, turn], -turn) for turn in range(1, sharers)]
         to_before, to_own = [], []
         for slot in (early_slot, 1 - early_slot):
             if parts == 1:
-                to_before.append(pick(terms[chunk], lax.rem(slot - place + sharers, sharers)))
+                to_before.append(pick(came, lax.rem(slot - place + sharers, sharers)))
                 to_own.append(None)
             else:
-                total = jnp.zeros((2, 2 * window, terms[chunk][0].shape[2]), jnp.float32)
+                total = jnp.zeros((2, 2 * window, came[0].shape[2]), jnp.float32)
                 for turn in range(sharers):
                     device = other(turn)
-                    mine = jnp.where(device // parts == slot, terms[chunk][turn].astype(jnp.float32), 0.0)
+                    mine = jnp.where(device // parts == slot, came[turn].astype(jnp.float32), 0.0)
                     wide = jnp.pad(mine, ((0, 0), (window, window), (0, 0)))
                     total += lax.dynamic_slice_in_dim(
                         wide, window - device % parts * rows, 2 * window, 1
@@ -392,8 +440,8 @@
         for_early, for_late = shifted(to_before[0], -1), shifted(to_before[1], 1)
         for_early = jnp.where(last_block, to_before[1], for_early)
         sums = [
-            came if more is None else (came.astype(jnp.float32) + more).astype(jnp.bfloat16)
-            for came, more in zip((for_early, for_late), to_own)
+            half if more is None else (half.astype(jnp.float32) + more).astype(jnp.bfloat16)
+            for half, more in zip((for_early, for_late), to_own)
         ]
 
         def rows_of(device):
@@ -405,7 +453,12 @@
                 back = turned(back, turn)
             results = finish(
                 groups[turn].reshape(1), own[chunk, turn], back,
-                chunk * per_piece, heads_per_group, key_heads, tuple(results),
+                first, count, heads_per_group, key_heads, tuple(results),
+            )
+        if chunk == 0 and direct:
+            results = finish(
+                jnp.zeros((1,), jnp.int32), own["direct"], direct_back,
+                0, direct, heads_per_group, key_heads, tuple(results),
             )
     return (query_grads, *results)
 

time: 126 us -> 148 us (1.17)
  starting transfers between devices: 30.1 us -> 50 us
  waiting for transfers between devices: 30 us -> 17.4 us
  other arithmetic: 11.1 us -> 17.4 us
  Pallas kernels: 46.1 us -> 50.4 us
  between operations: 3.46 us -> 6.22 us
    ppermute x8 -> x12, starting transfers between devices: 26.2 us -> 40.2 us  [shifted(): lax.ppermute(value, 'blk', [(source, source + step) for source in range(f...]
    ppermute x8 -> x10, waiting for transfers between devices: 18.4 us -> 11.7 us  [turned(): return lax.ppermute(value, 'head', pairs)]
    ppermute x8 -> x12, waiting for transfers between devices: 11.6 us -> 5.69 us  [shifted(): lax.ppermute(value, 'blk', [(source, source + step) for source in range(f...]
    ppermute x8 -> x10, starting transfers between devices: 3.92 us -> 9.77 us  [turned(): return lax.ppermute(value, 'head', pairs)]
    select_n x0 -> x4, other arithmetic: none -> 3.86 us  [the longest x1 1.97 us: local(): jnp.where(early, jnp.where(last_block, straight, from_right), from_left)]
    another operation x3 -> x7, other arithmetic: 1.79 us -> 5.35 us  [the longest x4 4.42 us: piece_of(): jnp.stack([pick([columns(array, g, first, count) for g in range(sharers)]...]
    select_n x2, other arithmetic: 3.87 us -> 1.67 us  [rows_of(): jnp.where(is_early(device), sums[0], sums[1])]
    pallas_call x4 -> x5, Pallas kernels: 28.4 us -> 30.3 us  [attention(): pl.pallas_call(functools.partial(attention_body, len(carried)), grid_spec...]
  transfers between devices with their start and end apart: 16 -> 22, of which waited for: 8 -> 7; matrix products, arithmetic and copies ran while one was open for 8% -> 11% of each run, Pallas kernels for 35% -> 28%
where the time goes in v7:
time: 148 us; the launch traced here: 147 us
  Pallas kernels  50.4 us (34%)
  starting transfers between devices  50 us (34%)
  other arithmetic  17.4 us (12%)
  waiting for transfers between devices  17.4 us (12%)
  between operations  6.22 us (4%)
  local copies, waits for them, and re-layouts  5.25 us (4%)
    ppermute x12, starting transfers between devices, shifted(): lax.ppermute(value, 'blk', [(source, source + step) for source in range(f...  40.2 us
    pallas_call x5, Pallas kernels, attention(): pl.pallas_call(functools.partial(attention_body, len(carried)), grid_spec...  30.3 us
    ppermute x10, waiting for transfers between devices, turned(): return lax.ppermute(value, 'head', pairs)  11.7 us
    pallas_call x3, Pallas kernels, arrange(): pl.pallas_call(arrange_body, grid=(groups, per_piece), in_specs=[query_sp...  10.5 us
    ppermute x10, starting transfers between devices, turned(): return lax.ppermute(value, 'head', pairs)  9.77 us
    pallas_call x5, Pallas kernels, finish(): pl.pallas_call(functools.partial(finish_body, len(carried)), grid_spec=pl...  9.62 us
    ppermute x12, waiting for transfers between devices, shifted(): lax.ppermute(value, 'blk', [(source, source + step) for source in range(f...  5.69 us
    another operation x4, other arithmetic, piece_of(): jnp.stack([pick([columns(array, g, first, count) for g in range(sharers)]...  4.42 us
  transfers between devices with their start and end apart: 22, of which 7 were waited for; matrix products, arithmetic and copies ran while one was open for 11% of the time, Pallas kernels for 28%

profile of v7, /device:TPU:11, one launch (start us, length us, event | category | flops | bytes accessed | tf_op | source)
XLA Modules:
  0.0 146.7 jit_solution(1317739738575590796)
XLA Ops:
  0.7 2.1 %select_bitcast_fusion = (bf16[1,512,256]{2,1,0:T(8,128)(2,1)S(1)}, bf16[1,512,256]{2,1,0:T(8,128)(2,1)S(1)}, bf16[1,512,256]{2,1,0:T(8,128)(2,1)S(1)}, bf16[1,512,256]{2,1,0:T(8,128)(2,1)}) fusion(pred[]{:T(512)S(6)} %eq.26, bf16[512,1024]{1,0:T(8,128)(2,1)} %v_ref.5, pred[]{:T(512)S(6)} %eq.27, bf16[512,1024]{1,0:T(8,128)(2,1)} %k_ref.5), kind=kLoop, calls=%fused_computation.22 | loop fusion | flops 524288 | bytes 2097154 | tf_op jit(solution)/shard_map/stack | solution.py:301
  2.8 0.8 pad_maximum_fusion
  3.8 0.9 pad_maximum_fusion.2
  4.7 2.6 %collective-permute-start.9 = (bf16[2,512,256]{2,1,0:T(8,128)(2,1)}, bf16[2,512,256]{2,1,0:T(8,128)(2,1)S(1)}, u32[]{:S(2)}, u32[]{:S(2)}) collective-permute-start(bf16[2,512,256]{2,1,0:T(8,128)(2,1)} %pad_maximum_fusion.2), channel_id=1, source_target_pairs={{2,0},{4,2},{6,4},{8,6},{10,8},{12,10},{14,12},{16,14},{18,16},{20... | collective-permute-start | bytes 1572872 | tf_op jit(solution)/shard_map/ppermute | solution.py:294
  7.3 3.0 %collective-permute-start.8 = (bf16[2,512,256]{2,1,0:T(8,128)(2,1)}, bf16[2,512,256]{2,1,0:T(8,128)(2,1)}, u32[]{:S(2)}, u32[]{:S(2)}) collective-permute-start(bf16[2,512,256]{2,1,0:T(8,128)(2,1)} %pad_maximum_fusion.2), channel_id=1, source_target_pairs={{0,2},{2,4},{4,6},{6,8},{8,10},{10,12},{12,14},{14,16},{16,18},{18... | collective-permute-start | bytes 1572872 | tf_op jit(solution)/shard_map/ppermute | solution.py:294
  12.1 1.2 collective-permute-start
  17.3 4.9 %arrange.4 = (bf16[4,1024,128]{2,1,0:T(8,128)(2,1)}, bf16[4,1024,128]{2,1,0:T(8,128)(2,1)}, f32[4,1,1024]{2,1,0:T(1,128)}, bf16[4,512,128]{2,1,0:T(8,128)(2,1)},...) custom-call(bf16[512,2048]{1,0:T(8,128)(2,1)} %q_ref.5, bf16[512,1024]{1,0:T(8,128)(2,1)} %k_ref.5, ...), custom_call_target="tpu_custom_call" | custom-call | tf_op jit(solution)/shard_map/arrange/pallas_call | solution.py:71
  22.2 0.9 convert_reduce_fusion
  23.2 1.3 collective-permute-done.1
  24.5 1.1 broadcast_select_fusion.5
  25.6 2.7 %collective-permute-start.3 = (bf16[2,512,256]{2,1,0:T(8,128)(2,1)S(1)}, bf16[2,512,256]{2,1,0:T(8,128)(2,1)S(1)}, u32[]{:S(2)}, u32[]{:S(2)}) collective-permute-start(bf16[2,512,256]{2,1,0:T(8,128)(2,1)S(1)} %get-tuple-element.153), channel_id=1, source_target_pairs={{2,0},{4,2},{6,4},{8,6},{10,8},{12,10},{14,12},{16,14},{18,16},{20... | collective-permute-start | bytes 1572872 | tf_op jit(solution)/shard_map/ppermute | solution.py:294
  28.3 2.9 %collective-permute-start.2 = (bf16[2,512,256]{2,1,0:T(8,128)(2,1)S(1)}, bf16[2,512,256]{2,1,0:T(8,128)(2,1)S(1)}, u32[]{:S(2)}, u32[]{:S(2)}) collective-permute-start(bf16[2,512,256]{2,1,0:T(8,128)(2,1)S(1)} %get-tuple-element.154), channel_id=1, source_target_pairs={{0,2},{2,4},{4,6},{6,8},{8,10},{10,12},{12,14},{14,16},{16,18},{18... | collective-permute-start | bytes 1572872 | tf_op jit(solution)/shard_map/ppermute | solution.py:294
  31.8 2.8 %arrange.3 = (bf16[2,1024,128]{2,1,0:T(8,128)(2,1)}, bf16[2,1024,128]{2,1,0:T(8,128)(2,1)}, f32[2,1,1024]{2,1,0:T(1,128)}, bf16[2,512,128]{2,1,0:T(8,128)(2,1)},...) custom-call(bf16[512,2048]{1,0:T(8,128)(2,1)} %q_ref.5, bf16[512,1024]{1,0:T(8,128)(2,1)} %k_ref.5, ...), custom_call_target="tpu_custom_call" | custom-call | tf_op jit(solution)/shard_map/arrange/pallas_call | solution.py:71
  34.6 2.8 %arrange.5 = (bf16[2,1024,128]{2,1,0:T(8,128)(2,1)}, bf16[2,1024,128]{2,1,0:T(8,128)(2,1)}, f32[2,1,1024]{2,1,0:T(1,128)}, bf16[2,512,128]{2,1,0:T(8,128)(2,1)},...) custom-call(bf16[512,2048]{1,0:T(8,128)(2,1)} %q_ref.5, bf16[512,1024]{1,0:T(8,128)(2,1)} %k_ref.5, ...), custom_call_target="tpu_custom_call" | custom-call | tf_op jit(solution)/shard_map/arrange/pallas_call | solution.py:71
  40.1 2.0 %select_select_fusion.2 = bf16[2,512,256]{2,1,0:T(8,128)(2,1)} fusion(bf16[2,512,256]{2,1,0:T(8,128)(2,1)} %collective-permute-done.8, bf16[2,512,256]{2,1,0:T(8,128)(2,1)S(1)} %collective-permute-done.9, pred[]{:T(512)S(6)} %eq.60, pred[]{:T(512)S(6)} %eq.29, bf16[1,512,256]{2,1,0:T(8,128)(2,1)S(1)} %maximum_bitcast_fusion.1, ...), kind=kLoop, calls=%fused_computation.6 | loop fusion | flops 786432 | bytes 2097154 | tf_op jit(solution)/shard_map/jit(_where)/select_n | solution.py:364
  42.1 1.7 %broadcast_select_fusion.16 = (bf16[2,512,128]{2,1,0:T(8,128)(2,1)}, bf16[2,512,128]{2,1,0:T(8,128)(2,1)S(1)}) fusion(bf16[2,512,128]{2,1,0:T(8,128)(2,1)} %collective-permute-done, pred[]{:T(512)S(6)} %eq.61, bf16[1,512,128]{2,1,0:T(8,128)(2,1)S(1)} %get-tuple-element.151, bf16[1,512,128]{2,1,0:T(8,128)(2,1)S(1)} %copy-done.4, pred[]{:T(512)S(6)} %eq.30), kind=kLoop, calls=%fused_computation.32 | loop fusion | flops 393216 | bytes 1048578 | tf_op jit(solution)/shard_map/jit(_where)/select_n | solution.py:256
  43.8 2.7 %collective-permute-start.5 = (bf16[2,512,128]{2,1,0:T(8,128)(2,1)}, bf16[2,512,128]{2,1,0:T(8,128)(2,1)S(1)}, u32[]{:S(2)}, u32[]{:S(2)}) collective-permute-start(bf16[2,512,128]{2,1,0:T(8,128)(2,1)} %get-tuple-element.165), channel_id=1, source_target_pairs={{2,0},{4,2},{6,4},{8,6},{10,8},{12,10},{14,12},{16,14},{18,16},{20... | collective-permute-start | bytes 786440 | tf_op jit(solution)/shard_map/ppermute | solution.py:294
  46.5 2.9 %collective-permute-start.4 = (bf16[2,512,128]{2,1,0:T(8,128)(2,1)S(1)}, bf16[2,512,128]{2,1,0:T(8,128)(2,1)}, u32[]{:S(2)}, u32[]{:S(2)}) collective-permute-start(bf16[2,512,128]{2,1,0:T(8,128)(2,1)S(1)} %get-tuple-element.166), channel_id=1, source_target_pairs={{0,2},{2,4},{4,6},{6,8},{8,10},{10,12},{12,14},{14,16},{16,18},{18... | collective-permute-start | bytes 786440 | tf_op jit(solution)/shard_map/ppermute | solution.py:294
  49.4 0.9 broadcast_select_fusion.4
  50.3 1.5 collective-permute-start.7
  51.8 7.1 %attention.5 = (bf16[512,2048]{1,0:T(8,128)(2,1)}, bf16[2,512,128]{2,1,0:T(8,128)(2,1)}, bf16[2,512,128]{2,1,0:T(8,128)(2,1)}, bf16[2,512,256]{2,1,0:T(8,128)(2,1)}) custom-call(s32[1]{0:T(128)} %bitcast.7.group_ref, s32[1,512]{1,0:T(1,128)} %bitcast.28, bf16[4,1024,128]{2,1,0:T(8,128)(2,1)} %get-tuple-element.89.q_ref, ...), custom_call_target="tpu_custom_call" | custom-call | tf_op jit(solution)/shard_map/attention/pallas_call | solution.py:179
  59.0 0.9 select_select_fusion.3.past_ref
  59.9 7.1 %attention.6 = (bf16[512,2048]{1,0:T(8,128)(2,1)}, bf16[2,512,128]{2,1,0:T(8,128)(2,1)}, bf16[2,512,128]{2,1,0:T(8,128)(2,1)}, bf16[2,512,256]{2,1,0:T(8,128)(2,1)}) custom-call(s32[1]{0:T(128)} %constant.91.clone.1.group_ref, s32[1,512]{1,0:T(1,128)} %bitcast.29, bf16[2,1024,128]{2,1,0:T(8,128)(2,1)} %get-tuple-element.101.q_ref, ...), custom_call_target="tpu_custom_call", output_to_operand_aliasing={{0}: (9, {})} | custom-call | tf_op jit(solution)/shard_map/attention/pallas_call | solution.py:179
  67.0 1.7 %broadcast_select_fusion.13 = (bf16[2,512,128]{2,1,0:T(8,128)(2,1)}, bf16[2,512,128]{2,1,0:T(8,128)(2,1)S(1)}) fusion(bf16[2,512,128]{2,1,0:T(8,128)(2,1)} %collective-permute-done.4, pred[]{:T(512)S(6)} %eq.29, bf16[2,512,128]{2,1,0:T(8,128)(2,1)S(1)} %get-tuple-element.166, bf16[2,512,128]{2,1,0:T(8,128)(2,1)S(1)} %collective-permute-done.5, pred[]{:T(512)S(6)} %eq.60, ...), kind=kLoop, calls=%fused_computation.29 | loop fusion | flops 393216 | bytes 1310723 | tf_op jit(solution)/shard_map/jit(_where)/select_n | solution.py:386
  69.5 7.2 %attention.7 = (bf16[512,2048]{1,0:T(8,128)(2,1)}, bf16[2,512,128]{2,1,0:T(8,128)(2,1)}, bf16[2,512,128]{2,1,0:T(8,128)(2,1)}, bf16[2,512,256]{2,1,0:T(8,128)(2,1)}) custom-call(s32[1]{0:T(128)} %bitcast.group_ref, s32[1,512]{1,0:T(1,128)} %bitcast.30, bf16[4,1024,128]{2,1,0:T(8,128)(2,1)} %get-tuple-element.89.q_ref, ...), custom_call_target="tpu_custom_call", output_to_operand_aliasing={{0}: (9, {})} | custom-call | tf_op jit(solution)/shard_map/attention/pallas_call | solution.py:179
  76.7 1.1 collective-permute-start.18
  78.2 5.6 %collective-permute-start.16 = (bf16[2,512,256]{2,1,0:T(8,128)(2,1)S(1)}, bf16[2,512,256]{2,1,0:T(8,128)(2,1)S(1)}, u32[]{:S(2)}, u32[]{:S(2)}) collective-permute-start(bf16[2,512,256]{2,1,0:T(8,128)(2,1)S(1)} %copy-done.6), channel_id=1, source_target_pairs={{0,2},{2,4},{4,6},{6,8},{8,10},{10,12},{12,14},{14,16},{16,18},{18... | collective-permute-start | bytes 1572872 | tf_op jit(solution)/shard_map/ppermute | solution.py:294
  83.8 2.1 %collective-permute-start.15 = (bf16[2,512,256]{2,1,0:T(8,128)(2,1)S(1)}, bf16[2,512,256]{2,1,0:T(8,128)(2,1)S(1)}, u32[]{:S(2)}, u32[]{:S(2)}) collective-permute-start(bf16[2,512,256]{2,1,0:T(8,128)(2,1)S(1)} %copy-done.6), channel_id=1, source_target_pairs={{2,0},{4,2},{6,4},{8,6},{10,8},{12,10},{14,12},{16,14},{18,16},{20... | collective-permute-start | bytes 1572872 | tf_op jit(solution)/shard_map/ppermute | solution.py:294
  85.9 4.4 %attention.8 = (bf16[512,2048]{1,0:T(8,128)(2,1)}, bf16[1,512,128]{2,1,0:T(8,128)(2,1)}, bf16[1,512,128]{2,1,0:T(8,128)(2,1)}, bf16[2,512,128]{2,1,0:T(8,128)(2,1)}) custom-call(s32[1]{0:T(128)} %bitcast.7.group_ref, s32[1,512]{1,0:T(1,128)} %bitcast.31, bf16[2,1024,128]{2,1,0:T(8,128)(2,1)} %get-tuple-element.77.q_ref, ...), custom_call_target="tpu_custom_call", output_to_operand_aliasing={{0}: (9, {})} | custom-call | tf_op jit(solution)/shard_map/attention/pallas_call | solution.py:179
  90.4 4.1 %collective-permute-done.6.past_ref = bf16[2,512,128]{2,1,0:T(8,128)(2,1)S(1)} collective-permute-done((bf16[2,512,128]{2,1,0:T(8,128)(2,1)S(1)}, bf16[2,512,128]{2,1,0:T(8,128)(2,1)S(1)}, u32[]{:S(2)}, u32[]{:S(2)}) %collective-permute-start.6) | collective-permute-done | bytes 262176 | tf_op jit(solution)/shard_map/ppermute | solution.py:290
  95.2 4.5 %attention.9 = (bf16[512,2048]{1,0:T(8,128)(2,1)}, bf16[1,512,128]{2,1,0:T(8,128)(2,1)}, bf16[1,512,128]{2,1,0:T(8,128)(2,1)}, bf16[2,512,128]{2,1,0:T(8,128)(2,1)}) custom-call(s32[1]{0:T(128)} %bitcast.group_ref, s32[1,512]{1,0:T(1,128)} %bitcast.32, bf16[2,1024,128]{2,1,0:T(8,128)(2,1)} %get-tuple-element.77.q_ref, ...), custom_call_target="tpu_custom_call", output_to_operand_aliasing={{0}: (9, {})} | custom-call | tf_op jit(solution)/shard_map/attention/pallas_call | solution.py:179
  100.1 5.3 %collective-permute-start.19 = (bf16[2,512,256]{2,1,0:T(8,128)(2,1)S(1)}, bf16[2,512,256]{2,1,0:T(8,128)(2,1)S(1)}, u32[]{:S(2)}, u32[]{:S(2)}) collective-permute-start(bf16[2,512,256]{2,1,0:T(8,128)(2,1)S(1)} %get-tuple-element.143), channel_id=1, source_target_pairs={{2,0},{4,2},{6,4},{8,6},{10,8},{12,10},{14,12},{16,14},{18,16},{20... | collective-permute-start | bytes 1572872 | tf_op jit(solution)/shard_map/ppermute | solution.py:294
  105.4 4.0 %collective-permute-start.20 = (bf16[2,512,256]{2,1,0:T(8,128)(2,1)S(1)}, bf16[2,512,256]{2,1,0:T(8,128)(2,1)S(1)}, u32[]{:S(2)}, u32[]{:S(2)}) collective-permute-start(bf16[2,512,256]{2,1,0:T(8,128)(2,1)S(1)} %get-tuple-element.144), channel_id=1, source_target_pairs={{0,2},{2,4},{4,6},{6,8},{8,10},{10,12},{12,14},{14,16},{16,18},{18... | collective-permute-start | bytes 1572872 | tf_op jit(solution)/shard_map/ppermute | solution.py:294
  109.5 1.8 %collective-permute-start.17 = (bf16[2,512,256]{2,1,0:T(8,128)(2,1)S(1)}, bf16[2,512,256]{2,1,0:T(8,128)(2,1)S(1)}, u32[]{:S(2)}, u32[]{:S(2)}) collective-permute-start(bf16[2,512,256]{2,1,0:T(8,128)(2,1)S(1)} %select_select_fusion), channel_id=1, source_target_pairs={{0,1},{1,0},{2,3},{3,2},{4,5},{5,4},{6,7},{7,6},{8,9},{9,8},{10,11... | collective-permute-start | bytes 1572872 | tf_op jit(solution)/shard_map/ppermute | solution.py:290
  111.3 1.9 %collective-permute-start.12 = (bf16[2,512,128]{2,1,0:T(8,128)(2,1)S(1)}, bf16[2,512,128]{2,1,0:T(8,128)(2,1)S(1)}, u32[]{:S(2)}, u32[]{:S(2)}) collective-permute-start(bf16[2,512,128]{2,1,0:T(8,128)(2,1)S(1)} %get-tuple-element.163), channel_id=1, source_target_pairs={{2,0},{4,2},{6,4},{8,6},{10,8},{12,10},{14,12},{16,14},{18,16},{20... | collective-permute-start | bytes 786440 | tf_op jit(solution)/shard_map/ppermute | solution.py:294
  113.3 4.6 %collective-permute-start.13 = (bf16[2,512,128]{2,1,0:T(8,128)(2,1)S(1)}, bf16[2,512,128]{2,1,0:T(8,128)(2,1)S(1)}, u32[]{:S(2)}, u32[]{:S(2)}) collective-permute-start(bf16[2,512,128]{2,1,0:T(8,128)(2,1)S(1)} %get-tuple-element.164), channel_id=1, source_target_pairs={{0,2},{2,4},{4,6},{6,8},{8,10},{10,12},{12,14},{14,16},{16,18},{18... | collective-permute-start | bytes 786440 | tf_op jit(solution)/shard_map/ppermute | solution.py:294
  117.9 5.2 %collective-permute-done.19 = bf16[2,512,256]{2,1,0:T(8,128)(2,1)S(1)} collective-permute-done((bf16[2,512,256]{2,1,0:T(8,128)(2,1)S(1)}, bf16[2,512,256]{2,1,0:T(8,128)(2,1)S(1)}, u32[]{:S(2)}, u32[]{:S(2)}) %collective-permute-start.19) | collective-permute-done | bytes 524320 | tf_op jit(solution)/shard_map/ppermute | solution.py:294
  123.2 0.9 broadcast_select_fusion
  124.1 1.6 %collective-permute-start.21 = (bf16[2,512,256]{2,1,0:T(8,128)(2,1)S(1)}, bf16[2,512,256]{2,1,0:T(8,128)(2,1)S(1)}, u32[]{:S(2)}, u32[]{:S(2)}) collective-permute-start(bf16[2,512,256]{2,1,0:T(8,128)(2,1)S(1)} %get-tuple-element.140), channel_id=1, source_target_pairs={{0,1},{1,0},{2,3},{3,2},{4,5},{5,4},{6,7},{7,6},{8,9},{9,8},{10,11... | collective-permute-start | bytes 1572872 | tf_op jit(solution)/shard_map/ppermute | solution.py:290
  126.8 1.6 %collective-permute-start.14 = (bf16[2,512,128]{2,1,0:T(8,128)(2,1)S(1)}, bf16[2,512,128]{2,1,0:T(8,128)(2,1)S(1)}, u32[]{:S(2)}, u32[]{:S(2)}) collective-permute-start(bf16[2,512,128]{2,1,0:T(8,128)(2,1)S(1)} %get-tuple-element.160), channel_id=1, source_target_pairs={{0,1},{1,0},{2,3},{3,2},{4,5},{5,4},{6,7},{7,6},{8,9},{9,8},{10,11... | collective-permute-start | bytes 786440 | tf_op jit(solution)/shard_map/ppermute | solution.py:290
  128.3 0.9 select_select_fusion.1.back_ref
  129.2 2.0 %finish.5 = (bf16[512,1024]{1,0:T(8,128)(2,1)}, bf16[512,1024]{1,0:T(8,128)(2,1)}) custom-call(s32[1]{0:T(128)} %bitcast.7.group_ref, bf16[2,512,128]{2,1,0:T(8,128)(2,1)} %get-tuple-element.127.dk_ref, bf16[2,512,128]{2,1,0:T(8,128)(2,1)} %get-tuple-element.128.dv_ref, bf16[2,512,256]{2,1,0:T(8,128)(2,1)} %get-tuple-element.139.back_ref), custom_call_target="tpu_custom_call" | custom-call | tf_op jit(solution)/shard_map/finish/pallas_call | solution.py:233
  131.2 6.3 %collective-permute-done.21.back_ref = bf16[2,512,256]{2,1,0:T(8,128)(2,1)S(1)} collective-permute-done((bf16[2,512,256]{2,1,0:T(8,128)(2,1)S(1)}, bf16[2,512,256]{2,1,0:T(8,128)(2,1)S(1)}, u32[]{:S(2)}, u32[]{:S(2)}) %collective-permute-start.21) | collective-permute-done | bytes 524320 | tf_op jit(solution)/shard_map/ppermute | solution.py:290
  137.5 0.8 copy-done.7
  138.3 2.0 %finish.6 = (bf16[512,1024]{1,0:T(8,128)(2,1)}, bf16[512,1024]{1,0:T(8,128)(2,1)}) custom-call(s32[1]{0:T(128)} %bitcast.group_ref, bf16[2,512,128]{2,1,0:T(8,128)(2,1)} %get-tuple-element.123.dk_ref, bf16[2,512,128]{2,1,0:T(8,128)(2,1)} %get-tuple-element.124.dv_ref, bf16[2,512,256]{2,1,0:T(8,128)(2,1)} %copy-done.7, ...), custom_call_target="tpu_custom_call", output_to_operand_aliasing={{0}: (4, {}), {1}: (5, {})} | custom-call | tf_op jit(solution)/shard_map/finish/pallas_call | solution.py:233
  140.3 2.0 %finish.7 = (bf16[512,1024]{1,0:T(8,128)(2,1)}, bf16[512,1024]{1,0:T(8,128)(2,1)}) custom-call(s32[1]{0:T(128)} %constant.91.clone.1.group_ref, bf16[2,512,128]{2,1,0:T(8,128)(2,1)} %get-tuple-element.120.dk_ref, bf16[2,512,128]{2,1,0:T(8,128)(2,1)} %get-tuple-element.121.dv_ref, ...), custom_call_target="tpu_custom_call", output_to_operand_aliasing={{0}: (4, {}), {1}: (5, {})} | custom-call | tf_op jit(solution)/shard_map/finish/pallas_call | solution.py:233
  142.3 1.8 %finish.8 = (bf16[512,1024]{1,0:T(8,128)(2,1)}, bf16[512,1024]{1,0:T(8,128)(2,1)}) custom-call(s32[1]{0:T(128)} %bitcast.7.group_ref, bf16[1,512,128]{2,1,0:T(8,128)(2,1)} %get-tuple-element.118.dk_ref, bf16[1,512,128]{2,1,0:T(8,128)(2,1)} %get-tuple-element.119.dv_ref, ...), custom_call_target="tpu_custom_call", output_to_operand_aliasing={{0}: (4, {}), {1}: (5, {})} | custom-call | tf_op jit(solution)/shard_map/finish/pallas_call | solution.py:233
  144.9 1.8 %finish.9 = (bf16[512,1024]{1,0:T(8,128)(2,1)}, bf16[512,1024]{1,0:T(8,128)(2,1)}) custom-call(s32[1]{0:T(128)} %bitcast.group_ref, bf16[1,512,128]{2,1,0:T(8,128)(2,1)} %get-tuple-element.114.dk_ref, bf16[1,512,128]{2,1,0:T(8,128)(2,1)} %get-tuple-element.115.dv_ref, bf16[2,512,128]{2,1,0:T(8,128)(2,1)} %copy-done.10, ...), custom_call_target="tpu_custom_call", output_to_operand_aliasing={{0}: (4, {}), {1}: (5, {})} | custom-call | tf_op jit(solution)/shard_map/finish/pallas_call | solution.py:233
  (60 shorter events, 8.5 us)
Async XLA Ops:
  0.6 3.1 %copy-start.1 = (bf16[512,1024]{1,0:T(8,128)(2,1)S(1)}, bf16[512,1024]{1,0:T(8,128)(2,1)}, u32[]{:S(2)}) copy-start(bf16[512,1024]{1,0:T(8,128)(2,1)} %v_ref.5) | copy-start | bytes 3145732
  0.6 3.0 %copy-start = (bf16[512,1024]{1,0:T(8,128)(2,1)S(1)}, bf16[512,1024]{1,0:T(8,128)(2,1)}, u32[]{:S(2)}) copy-start(bf16[512,1024]{1,0:T(8,128)(2,1)} %k_ref.5) | copy-start | bytes 3145732
  3.7 9.6 %copy-start.11 = (s32[32]{0:T(128)S(1)}, s32[32]{0:T(128)}, u32[]{:S(2)}) copy-start(s32[32]{0:T(128)} %param.13) | copy-start | bytes 388
  4.7 35.4 %collective-permute-start.9 = (bf16[2,512,256]{2,1,0:T(8,128)(2,1)}, bf16[2,512,256]{2,1,0:T(8,128)(2,1)S(1)}, u32[]{:S(2)}, u32[]{:S(2)}) collective-permute-start(bf16[2,512,256]{2,1,0:T(8,128)(2,1)} %pad_maximum_fusion.2), channel_id=1, source_target_pairs={{2,0},{4,2},{6,4},{8,6},{10,8},{12,10},{14,12},{16,14},{18,16},{20... | collective-permute-start | bytes 1572872 | tf_op jit(solution)/shard_map/ppermute | solution.py:294
  7.3 32.8 %collective-permute-start.8 = (bf16[2,512,256]{2,1,0:T(8,128)(2,1)}, bf16[2,512,256]{2,1,0:T(8,128)(2,1)}, u32[]{:S(2)}, u32[]{:S(2)}) collective-permute-start(bf16[2,512,256]{2,1,0:T(8,128)(2,1)} %pad_maximum_fusion.2), channel_id=1, source_target_pairs={{0,2},{2,4},{4,6},{6,8},{8,10},{10,12},{12,14},{14,16},{16,18},{18... | collective-permute-start | bytes 1572872 | tf_op jit(solution)/shard_map/ppermute | solution.py:294
  10.3 14.1 %collective-permute-start.1 = (bf16[2,512,256]{2,1,0:T(8,128)(2,1)}, bf16[2,512,256]{2,1,0:T(8,128)(2,1)}, u32[]{:S(2)}, u32[]{:S(2)}) collective-permute-start(bf16[2,512,256]{2,1,0:T(8,128)(2,1)} %pad_maximum_fusion), channel_id=1, source_target_pairs={{0,1},{1,0},{2,3},{3,2},{4,5},{5,4},{6,7},{7,6},{8,9},{9,8},{10,11... | collective-permute-start | bytes 1572872 | tf_op jit(solution)/shard_map/ppermute | solution.py:290
  12.1 28.0 %collective-permute-start = (bf16[2,512,128]{2,1,0:T(8,128)(2,1)}, bf16[2,512,128]{2,1,0:T(8,128)(2,1)}, u32[]{:S(2)}, u32[]{:S(2)}) collective-permute-start(bf16[2,512,128]{2,1,0:T(8,128)(2,1)} %pad_maximum_fusion.3), channel_id=1, source_target_pairs={{0,1},{1,0},{2,3},{3,2},{4,5},{5,4},{6,7},{7,6},{8,9},{9,8},{10,11... | collective-permute-start | bytes 786440 | tf_op jit(solution)/shard_map/ppermute | solution.py:290
  17.3 7.1 %copy-start.2 = (bf16[1,512,256]{2,1,0:T(8,128)(2,1)S(1)}, bf16[1,512,256]{2,1,0:T(8,128)(2,1)}, u32[]{:S(2)}) copy-start(bf16[1,512,256]{2,1,0:T(8,128)(2,1)} %get-tuple-element.180) | copy-start | bytes 786436
  25.6 23.8 %collective-permute-start.3 = (bf16[2,512,256]{2,1,0:T(8,128)(2,1)S(1)}, bf16[2,512,256]{2,1,0:T(8,128)(2,1)S(1)}, u32[]{:S(2)}, u32[]{:S(2)}) collective-permute-start(bf16[2,512,256]{2,1,0:T(8,128)(2,1)S(1)} %get-tuple-element.153), channel_id=1, source_target_pairs={{2,0},{4,2},{6,4},{8,6},{10,8},{12,10},{14,12},{16,14},{18,16},{20... | collective-permute-start | bytes 1572872 | tf_op jit(solution)/shard_map/ppermute | solution.py:294
  28.3 21.1 %collective-permute-start.2 = (bf16[2,512,256]{2,1,0:T(8,128)(2,1)S(1)}, bf16[2,512,256]{2,1,0:T(8,128)(2,1)S(1)}, u32[]{:S(2)}, u32[]{:S(2)}) collective-permute-start(bf16[2,512,256]{2,1,0:T(8,128)(2,1)S(1)} %get-tuple-element.154), channel_id=1, source_target_pairs={{0,2},{2,4},{4,6},{6,8},{8,10},{10,12},{12,14},{14,16},{16,18},{18... | collective-permute-start | bytes 1572872 | tf_op jit(solution)/shard_map/ppermute | solution.py:294
  37.4 4.7 %copy-start.4 = (bf16[1,512,128]{2,1,0:T(8,128)(2,1)S(1)}, bf16[1,512,128]{2,1,0:T(8,128)(2,1)}, u32[]{:S(2)}) copy-start(bf16[1,512,128]{2,1,0:T(8,128)(2,1)} %get-tuple-element.182) | copy-start | bytes 393220
  42.1 16.9 %collective-permute-start.10 = (bf16[2,512,256]{2,1,0:T(8,128)(2,1)}, bf16[2,512,256]{2,1,0:T(8,128)(2,1)S(1)}, u32[]{:S(2)}, u32[]{:S(2)}) collective-permute-start(bf16[2,512,256]{2,1,0:T(8,128)(2,1)} %select_select_fusion.2), channel_id=1, source_target_pairs={{0,1},{1,0},{2,3},{3,2},{4,5},{5,4},{6,7},{7,6},{8,9},{9,8},{10,11... | collective-permute-start | bytes 1572872 | tf_op jit(solution)/shard_map/ppermute | solution.py:290
  43.8 15.1 %collective-permute-start.5 = (bf16[2,512,128]{2,1,0:T(8,128)(2,1)}, bf16[2,512,128]{2,1,0:T(8,128)(2,1)S(1)}, u32[]{:S(2)}, u32[]{:S(2)}) collective-permute-start(bf16[2,512,128]{2,1,0:T(8,128)(2,1)} %get-tuple-element.165), channel_id=1, source_target_pairs={{2,0},{4,2},{6,4},{8,6},{10,8},{12,10},{14,12},{16,14},{18,16},{20... | collective-permute-start | bytes 786440 | tf_op jit(solution)/shard_map/ppermute | solution.py:294
  46.5 12.4 %collective-permute-start.4 = (bf16[2,512,128]{2,1,0:T(8,128)(2,1)S(1)}, bf16[2,512,128]{2,1,0:T(8,128)(2,1)}, u32[]{:S(2)}, u32[]{:S(2)}) collective-permute-start(bf16[2,512,128]{2,1,0:T(8,128)(2,1)S(1)} %get-tuple-element.166), channel_id=1, source_target_pairs={{0,2},{2,4},{4,6},{6,8},{8,10},{10,12},{12,14},{14,16},{16,18},{18... | collective-permute-start | bytes 786440 | tf_op jit(solution)/shard_map/ppermute | solution.py:294
  50.3 18.4 %collective-permute-start.7 = (bf16[2,512,256]{2,1,0:T(8,128)(2,1)S(1)}, bf16[2,512,256]{2,1,0:T(8,128)(2,1)S(1)}, u32[]{:S(2)}, u32[]{:S(2)}) collective-permute-start(bf16[2,512,256]{2,1,0:T(8,128)(2,1)S(1)} %get-tuple-element.141), channel_id=1, source_target_pairs={{0,1},{1,0},{2,3},{3,2},{4,5},{5,4},{6,7},{7,6},{8,9},{9,8},{10,11... | collective-permute-start | bytes 1572872 | tf_op jit(solution)/shard_map/ppermute | solution.py:290
  68.7 0.8 copy-start.3
  69.5 8.7 %copy-start.6 = (bf16[2,512,256]{2,1,0:T(8,128)(2,1)S(1)}, bf16[2,512,256]{2,1,0:T(8,128)(2,1)}, u32[]{:S(2)}) copy-start(bf16[2,512,256]{2,1,0:T(8,128)(2,1)} %get-tuple-element.122) | copy-start | bytes 1572868
  76.7 23.3 %collective-permute-start.18 = (bf16[2,512,256]{2,1,0:T(8,128)(2,1)}, bf16[2,512,256]{2,1,0:T(8,128)(2,1)S(1)}, u32[]{:S(2)}, u32[]{:S(2)}) collective-permute-start(bf16[2,512,256]{2,1,0:T(8,128)(2,1)} %get-tuple-element.126), channel_id=1, source_target_pairs={{0,1},{1,0},{2,3},{3,2},{4,5},{5,4},{6,7},{7,6},{8,9},{9,8},{10,11... | collective-permute-start | bytes 1572872 | tf_op jit(solution)/shard_map/ppermute | solution.py:290
  77.8 16.7 %collective-permute-start.6 = (bf16[2,512,128]{2,1,0:T(8,128)(2,1)S(1)}, bf16[2,512,128]{2,1,0:T(8,128)(2,1)S(1)}, u32[]{:S(2)}, u32[]{:S(2)}) collective-permute-start(bf16[2,512,128]{2,1,0:T(8,128)(2,1)S(1)} %get-tuple-element.162), channel_id=1, source_target_pairs={{0,1},{1,0},{2,3},{3,2},{4,5},{5,4},{6,7},{7,6},{8,9},{9,8},{10,11... | collective-permute-start | bytes 786440 | tf_op jit(solution)/shard_map/ppermute | solution.py:290
  78.2 31.2 %collective-permute-start.16 = (bf16[2,512,256]{2,1,0:T(8,128)(2,1)S(1)}, bf16[2,512,256]{2,1,0:T(8,128)(2,1)S(1)}, u32[]{:S(2)}, u32[]{:S(2)}) collective-permute-start(bf16[2,512,256]{2,1,0:T(8,128)(2,1)S(1)} %copy-done.6), channel_id=1, source_target_pairs={{0,2},{2,4},{4,6},{6,8},{8,10},{10,12},{12,14},{14,16},{16,18},{18... | collective-permute-start | bytes 1572872 | tf_op jit(solution)/shard_map/ppermute | solution.py:294
  83.8 25.6 %collective-permute-start.15 = (bf16[2,512,256]{2,1,0:T(8,128)(2,1)S(1)}, bf16[2,512,256]{2,1,0:T(8,128)(2,1)S(1)}, u32[]{:S(2)}, u32[]{:S(2)}) collective-permute-start(bf16[2,512,256]{2,1,0:T(8,128)(2,1)S(1)} %copy-done.6), channel_id=1, source_target_pairs={{2,0},{4,2},{6,4},{8,6},{10,8},{12,10},{14,12},{16,14},{18,16},{20... | collective-permute-start | bytes 1572872 | tf_op jit(solution)/shard_map/ppermute | solution.py:294
  94.4 0.7 copy-start.8
  95.2 4.8 %copy-start.5 = (bf16[2,512,256]{2,1,0:T(8,128)(2,1)S(1)}, bf16[2,512,256]{2,1,0:T(8,128)(2,1)}, u32[]{:S(2)}) copy-start(bf16[2,512,256]{2,1,0:T(8,128)(2,1)} %get-tuple-element.125) | copy-start | bytes 1572868
  99.7 11.6 %collective-permute-start.11 = (bf16[2,512,128]{2,1,0:T(8,128)(2,1)}, bf16[2,512,128]{2,1,0:T(8,128)(2,1)S(1)}, u32[]{:S(2)}, u32[]{:S(2)}) collective-permute-start(bf16[2,512,128]{2,1,0:T(8,128)(2,1)} %get-tuple-element.117), channel_id=1, source_target_pairs={{0,1},{1,0},{2,3},{3,2},{4,5},{5,4},{6,7},{7,6},{8,9},{9,8},{10,11... | collective-permute-start | bytes 786440 | tf_op jit(solution)/shard_map/ppermute | solution.py:290
  100.0 11.3 %copy-start.9 = (bf16[2,512,128]{2,1,0:T(8,128)(2,1)S(1)}, bf16[2,512,128]{2,1,0:T(8,128)(2,1)}, u32[]{:S(2)}) copy-start(bf16[2,512,128]{2,1,0:T(8,128)(2,1)} %get-tuple-element.116) | copy-start | bytes 786436
  100.1 23.0 %collective-permute-start.19 = (bf16[2,512,256]{2,1,0:T(8,128)(2,1)S(1)}, bf16[2,512,256]{2,1,0:T(8,128)(2,1)S(1)}, u32[]{:S(2)}, u32[]{:S(2)}) collective-permute-start(bf16[2,512,256]{2,1,0:T(8,128)(2,1)S(1)} %get-tuple-element.143), channel_id=1, source_target_pairs={{2,0},{4,2},{6,4},{8,6},{10,8},{12,10},{14,12},{16,14},{18,16},{20... | collective-permute-start | bytes 1572872 | tf_op jit(solution)/shard_map/ppermute | solution.py:294
  105.4 17.8 %collective-permute-start.20 = (bf16[2,512,256]{2,1,0:T(8,128)(2,1)S(1)}, bf16[2,512,256]{2,1,0:T(8,128)(2,1)S(1)}, u32[]{:S(2)}, u32[]{:S(2)}) collective-permute-start(bf16[2,512,256]{2,1,0:T(8,128)(2,1)S(1)} %get-tuple-element.144), channel_id=1, source_target_pairs={{0,2},{2,4},{4,6},{6,8},{8,10},{10,12},{12,14},{14,16},{16,18},{18... | collective-permute-start | bytes 1572872 | tf_op jit(solution)/shard_map/ppermute | solution.py:294
  109.5 18.8 %collective-permute-start.17 = (bf16[2,512,256]{2,1,0:T(8,128)(2,1)S(1)}, bf16[2,512,256]{2,1,0:T(8,128)(2,1)S(1)}, u32[]{:S(2)}, u32[]{:S(2)}) collective-permute-start(bf16[2,512,256]{2,1,0:T(8,128)(2,1)S(1)} %select_select_fusion), channel_id=1, source_target_pairs={{0,1},{1,0},{2,3},{3,2},{4,5},{5,4},{6,7},{7,6},{8,9},{9,8},{10,11... | collective-permute-start | bytes 1572872 | tf_op jit(solution)/shard_map/ppermute | solution.py:290
  111.3 14.5 %collective-permute-start.12 = (bf16[2,512,128]{2,1,0:T(8,128)(2,1)S(1)}, bf16[2,512,128]{2,1,0:T(8,128)(2,1)S(1)}, u32[]{:S(2)}, u32[]{:S(2)}) collective-permute-start(bf16[2,512,128]{2,1,0:T(8,128)(2,1)S(1)} %get-tuple-element.163), channel_id=1, source_target_pairs={{2,0},{4,2},{6,4},{8,6},{10,8},{12,10},{14,12},{16,14},{18,16},{20... | collective-permute-start | bytes 786440 | tf_op jit(solution)/shard_map/ppermute | solution.py:294
  113.3 12.7 %collective-permute-start.13 = (bf16[2,512,128]{2,1,0:T(8,128)(2,1)S(1)}, bf16[2,512,128]{2,1,0:T(8,128)(2,1)S(1)}, u32[]{:S(2)}, u32[]{:S(2)}) collective-permute-start(bf16[2,512,128]{2,1,0:T(8,128)(2,1)S(1)} %get-tuple-element.164), channel_id=1, source_target_pairs={{0,2},{2,4},{4,6},{6,8},{8,10},{10,12},{12,14},{14,16},{16,18},{18... | collective-permute-start | bytes 786440 | tf_op jit(solution)/shard_map/ppermute | solution.py:294
  124.1 13.4 %collective-permute-start.21 = (bf16[2,512,256]{2,1,0:T(8,128)(2,1)S(1)}, bf16[2,512,256]{2,1,0:T(8,128)(2,1)S(1)}, u32[]{:S(2)}, u32[]{:S(2)}) collective-permute-start(bf16[2,512,256]{2,1,0:T(8,128)(2,1)S(1)} %get-tuple-element.140), channel_id=1, source_target_pairs={{0,1},{1,0},{2,3},{3,2},{4,5},{5,4},{6,7},{7,6},{8,9},{9,8},{10,11... | collective-permute-start | bytes 1572872 | tf_op jit(solution)/shard_map/ppermute | solution.py:290
  126.8 17.4 %collective-permute-start.14 = (bf16[2,512,128]{2,1,0:T(8,128)(2,1)S(1)}, bf16[2,512,128]{2,1,0:T(8,128)(2,1)S(1)}, u32[]{:S(2)}, u32[]{:S(2)}) collective-permute-start(bf16[2,512,128]{2,1,0:T(8,128)(2,1)S(1)} %get-tuple-element.160), channel_id=1, source_target_pairs={{0,1},{1,0},{2,3},{3,2},{4,5},{5,4},{6,7},{7,6},{8,9},{9,8},{10,11... | collective-permute-start | bytes 786440 | tf_op jit(solution)/shard_map/ppermute | solution.py:290
  137.5 0.8 copy-start.7
  144.1 0.7 copy-start.10

commit v8 on v4

--- a/solution.py
+++ b/solution.py
@@ -60,29 +60,34 @@
         slopes[tile] = dot(v_all[keys], grads, 1, 1)
         return queries, grads
 
-    def weigh(tile, grads):
+    def bounds(tile, grads):
         start = tile * TILE
         product = grads.astype(jnp.float32) * stacked(o_ref, start).astype(jnp.float32)
         delta = jnp.sum(product.T, axis=0, keepdims=True)
-        low = jnp.concatenate([low_ref[:, start : start + TILE]] * members, axis=1) - start
-
-        def visible(strip):
-            index = strip.start + lax.broadcasted_iota(jnp.int32, (STRIP, lanes), 0)
-            seen = index >= low
-            return seen & (index <= window + lane) if strip.stop > window else seen
-
+        return delta, jnp.concatenate([low_ref[:, start : start + TILE]] * members, axis=1) - start
+
+    def visible(strip, low):
+        index = strip.start + lax.broadcasted_iota(jnp.int32, (STRIP, lanes), 0)
+        seen = index >= low
+        return seen & (index <= window + lane) if strip.stop > window else seen
+
+    def find_top(tile, low):
         top = jnp.full((8, lanes), NEGATIVE, jnp.float32)
         for strip in strips(span):
-            masked = jnp.where(visible(strip), scores[tile, strip], NEGATIVE)
+            masked = jnp.where(visible(strip, low), scores[tile, strip], NEGATIVE)
             top = jnp.maximum(top, folded(masked, jnp.max))
-        top = jnp.max(top, axis=0, keepdims=True)
+        return jnp.max(top, axis=0, keepdims=True)
+
+    def find_terms(tile, low, top):
         total = jnp.zeros((8, lanes), jnp.float32)
         for strip in strips(span):
             terms = jnp.exp2((scores[tile, strip] - top) * (scale * LOG2_E))
-            terms = jnp.where(visible(strip), terms, 0.0)
+            terms = jnp.where(visible(strip, low), terms, 0.0)
             total = total + folded(terms, jnp.sum)
             scores[tile, strip] = terms
-        inverse = 1.0 / jnp.sum(total, axis=0, keepdims=True)
+        return 1.0 / jnp.sum(total, axis=0, keepdims=True)
+
+    def weigh(tile, inverse, delta):
         for strip in strips(span):
             weights = scores[tile, strip] * inverse
             weights_b[tile, strip] = weights.astype(jnp.bfloat16)
@@ -99,11 +104,13 @@
                 m * TILE : (m + 1) * TILE
             ].astype(dq_ref.dtype)
 
-    entered = {0: enter(0)}
+    entered = [enter(tile) for tile in tiles]
+    limits = [bounds(tile, entered[tile][1]) for tile in tiles]
+    tops = [find_top(tile, limits[tile][1]) for tile in tiles]
+    inverses = [find_terms(tile, limits[tile][1], tops[tile]) for tile in tiles]
     for tile in tiles:
-        if tile + 1 in tiles:
-            entered[tile + 1] = enter(tile + 1)
-        weigh(tile, entered[tile][1])
+        weigh(tile, inverses[tile], limits[tile][0])
+    for tile in tiles:
         leave(tile, *entered[tile])
     back_ref[0] = dk_sum[:window].astype(back_ref.dtype)
     back_ref[1] = dv_sum[:window].astype(back_ref.dtype)

time: 126 us -> 126 us (level)
  no operation moved by 1% of the time
where the time goes in v8:
time: 126 us; the launch traced here: 125 us
  Pallas kernels  38.3 us (30%)
  waiting for transfers between devices  36.5 us (29%)
  starting transfers between devices  33.2 us (26%)
  other arithmetic  9.77 us (8%)
  local copies, waits for them, and re-layouts  3.96 us (3%)
  between operations  3.48 us (3%)
    pallas_call x4, Pallas kernels, attention(): pl.pallas_call(functools.partial(attention_body, len(carried)), grid_spec...  29.9 us
    ppermute x8, starting transfers between devices, shifted(): lax.ppermute(value, 'blk', [(source, source + step) for source in range(f...  28.6 us
    ppermute x8, waiting for transfers between devices, shifted(): lax.ppermute(value, 'blk', [(source, source + step) for source in range(f...  18.7 us
    ppermute x8, waiting for transfers between devices, turned(): return lax.ppermute(value, 'head', pairs)  17.8 us
    pallas_call x4, Pallas kernels, finish(): pl.pallas_call(functools.partial(finish_body, len(carried)), grid_spec=pl...  8.44 us
    ppermute x8, starting transfers between devices, turned(): return lax.ppermute(value, 'head', pairs)  4.66 us
    select_n x4, other arithmetic, pick(): result = jnp.where(index == place, items[place], result)  3.47 us
    unnamed x16, local copies, waits for them, and re-layouts  3.21 us
  transfers between devices with their start and end apart: 16, of which 8 were waited for; matrix products, arithmetic and copies ran while one was open for 7% of the time, Pallas kernels for 29%

profile of v8, /device:TPU:11, one launch (start us, length us, event | category | flops | bytes accessed | tf_op | source)
XLA Modules:
  0.0 125.3 jit_solution(10659387963985417502)
XLA Ops:
  0.6 1.7 %select_bitcast_fusion.2 = (bf16[1,512,256]{2,1,0:T(8,128)(2,1)S(1)}, bf16[1,512,256]{2,1,0:T(8,128)(2,1)S(1)}, bf16[1,512,256]{2,1,0:T(8,128)(2,1)S(1)}, bf16[1...) fusion(pred[]{:T(512)S(6)} %eq.22, ...), kind=kLoop, calls=%fused_computation.27 | loop fusion | flops 1048576 | bytes 4194306 | tf_op jit(solution)/shard_map/stack | solution.py:248
  2.4 0.1 pad_maximum_fusion.1
  2.4 0.3 collective-permute-start
  2.8 1.3 %collective-permute-start.3 = (bf16[2,512,256]{2,1,0:T(8,128)(2,1)S(1)}, bf16[2,512,256]{2,1,0:T(8,128)(2,1)S(1)}, u32[]{:S(2)}, u32[]{:S(2)}) collective-permute-start(bf16[2,512,256]{2,1,0:T(8,128)(2,1)S(1)} %pad_maximum_fusion.3), channel_id=1, source_target_pairs={{0,1},{1,0},{2,3},{3,2},{4,5},{5,4},{6,7},{7,6},{8,9},{9,8},{10,11... | collective-permute-start | bytes 1572872 | tf_op jit(solution)/shard_map/ppermute | solution.py:234
  4.1 0.1 dynamic_slice.6
  4.1 0.6 fusion
  6.0 9.2 %collective-permute-done = bf16[2,512,256]{2,1,0:T(8,128)(2,1)S(1)} collective-permute-done((bf16[2,512,256]{2,1,0:T(8,128)(2,1)S(1)}, bf16[2,512,256]{2,1,0:T(8,128)(2,1)S(1)}, u32[]{:S(2)}, u32[]{:S(2)}) %collective-permute-start) | collective-permute-done | bytes 524320 | tf_op jit(solution)/shard_map/ppermute | solution.py:234
  15.3 0.9 broadcast_select_fusion.7
  16.1 4.6 %collective-permute-start.2 = (bf16[2,512,256]{2,1,0:T(8,128)(2,1)}, bf16[2,512,256]{2,1,0:T(8,128)(2,1)S(1)}, u32[]{:S(2)}, u32[]{:S(2)}) collective-permute-start(bf16[2,512,256]{2,1,0:T(8,128)(2,1)} %get-tuple-element.83), channel_id=1, source_target_pairs={{2,0},{4,2},{6,4},{8,6},{10,8},{12,10},{14,12},{16,14},{18,16},{20... | collective-permute-start | bytes 1572872 | tf_op jit(solution)/shard_map/ppermute | solution.py:238
  20.7 3.0 %collective-permute-start.1 = (bf16[2,512,256]{2,1,0:T(8,128)(2,1)S(1)}, bf16[2,512,256]{2,1,0:T(8,128)(2,1)S(1)}, u32[]{:S(2)}, u32[]{:S(2)}) collective-permute-start(bf16[2,512,256]{2,1,0:T(8,128)(2,1)S(1)} %get-tuple-element.84), channel_id=1, source_target_pairs={{0,2},{2,4},{4,6},{6,8},{8,10},{10,12},{12,14},{14,16},{16,18},{18... | collective-permute-start | bytes 1572872 | tf_op jit(solution)/shard_map/ppermute | solution.py:238
  25.1 0.1 pad_dynamic-slice_fusion
  25.2 1.3 %collective-permute-done.3 = bf16[2,512,256]{2,1,0:T(8,128)(2,1)S(1)} collective-permute-done((bf16[2,512,256]{2,1,0:T(8,128)(2,1)S(1)}, bf16[2,512,256]{2,1,0:T(8,128)(2,1)S(1)}, u32[]{:S(2)}, u32[]{:S(2)}) %collective-permute-start.3) | collective-permute-done | bytes 524320 | tf_op jit(solution)/shard_map/ppermute | solution.py:234
  26.5 0.9 broadcast_select_fusion.6
  27.4 3.4 %collective-permute-start.5 = (bf16[2,512,256]{2,1,0:T(8,128)(2,1)}, bf16[2,512,256]{2,1,0:T(8,128)(2,1)S(1)}, u32[]{:S(2)}, u32[]{:S(2)}) collective-permute-start(bf16[2,512,256]{2,1,0:T(8,128)(2,1)} %get-tuple-element.73), channel_id=1, source_target_pairs={{2,0},{4,2},{6,4},{8,6},{10,8},{12,10},{14,12},{16,14},{18,16},{20... | collective-permute-start | bytes 1572872 | tf_op jit(solution)/shard_map/ppermute | solution.py:238
  30.8 3.0 %collective-permute-start.4 = (bf16[2,512,256]{2,1,0:T(8,128)(2,1)S(1)}, bf16[2,512,256]{2,1,0:T(8,128)(2,1)S(1)}, u32[]{:S(2)}, u32[]{:S(2)}) collective-permute-start(bf16[2,512,256]{2,1,0:T(8,128)(2,1)S(1)} %get-tuple-element.74), channel_id=1, source_target_pairs={{0,2},{2,4},{4,6},{6,8},{8,10},{10,12},{12,14},{14,16},{16,18},{18... | collective-permute-start | bytes 1572872 | tf_op jit(solution)/shard_map/ppermute | solution.py:238
  33.9 0.9 convert_reduce_fusion
  34.8 4.7 %collective-permute-done.1 = bf16[2,512,256]{2,1,0:T(8,128)(2,1)S(1)} collective-permute-done((bf16[2,512,256]{2,1,0:T(8,128)(2,1)S(1)}, bf16[2,512,256]{2,1,0:T(8,128)(2,1)S(1)}, u32[]{:S(2)}, u32[]{:S(2)}) %collective-permute-start.1) | collective-permute-done | bytes 524320 | tf_op jit(solution)/shard_map/ppermute | solution.py:238
  39.5 0.9 broadcast_select_fusion.18
  40.4 0.3 collective-permute-start.7
  40.6 7.5 %attention.4 = (bf16[512,2048]{1,0:T(8,128)(2,1)}, f32[512,1024]{1,0:T(8,128)}, f32[512,1024]{1,0:T(8,128)}, bf16[2,512,256]{2,1,0:T(8,128)(2,1)}) custom-call(s32[1]{0:T(128)} %bitcast.4.group_ref, s32[1,512]{1,0:T(1,128)} %bitcast.21, bf16[512,2048]{1,0:T(8,128)(2,1)} %q_ref.7, bf16[512,1024]{1,0:T(8,128)(2,1)} %k_ref.7, bf16[512,1024]{1,0:T(8,128)(2,1)} %v_ref.7, ...), custom_call_target="tpu_custom_call" | custom-call | flops 1677721600 | bytes 2457600 | tf_op jit(solution)/shard_map/attention/pallas_call | solution.py:135
  48.1 0.9 broadcast_select_fusion.14
  49.0 1.2 collective-permute-start.6
  50.2 7.5 %attention.5 = (bf16[512,2048]{1,0:T(8,128)(2,1)}, f32[512,1024]{1,0:T(8,128)}, f32[512,1024]{1,0:T(8,128)}, bf16[2,512,256]{2,1,0:T(8,128)(2,1)}) custom-call(s32[1]{0:T(128)} %bitcast.4.group_ref, s32[1,512]{1,0:T(1,128)} %bitcast.22, bf16[512,2048]{1,0:T(8,128)(2,1)} %q_ref.7, ...), custom_call_target="tpu_custom_call", output_to_operand_aliasing={{0}: (8, {}), {1}: (9, {}), {2}: (10, {})} | custom-call | flops 1677721600 | bytes 2457600 | tf_op jit(solution)/shard_map/attention/pallas_call | solution.py:135
  57.7 0.8 copy-done
  58.5 7.5 %attention.6 = (bf16[512,2048]{1,0:T(8,128)(2,1)}, f32[512,1024]{1,0:T(8,128)}, f32[512,1024]{1,0:T(8,128)}, bf16[2,512,256]{2,1,0:T(8,128)(2,1)}) custom-call(s32[1]{0:T(128)} %bitcast.group_ref, s32[1,512]{1,0:T(1,128)} %bitcast.23, bf16[512,2048]{1,0:T(8,128)(2,1)} %q_ref.7, ...), custom_call_target="tpu_custom_call", output_to_operand_aliasing={{0}: (8, {}), {1}: (9, {}), {2}: (10, {})} | custom-call | flops 1677721600 | bytes 2457600 | tf_op jit(solution)/shard_map/attention/pallas_call | solution.py:135
  66.0 0.3 collective-permute-start.12
  66.3 0.8 copy-done.1
  67.1 7.5 %attention.7 = (bf16[512,2048]{1,0:T(8,128)(2,1)}, f32[512,1024]{1,0:T(8,128)}, f32[512,1024]{1,0:T(8,128)}, bf16[2,512,256]{2,1,0:T(8,128)(2,1)}) custom-call(s32[1]{0:T(128)} %bitcast.group_ref, s32[1,512]{1,0:T(1,128)} %bitcast.24, bf16[512,2048]{1,0:T(8,128)(2,1)} %q_ref.7, ...), custom_call_target="tpu_custom_call", output_to_operand_aliasing={{0}: (8, {}), {1}: (9, {}), {2}: (10, {})} | custom-call | flops 1677721600 | bytes 2457600 | tf_op jit(solution)/shard_map/attention/pallas_call | solution.py:135
  74.6 1.3 %collective-permute-start.8 = (bf16[2,512,256]{2,1,0:T(8,128)(2,1)}, bf16[2,512,256]{2,1,0:T(8,128)(2,1)S(1)}, u32[]{:S(2)}, u32[]{:S(2)}) collective-permute-start(bf16[2,512,256]{2,1,0:T(8,128)(2,1)} %get-tuple-element.50), channel_id=1, source_target_pairs={{0,1},{1,0},{2,3},{3,2},{4,5},{5,4},{6,7},{7,6},{8,9},{9,8},{10,11... | collective-permute-start | bytes 1572872 | tf_op jit(solution)/shard_map/ppermute | solution.py:234
  75.9 2.3 %collective-permute-done.12 = bf16[2,512,256]{2,1,0:T(8,128)(2,1)S(1)} collective-permute-done((bf16[2,512,256]{2,1,0:T(8,128)(2,1)}, bf16[2,512,256]{2,1,0:T(8,128)(2,1)S(1)}, u32[]{:S(2)}, u32[]{:S(2)}) %collective-permute-start.12) | collective-permute-done | bytes 524320 | tf_op jit(solution)/shard_map/ppermute | solution.py:234
  78.2 0.9 broadcast_select_fusion.2
  79.0 1.9 %collective-permute-start.13 = (bf16[2,512,256]{2,1,0:T(8,128)(2,1)}, bf16[2,512,256]{2,1,0:T(8,128)(2,1)S(1)}, u32[]{:S(2)}, u32[]{:S(2)}) collective-permute-start(bf16[2,512,256]{2,1,0:T(8,128)(2,1)} %get-tuple-element.69), channel_id=1, source_target_pairs={{2,0},{4,2},{6,4},{8,6},{10,8},{12,10},{14,12},{16,14},{18,16},{20... | collective-permute-start | bytes 1572872 | tf_op jit(solution)/shard_map/ppermute | solution.py:238
  81.0 6.1 %collective-permute-start.14 = (bf16[2,512,256]{2,1,0:T(8,128)(2,1)S(1)}, bf16[2,512,256]{2,1,0:T(8,128)(2,1)S(1)}, u32[]{:S(2)}, u32[]{:S(2)}) collective-permute-start(bf16[2,512,256]{2,1,0:T(8,128)(2,1)S(1)} %get-tuple-element.70), channel_id=1, source_target_pairs={{0,2},{2,4},{4,6},{6,8},{8,10},{10,12},{12,14},{14,16},{16,18},{18... | collective-permute-start | bytes 1572872 | tf_op jit(solution)/shard_map/ppermute | solution.py:238
  87.1 0.9 broadcast_select_fusion.3
  88.0 1.9 %collective-permute-start.9 = (bf16[2,512,256]{2,1,0:T(8,128)(2,1)}, bf16[2,512,256]{2,1,0:T(8,128)(2,1)S(1)}, u32[]{:S(2)}, u32[]{:S(2)}) collective-permute-start(bf16[2,512,256]{2,1,0:T(8,128)(2,1)} %get-tuple-element.71), channel_id=1, source_target_pairs={{2,0},{4,2},{6,4},{8,6},{10,8},{12,10},{14,12},{16,14},{18,16},{20... | collective-permute-start | bytes 1572872 | tf_op jit(solution)/shard_map/ppermute | solution.py:238
  89.9 4.5 %collective-permute-start.10 = (bf16[2,512,256]{2,1,0:T(8,128)(2,1)S(1)}, bf16[2,512,256]{2,1,0:T(8,128)(2,1)S(1)}, u32[]{:S(2)}, u32[]{:S(2)}) collective-permute-start(bf16[2,512,256]{2,1,0:T(8,128)(2,1)S(1)} %get-tuple-element.72), channel_id=1, source_target_pairs={{0,2},{2,4},{4,6},{6,8},{8,10},{10,12},{12,14},{14,16},{16,18},{18... | collective-permute-start | bytes 1572872 | tf_op jit(solution)/shard_map/ppermute | solution.py:238
  94.4 9.4 %collective-permute-done.13 = bf16[2,512,256]{2,1,0:T(8,128)(2,1)S(1)} collective-permute-done((bf16[2,512,256]{2,1,0:T(8,128)(2,1)}, bf16[2,512,256]{2,1,0:T(8,128)(2,1)S(1)}, u32[]{:S(2)}, u32[]{:S(2)}) %collective-permute-start.13) | collective-permute-done | bytes 524320 | tf_op jit(solution)/shard_map/ppermute | solution.py:238
  103.8 0.9 broadcast_select_fusion
  104.7 4.7 %collective-permute-done.9 = bf16[2,512,256]{2,1,0:T(8,128)(2,1)S(1)} collective-permute-done((bf16[2,512,256]{2,1,0:T(8,128)(2,1)}, bf16[2,512,256]{2,1,0:T(8,128)(2,1)S(1)}, u32[]{:S(2)}, u32[]{:S(2)}) %collective-permute-start.9) | collective-permute-done | bytes 524320 | tf_op jit(solution)/shard_map/ppermute | solution.py:238
  109.4 0.9 broadcast_select_fusion.1
  110.3 2.1 %finish.4 = (bf16[512,1024]{1,0:T(8,128)(2,1)}, bf16[512,1024]{1,0:T(8,128)(2,1)}) custom-call(s32[1]{0:T(128)} %bitcast.4.group_ref, f32[512,1024]{1,0:T(8,128)} %get-tuple-element.47.dk_ref, f32[512,1024]{1,0:T(8,128)} %get-tuple-element.48.dv_ref, bf16[2,512,256]{2,1,0:T(8,128)(2,1)} %get-tuple-element.61.back_ref), custom_call_target="tpu_custom_call" | custom-call | flops 524288 | bytes 2097152 | tf_op jit(solution)/shard_map/finish/pallas_call | solution.py:185
  112.4 4.4 %collective-permute-done.15.back_ref = bf16[2,512,256]{2,1,0:T(8,128)(2,1)S(1)} collective-permute-done((bf16[2,512,256]{2,1,0:T(8,128)(2,1)S(1)}, bf16[2,512,256]{2,1,0:T(8,128)(2,1)S(1)}, u32[]{:S(2)}, u32[]{:S(2)}) %collective-permute-start.15) | collective-permute-done | bytes 524320 | tf_op jit(solution)/shard_map/ppermute | solution.py:234
  116.8 0.8 copy-done.5
  117.6 2.1 %finish.5 = (bf16[512,1024]{1,0:T(8,128)(2,1)}, bf16[512,1024]{1,0:T(8,128)(2,1)}) custom-call(s32[1]{0:T(128)} %bitcast.group_ref, f32[512,1024]{1,0:T(8,128)} %get-tuple-element.47.dk_ref, f32[512,1024]{1,0:T(8,128)} %get-tuple-element.48.dv_ref, bf16[2,512,256]{2,1,0:T(8,128)(2,1)} %copy-done.5, ...), custom_call_target="tpu_custom_call", output_to_operand_aliasing={{0}: (4, {}), {1}: (5, {})} | custom-call | flops 524288 | bytes 2097152 | tf_op jit(solution)/shard_map/finish/pallas_call | solution.py:185
  119.7 2.1 %finish.6 = (bf16[512,1024]{1,0:T(8,128)(2,1)}, bf16[512,1024]{1,0:T(8,128)(2,1)}) custom-call(s32[1]{0:T(128)} %bitcast.4.group_ref, f32[512,1024]{1,0:T(8,128)} %get-tuple-element.47.dk_ref, f32[512,1024]{1,0:T(8,128)} %get-tuple-element.48.dv_ref, bf16[2,512,256]{2,1,0:T(8,128)(2,1)} %get-tuple-element.63.back_ref, ...), custom_call_target="tpu_custom_call", output_to_operand_aliasing={{0}: (4, {}), {1}: (5, {})} | custom-call | flops 524288 | bytes 2097152 | tf_op jit(solution)/shard_map/finish/pallas_call | solution.py:185
  121.8 0.6 collective-permute-done.11.back_ref
  122.4 0.8 copy-done.4
  123.2 2.1 %finish.7 = (bf16[512,1024]{1,0:T(8,128)(2,1)}, bf16[512,1024]{1,0:T(8,128)(2,1)}) custom-call(s32[1]{0:T(128)} %bitcast.group_ref, f32[512,1024]{1,0:T(8,128)} %get-tuple-element.47.dk_ref, f32[512,1024]{1,0:T(8,128)} %get-tuple-element.48.dv_ref, bf16[2,512,256]{2,1,0:T(8,128)(2,1)} %copy-done.4, ...), custom_call_target="tpu_custom_call", output_to_operand_aliasing={{0}: (4, {}), {1}: (5, {})} | custom-call | flops 524288 | bytes 2097152 | tf_op jit(solution)/shard_map/finish/pallas_call | solution.py:185
  (24 shorter events, 0.1 us)
Async XLA Ops:
  2.3 1.7 %copy-start.7 = (s32[32]{0:T(128)S(1)}, s32[32]{0:T(128)}, u32[]{:S(2)}) copy-start(s32[32]{0:T(128)} %param.13) | copy-start | bytes 388
  2.4 22.8 %copy-start.6 = (s32[16384]{0:T(1024)S(1)}, s32[16384]{0:T(1024)}, u32[]{:S(2)}) copy-start(s32[16384]{0:T(1024)} %param.12) | copy-start | bytes 196612
  2.4 12.9 %collective-permute-start = (bf16[2,512,256]{2,1,0:T(8,128)(2,1)S(1)}, bf16[2,512,256]{2,1,0:T(8,128)(2,1)S(1)}, u32[]{:S(2)}, u32[]{:S(2)}) collective-permute-start(bf16[2,512,256]{2,1,0:T(8,128)(2,1)S(1)} %pad_maximum_fusion.1), channel_id=1, source_target_pairs={{0,1},{1,0},{2,3},{3,2},{4,5},{5,4},{6,7},{7,6},{8,9},{9,8},{10,11... | collective-permute-start | bytes 1572872 | tf_op jit(solution)/shard_map/ppermute | solution.py:234
  2.8 23.7 %collective-permute-start.3 = (bf16[2,512,256]{2,1,0:T(8,128)(2,1)S(1)}, bf16[2,512,256]{2,1,0:T(8,128)(2,1)S(1)}, u32[]{:S(2)}, u32[]{:S(2)}) collective-permute-start(bf16[2,512,256]{2,1,0:T(8,128)(2,1)S(1)} %pad_maximum_fusion.3), channel_id=1, source_target_pairs={{0,1},{1,0},{2,3},{3,2},{4,5},{5,4},{6,7},{7,6},{8,9},{9,8},{10,11... | collective-permute-start | bytes 1572872 | tf_op jit(solution)/shard_map/ppermute | solution.py:234
  16.1 18.7 %collective-permute-start.2 = (bf16[2,512,256]{2,1,0:T(8,128)(2,1)}, bf16[2,512,256]{2,1,0:T(8,128)(2,1)S(1)}, u32[]{:S(2)}, u32[]{:S(2)}) collective-permute-start(bf16[2,512,256]{2,1,0:T(8,128)(2,1)} %get-tuple-element.83), channel_id=1, source_target_pairs={{2,0},{4,2},{6,4},{8,6},{10,8},{12,10},{14,12},{16,14},{18,16},{20... | collective-permute-start | bytes 1572872 | tf_op jit(solution)/shard_map/ppermute | solution.py:238
  20.7 18.8 %collective-permute-start.1 = (bf16[2,512,256]{2,1,0:T(8,128)(2,1)S(1)}, bf16[2,512,256]{2,1,0:T(8,128)(2,1)S(1)}, u32[]{:S(2)}, u32[]{:S(2)}) collective-permute-start(bf16[2,512,256]{2,1,0:T(8,128)(2,1)S(1)} %get-tuple-element.84), channel_id=1, source_target_pairs={{0,2},{2,4},{4,6},{6,8},{8,10},{10,12},{12,14},{14,16},{16,18},{18... | collective-permute-start | bytes 1572872 | tf_op jit(solution)/shard_map/ppermute | solution.py:238
  27.4 20.7 %collective-permute-start.5 = (bf16[2,512,256]{2,1,0:T(8,128)(2,1)}, bf16[2,512,256]{2,1,0:T(8,128)(2,1)S(1)}, u32[]{:S(2)}, u32[]{:S(2)}) collective-permute-start(bf16[2,512,256]{2,1,0:T(8,128)(2,1)} %get-tuple-element.73), channel_id=1, source_target_pairs={{2,0},{4,2},{6,4},{8,6},{10,8},{12,10},{14,12},{16,14},{18,16},{20... | collective-permute-start | bytes 1572872 | tf_op jit(solution)/shard_map/ppermute | solution.py:238
  30.8 17.3 %collective-permute-start.4 = (bf16[2,512,256]{2,1,0:T(8,128)(2,1)S(1)}, bf16[2,512,256]{2,1,0:T(8,128)(2,1)S(1)}, u32[]{:S(2)}, u32[]{:S(2)}) collective-permute-start(bf16[2,512,256]{2,1,0:T(8,128)(2,1)S(1)} %get-tuple-element.74), channel_id=1, source_target_pairs={{0,2},{2,4},{4,6},{6,8},{8,10},{10,12},{12,14},{14,16},{16,18},{18... | collective-permute-start | bytes 1572872 | tf_op jit(solution)/shard_map/ppermute | solution.py:238
  40.4 17.3 %collective-permute-start.7 = (bf16[2,512,256]{2,1,0:T(8,128)(2,1)S(1)}, bf16[2,512,256]{2,1,0:T(8,128)(2,1)S(1)}, u32[]{:S(2)}, u32[]{:S(2)}) collective-permute-start(bf16[2,512,256]{2,1,0:T(8,128)(2,1)S(1)} %get-tuple-element.67), channel_id=1, source_target_pairs={{0,1},{1,0},{2,3},{3,2},{4,5},{5,4},{6,7},{7,6},{8,9},{9,8},{10,11... | collective-permute-start | bytes 1572872 | tf_op jit(solution)/shard_map/ppermute | solution.py:234
  49.0 17.3 %collective-permute-start.6 = (bf16[2,512,256]{2,1,0:T(8,128)(2,1)S(1)}, bf16[2,512,256]{2,1,0:T(8,128)(2,1)S(1)}, u32[]{:S(2)}, u32[]{:S(2)}) collective-permute-start(bf16[2,512,256]{2,1,0:T(8,128)(2,1)S(1)} %get-tuple-element.66), channel_id=1, source_target_pairs={{0,1},{1,0},{2,3},{3,2},{4,5},{5,4},{6,7},{7,6},{8,9},{9,8},{10,11... | collective-permute-start | bytes 1572872 | tf_op jit(solution)/shard_map/ppermute | solution.py:234
  57.7 0.8 copy-start
  66.0 12.2 %collective-permute-start.12 = (bf16[2,512,256]{2,1,0:T(8,128)(2,1)}, bf16[2,512,256]{2,1,0:T(8,128)(2,1)S(1)}, u32[]{:S(2)}, u32[]{:S(2)}) collective-permute-start(bf16[2,512,256]{2,1,0:T(8,128)(2,1)} %get-tuple-element.52), channel_id=1, source_target_pairs={{0,1},{1,0},{2,3},{3,2},{4,5},{5,4},{6,7},{7,6},{8,9},{9,8},{10,11... | collective-permute-start | bytes 1572872 | tf_op jit(solution)/shard_map/ppermute | solution.py:234
  66.3 0.8 copy-start.1
  67.1 11.1 %copy-start.2 = (bf16[2,512,256]{2,1,0:T(8,128)(2,1)S(1)}, bf16[2,512,256]{2,1,0:T(8,128)(2,1)}, u32[]{:S(2)}) copy-start(bf16[2,512,256]{2,1,0:T(8,128)(2,1)} %get-tuple-element.51) | copy-start | bytes 1572868
  74.6 12.5 %copy-start.3 = (bf16[2,512,256]{2,1,0:T(8,128)(2,1)S(1)}, bf16[2,512,256]{2,1,0:T(8,128)(2,1)}, u32[]{:S(2)}) copy-start(bf16[2,512,256]{2,1,0:T(8,128)(2,1)} %get-tuple-element.49) | copy-start | bytes 1572868
  74.6 12.5 %collective-permute-start.8 = (bf16[2,512,256]{2,1,0:T(8,128)(2,1)}, bf16[2,512,256]{2,1,0:T(8,128)(2,1)S(1)}, u32[]{:S(2)}, u32[]{:S(2)}) collective-permute-start(bf16[2,512,256]{2,1,0:T(8,128)(2,1)} %get-tuple-element.50), channel_id=1, source_target_pairs={{0,1},{1,0},{2,3},{3,2},{4,5},{5,4},{6,7},{7,6},{8,9},{9,8},{10,11... | collective-permute-start | bytes 1572872 | tf_op jit(solution)/shard_map/ppermute | solution.py:234
  79.0 24.7 %collective-permute-start.13 = (bf16[2,512,256]{2,1,0:T(8,128)(2,1)}, bf16[2,512,256]{2,1,0:T(8,128)(2,1)S(1)}, u32[]{:S(2)}, u32[]{:S(2)}) collective-permute-start(bf16[2,512,256]{2,1,0:T(8,128)(2,1)} %get-tuple-element.69), channel_id=1, source_target_pairs={{2,0},{4,2},{6,4},{8,6},{10,8},{12,10},{14,12},{16,14},{18,16},{20... | collective-permute-start | bytes 1572872 | tf_op jit(solution)/shard_map/ppermute | solution.py:238
  81.0 22.8 %collective-permute-start.14 = (bf16[2,512,256]{2,1,0:T(8,128)(2,1)S(1)}, bf16[2,512,256]{2,1,0:T(8,128)(2,1)S(1)}, u32[]{:S(2)}, u32[]{:S(2)}) collective-permute-start(bf16[2,512,256]{2,1,0:T(8,128)(2,1)S(1)} %get-tuple-element.70), channel_id=1, source_target_pairs={{0,2},{2,4},{4,6},{6,8},{8,10},{10,12},{12,14},{14,16},{16,18},{18... | collective-permute-start | bytes 1572872 | tf_op jit(solution)/shard_map/ppermute | solution.py:238
  88.0 21.4 %collective-permute-start.9 = (bf16[2,512,256]{2,1,0:T(8,128)(2,1)}, bf16[2,512,256]{2,1,0:T(8,128)(2,1)S(1)}, u32[]{:S(2)}, u32[]{:S(2)}) collective-permute-start(bf16[2,512,256]{2,1,0:T(8,128)(2,1)} %get-tuple-element.71), channel_id=1, source_target_pairs={{2,0},{4,2},{6,4},{8,6},{10,8},{12,10},{14,12},{16,14},{18,16},{20... | collective-permute-start | bytes 1572872 | tf_op jit(solution)/shard_map/ppermute | solution.py:238
  89.9 19.5 %collective-permute-start.10 = (bf16[2,512,256]{2,1,0:T(8,128)(2,1)S(1)}, bf16[2,512,256]{2,1,0:T(8,128)(2,1)S(1)}, u32[]{:S(2)}, u32[]{:S(2)}) collective-permute-start(bf16[2,512,256]{2,1,0:T(8,128)(2,1)S(1)} %get-tuple-element.72), channel_id=1, source_target_pairs={{0,2},{2,4},{4,6},{6,8},{8,10},{10,12},{12,14},{14,16},{16,18},{18... | collective-permute-start | bytes 1572872 | tf_op jit(solution)/shard_map/ppermute | solution.py:238
  104.7 12.1 %collective-permute-start.15 = (bf16[2,512,256]{2,1,0:T(8,128)(2,1)S(1)}, bf16[2,512,256]{2,1,0:T(8,128)(2,1)S(1)}, u32[]{:S(2)}, u32[]{:S(2)}) collective-permute-start(bf16[2,512,256]{2,1,0:T(8,128)(2,1)S(1)} %get-tuple-element.62), channel_id=1, source_target_pairs={{0,1},{1,0},{2,3},{3,2},{4,5},{5,4},{6,7},{7,6},{8,9},{9,8},{10,11... | collective-permute-start | bytes 1572872 | tf_op jit(solution)/shard_map/ppermute | solution.py:234
  110.3 12.2 %collective-permute-start.11 = (bf16[2,512,256]{2,1,0:T(8,128)(2,1)S(1)}, bf16[2,512,256]{2,1,0:T(8,128)(2,1)S(1)}, u32[]{:S(2)}, u32[]{:S(2)}) collective-permute-start(bf16[2,512,256]{2,1,0:T(8,128)(2,1)S(1)} %get-tuple-element.64), channel_id=1, source_target_pairs={{0,1},{1,0},{2,3},{3,2},{4,5},{5,4},{6,7},{7,6},{8,9},{9,8},{10,11... | collective-permute-start | bytes 1572872 | tf_op jit(solution)/shard_map/ppermute | solution.py:234
  116.8 0.8 copy-start.5
  122.4 0.8 copy-start.4

commit v9 on v4

--- a/solution.py
+++ b/solution.py
@@ -30,17 +30,25 @@
     return reduce(strip.reshape(strip.shape[0] // 8, 8, strip.shape[1]), axis=0)
 
 
-def attention_body(carried, group_ref, low_ref, q_ref, k_ref, v_ref, o_ref, do_ref, past_ref, *refs):
-    dq_ref, dk_ref, dv_ref, back_ref = refs[carried : carried + 4]
-    k_all, v_all, k_turned, dk_sum, dv_sum, scores, slopes, weights_b, slopes_b = refs[carried + 4 :]
+def attention_body(count, per_piece, carried, group_ref, low_ref, q_ref, k_ref, v_ref, o_ref, do_ref, *refs):
+    past_refs, refs = refs[:count], refs[count + carried :]
+    dq_ref, dk_ref, dv_ref = refs[:3]
+    back_refs, refs = refs[3 : 3 + count], refs[3 + count :]
+    k_all, v_all, k_turned, dk_sum, dv_sum, scores, slopes, weights_b, slopes_b = refs
     rows, head = k_ref.shape
-    window = past_ref.shape[1]
+    window = past_refs[0].shape[1]
+    piece = pl.program_id(0) // per_piece
     members = q_ref.shape[1] // head
     span, lanes = window + TILE, members * TILE
     scale = head**-0.5
-    k_all[:window] = past_ref[0]
+    for i, past_ref in enumerate(past_refs):
+
+        @pl.when(piece == i)
+        def _(past_ref=past_ref):
+            k_all[:window] = past_ref[0]
+            v_all[:window] = past_ref[1]
+
     k_all[window:] = k_ref[...]
-    v_all[:window] = past_ref[1]
     v_all[window:] = v_ref[...]
     k_turned[...] = k_all[...].T
     dk_sum[...] = jnp.zeros_like(dk_sum)
@@ -105,34 +113,48 @@
             entered[tile + 1] = enter(tile + 1)
         weigh(tile, entered[tile][1])
         leave(tile, *entered[tile])
-    back_ref[0] = dk_sum[:window].astype(back_ref.dtype)
-    back_ref[1] = dv_sum[:window].astype(back_ref.dtype)
+    for i, back_ref in enumerate(back_refs):
+
+        @pl.when(piece == i)
+        def _(back_ref=back_ref):
+            back_ref[0] = dk_sum[:window].astype(back_ref.dtype)
+            back_ref[1] = dv_sum[:window].astype(back_ref.dtype)
+
     dk_ref[...] = dk_sum[window:]
     dv_ref[...] = dv_sum[window:]
 
 
-def attention(group, low, row_arrays, past, first_head, heads_per_group, carried):
+def attention(groups, low, row_arrays, pasts, first_head, heads_per_group, carried):
     queries, keys, values, outputs, grads = row_arrays
-    rows, window, count = keys.shape[0], past.shape[1], past.shape[2] // HEAD_SIZE
+    rows, window, per_piece = keys.shape[0], pasts[0].shape[1], pasts[0].shape[2] // HEAD_SIZE
     wide = queries.shape[1] // keys.shape[1] * HEAD_SIZE
 
     def column(step, group_ref):
-        return (0, group_ref[0] * heads_per_group + first_head + step)
+        group = group_ref[step // per_piece]
+        return (0, group * heads_per_group + first_head + step % per_piece)
+
+    def past_spec(piece):
+        def place(step, group_ref):
+            return (0, 0, jnp.clip(step - piece * per_piece, 0, per_piece - 1))
+
+        return pl.BlockSpec((2, window, HEAD_SIZE), place)
 
     query_spec = pl.BlockSpec((rows, wide), column)
     key_spec = pl.BlockSpec((rows, HEAD_SIZE), column)
-    past_spec = pl.BlockSpec((2, window, HEAD_SIZE), lambda step, group_ref: (0, 0, step))
+    past_specs = [past_spec(piece) for piece in range(len(pasts))]
     low_spec = pl.BlockSpec((1, rows), lambda step, group_ref: (0, 0))
     square = (rows // TILE, window + TILE, wide // HEAD_SIZE * TILE)
+    count = len(pasts) * per_piece
     tiles = count * queries.shape[1] // keys.shape[1] * rows * (window + TILE)
     return pl.pallas_call(
-        functools.partial(attention_body, len(carried)),
+        functools.partial(attention_body, len(pasts), per_piece, len(carried)),
         grid_spec=pltpu.PrefetchScalarGridSpec(
             num_scalar_prefetch=1,
             grid=(count,),
-            in_specs=[low_spec, query_spec, key_spec, key_spec, query_spec, query_spec, past_spec]
+            in_specs=[low_spec, query_spec, key_spec, key_spec, query_spec, query_spec]
+            + past_specs
             + [pl.BlockSpec(memory_space=pl.ANY)] * len(carried),
-            out_specs=[query_spec, key_spec, key_spec, past_spec],
+            out_specs=[query_spec, key_spec, key_spec] + past_specs,
             scratch_shapes=[
                 pltpu.VMEM((window + rows, HEAD_SIZE), jnp.bfloat16),
                 pltpu.VMEM((window + rows, HEAD_SIZE), jnp.bfloat16),
@@ -149,15 +171,15 @@
             jax.ShapeDtypeStruct(queries.shape, jnp.bfloat16),
             jax.ShapeDtypeStruct(keys.shape, jnp.float32),
             jax.ShapeDtypeStruct(keys.shape, jnp.float32),
-            jax.ShapeDtypeStruct(past.shape, jnp.bfloat16),
-        ],
-        input_output_aliases={8 + i: i for i in range(len(carried))},
+        ]
+        + [jax.ShapeDtypeStruct(past.shape, jnp.bfloat16) for past in pasts],
+        input_output_aliases={7 + len(pasts) + i: i for i in range(len(carried))},
         compiler_params=pltpu.CompilerParams(vmem_limit_bytes=VMEM_BYTES),
         cost_estimate=pl.CostEstimate(
             flops=10 * tiles * HEAD_SIZE, bytes_accessed=count * rows * 2400, transcendentals=tiles
         ),
         name="attention",
-    )(group, low, *row_arrays, past, *carried)
+    )(groups, low, *row_arrays, *pasts, *carried)
 
 
 def finish_body(carried, group_ref, dk_ref, dv_ref, back_ref, *refs):
@@ -168,18 +190,19 @@
 
 
 def finish(group, own, back, first_head, heads_per_group, carried):
-    rows, count = back.shape[1], back.shape[2] // HEAD_SIZE
+    rows, wide = back.shape[1:]
+    per_piece = wide // HEAD_SIZE
 
     def column(step, group_ref):
-        return (0, group_ref[0] * heads_per_group + first_head + step)
-
-    key_spec = pl.BlockSpec((rows, HEAD_SIZE), column)
-    back_spec = pl.BlockSpec((2, rows, HEAD_SIZE), lambda step, group_ref: (0, 0, step))
+        return (0, (group_ref[0] * heads_per_group + first_head) // per_piece)
+
+    key_spec = pl.BlockSpec((rows, wide), column)
+    back_spec = pl.BlockSpec((2, rows, wide), lambda step, group_ref: (0, 0, 0))
     return pl.pallas_call(
         functools.partial(finish_body, len(carried)),
         grid_spec=pltpu.PrefetchScalarGridSpec(
             num_scalar_prefetch=1,
-            grid=(count,),
+            grid=(1,),
             in_specs=[key_spec, key_spec, back_spec]
             + [pl.BlockSpec(memory_space=pl.ANY)] * len(carried),
             out_specs=[key_spec, key_spec],
@@ -188,7 +211,7 @@
         input_output_aliases={4 + i: i for i in range(len(carried))},
         compiler_params=pltpu.CompilerParams(vmem_limit_bytes=VMEM_BYTES),
         cost_estimate=pl.CostEstimate(
-            flops=count * rows * 512, bytes_accessed=count * rows * 2048, transcendentals=0
+            flops=2 * rows * wide, bytes_accessed=rows * wide * 16, transcendentals=0
         ),
         name="finish",
     )(group, *own, back, *carried)
@@ -276,18 +299,20 @@
         halves.append(halves_of(pieces))
     before = [(shifted(early, 1), shifted(late, -1)) for early, late in halves]
 
-    def run(turn, chunk, past, carried):
-        *carried, back = attention(
-            groups[turn].reshape(1), low, row_arrays, past,
-            chunk * per_piece, heads_per_group, tuple(carried),
+    def run(chunk, turns, carried):
+        query_grads, key_sums, value_sums, *backs = attention(
+            jnp.stack([groups[turn] for turn in turns]), low, row_arrays,
+            [pasts[chunk][turn] for turn in turns],
+            chunk * per_piece, heads_per_group, carried,
         )
-        return carried, back
+        return (query_grads, key_sums, value_sums), backs
 
     carried, terms, pasts = (), [], []
     for chunk in range(chunks):
         (early, late), (before_early, before_late) = halves[chunk], before[chunk]
         if chunk:
             *carried, before_early, before_late = together(*carried, before_early, before_late)
+            carried = tuple(carried)
         before_late = jnp.where(last_block, early, before_late)
 
         def past_of(device):
@@ -297,14 +322,20 @@
             own = jnp.where(is_early(device), early, late)
             return part_rows(jnp.concatenate([before, own], axis=1), device, window)
 
-        pasts.append([turned(past_of(other(turn)), turn) for turn in range(1, sharers)])
-        carried, back = run(0, chunk, past_of(place), carried)
-        terms.append([back])
-
-    for chunk in range(chunks):
-        for turn in range(1, sharers):
-            carried, back = run(turn, chunk, pasts[chunk][turn - 1], carried)
-            terms[chunk].append(turned(back, -turn))
+        pasts.append(
+            [past_of(place)] + [turned(past_of(other(turn)), turn) for turn in range(1, sharers)]
+        )
+        if chunk == 0:
+            carried, backs = run(0, [0], carried)
+            terms.append(backs)
+
+    if chunks > 1:
+        pasts[0][1], _ = together(pasts[0][1], pasts[1][0])
+    carried, backs = run(0, range(1, sharers), carried)
+    terms[0] += [turned(back, -turn) for turn, back in enumerate(backs, 1)]
+    for chunk in range(1, chunks):
+        carried, (back, *backs) = run(chunk, range(sharers), carried)
+        terms.append([back] + [turned(back, -turn) for turn, back in enumerate(backs, 1)])
 
     query_grads, *own = carried
     results = ()

time: 126 us -> 128 us (1.016)
  starting transfers between devices: 33.2 us -> 34.6 us
    ppermute x8, waiting for transfers between devices: 18.8 us -> 14.2 us  [shifted(): lax.ppermute(value, 'blk', [(source, source + step) for source in range(f...]
    ppermute x8, waiting for transfers between devices: 17.9 us -> 21.7 us  [turned(): return lax.ppermute(value, 'head', pairs)]
    pallas_call x4 -> x3, Pallas kernels: 29.5 us -> 29.8 us  [attention(): pl.pallas_call(functools.partial(attention_body, len(pasts), per_piece, l...]
  transfers between devices with their start and end apart: 16 -> 16, of which waited for: 8 -> 10; matrix products, arithmetic and copies ran while one was open for 7% -> 8% of each run, Pallas kernels for 29% -> 29%
where the time goes in v9:
time: 128 us; the launch traced here: 127 us
  Pallas kernels  38.7 us (30%)
  waiting for transfers between devices  35.9 us (28%)
  starting transfers between devices  34.6 us (27%)
  other arithmetic  10.6 us (8%)
  local copies, waits for them, and re-layouts  3.96 us (3%)
  between operations  3.45 us (3%)
    pallas_call x3, Pallas kernels, attention(): pl.pallas_call(functools.partial(attention_body, len(pasts), per_piece, l...  29.8 us
    ppermute x8, starting transfers between devices, shifted(): lax.ppermute(value, 'blk', [(source, source + step) for source in range(f...  29 us
    ppermute x8, waiting for transfers between devices, turned(): return lax.ppermute(value, 'head', pairs)  21.7 us
    ppermute x8, waiting for transfers between devices, shifted(): lax.ppermute(value, 'blk', [(source, source + step) for source in range(f...  14.2 us
    pallas_call x4, Pallas kernels, finish(): pl.pallas_call(functools.partial(finish_body, len(carried)), grid_spec=pl...  8.87 us
    ppermute x8, starting transfers between devices, turned(): return lax.ppermute(value, 'head', pairs)  5.62 us
    unnamed x16, local copies, waits for them, and re-layouts  3.21 us
    select_n x2, other arithmetic, rows_of(): jnp.where(is_early(device), sums[0], sums[1])  2.83 us
  transfers between devices with their start and end apart: 16, of which 10 were waited for; matrix products, arithmetic and copies ran while one was open for 8% of the time, Pallas kernels for 29%

profile of v9, /device:TPU:11, one launch (start us, length us, event | category | flops | bytes accessed | tf_op | source)
XLA Modules:
  0.0 127.2 jit_solution(13858512730866420976)
XLA Ops:
  0.6 1.7 %select_bitcast_fusion.2 = (bf16[1,512,256]{2,1,0:T(8,128)(2,1)S(1)}, bf16[1,512,256]{2,1,0:T(8,128)(2,1)S(1)}, bf16[1,512,256]{2,1,0:T(8,128)(2,1)S(1)}, bf16[1...) fusion(pred[]{:T(512)S(6)} %eq.22, ...), kind=kLoop, calls=%fused_computation.27 | loop fusion | flops 1048576 | bytes 4194306 | tf_op jit(solution)/shard_map/stack | solution.py:264
  2.4 0.3 collective-permute-start
  2.8 1.3 %collective-permute-start.3 = (bf16[2,512,256]{2,1,0:T(8,128)(2,1)S(1)}, bf16[2,512,256]{2,1,0:T(8,128)(2,1)S(1)}, u32[]{:S(2)}, u32[]{:S(2)}) collective-permute-start(bf16[2,512,256]{2,1,0:T(8,128)(2,1)S(1)} %pad_maximum_fusion.3), channel_id=1, source_target_pairs={{0,1},{1,0},{2,3},{3,2},{4,5},{5,4},{6,7},{7,6},{8,9},{9,8},{10,11... | collective-permute-start | bytes 1572872 | tf_op jit(solution)/shard_map/ppermute | solution.py:250
  4.1 0.6 fusion
  6.0 9.2 %collective-permute-done = bf16[2,512,256]{2,1,0:T(8,128)(2,1)S(1)} collective-permute-done((bf16[2,512,256]{2,1,0:T(8,128)(2,1)S(1)}, bf16[2,512,256]{2,1,0:T(8,128)(2,1)S(1)}, u32[]{:S(2)}, u32[]{:S(2)}) %collective-permute-start) | collective-permute-done | bytes 524320 | tf_op jit(solution)/shard_map/ppermute | solution.py:250
  15.3 0.9 broadcast_select_fusion.11
  16.1 4.6 %collective-permute-start.2 = (bf16[2,512,256]{2,1,0:T(8,128)(2,1)}, bf16[2,512,256]{2,1,0:T(8,128)(2,1)S(1)}, u32[]{:S(2)}, u32[]{:S(2)}) collective-permute-start(bf16[2,512,256]{2,1,0:T(8,128)(2,1)} %get-tuple-element.79), channel_id=1, source_target_pairs={{2,0},{4,2},{6,4},{8,6},{10,8},{12,10},{14,12},{16,14},{18,16},{20... | collective-permute-start | bytes 1572872 | tf_op jit(solution)/shard_map/ppermute | solution.py:254
  20.7 3.0 %collective-permute-start.1 = (bf16[2,512,256]{2,1,0:T(8,128)(2,1)S(1)}, bf16[2,512,256]{2,1,0:T(8,128)(2,1)S(1)}, u32[]{:S(2)}, u32[]{:S(2)}) collective-permute-start(bf16[2,512,256]{2,1,0:T(8,128)(2,1)S(1)} %get-tuple-element.80), channel_id=1, source_target_pairs={{0,2},{2,4},{4,6},{6,8},{8,10},{10,12},{12,14},{14,16},{16,18},{18... | collective-permute-start | bytes 1572872 | tf_op jit(solution)/shard_map/ppermute | solution.py:254
  25.1 0.1 pad_dynamic-slice_fusion
  25.2 1.3 %collective-permute-done.3 = bf16[2,512,256]{2,1,0:T(8,128)(2,1)S(1)} collective-permute-done((bf16[2,512,256]{2,1,0:T(8,128)(2,1)S(1)}, bf16[2,512,256]{2,1,0:T(8,128)(2,1)S(1)}, u32[]{:S(2)}, u32[]{:S(2)}) %collective-permute-start.3) | collective-permute-done | bytes 524320 | tf_op jit(solution)/shard_map/ppermute | solution.py:250
  26.5 0.9 broadcast_select_fusion.10
  27.4 3.4 %collective-permute-start.5 = (bf16[2,512,256]{2,1,0:T(8,128)(2,1)}, bf16[2,512,256]{2,1,0:T(8,128)(2,1)S(1)}, u32[]{:S(2)}, u32[]{:S(2)}) collective-permute-start(bf16[2,512,256]{2,1,0:T(8,128)(2,1)} %get-tuple-element.69), channel_id=1, source_target_pairs={{2,0},{4,2},{6,4},{8,6},{10,8},{12,10},{14,12},{16,14},{18,16},{20... | collective-permute-start | bytes 1572872 | tf_op jit(solution)/shard_map/ppermute | solution.py:254
  30.8 3.0 %collective-permute-start.4 = (bf16[2,512,256]{2,1,0:T(8,128)(2,1)S(1)}, bf16[2,512,256]{2,1,0:T(8,128)(2,1)S(1)}, u32[]{:S(2)}, u32[]{:S(2)}) collective-permute-start(bf16[2,512,256]{2,1,0:T(8,128)(2,1)S(1)} %get-tuple-element.70), channel_id=1, source_target_pairs={{0,2},{2,4},{4,6},{6,8},{8,10},{10,12},{12,14},{14,16},{16,18},{18... | collective-permute-start | bytes 1572872 | tf_op jit(solution)/shard_map/ppermute | solution.py:254
  33.9 0.9 convert_reduce_fusion
  34.8 4.7 %collective-permute-done.1 = bf16[2,512,256]{2,1,0:T(8,128)(2,1)S(1)} collective-permute-done((bf16[2,512,256]{2,1,0:T(8,128)(2,1)S(1)}, bf16[2,512,256]{2,1,0:T(8,128)(2,1)S(1)}, u32[]{:S(2)}, u32[]{:S(2)}) %collective-permute-start.1) | collective-permute-done | bytes 524320 | tf_op jit(solution)/shard_map/ppermute | solution.py:254
  39.5 0.9 broadcast_select_fusion.8
  40.4 0.3 collective-permute-start.7
  40.6 7.7 %attention.3 = (bf16[512,2048]{1,0:T(8,128)(2,1)}, f32[512,1024]{1,0:T(8,128)}, f32[512,1024]{1,0:T(8,128)}, bf16[2,512,256]{2,1,0:T(8,128)(2,1)}) custom-call(s32[1]{0:T(128)} %bitcast.group_ref, s32[1,512]{1,0:T(1,128)} %bitcast.21, bf16[512,2048]{1,0:T(8,128)(2,1)} %q_ref.5, bf16[512,1024]{1,0:T(8,128)(2,1)} %k_ref.5, bf16[512,1024]{1,0:T(8,128)(2,1)} %v_ref.5, ...), custom_call_target="tpu_custom_call" | custom-call | flops 1677721600 | bytes 2457600 | tf_op jit(solution)/shard_map/attention/pallas_call | solution.py:149
  48.4 0.9 broadcast_select_fusion.9
  49.3 1.2 collective-permute-start.6
  50.5 0.6 pad_add_fusion.group_ref
  51.1 0.4 collective-permute-done.7.refs_0_
  51.5 0.8 copy-done
  52.3 7.7 %attention.4 = (bf16[512,2048]{1,0:T(8,128)(2,1)}, f32[512,1024]{1,0:T(8,128)}, f32[512,1024]{1,0:T(8,128)}, bf16[2,512,256]{2,1,0:T(8,128)(2,1)}) custom-call(s32[1]{0:T(128)} %bitcast.1.group_ref, s32[1,512]{1,0:T(1,128)} %bitcast.22, bf16[512,2048]{1,0:T(8,128)(2,1)} %q_ref.5, ...), custom_call_target="tpu_custom_call", output_to_operand_aliasing={{0}: (8, {}), {1}: (9, {}), {2}: (10, {})} | custom-call | flops 1677721600 | bytes 2457600 | tf_op jit(solution)/shard_map/attention/pallas_call | solution.py:149
  60.1 3.0 %collective-permute-done.6.refs_1_ = bf16[2,512,256]{2,1,0:T(8,128)(2,1)S(1)} collective-permute-done((bf16[2,512,256]{2,1,0:T(8,128)(2,1)S(1)}, bf16[2,512,256]{2,1,0:T(8,128)(2,1)S(1)}, u32[]{:S(2)}, u32[]{:S(2)}) %collective-permute-start.6) | collective-permute-done | bytes 524320 | tf_op jit(solution)/shard_map/ppermute | solution.py:250
  63.1 0.8 copy-done.1
  63.8 14.4 %attention.5 = (bf16[512,2048]{1,0:T(8,128)(2,1)}, f32[512,1024]{1,0:T(8,128)}, f32[512,1024]{1,0:T(8,128)}, bf16[2,512,256]{2,1,0:T(8,128)(2,1)}, bf16[2,512,256]{2,1,0:T(8,128)(2,1)}) custom-call(s32[2]{0:T(128)} %pad_add_fusion.group_ref, s32[1,512]{1,0:T(1,128)} %bitcast.23, ...), custom_call_target="tpu_custom_call", output_to_operand_aliasing={{0}: (9, {}), {1}: (10, {}), {2}: (11, {})} | custom-call | flops 3355443200 | bytes 4915200 | tf_op jit(solution)/shard_map/attention/pallas_call | solution.py:149
  78.2 0.3 collective-permute-start.8
  78.7 1.9 %collective-permute-start.13 = (bf16[2,512,256]{2,1,0:T(8,128)(2,1)S(1)}, bf16[2,512,256]{2,1,0:T(8,128)(2,1)S(1)}, u32[]{:S(2)}, u32[]{:S(2)}) collective-permute-start(bf16[2,512,256]{2,1,0:T(8,128)(2,1)S(1)} %get-tuple-element.65), channel_id=1, source_target_pairs={{2,0},{4,2},{6,4},{8,6},{10,8},{12,10},{14,12},{16,14},{18,16},{20... | collective-permute-start | bytes 1572872 | tf_op jit(solution)/shard_map/ppermute | solution.py:254
  80.6 6.2 %collective-permute-start.14 = (bf16[2,512,256]{2,1,0:T(8,128)(2,1)S(1)}, bf16[2,512,256]{2,1,0:T(8,128)(2,1)}, u32[]{:S(2)}, u32[]{:S(2)}) collective-permute-start(bf16[2,512,256]{2,1,0:T(8,128)(2,1)S(1)} %get-tuple-element.66), channel_id=1, source_target_pairs={{0,2},{2,4},{4,6},{6,8},{8,10},{10,12},{12,14},{14,16},{16,18},{18... | collective-permute-start | bytes 1572872 | tf_op jit(solution)/shard_map/ppermute | solution.py:254
  86.7 1.8 %collective-permute-done.8 = bf16[2,512,256]{2,1,0:T(8,128)(2,1)S(1)} collective-permute-done((bf16[2,512,256]{2,1,0:T(8,128)(2,1)}, bf16[2,512,256]{2,1,0:T(8,128)(2,1)S(1)}, u32[]{:S(2)}, u32[]{:S(2)}) %collective-permute-start.8) | collective-permute-done | bytes 524320 | tf_op jit(solution)/shard_map/ppermute | solution.py:250
  88.5 0.9 broadcast_select_fusion.3
  89.4 1.9 %collective-permute-start.9 = (bf16[2,512,256]{2,1,0:T(8,128)(2,1)}, bf16[2,512,256]{2,1,0:T(8,128)(2,1)S(1)}, u32[]{:S(2)}, u32[]{:S(2)}) collective-permute-start(bf16[2,512,256]{2,1,0:T(8,128)(2,1)} %get-tuple-element.67), channel_id=1, source_target_pairs={{2,0},{4,2},{6,4},{8,6},{10,8},{12,10},{14,12},{16,14},{18,16},{20... | collective-permute-start | bytes 1572872 | tf_op jit(solution)/shard_map/ppermute | solution.py:254
  91.3 4.9 %collective-permute-start.10 = (bf16[2,512,256]{2,1,0:T(8,128)(2,1)S(1)}, bf16[2,512,256]{2,1,0:T(8,128)(2,1)S(1)}, u32[]{:S(2)}, u32[]{:S(2)}) collective-permute-start(bf16[2,512,256]{2,1,0:T(8,128)(2,1)S(1)} %get-tuple-element.68), channel_id=1, source_target_pairs={{0,2},{2,4},{4,6},{6,8},{8,10},{10,12},{12,14},{14,16},{16,18},{18... | collective-permute-start | bytes 1572872 | tf_op jit(solution)/shard_map/ppermute | solution.py:254
  96.2 7.0 %collective-permute-done.13 = bf16[2,512,256]{2,1,0:T(8,128)(2,1)S(1)} collective-permute-done((bf16[2,512,256]{2,1,0:T(8,128)(2,1)S(1)}, bf16[2,512,256]{2,1,0:T(8,128)(2,1)S(1)}, u32[]{:S(2)}, u32[]{:S(2)}) %collective-permute-start.13) | collective-permute-done | bytes 524320 | tf_op jit(solution)/shard_map/ppermute | solution.py:254
  103.2 1.9 %broadcast_select_fusion = (bf16[2,512,256]{2,1,0:T(8,128)(2,1)}, bf16[2,512,256]{2,1,0:T(8,128)(2,1)S(1)}) fusion(bf16[2,512,256]{2,1,0:T(8,128)(2,1)} %collective-permute-done.14, pred[]{:T(512)S(6)} %eq.57, bf16[2,512,256]{2,1,0:T(8,128)(2,1)S(1)} %get-tuple-element.66, bf16[2,512,256]{2,1,0:T(8,128)(2,1)S(1)} %collective-permute-done.13, pred[]{:T(512)S(6)} %eq.26, ...), kind=kLoop, calls=%fused_computation.5 | loop fusion | flops 786432 | bytes 2621443 | tf_op jit(solution)/shard_map/jit(_where)/select_n | solution.py:367
  105.1 1.1 collective-permute-start.15
  106.2 2.6 %collective-permute-done.9 = bf16[2,512,256]{2,1,0:T(8,128)(2,1)S(1)} collective-permute-done((bf16[2,512,256]{2,1,0:T(8,128)(2,1)}, bf16[2,512,256]{2,1,0:T(8,128)(2,1)S(1)}, u32[]{:S(2)}, u32[]{:S(2)}) %collective-permute-start.9) | collective-permute-done | bytes 524320 | tf_op jit(solution)/shard_map/ppermute | solution.py:254
  108.8 0.9 broadcast_select_fusion.1
  109.7 1.1 collective-permute-start.11
  110.8 2.2 %finish.4 = (bf16[512,1024]{1,0:T(8,128)(2,1)}, bf16[512,1024]{1,0:T(8,128)(2,1)}) custom-call(s32[1]{0:T(128)} %bitcast.group_ref, f32[512,1024]{1,0:T(8,128)} %get-tuple-element.43.dk_ref, f32[512,1024]{1,0:T(8,128)} %get-tuple-element.44.dv_ref, bf16[2,512,256]{2,1,0:T(8,128)(2,1)} %get-tuple-element.57.back_ref), custom_call_target="tpu_custom_call" | custom-call | flops 262144 | bytes 2097152 | tf_op jit(solution)/shard_map/finish/pallas_call | solution.py:201
  113.0 5.7 %collective-permute-done.15.back_ref = bf16[2,512,256]{2,1,0:T(8,128)(2,1)S(1)} collective-permute-done((bf16[2,512,256]{2,1,0:T(8,128)(2,1)S(1)}, bf16[2,512,256]{2,1,0:T(8,128)(2,1)S(1)}, u32[]{:S(2)}, u32[]{:S(2)}) %collective-permute-start.15) | collective-permute-done | bytes 524320 | tf_op jit(solution)/shard_map/ppermute | solution.py:250
  118.7 0.8 copy-done.5
  119.5 2.2 %finish.5 = (bf16[512,1024]{1,0:T(8,128)(2,1)}, bf16[512,1024]{1,0:T(8,128)(2,1)}) custom-call(s32[1]{0:T(128)} %bitcast.1.group_ref, f32[512,1024]{1,0:T(8,128)} %get-tuple-element.43.dk_ref, f32[512,1024]{1,0:T(8,128)} %get-tuple-element.44.dv_ref, bf16[2,512,256]{2,1,0:T(8,128)(2,1)} %copy-done.5, ...), custom_call_target="tpu_custom_call", output_to_operand_aliasing={{0}: (4, {}), {1}: (5, {})} | custom-call | flops 262144 | bytes 2097152 | tf_op jit(solution)/shard_map/finish/pallas_call | solution.py:201
  121.7 2.2 %finish.6 = (bf16[512,1024]{1,0:T(8,128)(2,1)}, bf16[512,1024]{1,0:T(8,128)(2,1)}) custom-call(s32[1]{0:T(128)} %bitcast.group_ref, f32[512,1024]{1,0:T(8,128)} %get-tuple-element.43.dk_ref, f32[512,1024]{1,0:T(8,128)} %get-tuple-element.44.dv_ref, bf16[2,512,256]{2,1,0:T(8,128)(2,1)} %get-tuple-element.59.back_ref, ...), custom_call_target="tpu_custom_call", output_to_operand_aliasing={{0}: (4, {}), {1}: (5, {})} | custom-call | flops 262144 | bytes 2097152 | tf_op jit(solution)/shard_map/finish/pallas_call | solution.py:201
  123.9 0.3 collective-permute-done.11.back_ref
  124.2 0.8 copy-done.4
  125.0 2.2 %finish.7 = (bf16[512,1024]{1,0:T(8,128)(2,1)}, bf16[512,1024]{1,0:T(8,128)(2,1)}) custom-call(s32[1]{0:T(128)} %bitcast.1.group_ref, f32[512,1024]{1,0:T(8,128)} %get-tuple-element.43.dk_ref, f32[512,1024]{1,0:T(8,128)} %get-tuple-element.44.dv_ref, bf16[2,512,256]{2,1,0:T(8,128)(2,1)} %copy-done.4, ...), custom_call_target="tpu_custom_call", output_to_operand_aliasing={{0}: (4, {}), {1}: (5, {})} | custom-call | flops 262144 | bytes 2097152 | tf_op jit(solution)/shard_map/finish/pallas_call | solution.py:201
  (24 shorter events, 0.4 us)
Async XLA Ops:
  2.3 1.7 %copy-start.7 = (s32[32]{0:T(128)S(1)}, s32[32]{0:T(128)}, u32[]{:S(2)}) copy-start(s32[32]{0:T(128)} %param.13) | copy-start | bytes 388
  2.4 22.8 %copy-start.6 = (s32[16384]{0:T(1024)S(1)}, s32[16384]{0:T(1024)}, u32[]{:S(2)}) copy-start(s32[16384]{0:T(1024)} %param.12) | copy-start | bytes 196612
  2.4 12.9 %collective-permute-start = (bf16[2,512,256]{2,1,0:T(8,128)(2,1)S(1)}, bf16[2,512,256]{2,1,0:T(8,128)(2,1)S(1)}, u32[]{:S(2)}, u32[]{:S(2)}) collective-permute-start(bf16[2,512,256]{2,1,0:T(8,128)(2,1)S(1)} %pad_maximum_fusion.1), channel_id=1, source_target_pairs={{0,1},{1,0},{2,3},{3,2},{4,5},{5,4},{6,7},{7,6},{8,9},{9,8},{10,11... | collective-permute-start | bytes 1572872 | tf_op jit(solution)/shard_map/ppermute | solution.py:250
  2.8 23.7 %collective-permute-start.3 = (bf16[2,512,256]{2,1,0:T(8,128)(2,1)S(1)}, bf16[2,512,256]{2,1,0:T(8,128)(2,1)S(1)}, u32[]{:S(2)}, u32[]{:S(2)}) collective-permute-start(bf16[2,512,256]{2,1,0:T(8,128)(2,1)S(1)} %pad_maximum_fusion.3), channel_id=1, source_target_pairs={{0,1},{1,0},{2,3},{3,2},{4,5},{5,4},{6,7},{7,6},{8,9},{9,8},{10,11... | collective-permute-start | bytes 1572872 | tf_op jit(solution)/shard_map/ppermute | solution.py:250
  16.1 18.7 %collective-permute-start.2 = (bf16[2,512,256]{2,1,0:T(8,128)(2,1)}, bf16[2,512,256]{2,1,0:T(8,128)(2,1)S(1)}, u32[]{:S(2)}, u32[]{:S(2)}) collective-permute-start(bf16[2,512,256]{2,1,0:T(8,128)(2,1)} %get-tuple-element.79), channel_id=1, source_target_pairs={{2,0},{4,2},{6,4},{8,6},{10,8},{12,10},{14,12},{16,14},{18,16},{20... | collective-permute-start | bytes 1572872 | tf_op jit(solution)/shard_map/ppermute | solution.py:254
  20.7 18.8 %collective-permute-start.1 = (bf16[2,512,256]{2,1,0:T(8,128)(2,1)S(1)}, bf16[2,512,256]{2,1,0:T(8,128)(2,1)S(1)}, u32[]{:S(2)}, u32[]{:S(2)}) collective-permute-start(bf16[2,512,256]{2,1,0:T(8,128)(2,1)S(1)} %get-tuple-element.80), channel_id=1, source_target_pairs={{0,2},{2,4},{4,6},{6,8},{8,10},{10,12},{12,14},{14,16},{16,18},{18... | collective-permute-start | bytes 1572872 | tf_op jit(solution)/shard_map/ppermute | solution.py:254
  27.4 21.0 %collective-permute-start.5 = (bf16[2,512,256]{2,1,0:T(8,128)(2,1)}, bf16[2,512,256]{2,1,0:T(8,128)(2,1)S(1)}, u32[]{:S(2)}, u32[]{:S(2)}) collective-permute-start(bf16[2,512,256]{2,1,0:T(8,128)(2,1)} %get-tuple-element.69), channel_id=1, source_target_pairs={{2,0},{4,2},{6,4},{8,6},{10,8},{12,10},{14,12},{16,14},{18,16},{20... | collective-permute-start | bytes 1572872 | tf_op jit(solution)/shard_map/ppermute | solution.py:254
  30.8 17.5 %collective-permute-start.4 = (bf16[2,512,256]{2,1,0:T(8,128)(2,1)S(1)}, bf16[2,512,256]{2,1,0:T(8,128)(2,1)S(1)}, u32[]{:S(2)}, u32[]{:S(2)}) collective-permute-start(bf16[2,512,256]{2,1,0:T(8,128)(2,1)S(1)} %get-tuple-element.70), channel_id=1, source_target_pairs={{0,2},{2,4},{4,6},{6,8},{8,10},{10,12},{12,14},{14,16},{16,18},{18... | collective-permute-start | bytes 1572872 | tf_op jit(solution)/shard_map/ppermute | solution.py:254
  40.4 11.1 %collective-permute-start.7 = (bf16[2,512,256]{2,1,0:T(8,128)(2,1)S(1)}, bf16[2,512,256]{2,1,0:T(8,128)(2,1)S(1)}, u32[]{:S(2)}, u32[]{:S(2)}) collective-permute-start(bf16[2,512,256]{2,1,0:T(8,128)(2,1)S(1)} %get-tuple-element.61), channel_id=1, source_target_pairs={{0,1},{1,0},{2,3},{3,2},{4,5},{5,4},{6,7},{7,6},{8,9},{9,8},{10,11... | collective-permute-start | bytes 1572872 | tf_op jit(solution)/shard_map/ppermute | solution.py:250
  49.3 13.8 %collective-permute-start.6 = (bf16[2,512,256]{2,1,0:T(8,128)(2,1)S(1)}, bf16[2,512,256]{2,1,0:T(8,128)(2,1)S(1)}, u32[]{:S(2)}, u32[]{:S(2)}) collective-permute-start(bf16[2,512,256]{2,1,0:T(8,128)(2,1)S(1)} %get-tuple-element.63), channel_id=1, source_target_pairs={{0,1},{1,0},{2,3},{3,2},{4,5},{5,4},{6,7},{7,6},{8,9},{9,8},{10,11... | collective-permute-start | bytes 1572872 | tf_op jit(solution)/shard_map/ppermute | solution.py:250
  51.5 0.8 copy-start
  60.0 18.6 %collective-permute-start.12 = (bf16[2,512,256]{2,1,0:T(8,128)(2,1)}, bf16[2,512,256]{2,1,0:T(8,128)(2,1)S(1)}, u32[]{:S(2)}, u32[]{:S(2)}) collective-permute-start(bf16[2,512,256]{2,1,0:T(8,128)(2,1)} %get-tuple-element.48), channel_id=1, source_target_pairs={{0,1},{1,0},{2,3},{3,2},{4,5},{5,4},{6,7},{7,6},{8,9},{9,8},{10,11... | collective-permute-start | bytes 1572872 | tf_op jit(solution)/shard_map/ppermute | solution.py:250
  63.1 0.8 copy-start.1
  63.8 14.7 %copy-start.2 = (bf16[2,512,256]{2,1,0:T(8,128)(2,1)S(1)}, bf16[2,512,256]{2,1,0:T(8,128)(2,1)}, u32[]{:S(2)}) copy-start(bf16[2,512,256]{2,1,0:T(8,128)(2,1)} %get-tuple-element.47) | copy-start | bytes 1572868
  78.2 10.3 %copy-start.3 = (bf16[2,512,256]{2,1,0:T(8,128)(2,1)S(1)}, bf16[2,512,256]{2,1,0:T(8,128)(2,1)}, u32[]{:S(2)}) copy-start(bf16[2,512,256]{2,1,0:T(8,128)(2,1)} %get-tuple-element.45) | copy-start | bytes 1572868
  78.2 10.3 %collective-permute-start.8 = (bf16[2,512,256]{2,1,0:T(8,128)(2,1)}, bf16[2,512,256]{2,1,0:T(8,128)(2,1)S(1)}, u32[]{:S(2)}, u32[]{:S(2)}) collective-permute-start(bf16[2,512,256]{2,1,0:T(8,128)(2,1)} %get-tuple-element.46), channel_id=1, source_target_pairs={{0,1},{1,0},{2,3},{3,2},{4,5},{5,4},{6,7},{7,6},{8,9},{9,8},{10,11... | collective-permute-start | bytes 1572872 | tf_op jit(solution)/shard_map/ppermute | solution.py:250
  78.7 24.5 %collective-permute-start.13 = (bf16[2,512,256]{2,1,0:T(8,128)(2,1)S(1)}, bf16[2,512,256]{2,1,0:T(8,128)(2,1)S(1)}, u32[]{:S(2)}, u32[]{:S(2)}) collective-permute-start(bf16[2,512,256]{2,1,0:T(8,128)(2,1)S(1)} %get-tuple-element.65), channel_id=1, source_target_pairs={{2,0},{4,2},{6,4},{8,6},{10,8},{12,10},{14,12},{16,14},{18,16},{20... | collective-permute-start | bytes 1572872 | tf_op jit(solution)/shard_map/ppermute | solution.py:254
  80.6 22.6 %collective-permute-start.14 = (bf16[2,512,256]{2,1,0:T(8,128)(2,1)S(1)}, bf16[2,512,256]{2,1,0:T(8,128)(2,1)}, u32[]{:S(2)}, u32[]{:S(2)}) collective-permute-start(bf16[2,512,256]{2,1,0:T(8,128)(2,1)S(1)} %get-tuple-element.66), channel_id=1, source_target_pairs={{0,2},{2,4},{4,6},{6,8},{8,10},{10,12},{12,14},{14,16},{16,18},{18... | collective-permute-start | bytes 1572872 | tf_op jit(solution)/shard_map/ppermute | solution.py:254
  89.4 19.4 %collective-permute-start.9 = (bf16[2,512,256]{2,1,0:T(8,128)(2,1)}, bf16[2,512,256]{2,1,0:T(8,128)(2,1)S(1)}, u32[]{:S(2)}, u32[]{:S(2)}) collective-permute-start(bf16[2,512,256]{2,1,0:T(8,128)(2,1)} %get-tuple-element.67), channel_id=1, source_target_pairs={{2,0},{4,2},{6,4},{8,6},{10,8},{12,10},{14,12},{16,14},{18,16},{20... | collective-permute-start | bytes 1572872 | tf_op jit(solution)/shard_map/ppermute | solution.py:254
  91.3 17.5 %collective-permute-start.10 = (bf16[2,512,256]{2,1,0:T(8,128)(2,1)S(1)}, bf16[2,512,256]{2,1,0:T(8,128)(2,1)S(1)}, u32[]{:S(2)}, u32[]{:S(2)}) collective-permute-start(bf16[2,512,256]{2,1,0:T(8,128)(2,1)S(1)} %get-tuple-element.68), channel_id=1, source_target_pairs={{0,2},{2,4},{4,6},{6,8},{8,10},{10,12},{12,14},{14,16},{16,18},{18... | collective-permute-start | bytes 1572872 | tf_op jit(solution)/shard_map/ppermute | solution.py:254
  105.1 13.5 %collective-permute-start.15 = (bf16[2,512,256]{2,1,0:T(8,128)(2,1)S(1)}, bf16[2,512,256]{2,1,0:T(8,128)(2,1)S(1)}, u32[]{:S(2)}, u32[]{:S(2)}) collective-permute-start(bf16[2,512,256]{2,1,0:T(8,128)(2,1)S(1)} %get-tuple-element.58), channel_id=1, source_target_pairs={{0,1},{1,0},{2,3},{3,2},{4,5},{5,4},{6,7},{7,6},{8,9},{9,8},{10,11... | collective-permute-start | bytes 1572872 | tf_op jit(solution)/shard_map/ppermute | solution.py:250
  109.7 14.5 %collective-permute-start.11 = (bf16[2,512,256]{2,1,0:T(8,128)(2,1)S(1)}, bf16[2,512,256]{2,1,0:T(8,128)(2,1)S(1)}, u32[]{:S(2)}, u32[]{:S(2)}) collective-permute-start(bf16[2,512,256]{2,1,0:T(8,128)(2,1)S(1)} %get-tuple-element.60), channel_id=1, source_target_pairs={{0,1},{1,0},{2,3},{3,2},{4,5},{5,4},{6,7},{7,6},{8,9},{9,8},{10,11... | collective-permute-start | bytes 1572872 | tf_op jit(solution)/shard_map/ppermute | solution.py:250
  118.7 0.8 copy-start.5
  124.2 0.8 copy-start.4

commit v10 on v4

--- a/solution.py
+++ b/solution.py
@@ -11,6 +11,7 @@
 NEGATIVE = -1e30
 LOG2_E = 1.4426950408889634
 CHUNKS = 2
+DIRECT_CHUNKS = 4
 TILE = 128
 STRIP = 64
 VMEM_BYTES = 60 * 1024 * 1024
@@ -30,17 +31,25 @@
     return reduce(strip.reshape(strip.shape[0] // 8, 8, strip.shape[1]), axis=0)
 
 
-def attention_body(carried, group_ref, low_ref, q_ref, k_ref, v_ref, o_ref, do_ref, past_ref, *refs):
+def attention_body(
+    choices, carried, group_ref, which_ref, low_ref, q_ref, k_ref, v_ref, o_ref, do_ref, *refs
+):
+    past_refs, refs = refs[:choices], refs[choices:]
     dq_ref, dk_ref, dv_ref, back_ref = refs[carried : carried + 4]
     k_all, v_all, k_turned, dk_sum, dv_sum, scores, slopes, weights_b, slopes_b = refs[carried + 4 :]
     rows, head = k_ref.shape
-    window = past_ref.shape[1]
+    window = past_refs[0].shape[1]
     members = q_ref.shape[1] // head
     span, lanes = window + TILE, members * TILE
     scale = head**-0.5
-    k_all[:window] = past_ref[0]
+    for choice, past_ref in enumerate(past_refs):
+
+        @pl.when(which_ref[0] == choice)
+        def _(past_ref=past_ref):
+            k_all[:window] = past_ref[0]
+            v_all[:window] = past_ref[1]
+
     k_all[window:] = k_ref[...]
-    v_all[:window] = past_ref[1]
     v_all[window:] = v_ref[...]
     k_turned[...] = k_all[...].T
     dk_sum[...] = jnp.zeros_like(dk_sum)
@@ -111,28 +120,39 @@
     dv_ref[...] = dv_sum[window:]
 
 
-def attention(group, low, row_arrays, past, first_head, heads_per_group, carried):
+def choice_specs(arrays):
+    def place(choice, step, group_ref, which_ref):
+        return (0, 0, jnp.where(which_ref[0] == choice, step, 0))
+
+    return [
+        pl.BlockSpec((2, array.shape[1], HEAD_SIZE), functools.partial(place, choice))
+        for choice, array in enumerate(arrays)
+    ]
+
+
+def attention(group, which, low, row_arrays, pasts, first_head, heads_per_group, carried):
     queries, keys, values, outputs, grads = row_arrays
-    rows, window, count = keys.shape[0], past.shape[1], past.shape[2] // HEAD_SIZE
+    rows, window, count = keys.shape[0], pasts[0].shape[1], pasts[0].shape[2] // HEAD_SIZE
     wide = queries.shape[1] // keys.shape[1] * HEAD_SIZE
 
-    def column(step, group_ref):
+    def column(step, group_ref, which_ref):
         return (0, group_ref[0] * heads_per_group + first_head + step)
 
     query_spec = pl.BlockSpec((rows, wide), column)
     key_spec = pl.BlockSpec((rows, HEAD_SIZE), column)
-    past_spec = pl.BlockSpec((2, window, HEAD_SIZE), lambda step, group_ref: (0, 0, step))
-    low_spec = pl.BlockSpec((1, rows), lambda step, group_ref: (0, 0))
+    back_spec = pl.BlockSpec((2, window, HEAD_SIZE), lambda step, *refs: (0, 0, step))
+    low_spec = pl.BlockSpec((1, rows), lambda step, *refs: (0, 0))
     square = (rows // TILE, window + TILE, wide // HEAD_SIZE * TILE)
     tiles = count * queries.shape[1] // keys.shape[1] * rows * (window + TILE)
     return pl.pallas_call(
-        functools.partial(attention_body, len(carried)),
+        functools.partial(attention_body, len(pasts), len(carried)),
         grid_spec=pltpu.PrefetchScalarGridSpec(
-            num_scalar_prefetch=1,
+            num_scalar_prefetch=2,
             grid=(count,),
-            in_specs=[low_spec, query_spec, key_spec, key_spec, query_spec, query_spec, past_spec]
+            in_specs=[low_spec, query_spec, key_spec, key_spec, query_spec, query_spec]
+            + choice_specs(pasts)
             + [pl.BlockSpec(memory_space=pl.ANY)] * len(carried),
-            out_specs=[query_spec, key_spec, key_spec, past_spec],
+            out_specs=[query_spec, key_spec, key_spec, back_spec],
             scratch_shapes=[
                 pltpu.VMEM((window + rows, HEAD_SIZE), jnp.bfloat16),
                 pltpu.VMEM((window + rows, HEAD_SIZE), jnp.bfloat16),
@@ -149,49 +169,54 @@
             jax.ShapeDtypeStruct(queries.shape, jnp.bfloat16),
             jax.ShapeDtypeStruct(keys.shape, jnp.float32),
             jax.ShapeDtypeStruct(keys.shape, jnp.float32),
-            jax.ShapeDtypeStruct(past.shape, jnp.bfloat16),
+            jax.ShapeDtypeStruct(pasts[0].shape, jnp.bfloat16),
         ],
-        input_output_aliases={8 + i: i for i in range(len(carried))},
+        input_output_aliases={8 + len(pasts) + i: i for i in range(len(carried))},
         compiler_params=pltpu.CompilerParams(vmem_limit_bytes=VMEM_BYTES),
         cost_estimate=pl.CostEstimate(
             flops=10 * tiles * HEAD_SIZE, bytes_accessed=count * rows * 2400, transcendentals=tiles
         ),
         name="attention",
-    )(group, low, *row_arrays, past, *carried)
-
-
-def finish_body(carried, group_ref, dk_ref, dv_ref, back_ref, *refs):
-    key_out, value_out = refs[carried:]
+    )(group, which, low, *row_arrays, *pasts, *carried)
+
+
+def finish_body(choices, carried, group_ref, which_ref, dk_ref, dv_ref, *refs):
+    key_out, value_out = refs[choices + carried :]
     scale = HEAD_SIZE**-0.5
-    key_out[...] = ((dk_ref[...] + back_ref[0].astype(jnp.float32)) * scale).astype(key_out.dtype)
-    value_out[...] = (dv_ref[...] + back_ref[1].astype(jnp.float32)).astype(value_out.dtype)
-
-
-def finish(group, own, back, first_head, heads_per_group, carried):
-    rows, count = back.shape[1], back.shape[2] // HEAD_SIZE
-
-    def column(step, group_ref):
+    for choice, back_ref in enumerate(refs[:choices]):
+
+        @pl.when(which_ref[0] == choice)
+        def _(back_ref=back_ref):
+            key_sum = dk_ref[...] + back_ref[0].astype(jnp.float32)
+            key_out[...] = (key_sum * scale).astype(key_out.dtype)
+            value_out[...] = (dv_ref[...] + back_ref[1].astype(jnp.float32)).astype(value_out.dtype)
+
+
+def finish(group, which, own, backs, first_head, heads_per_group, carried):
+    rows, count = backs[0].shape[1], backs[0].shape[2] // HEAD_SIZE
+
+    def column(step, group_ref, which_ref):
         return (0, group_ref[0] * heads_per_group + first_head + step)
 
     key_spec = pl.BlockSpec((rows, HEAD_SIZE), column)
-    back_spec = pl.BlockSpec((2, rows, HEAD_SIZE), lambda step, group_ref: (0, 0, step))
     return pl.pallas_call(
-        functools.partial(finish_body, len(carried)),
+        functools.partial(finish_body, len(backs), len(carried)),
         grid_spec=pltpu.PrefetchScalarGridSpec(
-            num_scalar_prefetch=1,
+            num_scalar_prefetch=2,
             grid=(count,),
-            in_specs=[key_spec, key_spec, back_spec]
+            in_specs=[key_spec, key_spec]
+            + choice_specs(backs)
             + [pl.BlockSpec(memory_space=pl.ANY)] * len(carried),
             out_specs=[key_spec, key_spec],
         ),
         out_shape=[jax.ShapeDtypeStruct(own[0].shape, jnp.bfloat16)] * 2,
-        input_output_aliases={4 + i: i for i in range(len(carried))},
+        input_output_aliases={4 + len(backs) + i: i for i in range(len(carried))},
         compiler_params=pltpu.CompilerParams(vmem_limit_bytes=VMEM_BYTES),
         cost_estimate=pl.CostEstimate(
             flops=count * rows * 512, bytes_accessed=count * rows * 2048, transcendentals=0
         ),
         name="finish",
-    )(group, *own, back, *carried)
+    )(group, which, *own, *backs, *carried)
 
 
 def together(*values):
@@ -205,7 +230,96 @@
     return result
 
 
-def local(queries, keys, values, outputs, out_grads, segment_ids, block_order):
+def first_visible(segment_ids, start, window, rows):
+    padded = jnp.concatenate([jnp.full((window,), -1, jnp.int32), segment_ids])
+    near = lax.dynamic_slice_in_dim(padded, start, window + rows)
+    return jnp.sum((near[None, :] < near[window:, None]).astype(jnp.int32), axis=1)[None, :]
+
+
+def local_direct(queries, keys, values, outputs, out_grads, segment_ids, block_order):
+    blocks = lax.axis_size("blk")
+    block, place = lax.axis_index("blk"), lax.axis_index("head")
+    rows, key_heads = keys.shape[0], keys.shape[1] // HEAD_SIZE
+    per_chunk = key_heads // DIRECT_CHUNKS
+    last_block = block == blocks - 1
+
+    def slots_of(block):
+        return lax.dynamic_slice_in_dim(block_order, 2 * jnp.clip(block, 0, blocks - 1), 2)
+
+    def early_slot_of(block):
+        slots = slots_of(block)
+        return (slots[0] > slots[1]).astype(jnp.int32)
+
+    def swapped(value):
+        return lax.ppermute(value, "head", [(0, 1), (1, 0)])
+
+    def shifted(value, step):
+        first, end = max(0, -step), min(blocks, blocks - step)
+        return lax.ppermute(value, "blk", [(source, source + step) for source in range(first, end)])
+
+    early_slot = early_slot_of(block)
+    early = place == early_slot
+    same_left = early_slot_of(block - 1) == early_slot
+    same_right = (early_slot_of(block + 1) == early_slot) & ~last_block
+    which_past = jnp.where(early, jnp.where(same_left, 0, 2), jnp.where(same_right, 1, 2)).reshape(1)
+    which_back = jnp.where(early, jnp.where(same_right, 1, 2), jnp.where(same_left, 0, 2)).reshape(1)
+    slots = slots_of(block)
+    low = first_visible(segment_ids, pick([slots[0], slots[1]], place) * rows, rows, rows)
+    zero = jnp.zeros((1,), jnp.int32)
+    row_arrays = (queries, keys, values, outputs, out_grads)
+
+    shifts, theirs, pasts = [], [], []
+
+    def shift(chunk):
+        columns = slice(chunk * per_chunk * HEAD_SIZE, (chunk + 1) * per_chunk * HEAD_SIZE)
+        piece = jnp.stack([keys[:, columns], values[:, columns]])
+        if chunk >= 2:
+            piece, *_ = together(piece, theirs[chunk - 2], *(past[2] for past in pasts[: chunk - 2]))
+        shifts.append((piece, shifted(piece, 1), shifted(piece, -1)))
+
+    def swap(chunk):
+        piece, from_left, from_right = shifts[chunk]
+        if chunk:
+            from_left, from_right, _ = together(from_left, from_right, theirs[chunk - 1])
+        theirs.append(jnp.where(early, jnp.where(last_block, piece, from_right), from_left))
+        return from_left, from_right, swapped(theirs[chunk])
+
+    shift(0)
+    for chunk in range(DIRECT_CHUNKS):
+        if chunk + 1 < DIRECT_CHUNKS:
+            shift(chunk + 1)
+        pasts.append(swap(chunk))
+
+    carried, terms, backs = (), [], []
+
+    def swap_back(chunk):
+        term, from_left, from_right = terms[chunk]
+        if backs:
+            from_left, from_right, _ = together(from_left, from_right, backs[-1][0])
+        theirs = jnp.where(early, from_left, jnp.where(last_block, term, from_right))
+        backs.append((theirs, (from_left, from_right, swapped(theirs))))
+
+    for chunk in range(DIRECT_CHUNKS):
+        if chunk == DIRECT_CHUNKS - 1:
+            swap_back(0)
+            *carried, _ = together(*carried, backs[0][0])
+        *carried, term = attention(
+            zero, which_past, low, row_arrays, pasts[chunk], chunk * per_chunk, 0, tuple(carried)
+        )
+        terms.append((term, shifted(term, 1), shifted(term, -1)))
+    query_grads, *own = carried
+
+    results = ()
+    for chunk in range(DIRECT_CHUNKS):
+        if chunk:
+            swap_back(chunk)
+        results = finish(
+            zero, which_back, own, backs[chunk][1], chunk * per_chunk, 0, tuple(results)
+        )
+    return (query_grads, *results)
+
+
+def local_exchanged(queries, keys, values, outputs, out_grads, segment_ids, block_order):
     blocks, sharers = lax.axis_size("blk"), lax.axis_size("head")
     block, place = lax.axis_index("blk"), lax.axis_index("head")
     rows = keys.shape[0]
@@ -249,10 +363,8 @@
         return lax.dynamic_slice_in_dim(array, device % parts * rows, count, 1)
 
     my_half = pick([slots[0], slots[1]], place // parts)
-    start = my_half * window + place % parts * rows
-    padded = jnp.concatenate([jnp.full((window,), -1, jnp.int32), segment_ids])
-    near = lax.dynamic_slice_in_dim(padded, start, window + rows)
-    low = jnp.sum((near[None, :] < near[window:, None]).astype(jnp.int32), axis=1)[None, :]
+    zero = jnp.zeros((1,), jnp.int32)
+    low = first_visible(segment_ids, my_half * window + place % parts * rows, window, rows)
 
     row_arrays = (queries, keys, values, outputs, out_grads)
     groups = [other(-turn) for turn in range(sharers)]
@@ -278,7 +390,7 @@
 
     def run(turn, chunk, past, carried):
         *carried, back = attention(
-            groups[turn].reshape(1), low, row_arrays, past,
+            groups[turn].reshape(1), zero, low, row_arrays, [past],
             chunk * per_piece, heads_per_group, tuple(carried),
         )
         return carried, back
@@ -340,12 +452,8 @@
             if turn:
                 back = turned(back, turn)
             results = finish(
-                groups[turn].reshape(1),
-                own,
-                back,
-                chunk * per_piece,
-                heads_per_group,
-                tuple(results),
+                groups[turn].reshape(1), zero, own, [back],
+                chunk * per_piece, heads_per_group, tuple(results),
             )
     return (query_grads, *results)
 
@@ -353,7 +461,7 @@
 def solution(mesh):
     spread = P(("blk", "head"), None)
     return jax.shard_map(
-        local,
+        local_direct if mesh.shape["head"] == 2 else local_exchanged,
         mesh=mesh,
         in_specs=(spread,) * 5 + (P(), P()),
         out_specs=(spread,) * 3,

time: 126 us -> 151 us (1.20)
  the two profiles are of different devices: /device:TPU:11 before, /device:TPU:16 now
where the time goes in v10:
time: 151 us; the launch traced here: 150 us
  starting transfers between devices  62 us (41%)
  Pallas kernels  40.1 us (27%)
  waiting for transfers between devices  21.9 us (15%)
  other arithmetic  13.5 us (9%)
  local copies, waits for them, and re-layouts  6.52 us (4%)
  between operations  5.95 us (4%)
    ppermute x16, starting transfers between devices, shifted(): lax.ppermute(value, 'blk', [(source, source + step) for source in range(f...  54.1 us
    pallas_call x4, Pallas kernels, attention(): pl.pallas_call(functools.partial(attention_body, len(pasts), len(carried)...  31 us
    ppermute x8, waiting for transfers between devices, swapped(): return lax.ppermute(value, 'head', [(0, 1), (1, 0)])  18.8 us
    pallas_call x4, Pallas kernels, finish(): pl.pallas_call(functools.partial(finish_body, len(backs), len(carried)),...  9.18 us
    ppermute x8, starting transfers between devices, swapped(): return lax.ppermute(value, 'head', [(0, 1), (1, 0)])  7.91 us
    select_n x4, other arithmetic, swap(): jnp.where(early, jnp.where(last_block, piece, from_right), from_left)  4.93 us
    another operation x3, other arithmetic, shift(): piece = jnp.stack([keys[:, columns], values[:, columns]])  3.91 us
    select_n x4, other arithmetic, swap_back(): jnp.where(early, from_left, jnp.where(last_block, term, from_right))  3.72 us
  transfers between devices with their start and end apart: 24, of which 5 were waited for; matrix products, arithmetic and copies ran while one was open for 9% of the time, Pallas kernels for 25%

profile of v10, /device:TPU:16, one launch (start us, length us, event | category | flops | bytes accessed | tf_op | source)
XLA Modules:
  0.0 150.1 jit_solution(16526447152426206522)
XLA Ops:
  0.6 2.1 %slice_bitcast_fusion = (bf16[1,512,256]{2,1,0:T(8,128)(2,1)S(1)}, bf16[1,512,256]{2,1,0:T(8,128)(2,1)S(1)}, bf16[1,512,256]{2,1,0:T(8,128)(2,1)S(1)}, bf16[1,512,256]{2,1,0:T(8,128)(2,1)}) fusion(bf16[512,1024]{1,0:T(8,128)(2,1)} %v_ref.7), kind=kLoop, calls=%fused_computation.13 | loop fusion | bytes 2097152 | tf_op jit(solution)/shard_map/stack | solution.py:275
  2.7 0.9 slice_bitcast_fusion.1
  3.6 0.9 pad_maximum_fusion.2
  4.4 1.9 %collective-permute-start.3 = (bf16[2,512,256]{2,1,0:T(8,128)(2,1)}, bf16[2,512,256]{2,1,0:T(8,128)(2,1)S(1)}, u32[]{:S(2)}, u32[]{:S(2)}) collective-permute-start(bf16[2,512,256]{2,1,0:T(8,128)(2,1)} %pad_maximum_fusion.2), channel_id=1, source_target_pairs={{0,2},{2,4},{4,6},{6,8},{8,10},{10,12},{12,14},{14,16},{16,18},{18... | collective-permute-start | bytes 1572872 | tf_op jit(solution)/shard_map/ppermute | solution.py:258
  6.4 4.5 %collective-permute-start.2 = (bf16[2,512,256]{2,1,0:T(8,128)(2,1)}, bf16[2,512,256]{2,1,0:T(8,128)(2,1)S(1)}, u32[]{:S(2)}, u32[]{:S(2)}) collective-permute-start(bf16[2,512,256]{2,1,0:T(8,128)(2,1)} %pad_maximum_fusion.2), channel_id=1, source_target_pairs={{2,0},{4,2},{6,4},{8,6},{10,8},{12,10},{14,12},{16,14},{18,16},{20... | collective-permute-start | bytes 1572872 | tf_op jit(solution)/shard_map/ppermute | solution.py:258
  11.8 1.9 %collective-permute-start = (bf16[2,512,256]{2,1,0:T(8,128)(2,1)}, bf16[2,512,256]{2,1,0:T(8,128)(2,1)S(1)}, u32[]{:S(2)}, u32[]{:S(2)}) collective-permute-start(bf16[2,512,256]{2,1,0:T(8,128)(2,1)} %pad_maximum_fusion.1), channel_id=1, source_target_pairs={{0,2},{2,4},{4,6},{6,8},{8,10},{10,12},{12,14},{14,16},{16,18},{18... | collective-permute-start | bytes 1572872 | tf_op jit(solution)/shard_map/ppermute | solution.py:258
  13.7 4.5 %collective-permute-start.1 = (bf16[2,512,256]{2,1,0:T(8,128)(2,1)}, bf16[2,512,256]{2,1,0:T(8,128)(2,1)S(1)}, u32[]{:S(2)}, u32[]{:S(2)}) collective-permute-start(bf16[2,512,256]{2,1,0:T(8,128)(2,1)} %pad_maximum_fusion.1), channel_id=1, source_target_pairs={{2,0},{4,2},{6,4},{8,6},{10,8},{12,10},{14,12},{16,14},{18,16},{20... | collective-permute-start | bytes 1572872 | tf_op jit(solution)/shard_map/ppermute | solution.py:258
  18.3 2.2 %pad_maximum_fusion = (bf16[2,512,256]{2,1,0:T(8,128)(2,1)}, bf16[2,512,256]{2,1,0:T(8,128)(2,1)}) fusion(bf16[1,512,256]{2,1,0:T(8,128)(2,1)} %get-tuple-element.92, bf16[1,512,256]{2,1,0:T(8,128)(2,1)} %get-tuple-element.88, bf16[1,512,256]{2,1,0:T(8,128)(2,1)S(1)} %get-tuple-element.89, bf16[1,512,256]{2,1,0:T(8,128)(2,1)} %get-tuple-element.85), kind=kLoop, calls=%fused_computation.1 | loop fusion | flops 524288 | bytes 2097152 | tf_op jit(solution)/shard_map/stack | solution.py:275
  22.4 1.0 select_select_fusion.7
  23.4 1.5 collective-permute-start.4
  24.9 6.7 %collective-permute-start.7 = (bf16[2,512,256]{2,1,0:T(8,128)(2,1)}, bf16[2,512,256]{2,1,0:T(8,128)(2,1)S(1)}, u32[]{:S(2)}, u32[]{:S(2)}) collective-permute-start(bf16[2,512,256]{2,1,0:T(8,128)(2,1)} %get-tuple-element.47), channel_id=1, source_target_pairs={{0,2},{2,4},{4,6},{6,8},{8,10},{10,12},{12,14},{14,16},{16,18},{18... | collective-permute-start | bytes 1572872 | tf_op jit(solution)/shard_map/ppermute | solution.py:258
  31.6 1.9 %collective-permute-start.8 = (bf16[2,512,256]{2,1,0:T(8,128)(2,1)}, bf16[2,512,256]{2,1,0:T(8,128)(2,1)}, u32[]{:S(2)}, u32[]{:S(2)}) collective-permute-start(bf16[2,512,256]{2,1,0:T(8,128)(2,1)} %get-tuple-element.47), channel_id=1, source_target_pairs={{2,0},{4,2},{6,4},{8,6},{10,8},{12,10},{14,12},{16,14},{18,16},{20... | collective-permute-start | bytes 1572872 | tf_op jit(solution)/shard_map/ppermute | solution.py:258
  37.9 1.0 select_select_fusion.6
  39.4 0.9 convert_reduce_fusion
  40.4 3.1 %collective-permute-start.5 = (bf16[2,512,256]{2,1,0:T(8,128)(2,1)}, bf16[2,512,256]{2,1,0:T(8,128)(2,1)S(1)}, u32[]{:S(2)}, u32[]{:S(2)}) collective-permute-start(bf16[2,512,256]{2,1,0:T(8,128)(2,1)} %get-tuple-element.46), channel_id=1, source_target_pairs={{0,2},{2,4},{4,6},{6,8},{8,10},{10,12},{12,14},{14,16},{16,18},{18... | collective-permute-start | bytes 1572872 | tf_op jit(solution)/shard_map/ppermute | solution.py:258
  43.4 3.4 %collective-permute-start.6 = (bf16[2,512,256]{2,1,0:T(8,128)(2,1)}, bf16[2,512,256]{2,1,0:T(8,128)(2,1)S(1)}, u32[]{:S(2)}, u32[]{:S(2)}) collective-permute-start(bf16[2,512,256]{2,1,0:T(8,128)(2,1)} %get-tuple-element.46), channel_id=1, source_target_pairs={{2,0},{4,2},{6,4},{8,6},{10,8},{12,10},{14,12},{16,14},{18,16},{20... | collective-permute-start | bytes 1572872 | tf_op jit(solution)/shard_map/ppermute | solution.py:258
  46.9 2.1 %select_select_fusion.5 = bf16[2,512,256]{2,1,0:T(8,128)(2,1)} fusion(bf16[2,512,256]{2,1,0:T(8,128)(2,1)S(1)} %collective-permute-done.7.refs_0_, bf16[2,512,256]{2,1,0:T(8,128)(2,1)} %get-tuple-element.47, bf16[2,512,256]{2,1,0:T(8,128)(2,1)} %collective-permute-done.8.refs_1_, pred[]{:T(512)S(6)} %eq.18, pred[]{:T(512)S(6)} %eq.15), kind=kLoop, calls=%fused_computation.10 | loop fusion | flops 524288 | bytes 2097154 | tf_op jit(solution)/shard_map/jit(_where)/select_n | solution.py:284
  49.0 1.5 collective-permute-start.10
  50.4 7.8 %attention.4 = (bf16[512,2048]{1,0:T(8,128)(2,1)}, f32[512,1024]{1,0:T(8,128)}, f32[512,1024]{1,0:T(8,128)}, bf16[2,512,256]{2,1,0:T(8,128)(2,1)}) custom-call(s32[1]{0:T(128)} %constant.11.clone.1.group_ref, s32[1]{0:T(128)} %bitcast.4.which_ref, s32[1,512]{1,0:T(1,128)} %bitcast.23, bf16[512,2048]{1,0:T(8,128)(2,1)} %q_ref.7, bf16[512,1024]{1,0:T(8,128)(2,1)} %k_ref.7, ...), custom_call_target="tpu_custom_call" | custom-call | flops 1677721600 | bytes 2457600 | tf_op jit(solution)/shard_map/attention/pallas_call | solution.py:147
  58.2 1.9 %collective-permute-start.12 = (bf16[2,512,256]{2,1,0:T(8,128)(2,1)}, bf16[2,512,256]{2,1,0:T(8,128)(2,1)S(1)}, u32[]{:S(2)}, u32[]{:S(2)}) collective-permute-start(bf16[2,512,256]{2,1,0:T(8,128)(2,1)} %get-tuple-element.61), channel_id=1, source_target_pairs={{0,2},{2,4},{4,6},{6,8},{8,10},{10,12},{12,14},{14,16},{16,18},{18... | collective-permute-start | bytes 1572872 | tf_op jit(solution)/shard_map/ppermute | solution.py:258
  60.2 4.5 %collective-permute-start.13 = (bf16[2,512,256]{2,1,0:T(8,128)(2,1)}, bf16[2,512,256]{2,1,0:T(8,128)(2,1)S(1)}, u32[]{:S(2)}, u32[]{:S(2)}) collective-permute-start(bf16[2,512,256]{2,1,0:T(8,128)(2,1)} %get-tuple-element.61), channel_id=1, source_target_pairs={{2,0},{4,2},{6,4},{8,6},{10,8},{12,10},{14,12},{16,14},{18,16},{20... | collective-permute-start | bytes 1572872 | tf_op jit(solution)/shard_map/ppermute | solution.py:258
  64.8 7.7 %attention.5 = (bf16[512,2048]{1,0:T(8,128)(2,1)}, f32[512,1024]{1,0:T(8,128)}, f32[512,1024]{1,0:T(8,128)}, bf16[2,512,256]{2,1,0:T(8,128)(2,1)}) custom-call(s32[1]{0:T(128)} %constant.11.clone.1.group_ref, s32[1]{0:T(128)} %bitcast.4.which_ref, s32[1,512]{1,0:T(1,128)} %bitcast.24, ...), custom_call_target="tpu_custom_call", output_to_operand_aliasing={{0}: (11, {}), {1}: (12, {}), {2}: (13, {})} | custom-call | flops 1677721600 | bytes 2457600 | tf_op jit(solution)/shard_map/attention/pallas_call | solution.py:147
  72.5 1.9 %collective-permute-start.18 = (bf16[2,512,256]{2,1,0:T(8,128)(2,1)}, bf16[2,512,256]{2,1,0:T(8,128)(2,1)S(1)}, u32[]{:S(2)}, u32[]{:S(2)}) collective-permute-start(bf16[2,512,256]{2,1,0:T(8,128)(2,1)} %get-tuple-element.70), channel_id=1, source_target_pairs={{0,2},{2,4},{4,6},{6,8},{8,10},{10,12},{12,14},{14,16},{16,18},{18... | collective-permute-start | bytes 1572872 | tf_op jit(solution)/shard_map/ppermute | solution.py:258
  74.4 4.5 %collective-permute-start.19 = (bf16[2,512,256]{2,1,0:T(8,128)(2,1)}, bf16[2,512,256]{2,1,0:T(8,128)(2,1)S(1)}, u32[]{:S(2)}, u32[]{:S(2)}) collective-permute-start(bf16[2,512,256]{2,1,0:T(8,128)(2,1)} %get-tuple-element.70), channel_id=1, source_target_pairs={{2,0},{4,2},{6,4},{8,6},{10,8},{12,10},{14,12},{16,14},{18,16},{20... | collective-permute-start | bytes 1572872 | tf_op jit(solution)/shard_map/ppermute | solution.py:258
  79.0 0.9 select_select_fusion.4
  80.7 7.7 %attention.6 = (bf16[512,2048]{1,0:T(8,128)(2,1)}, f32[512,1024]{1,0:T(8,128)}, f32[512,1024]{1,0:T(8,128)}, bf16[2,512,256]{2,1,0:T(8,128)(2,1)}) custom-call(s32[1]{0:T(128)} %constant.11.clone.1.group_ref, s32[1]{0:T(128)} %bitcast.4.which_ref, s32[1,512]{1,0:T(1,128)} %bitcast.25, ...), custom_call_target="tpu_custom_call", output_to_operand_aliasing={{0}: (11, {}), {1}: (12, {}), {2}: (13, {})} | custom-call | flops 1677721600 | bytes 2457600 | tf_op jit(solution)/shard_map/attention/pallas_call | solution.py:147
  88.4 1.9 %collective-permute-start.16 = (bf16[2,512,256]{2,1,0:T(8,128)(2,1)}, bf16[2,512,256]{2,1,0:T(8,128)(2,1)S(1)}, u32[]{:S(2)}, u32[]{:S(2)}) collective-permute-start(bf16[2,512,256]{2,1,0:T(8,128)(2,1)} %get-tuple-element.69), channel_id=1, source_target_pairs={{0,2},{2,4},{4,6},{6,8},{8,10},{10,12},{12,14},{14,16},{16,18},{18... | collective-permute-start | bytes 1572872 | tf_op jit(solution)/shard_map/ppermute | solution.py:258
  90.4 4.7 %collective-permute-start.17 = (bf16[2,512,256]{2,1,0:T(8,128)(2,1)}, bf16[2,512,256]{2,1,0:T(8,128)(2,1)S(1)}, u32[]{:S(2)}, u32[]{:S(2)}) collective-permute-start(bf16[2,512,256]{2,1,0:T(8,128)(2,1)} %get-tuple-element.69), channel_id=1, source_target_pairs={{2,0},{4,2},{6,4},{8,6},{10,8},{12,10},{14,12},{16,14},{18,16},{20... | collective-permute-start | bytes 1572872 | tf_op jit(solution)/shard_map/ppermute | solution.py:258
  95.1 0.9 select_select_fusion.3
  96.0 1.1 collective-permute-start.23
  97.2 7.8 %attention.7 = (bf16[512,2048]{1,0:T(8,128)(2,1)}, f32[512,1024]{1,0:T(8,128)}, f32[512,1024]{1,0:T(8,128)}, bf16[2,512,256]{2,1,0:T(8,128)(2,1)}) custom-call(s32[1]{0:T(128)} %constant.11.clone.1.group_ref, s32[1]{0:T(128)} %bitcast.4.which_ref, s32[1,512]{1,0:T(1,128)} %bitcast.26, ...), custom_call_target="tpu_custom_call", output_to_operand_aliasing={{0}: (11, {}), {1}: (12, {}), {2}: (13, {})} | custom-call | flops 1677721600 | bytes 2457600 | tf_op jit(solution)/shard_map/attention/pallas_call | solution.py:147
  105.1 2.1 %collective-permute-start.14 = (bf16[2,512,256]{2,1,0:T(8,128)(2,1)}, bf16[2,512,256]{2,1,0:T(8,128)(2,1)S(1)}, u32[]{:S(2)}, u32[]{:S(2)}) collective-permute-start(bf16[2,512,256]{2,1,0:T(8,128)(2,1)} %get-tuple-element.68), channel_id=1, source_target_pairs={{0,2},{2,4},{4,6},{6,8},{8,10},{10,12},{12,14},{14,16},{16,18},{18... | collective-permute-start | bytes 1572872 | tf_op jit(solution)/shard_map/ppermute | solution.py:258
  107.1 4.5 %collective-permute-start.15 = (bf16[2,512,256]{2,1,0:T(8,128)(2,1)}, bf16[2,512,256]{2,1,0:T(8,128)(2,1)S(1)}, u32[]{:S(2)}, u32[]{:S(2)}) collective-permute-start(bf16[2,512,256]{2,1,0:T(8,128)(2,1)} %get-tuple-element.68), channel_id=1, source_target_pairs={{2,0},{4,2},{6,4},{8,6},{10,8},{12,10},{14,12},{16,14},{18,16},{20... | collective-permute-start | bytes 1572872 | tf_op jit(solution)/shard_map/ppermute | solution.py:258
  111.7 0.9 select_select_fusion.2
  112.6 0.9 collective-permute-start.22
  113.4 0.9 select_select_fusion.1
  114.4 1.2 collective-permute-start.21
  115.6 1.4 collective-permute-done.14.refs_0_
  116.9 1.8 %collective-permute-done.15.refs_1_ = bf16[2,512,256]{2,1,0:T(8,128)(2,1)S(1)} collective-permute-done((bf16[2,512,256]{2,1,0:T(8,128)(2,1)}, bf16[2,512,256]{2,1,0:T(8,128)(2,1)S(1)}, u32[]{:S(2)}, u32[]{:S(2)}) %collective-permute-start.15) | collective-permute-done | bytes 524320 | tf_op jit(solution)/shard_map/ppermute | solution.py:258
  118.7 1.0 select_select_fusion
  119.7 0.9 collective-permute-start.20
  120.5 2.3 %finish.4 = (bf16[512,1024]{1,0:T(8,128)(2,1)}, bf16[512,1024]{1,0:T(8,128)(2,1)}) custom-call(s32[1]{0:T(128)} %constant.11.clone.1.group_ref, s32[1]{0:T(128)} %bitcast.14.which_ref, f32[512,1024]{1,0:T(8,128)} %get-tuple-element.66.dk_ref, f32[512,1024]{1,0:T(8,128)} %get-tuple-element.67.dv_ref, bf16[2,512,256]{2,1,0:T(8,128)(2,1)} %copy-done.6, ...), custom_call_target="tpu_custom_call" | custom-call | flops 524288 | bytes 2097152 | tf_op jit(solution)/shard_map/finish/pallas_call | solution.py:202
  122.8 4.9 %collective-permute-done.22.refs_2_ = bf16[2,512,256]{2,1,0:T(8,128)(2,1)} collective-permute-done((bf16[2,512,256]{2,1,0:T(8,128)(2,1)}, bf16[2,512,256]{2,1,0:T(8,128)(2,1)}, u32[]{:S(2)}, u32[]{:S(2)}) %collective-permute-start.22) | collective-permute-done | bytes 524320 | tf_op jit(solution)/shard_map/ppermute | solution.py:254
  127.8 2.3 %finish.5 = (bf16[512,1024]{1,0:T(8,128)(2,1)}, bf16[512,1024]{1,0:T(8,128)(2,1)}) custom-call(s32[1]{0:T(128)} %constant.11.clone.1.group_ref, s32[1]{0:T(128)} %bitcast.14.which_ref, f32[512,1024]{1,0:T(8,128)} %get-tuple-element.66.dk_ref, f32[512,1024]{1,0:T(8,128)} %get-tuple-element.67.dv_ref, ...), custom_call_target="tpu_custom_call", output_to_operand_aliasing={{0}: (7, {}), {1}: (8, {})} | custom-call | flops 524288 | bytes 2097152 | tf_op jit(solution)/shard_map/finish/pallas_call | solution.py:202
  130.1 8.8 %collective-permute-done.21.refs_2_ = bf16[2,512,256]{2,1,0:T(8,128)(2,1)S(1)} collective-permute-done((bf16[2,512,256]{2,1,0:T(8,128)(2,1)}, bf16[2,512,256]{2,1,0:T(8,128)(2,1)S(1)}, u32[]{:S(2)}, u32[]{:S(2)}) %collective-permute-start.21) | collective-permute-done | bytes 524320 | tf_op jit(solution)/shard_map/ppermute | solution.py:254
  139.7 2.3 %finish.6 = (bf16[512,1024]{1,0:T(8,128)(2,1)}, bf16[512,1024]{1,0:T(8,128)(2,1)}) custom-call(s32[1]{0:T(128)} %constant.11.clone.1.group_ref, s32[1]{0:T(128)} %bitcast.14.which_ref, f32[512,1024]{1,0:T(8,128)} %get-tuple-element.66.dk_ref, f32[512,1024]{1,0:T(8,128)} %get-tuple-element.67.dv_ref, ...), custom_call_target="tpu_custom_call", output_to_operand_aliasing={{0}: (7, {}), {1}: (8, {})} | custom-call | flops 524288 | bytes 2097152 | tf_op jit(solution)/shard_map/finish/pallas_call | solution.py:202
  142.0 5.0 %collective-permute-done.20.refs_2_ = bf16[2,512,256]{2,1,0:T(8,128)(2,1)S(1)} collective-permute-done((bf16[2,512,256]{2,1,0:T(8,128)(2,1)}, bf16[2,512,256]{2,1,0:T(8,128)(2,1)S(1)}, u32[]{:S(2)}, u32[]{:S(2)}) %collective-permute-start.20) | collective-permute-done | bytes 524320 | tf_op jit(solution)/shard_map/ppermute | solution.py:254
  147.8 2.3 %finish.7 = (bf16[512,1024]{1,0:T(8,128)(2,1)}, bf16[512,1024]{1,0:T(8,128)(2,1)}) custom-call(s32[1]{0:T(128)} %constant.11.clone.1.group_ref, s32[1]{0:T(128)} %bitcast.14.which_ref, f32[512,1024]{1,0:T(8,128)} %get-tuple-element.66.dk_ref, f32[512,1024]{1,0:T(8,128)} %get-tuple-element.67.dv_ref, ...), custom_call_target="tpu_custom_call", output_to_operand_aliasing={{0}: (7, {}), {1}: (8, {})} | custom-call | flops 524288 | bytes 2097152 | tf_op jit(solution)/shard_map/finish/pallas_call | solution.py:202
  (77 shorter events, 5.4 us)
Async XLA Ops:
  0.6 2.1 %copy-start = (bf16[512,1024]{1,0:T(8,128)(2,1)S(1)}, bf16[512,1024]{1,0:T(8,128)(2,1)}, u32[]{:S(2)}) copy-start(bf16[512,1024]{1,0:T(8,128)(2,1)} %k_ref.7) | copy-start | bytes 3145732
  2.7 15.5 %copy-start.24 = (s32[32]{0:T(128)S(1)}, s32[32]{0:T(128)}, u32[]{:S(2)}) copy-start(s32[32]{0:T(128)} %param.13) | copy-start | bytes 388
  4.4 17.9 %collective-permute-start.3 = (bf16[2,512,256]{2,1,0:T(8,128)(2,1)}, bf16[2,512,256]{2,1,0:T(8,128)(2,1)S(1)}, u32[]{:S(2)}, u32[]{:S(2)}) collective-permute-start(bf16[2,512,256]{2,1,0:T(8,128)(2,1)} %pad_maximum_fusion.2), channel_id=1, source_target_pairs={{0,2},{2,4},{4,6},{6,8},{8,10},{10,12},{12,14},{14,16},{16,18},{18... | collective-permute-start | bytes 1572872 | tf_op jit(solution)/shard_map/ppermute | solution.py:258
  6.4 16.0 %collective-permute-start.2 = (bf16[2,512,256]{2,1,0:T(8,128)(2,1)}, bf16[2,512,256]{2,1,0:T(8,128)(2,1)S(1)}, u32[]{:S(2)}, u32[]{:S(2)}) collective-permute-start(bf16[2,512,256]{2,1,0:T(8,128)(2,1)} %pad_maximum_fusion.2), channel_id=1, source_target_pairs={{2,0},{4,2},{6,4},{8,6},{10,8},{12,10},{14,12},{16,14},{18,16},{20... | collective-permute-start | bytes 1572872 | tf_op jit(solution)/shard_map/ppermute | solution.py:258
  11.8 26.1 %collective-permute-start = (bf16[2,512,256]{2,1,0:T(8,128)(2,1)}, bf16[2,512,256]{2,1,0:T(8,128)(2,1)S(1)}, u32[]{:S(2)}, u32[]{:S(2)}) collective-permute-start(bf16[2,512,256]{2,1,0:T(8,128)(2,1)} %pad_maximum_fusion.1), channel_id=1, source_target_pairs={{0,2},{2,4},{4,6},{6,8},{8,10},{10,12},{12,14},{14,16},{16,18},{18... | collective-permute-start | bytes 1572872 | tf_op jit(solution)/shard_map/ppermute | solution.py:258
  13.7 24.2 %collective-permute-start.1 = (bf16[2,512,256]{2,1,0:T(8,128)(2,1)}, bf16[2,512,256]{2,1,0:T(8,128)(2,1)S(1)}, u32[]{:S(2)}, u32[]{:S(2)}) collective-permute-start(bf16[2,512,256]{2,1,0:T(8,128)(2,1)} %pad_maximum_fusion.1), channel_id=1, source_target_pairs={{2,0},{4,2},{6,4},{8,6},{10,8},{12,10},{14,12},{16,14},{18,16},{20... | collective-permute-start | bytes 1572872 | tf_op jit(solution)/shard_map/ppermute | solution.py:258
  18.3 19.5 %copy-start.23 = (s32[16384]{0:T(1024)S(1)}, s32[16384]{0:T(1024)}, u32[]{:S(2)}) copy-start(s32[16384]{0:T(1024)} %param.12) | copy-start | bytes 196612
  22.4 16.5 %copy-start.3 = (bf16[2,512,256]{2,1,0:T(8,128)(2,1)}, bf16[2,512,256]{2,1,0:T(8,128)(2,1)S(1)}, u32[]{:S(2)}) copy-start(bf16[2,512,256]{2,1,0:T(8,128)(2,1)S(1)} %collective-permute-done.3.refs_0_) | copy-start | bytes 1572868
  22.4 16.5 %copy-start.4 = (bf16[2,512,256]{2,1,0:T(8,128)(2,1)}, bf16[2,512,256]{2,1,0:T(8,128)(2,1)S(1)}, u32[]{:S(2)}) copy-start(bf16[2,512,256]{2,1,0:T(8,128)(2,1)S(1)} %collective-permute-done.2.refs_1_) | copy-start | bytes 1572868
  23.4 17.0 %collective-permute-start.4 = (bf16[2,512,256]{2,1,0:T(8,128)(2,1)}, bf16[2,512,256]{2,1,0:T(8,128)(2,1)}, u32[]{:S(2)}, u32[]{:S(2)}) collective-permute-start(bf16[2,512,256]{2,1,0:T(8,128)(2,1)} %select_select_fusion.7), channel_id=1, source_target_pairs={{0,1},{1,0},{2,3},{3,2},{4,5},{5,4},{6,7},{7,6},{8,9},{9,8},{10,11... | collective-permute-start | bytes 1572872 | tf_op jit(solution)/shard_map/ppermute | solution.py:254
  24.9 22.0 %collective-permute-start.7 = (bf16[2,512,256]{2,1,0:T(8,128)(2,1)}, bf16[2,512,256]{2,1,0:T(8,128)(2,1)S(1)}, u32[]{:S(2)}, u32[]{:S(2)}) collective-permute-start(bf16[2,512,256]{2,1,0:T(8,128)(2,1)} %get-tuple-element.47), channel_id=1, source_target_pairs={{0,2},{2,4},{4,6},{6,8},{8,10},{10,12},{12,14},{14,16},{16,18},{18... | collective-permute-start | bytes 1572872 | tf_op jit(solution)/shard_map/ppermute | solution.py:258
  31.6 15.3 %collective-permute-start.8 = (bf16[2,512,256]{2,1,0:T(8,128)(2,1)}, bf16[2,512,256]{2,1,0:T(8,128)(2,1)}, u32[]{:S(2)}, u32[]{:S(2)}) collective-permute-start(bf16[2,512,256]{2,1,0:T(8,128)(2,1)} %get-tuple-element.47), channel_id=1, source_target_pairs={{2,0},{4,2},{6,4},{8,6},{10,8},{12,10},{14,12},{16,14},{18,16},{20... | collective-permute-start | bytes 1572872 | tf_op jit(solution)/shard_map/ppermute | solution.py:258
  37.9 11.1 %copy-start.1 = (bf16[2,512,256]{2,1,0:T(8,128)(2,1)}, bf16[2,512,256]{2,1,0:T(8,128)(2,1)S(1)}, u32[]{:S(2)}) copy-start(bf16[2,512,256]{2,1,0:T(8,128)(2,1)S(1)} %collective-permute-done.refs_0_) | copy-start | bytes 1572868
  37.9 11.1 %copy-start.2 = (bf16[2,512,256]{2,1,0:T(8,128)(2,1)}, bf16[2,512,256]{2,1,0:T(8,128)(2,1)S(1)}, u32[]{:S(2)}) copy-start(bf16[2,512,256]{2,1,0:T(8,128)(2,1)S(1)} %collective-permute-done.1.refs_1_) | copy-start | bytes 1572868
  38.9 21.3 %collective-permute-start.11 = (bf16[2,512,256]{2,1,0:T(8,128)(2,1)}, bf16[2,512,256]{2,1,0:T(8,128)(2,1)S(1)}, u32[]{:S(2)}, u32[]{:S(2)}) collective-permute-start(bf16[2,512,256]{2,1,0:T(8,128)(2,1)} %select_select_fusion.6), channel_id=1, source_target_pairs={{0,1},{1,0},{2,3},{3,2},{4,5},{5,4},{6,7},{7,6},{8,9},{9,8},{10,11... | collective-permute-start | bytes 1572872 | tf_op jit(solution)/shard_map/ppermute | solution.py:254
  40.4 32.1 %collective-permute-start.5 = (bf16[2,512,256]{2,1,0:T(8,128)(2,1)}, bf16[2,512,256]{2,1,0:T(8,128)(2,1)S(1)}, u32[]{:S(2)}, u32[]{:S(2)}) collective-permute-start(bf16[2,512,256]{2,1,0:T(8,128)(2,1)} %get-tuple-element.46), channel_id=1, source_target_pairs={{0,2},{2,4},{4,6},{6,8},{8,10},{10,12},{12,14},{14,16},{16,18},{18... | collective-permute-start | bytes 1572872 | tf_op jit(solution)/shard_map/ppermute | solution.py:258
  43.4 31.0 %collective-permute-start.6 = (bf16[2,512,256]{2,1,0:T(8,128)(2,1)}, bf16[2,512,256]{2,1,0:T(8,128)(2,1)S(1)}, u32[]{:S(2)}, u32[]{:S(2)}) collective-permute-start(bf16[2,512,256]{2,1,0:T(8,128)(2,1)} %get-tuple-element.46), channel_id=1, source_target_pairs={{2,0},{4,2},{6,4},{8,6},{10,8},{12,10},{14,12},{16,14},{18,16},{20... | collective-permute-start | bytes 1572872 | tf_op jit(solution)/shard_map/ppermute | solution.py:258
  46.8 11.4 %copy-start.5 = (bf16[2,512,256]{2,1,0:T(8,128)(2,1)}, bf16[2,512,256]{2,1,0:T(8,128)(2,1)S(1)}, u32[]{:S(2)}) copy-start(bf16[2,512,256]{2,1,0:T(8,128)(2,1)S(1)} %collective-permute-done.7.refs_0_) | copy-start | bytes 1572868
  49.0 30.9 %collective-permute-start.10 = (bf16[2,512,256]{2,1,0:T(8,128)(2,1)}, bf16[2,512,256]{2,1,0:T(8,128)(2,1)S(1)}, u32[]{:S(2)}, u32[]{:S(2)}) collective-permute-start(bf16[2,512,256]{2,1,0:T(8,128)(2,1)} %select_select_fusion.5), channel_id=1, source_target_pairs={{0,1},{1,0},{2,3},{3,2},{4,5},{5,4},{6,7},{7,6},{8,9},{9,8},{10,11... | collective-permute-start | bytes 1572872 | tf_op jit(solution)/shard_map/ppermute | solution.py:254
  58.2 30.1 %collective-permute-start.12 = (bf16[2,512,256]{2,1,0:T(8,128)(2,1)}, bf16[2,512,256]{2,1,0:T(8,128)(2,1)S(1)}, u32[]{:S(2)}, u32[]{:S(2)}) collective-permute-start(bf16[2,512,256]{2,1,0:T(8,128)(2,1)} %get-tuple-element.61), channel_id=1, source_target_pairs={{0,2},{2,4},{4,6},{6,8},{8,10},{10,12},{12,14},{14,16},{16,18},{18... | collective-permute-start | bytes 1572872 | tf_op jit(solution)/shard_map/ppermute | solution.py:258
  60.2 4.6 %copy-start.17 = (bf16[2,512,256]{2,1,0:T(8,128)(2,1)}, bf16[2,512,256]{2,1,0:T(8,128)(2,1)S(1)}, u32[]{:S(2)}) copy-start(bf16[2,512,256]{2,1,0:T(8,128)(2,1)S(1)} %collective-permute-done.11.refs_2_) | copy-start | bytes 1572868
  60.2 30.1 %collective-permute-start.13 = (bf16[2,512,256]{2,1,0:T(8,128)(2,1)}, bf16[2,512,256]{2,1,0:T(8,128)(2,1)S(1)}, u32[]{:S(2)}, u32[]{:S(2)}) collective-permute-start(bf16[2,512,256]{2,1,0:T(8,128)(2,1)} %get-tuple-element.61), channel_id=1, source_target_pairs={{2,0},{4,2},{6,4},{8,6},{10,8},{12,10},{14,12},{16,14},{18,16},{20... | collective-permute-start | bytes 1572872 | tf_op jit(solution)/shard_map/ppermute | solution.py:258
  72.4 15.9 %copy-start.10 = (bf16[2,512,256]{2,1,0:T(8,128)(2,1)}, bf16[2,512,256]{2,1,0:T(8,128)(2,1)S(1)}, u32[]{:S(2)}) copy-start(bf16[2,512,256]{2,1,0:T(8,128)(2,1)S(1)} %collective-permute-done.5.refs_0_) | copy-start | bytes 1572868
  72.5 23.6 %collective-permute-start.18 = (bf16[2,512,256]{2,1,0:T(8,128)(2,1)}, bf16[2,512,256]{2,1,0:T(8,128)(2,1)S(1)}, u32[]{:S(2)}, u32[]{:S(2)}) collective-permute-start(bf16[2,512,256]{2,1,0:T(8,128)(2,1)} %get-tuple-element.70), channel_id=1, source_target_pairs={{0,2},{2,4},{4,6},{6,8},{8,10},{10,12},{12,14},{14,16},{16,18},{18... | collective-permute-start | bytes 1572872 | tf_op jit(solution)/shard_map/ppermute | solution.py:258
  74.4 14.0 %copy-start.11 = (bf16[2,512,256]{2,1,0:T(8,128)(2,1)}, bf16[2,512,256]{2,1,0:T(8,128)(2,1)S(1)}, u32[]{:S(2)}) copy-start(bf16[2,512,256]{2,1,0:T(8,128)(2,1)S(1)} %collective-permute-done.6.refs_1_) | copy-start | bytes 1572868
  74.4 22.8 %collective-permute-start.19 = (bf16[2,512,256]{2,1,0:T(8,128)(2,1)}, bf16[2,512,256]{2,1,0:T(8,128)(2,1)S(1)}, u32[]{:S(2)}, u32[]{:S(2)}) collective-permute-start(bf16[2,512,256]{2,1,0:T(8,128)(2,1)} %get-tuple-element.70), channel_id=1, source_target_pairs={{2,0},{4,2},{6,4},{8,6},{10,8},{12,10},{14,12},{16,14},{18,16},{20... | collective-permute-start | bytes 1572872 | tf_op jit(solution)/shard_map/ppermute | solution.py:258
  79.8 0.9 copy-start.16
  79.8 17.3 %collective-permute-start.9 = (bf16[2,512,256]{2,1,0:T(8,128)(2,1)}, bf16[2,512,256]{2,1,0:T(8,128)(2,1)}, u32[]{:S(2)}, u32[]{:S(2)}) collective-permute-start(bf16[2,512,256]{2,1,0:T(8,128)(2,1)} %select_select_fusion.4), channel_id=1, source_target_pairs={{0,1},{1,0},{2,3},{3,2},{4,5},{5,4},{6,7},{7,6},{8,9},{9,8},{10,11... | collective-permute-start | bytes 1572872 | tf_op jit(solution)/shard_map/ppermute | solution.py:254
  88.4 16.6 %copy-start.6 = (bf16[2,512,256]{2,1,0:T(8,128)(2,1)}, bf16[2,512,256]{2,1,0:T(8,128)(2,1)S(1)}, u32[]{:S(2)}) copy-start(bf16[2,512,256]{2,1,0:T(8,128)(2,1)S(1)} %collective-permute-done.12.refs_0_) | copy-start | bytes 1572868
  88.4 24.2 %collective-permute-start.16 = (bf16[2,512,256]{2,1,0:T(8,128)(2,1)}, bf16[2,512,256]{2,1,0:T(8,128)(2,1)S(1)}, u32[]{:S(2)}, u32[]{:S(2)}) collective-permute-start(bf16[2,512,256]{2,1,0:T(8,128)(2,1)} %get-tuple-element.69), channel_id=1, source_target_pairs={{0,2},{2,4},{4,6},{6,8},{8,10},{10,12},{12,14},{14,16},{16,18},{18... | collective-permute-start | bytes 1572872 | tf_op jit(solution)/shard_map/ppermute | solution.py:258
  90.3 14.7 %copy-start.7 = (bf16[2,512,256]{2,1,0:T(8,128)(2,1)}, bf16[2,512,256]{2,1,0:T(8,128)(2,1)S(1)}, u32[]{:S(2)}) copy-start(bf16[2,512,256]{2,1,0:T(8,128)(2,1)S(1)} %collective-permute-done.13.refs_1_) | copy-start | bytes 1572868
  90.4 23.1 %collective-permute-start.17 = (bf16[2,512,256]{2,1,0:T(8,128)(2,1)}, bf16[2,512,256]{2,1,0:T(8,128)(2,1)S(1)}, u32[]{:S(2)}, u32[]{:S(2)}) collective-permute-start(bf16[2,512,256]{2,1,0:T(8,128)(2,1)} %get-tuple-element.69), channel_id=1, source_target_pairs={{2,0},{4,2},{6,4},{8,6},{10,8},{12,10},{14,12},{16,14},{18,16},{20... | collective-permute-start | bytes 1572872 | tf_op jit(solution)/shard_map/ppermute | solution.py:258
  96.0 15.7 %copy-start.20 = (bf16[2,512,256]{2,1,0:T(8,128)(2,1)S(1)}, bf16[2,512,256]{2,1,0:T(8,128)(2,1)}, u32[]{:S(2)}) copy-start(bf16[2,512,256]{2,1,0:T(8,128)(2,1)} %get-tuple-element.70) | copy-start | bytes 1572868
  96.0 15.7 %copy-start.8 = (bf16[2,512,256]{2,1,0:T(8,128)(2,1)}, bf16[2,512,256]{2,1,0:T(8,128)(2,1)S(1)}, u32[]{:S(2)}) copy-start(bf16[2,512,256]{2,1,0:T(8,128)(2,1)S(1)} %collective-permute-done.18.refs_0_) | copy-start | bytes 1572868
  96.0 24.5 %collective-permute-start.23 = (bf16[2,512,256]{2,1,0:T(8,128)(2,1)}, bf16[2,512,256]{2,1,0:T(8,128)(2,1)}, u32[]{:S(2)}, u32[]{:S(2)}) collective-permute-start(bf16[2,512,256]{2,1,0:T(8,128)(2,1)} %select_select_fusion.3), channel_id=1, source_target_pairs={{0,1},{1,0},{2,3},{3,2},{4,5},{5,4},{6,7},{7,6},{8,9},{9,8},{10,11... | collective-permute-start | bytes 1572872 | tf_op jit(solution)/shard_map/ppermute | solution.py:254
  97.2 14.5 %copy-start.9 = (bf16[2,512,256]{2,1,0:T(8,128)(2,1)}, bf16[2,512,256]{2,1,0:T(8,128)(2,1)S(1)}, u32[]{:S(2)}) copy-start(bf16[2,512,256]{2,1,0:T(8,128)(2,1)S(1)} %collective-permute-done.19.refs_1_) | copy-start | bytes 1572868
  105.1 8.4 %copy-start.21 = (bf16[2,512,256]{2,1,0:T(8,128)(2,1)S(1)}, bf16[2,512,256]{2,1,0:T(8,128)(2,1)}, u32[]{:S(2)}) copy-start(bf16[2,512,256]{2,1,0:T(8,128)(2,1)} %get-tuple-element.69) | copy-start | bytes 1572868
  105.1 13.6 %copy-start.22 = (bf16[2,512,256]{2,1,0:T(8,128)(2,1)S(1)}, bf16[2,512,256]{2,1,0:T(8,128)(2,1)}, u32[]{:S(2)}) copy-start(bf16[2,512,256]{2,1,0:T(8,128)(2,1)} %get-tuple-element.68) | copy-start | bytes 1572868
  105.1 11.8 %collective-permute-start.14 = (bf16[2,512,256]{2,1,0:T(8,128)(2,1)}, bf16[2,512,256]{2,1,0:T(8,128)(2,1)S(1)}, u32[]{:S(2)}, u32[]{:S(2)}) collective-permute-start(bf16[2,512,256]{2,1,0:T(8,128)(2,1)} %get-tuple-element.68), channel_id=1, source_target_pairs={{0,2},{2,4},{4,6},{6,8},{8,10},{10,12},{12,14},{14,16},{16,18},{18... | collective-permute-start | bytes 1572872 | tf_op jit(solution)/shard_map/ppermute | solution.py:258
  107.1 11.5 %collective-permute-start.15 = (bf16[2,512,256]{2,1,0:T(8,128)(2,1)}, bf16[2,512,256]{2,1,0:T(8,128)(2,1)S(1)}, u32[]{:S(2)}, u32[]{:S(2)}) collective-permute-start(bf16[2,512,256]{2,1,0:T(8,128)(2,1)} %get-tuple-element.68), channel_id=1, source_target_pairs={{2,0},{4,2},{6,4},{8,6},{10,8},{12,10},{14,12},{16,14},{18,16},{20... | collective-permute-start | bytes 1572872 | tf_op jit(solution)/shard_map/ppermute | solution.py:258
  112.6 7.1 %copy-start.12 = (bf16[2,512,256]{2,1,0:T(8,128)(2,1)}, bf16[2,512,256]{2,1,0:T(8,128)(2,1)S(1)}, u32[]{:S(2)}) copy-start(bf16[2,512,256]{2,1,0:T(8,128)(2,1)S(1)} %collective-permute-done.16.refs_0_) | copy-start | bytes 1572868
  112.6 15.2 %collective-permute-start.22 = (bf16[2,512,256]{2,1,0:T(8,128)(2,1)}, bf16[2,512,256]{2,1,0:T(8,128)(2,1)}, u32[]{:S(2)}, u32[]{:S(2)}) collective-permute-start(bf16[2,512,256]{2,1,0:T(8,128)(2,1)} %select_select_fusion.2), channel_id=1, source_target_pairs={{0,1},{1,0},{2,3},{3,2},{4,5},{5,4},{6,7},{7,6},{8,9},{9,8},{10,11... | collective-permute-start | bytes 1572872 | tf_op jit(solution)/shard_map/ppermute | solution.py:254
  113.4 6.2 %copy-start.13 = (bf16[2,512,256]{2,1,0:T(8,128)(2,1)}, bf16[2,512,256]{2,1,0:T(8,128)(2,1)S(1)}, u32[]{:S(2)}) copy-start(bf16[2,512,256]{2,1,0:T(8,128)(2,1)S(1)} %collective-permute-done.17.refs_1_) | copy-start | bytes 1572868
  114.4 24.5 %collective-permute-start.21 = (bf16[2,512,256]{2,1,0:T(8,128)(2,1)}, bf16[2,512,256]{2,1,0:T(8,128)(2,1)S(1)}, u32[]{:S(2)}, u32[]{:S(2)}) collective-permute-start(bf16[2,512,256]{2,1,0:T(8,128)(2,1)} %select_select_fusion.1), channel_id=1, source_target_pairs={{0,1},{1,0},{2,3},{3,2},{4,5},{5,4},{6,7},{7,6},{8,9},{9,8},{10,11... | collective-permute-start | bytes 1572872 | tf_op jit(solution)/shard_map/ppermute | solution.py:254
  116.9 5.9 %copy-start.14 = (bf16[2,512,256]{2,1,0:T(8,128)(2,1)}, bf16[2,512,256]{2,1,0:T(8,128)(2,1)S(1)}, u32[]{:S(2)}) copy-start(bf16[2,512,256]{2,1,0:T(8,128)(2,1)S(1)} %collective-permute-done.14.refs_0_) | copy-start | bytes 1572868
  118.7 4.1 %copy-start.15 = (bf16[2,512,256]{2,1,0:T(8,128)(2,1)}, bf16[2,512,256]{2,1,0:T(8,128)(2,1)S(1)}, u32[]{:S(2)}) copy-start(bf16[2,512,256]{2,1,0:T(8,128)(2,1)S(1)} %collective-permute-done.15.refs_1_) | copy-start | bytes 1572868
  119.7 27.3 %collective-permute-start.20 = (bf16[2,512,256]{2,1,0:T(8,128)(2,1)}, bf16[2,512,256]{2,1,0:T(8,128)(2,1)S(1)}, u32[]{:S(2)}, u32[]{:S(2)}) collective-permute-start(bf16[2,512,256]{2,1,0:T(8,128)(2,1)} %select_select_fusion), channel_id=1, source_target_pairs={{0,1},{1,0},{2,3},{3,2},{4,5},{5,4},{6,7},{7,6},{8,9},{9,8},{10,11... | collective-permute-start | bytes 1572872 | tf_op jit(solution)/shard_map/ppermute | solution.py:254
  147.0 0.8 copy-start.18
  (1 other events, 0.8 us)

commit v11 on v6

--- a/solution.py
+++ b/solution.py
@@ -13,7 +13,7 @@
 CHUNKS = 2
 TILE = 128
 STRIP = 64
-VMEM_BYTES = 60 * 1024 * 1024
+VMEM_BYTES = 24 * 1024 * 1024
 
 
 def dot(left, right, left_dim, right_dim):

time: 126 us -> 134 us (1.063)
  local copies, waits for them, and re-layouts: 3.97 us -> 21.9 us
  Pallas kernels: 46.1 us -> 32.9 us
  waiting for transfers between devices: 30 us -> 24.2 us
  starting transfers between devices: 30.1 us -> 34.5 us
  other arithmetic: 11.1 us -> 15.1 us
    unnamed x16 -> x106, local copies, waits for them, and re-layouts: 3.22 us -> 21.2 us
    pallas_call x2, Pallas kernels: 9.73 us -> 3.88 us  [arrange(): pl.pallas_call(arrange_body, grid=(groups, per_piece), in_specs=[query_sp...]
    ppermute x8, waiting for transfers between devices: 18.4 us -> 14.2 us  [turned(): return lax.ppermute(value, 'head', pairs)]
    pallas_call x4, Pallas kernels: 7.96 us -> 3.9 us  [finish(): pl.pallas_call(functools.partial(finish_body, len(carried)), grid_spec=pl...]
    select_n x4, other arithmetic: 2.7 us -> 6.03 us  [pick(): result = jnp.where(index == place, items[place], result)]
    pallas_call x4, Pallas kernels: 28.4 us -> 25.1 us  [attention(): pl.pallas_call(functools.partial(attention_body, len(carried)), grid_spec...]
    ppermute x8, starting transfers between devices: 3.92 us -> 6.66 us  [turned(): return lax.ppermute(value, 'head', pairs)]
    ppermute x8, waiting for transfers between devices: 11.6 us -> 9.95 us  [shifted(): lax.ppermute(value, 'blk', [(source, source + step) for source in range(f...]
  transfers between devices with their start and end apart: 16 -> 16, of which waited for: 8 -> 8; matrix products, arithmetic and copies ran while one was open for 8% -> 10% of each run, Pallas kernels for 35% -> 24%
where the time goes in v11:
time: 134 us; the launch traced here: 132 us
  starting transfers between devices  34.5 us (26%)
  Pallas kernels  32.9 us (25%)
  waiting for transfers between devices  24.2 us (18%)
  local copies, waits for them, and re-layouts  21.9 us (16%)
  other arithmetic  15.1 us (11%)
  between operations  3.64 us (3%)
    ppermute x8, starting transfers between devices, shifted(): lax.ppermute(value, 'blk', [(source, source + step) for source in range(f...  27.8 us
    pallas_call x4, Pallas kernels, attention(): pl.pallas_call(functools.partial(attention_body, len(carried)), grid_spec...  25.1 us
    unnamed x106, local copies, waits for them, and re-layouts  21.2 us
    ppermute x8, waiting for transfers between devices, turned(): return lax.ppermute(value, 'head', pairs)  14.2 us
    ppermute x8, waiting for transfers between devices, shifted(): lax.ppermute(value, 'blk', [(source, source + step) for source in range(f...  9.95 us
    ppermute x8, starting transfers between devices, turned(): return lax.ppermute(value, 'head', pairs)  6.66 us
    select_n x4, other arithmetic, pick(): result = jnp.where(index == place, items[place], result)  6.03 us
    pallas_call x4, Pallas kernels, finish(): pl.pallas_call(functools.partial(finish_body, len(carried)), grid_spec=pl...  3.9 us
  transfers between devices with their start and end apart: 16, of which 8 were waited for; matrix products, arithmetic and copies ran while one was open for 10% of the time, Pallas kernels for 24%

profile of v11, /device:TPU:11, one launch (start us, length us, event | category | flops | bytes accessed | tf_op | source)
XLA Modules:
  0.0 132.3 jit_solution(2166961141576607934)
XLA Ops:
  0.6 2.4 %select_bitcast_fusion = (bf16[1,512,256]{2,1,0:T(8,128)(2,1)S(1)}, bf16[1,512,256]{2,1,0:T(8,128)(2,1)S(1)}, bf16[1,512,256]{2,1,0:T(8,128)(2,1)S(1)}, bf16[1,5...) fusion(pred[]{:T(512)S(6)} %eq.22, ...), kind=kLoop, calls=%fused_computation.25 | loop fusion | flops 1048576 | bytes 4194306 | tf_op jit(solution)/shard_map/stack | solution.py:302
  3.4 0.8 pad_maximum_fusion
  4.3 1.2 collective-permute-start
  7.4 1.6 %copy-done.2 = bf16[512,2048]{1,0:T(8,128)(2,1)S(1)} copy-done((bf16[512,2048]{1,0:T(8,128)(2,1)S(1)}, bf16[512,2048]{1,0:T(8,128)(2,1)}, u32[]{:S(2)}) %copy-start.2) | copy-done | bytes 2097176
  9.0 1.6 %copy-done.4 = bf16[512,2048]{1,0:T(8,128)(2,1)S(1)} copy-done((bf16[512,2048]{1,0:T(8,128)(2,1)S(1)}, bf16[512,2048]{1,0:T(8,128)(2,1)}, u32[]{:S(2)}) %copy-start.4) | copy-done | bytes 2097176
  10.6 1.6 %copy-done.6 = bf16[512,2048]{1,0:T(8,128)(2,1)S(1)} copy-done((bf16[512,2048]{1,0:T(8,128)(2,1)S(1)}, bf16[512,2048]{1,0:T(8,128)(2,1)}, u32[]{:S(2)}) %copy-start.6) | copy-done | bytes 2097176
  12.2 1.9 %arrange.3 = (bf16[4,1024,128]{2,1,0:T(8,128)(2,1)S(1)}, bf16[4,1024,128]{2,1,0:T(8,128)(2,1)S(1)}, f32[4,1,1024]{2,1,0:T(1,128)S(1)}, bf16[4,512,128]{2,1,0:T(8...) custom-call(bf16[512,2048]{1,0:T(8,128)(2,1)S(1)} %copy-done.2, ...), custom_call_target="tpu_custom_call" | custom-call | flops 2097152 | bytes 8388608 | tf_op jit(solution)/shard_map/arrange/pallas_call | solution.py:72
  14.2 1.0 copy-done.18
  15.1 1.0 copy-done.21
  16.9 0.8 copy-done.27
  18.5 2.2 %broadcast_select_fusion.7 = (bf16[2,512,256]{2,1,0:T(8,128)(2,1)}, bf16[2,512,256]{2,1,0:T(8,128)(2,1)}) fusion(bf16[2,512,256]{2,1,0:T(8,128)(2,1)} %collective-permute-done.1, pred[]{:T(512)S(6)} %eq.54, bf16[1,512,256]{2,1,0:T(8,128)(2,1)S(1)} %get-tuple-element.130, bf16[1,512,256]{2,1,0:T(8,128)(2,1)S(1)} %get-tuple-element.135, pred[]{:T(512)S(6)} %eq.26), kind=kLoop, calls=%fused_computation.12 | loop fusion | flops 786432 | bytes 2097154 | tf_op jit(solution)/shard_map/jit(_where)/select_n | solution.py:265
  20.6 3.1 %collective-permute-start.3 = (bf16[2,512,256]{2,1,0:T(8,128)(2,1)}, bf16[2,512,256]{2,1,0:T(8,128)(2,1)}, u32[]{:S(2)}, u32[]{:S(2)}) collective-permute-start(bf16[2,512,256]{2,1,0:T(8,128)(2,1)} %get-tuple-element.131), channel_id=1, source_target_pairs={{2,0},{4,2},{6,4},{8,6},{10,8},{12,10},{14,12},{16,14},{18,16},{20... | collective-permute-start | bytes 1572872 | tf_op jit(solution)/shard_map/ppermute | solution.py:292
  23.8 3.0 %collective-permute-start.2 = (bf16[2,512,256]{2,1,0:T(8,128)(2,1)}, bf16[2,512,256]{2,1,0:T(8,128)(2,1)}, u32[]{:S(2)}, u32[]{:S(2)}) collective-permute-start(bf16[2,512,256]{2,1,0:T(8,128)(2,1)} %get-tuple-element.132), channel_id=1, source_target_pairs={{0,2},{2,4},{4,6},{6,8},{8,10},{10,12},{12,14},{14,16},{16,18},{18... | collective-permute-start | bytes 1572872 | tf_op jit(solution)/shard_map/ppermute | solution.py:292
  28.2 1.6 %copy-done.3 = bf16[512,2048]{1,0:T(8,128)(2,1)S(1)} copy-done((bf16[512,2048]{1,0:T(8,128)(2,1)S(1)}, bf16[512,2048]{1,0:T(8,128)(2,1)}, u32[]{:S(2)}) %copy-start.3) | copy-done | bytes 2097176
  29.8 1.6 %copy-done.5 = bf16[512,2048]{1,0:T(8,128)(2,1)S(1)} copy-done((bf16[512,2048]{1,0:T(8,128)(2,1)S(1)}, bf16[512,2048]{1,0:T(8,128)(2,1)}, u32[]{:S(2)}) %copy-start.5) | copy-done | bytes 2097176
  31.4 1.6 %copy-done.7 = bf16[512,2048]{1,0:T(8,128)(2,1)S(1)} copy-done((bf16[512,2048]{1,0:T(8,128)(2,1)S(1)}, bf16[512,2048]{1,0:T(8,128)(2,1)}, u32[]{:S(2)}) %copy-start.7) | copy-done | bytes 2097176
  33.0 1.9 %arrange.2 = (bf16[4,1024,128]{2,1,0:T(8,128)(2,1)S(1)}, bf16[4,1024,128]{2,1,0:T(8,128)(2,1)S(1)}, f32[4,1,1024]{2,1,0:T(1,128)S(1)}, bf16[4,512,128]{2,1,0:T(8...) custom-call(bf16[512,2048]{1,0:T(8,128)(2,1)S(1)} %copy-done.3, ...), custom_call_target="tpu_custom_call" | custom-call | flops 2097152 | bytes 8388608 | tf_op jit(solution)/shard_map/arrange/pallas_call | solution.py:72
  35.1 1.7 %broadcast_select_fusion.6 = (bf16[2,512,256]{2,1,0:T(8,128)(2,1)S(1)}, bf16[2,512,256]{2,1,0:T(8,128)(2,1)S(1)}) fusion(bf16[2,512,256]{2,1,0:T(8,128)(2,1)} %collective-permute-done, pred[]{:T(512)S(6)} %eq.54, bf16[1,512,256]{2,1,0:T(8,128)(2,1)S(1)} %get-tuple-element.127, bf16[1,512,256]{2,1,0:T(8,128)(2,1)S(1)} %copy-done.50, pred[]{:T(512)S(6)} %eq.26), kind=kLoop, calls=%fused_computation.11 | loop fusion | flops 786432 | bytes 2097154 | tf_op jit(solution)/shard_map/jit(_where)/select_n | solution.py:265
  36.8 2.1 %collective-permute-start.5 = (bf16[2,512,256]{2,1,0:T(8,128)(2,1)S(1)}, bf16[2,512,256]{2,1,0:T(8,128)(2,1)S(1)}, u32[]{:S(2)}, u32[]{:S(2)}) collective-permute-start(bf16[2,512,256]{2,1,0:T(8,128)(2,1)S(1)} %get-tuple-element.121), channel_id=1, source_target_pairs={{2,0},{4,2},{6,4},{8,6},{10,8},{12,10},{14,12},{16,14},{18,16},{20... | collective-permute-start | bytes 1572872 | tf_op jit(solution)/shard_map/ppermute | solution.py:292
  38.9 3.8 %collective-permute-start.4 = (bf16[2,512,256]{2,1,0:T(8,128)(2,1)S(1)}, bf16[2,512,256]{2,1,0:T(8,128)(2,1)S(1)}, u32[]{:S(2)}, u32[]{:S(2)}) collective-permute-start(bf16[2,512,256]{2,1,0:T(8,128)(2,1)S(1)} %get-tuple-element.122), channel_id=1, source_target_pairs={{0,2},{2,4},{4,6},{6,8},{8,10},{10,12},{12,14},{14,16},{16,18},{18... | collective-permute-start | bytes 1572872 | tf_op jit(solution)/shard_map/ppermute | solution.py:292
  43.1 2.1 %broadcast_select_fusion.18 = (bf16[2,512,256]{2,1,0:T(8,128)(2,1)}, bf16[2,512,256]{2,1,0:T(8,128)(2,1)S(1)}) fusion(bf16[2,512,256]{2,1,0:T(8,128)(2,1)} %collective-permute-done.2, pred[]{:T(512)S(6)} %eq.24, bf16[2,512,256]{2,1,0:T(8,128)(2,1)} %get-tuple-element.132, bf16[2,512,256]{2,1,0:T(8,128)(2,1)} %collective-permute-done.3, pred[]{:T(512)S(6)} %eq.27, ...), kind=kLoop, calls=%fused_computation.23 | loop fusion | flops 786432 | bytes 2621443 | tf_op jit(solution)/shard_map/jit(_where)/select_n | solution.py:358
  45.5 5.9 %attention.4 = (bf16[512,2048]{1,0:T(8,128)(2,1)}, bf16[2,512,128]{2,1,0:T(8,128)(2,1)S(1)}, bf16[2,512,128]{2,1,0:T(8,128)(2,1)S(1)}, bf16[2,512,256]{2,1,0:T(8,128)(2,1)S(1)}) custom-call(s32[1]{0:T(128)} %bitcast.6.group_ref, s32[1,512]{1,0:T(1,128)S(1)} %bitcast.21, bf16[4,1024,128]{2,1,0:T(8,128)(2,1)S(1)} %copy-done.19, ...), custom_call_target="tpu_custom_call" | custom-call | flops 1677721600 | bytes 2457600 | tf_op jit(solution)/shard_map/attention/pallas_call | solution.py:183
  51.4 0.8 copy-done.33
  53.6 1.1 broadcast_select_fusion.14
  55.3 1.0 copy-done.15
  56.3 1.0 copy-done.17
  57.4 5.9 %attention.5 = (bf16[512,2048]{1,0:T(8,128)(2,1)}, bf16[2,512,128]{2,1,0:T(8,128)(2,1)S(1)}, bf16[2,512,128]{2,1,0:T(8,128)(2,1)S(1)}, bf16[2,512,256]{2,1,0:T(8,128)(2,1)S(1)}) custom-call(s32[1]{0:T(128)} %bitcast.6.group_ref, s32[1,512]{1,0:T(1,128)S(1)} %bitcast.22, ...), custom_call_target="tpu_custom_call", output_to_operand_aliasing={{0}: (9, {})} | custom-call | flops 1677721600 | bytes 2457600 | tf_op jit(solution)/shard_map/attention/pallas_call | solution.py:183
  65.5 6.7 %attention.6 = (bf16[512,2048]{1,0:T(8,128)(2,1)}, bf16[2,512,128]{2,1,0:T(8,128)(2,1)S(1)}, bf16[2,512,128]{2,1,0:T(8,128)(2,1)S(1)}, bf16[2,512,256]{2,1,0:T(8,128)(2,1)}) custom-call(s32[1]{0:T(128)} %bitcast.group_ref, s32[1,512]{1,0:T(1,128)S(1)} %bitcast.23, bf16[4,1024,128]{2,1,0:T(8,128)(2,1)S(1)} %copy-done.20, ...), custom_call_target="tpu_custom_call", output_to_operand_aliasing={{0}: (9, {})} | custom-call | flops 1677721600 | bytes 2457600 | tf_op jit(solution)/shard_map/attention/pallas_call | solution.py:183
  72.2 0.9 collective-permute-start.12
  73.2 6.7 %attention.7 = (bf16[512,2048]{1,0:T(8,128)(2,1)}, bf16[2,512,128]{2,1,0:T(8,128)(2,1)S(1)}, bf16[2,512,128]{2,1,0:T(8,128)(2,1)S(1)}, bf16[2,512,256]{2,1,0:T(8,128)(2,1)}) custom-call(s32[1]{0:T(128)} %bitcast.group_ref, s32[1,512]{1,0:T(1,128)S(1)} %bitcast.24, ...), custom_call_target="tpu_custom_call", output_to_operand_aliasing={{0}: (9, {})} | custom-call | flops 1677721600 | bytes 2457600 | tf_op jit(solution)/shard_map/attention/pallas_call | solution.py:183
  81.9 3.6 %collective-permute-done.12 = bf16[2,512,256]{2,1,0:T(8,128)(2,1)} collective-permute-done((bf16[2,512,256]{2,1,0:T(8,128)(2,1)}, bf16[2,512,256]{2,1,0:T(8,128)(2,1)}, u32[]{:S(2)}, u32[]{:S(2)}) %collective-permute-start.12) | collective-permute-done | bytes 524320 | tf_op jit(solution)/shard_map/ppermute | solution.py:288
  85.5 1.3 broadcast_select_fusion.2
  86.7 4.5 %collective-permute-start.13 = (bf16[2,512,256]{2,1,0:T(8,128)(2,1)S(1)}, bf16[2,512,256]{2,1,0:T(8,128)(2,1)S(1)}, u32[]{:S(2)}, u32[]{:S(2)}) collective-permute-start(bf16[2,512,256]{2,1,0:T(8,128)(2,1)S(1)} %get-tuple-element.117), channel_id=1, source_target_pairs={{2,0},{4,2},{6,4},{8,6},{10,8},{12,10},{14,12},{16,14},{18,16},{20... | collective-permute-start | bytes 1572872 | tf_op jit(solution)/shard_map/ppermute | solution.py:292
  91.2 3.6 %collective-permute-start.14 = (bf16[2,512,256]{2,1,0:T(8,128)(2,1)S(1)}, bf16[2,512,256]{2,1,0:T(8,128)(2,1)}, u32[]{:S(2)}, u32[]{:S(2)}) collective-permute-start(bf16[2,512,256]{2,1,0:T(8,128)(2,1)S(1)} %get-tuple-element.118), channel_id=1, source_target_pairs={{0,2},{2,4},{4,6},{6,8},{8,10},{10,12},{12,14},{14,16},{16,18},{18... | collective-permute-start | bytes 1572872 | tf_op jit(solution)/shard_map/ppermute | solution.py:292
  94.9 1.7 %collective-permute-done.8 = bf16[2,512,256]{2,1,0:T(8,128)(2,1)S(1)} collective-permute-done((bf16[2,512,256]{2,1,0:T(8,128)(2,1)}, bf16[2,512,256]{2,1,0:T(8,128)(2,1)S(1)}, u32[]{:S(2)}, u32[]{:S(2)}) %collective-permute-start.8) | collective-permute-done | bytes 524320 | tf_op jit(solution)/shard_map/ppermute | solution.py:288
  96.6 0.9 broadcast_select_fusion.3
  97.5 3.4 %collective-permute-start.9 = (bf16[2,512,256]{2,1,0:T(8,128)(2,1)}, bf16[2,512,256]{2,1,0:T(8,128)(2,1)S(1)}, u32[]{:S(2)}, u32[]{:S(2)}) collective-permute-start(bf16[2,512,256]{2,1,0:T(8,128)(2,1)} %get-tuple-element.119), channel_id=1, source_target_pairs={{2,0},{4,2},{6,4},{8,6},{10,8},{12,10},{14,12},{16,14},{18,16},{20... | collective-permute-start | bytes 1572872 | tf_op jit(solution)/shard_map/ppermute | solution.py:292
  100.9 4.2 %collective-permute-start.10 = (bf16[2,512,256]{2,1,0:T(8,128)(2,1)S(1)}, bf16[2,512,256]{2,1,0:T(8,128)(2,1)}, u32[]{:S(2)}, u32[]{:S(2)}) collective-permute-start(bf16[2,512,256]{2,1,0:T(8,128)(2,1)S(1)} %get-tuple-element.120), channel_id=1, source_target_pairs={{0,2},{2,4},{4,6},{6,8},{8,10},{10,12},{12,14},{14,16},{16,18},{18... | collective-permute-start | bytes 1572872 | tf_op jit(solution)/shard_map/ppermute | solution.py:292
  105.4 1.1 broadcast_select_fusion
  106.6 1.3 %collective-permute-start.15 = (bf16[2,512,256]{2,1,0:T(8,128)(2,1)S(1)}, bf16[2,512,256]{2,1,0:T(8,128)(2,1)S(1)}, u32[]{:S(2)}, u32[]{:S(2)}) collective-permute-start(bf16[2,512,256]{2,1,0:T(8,128)(2,1)S(1)} %get-tuple-element.110), channel_id=1, source_target_pairs={{0,1},{1,0},{2,3},{3,2},{4,5},{5,4},{6,7},{7,6},{8,9},{9,8},{10,11... | collective-permute-start | bytes 1572872 | tf_op jit(solution)/shard_map/ppermute | solution.py:288
  107.9 9.0 %collective-permute-done.9 = bf16[2,512,256]{2,1,0:T(8,128)(2,1)S(1)} collective-permute-done((bf16[2,512,256]{2,1,0:T(8,128)(2,1)}, bf16[2,512,256]{2,1,0:T(8,128)(2,1)S(1)}, u32[]{:S(2)}, u32[]{:S(2)}) %collective-permute-start.9) | collective-permute-done | bytes 524320 | tf_op jit(solution)/shard_map/ppermute | solution.py:292
  116.9 1.1 broadcast_select_fusion.1
  118.1 1.3 %collective-permute-start.11 = (bf16[2,512,256]{2,1,0:T(8,128)(2,1)S(1)}, bf16[2,512,256]{2,1,0:T(8,128)(2,1)S(1)}, u32[]{:S(2)}, u32[]{:S(2)}) collective-permute-start(bf16[2,512,256]{2,1,0:T(8,128)(2,1)S(1)} %get-tuple-element.112), channel_id=1, source_target_pairs={{0,1},{1,0},{2,3},{3,2},{4,5},{5,4},{6,7},{7,6},{8,9},{9,8},{10,11... | collective-permute-start | bytes 1572872 | tf_op jit(solution)/shard_map/ppermute | solution.py:288
  119.4 1.0 finish.4
  120.6 1.0 finish.5
  121.6 1.0 finish.6
  122.6 8.7 %collective-permute-done.11.back_ref = bf16[2,512,256]{2,1,0:T(8,128)(2,1)S(1)} collective-permute-done((bf16[2,512,256]{2,1,0:T(8,128)(2,1)S(1)}, bf16[2,512,256]{2,1,0:T(8,128)(2,1)S(1)}, u32[]{:S(2)}, u32[]{:S(2)}) %collective-permute-start.11) | collective-permute-done | bytes 524320 | tf_op jit(solution)/shard_map/ppermute | solution.py:288
  131.3 1.0 finish.7
  (116 shorter events, 10.2 us)
Async XLA Ops:
  3.0 2.4 %copy-start.52 = (s32[32]{0:T(128)S(1)}, s32[32]{0:T(128)}, u32[]{:S(2)}) copy-start(s32[32]{0:T(128)} %param.13) | copy-start | bytes 388
  3.0 4.4 %copy-start = (bf16[512,1024]{1,0:T(8,128)(2,1)S(1)}, bf16[512,1024]{1,0:T(8,128)(2,1)}, u32[]{:S(2)}) copy-start(bf16[512,1024]{1,0:T(8,128)(2,1)} %k_ref.3) | copy-start | bytes 3145732
  3.0 4.4 %copy-start.1 = (bf16[512,1024]{1,0:T(8,128)(2,1)S(1)}, bf16[512,1024]{1,0:T(8,128)(2,1)}, u32[]{:S(2)}) copy-start(bf16[512,1024]{1,0:T(8,128)(2,1)} %v_ref.3) | copy-start | bytes 3145732
  3.1 15.4 %collective-permute-start.1 = (bf16[2,512,256]{2,1,0:T(8,128)(2,1)S(1)}, bf16[2,512,256]{2,1,0:T(8,128)(2,1)}, u32[]{:S(2)}, u32[]{:S(2)}) collective-permute-start(bf16[2,512,256]{2,1,0:T(8,128)(2,1)S(1)} %pad_maximum_fusion.1), channel_id=1, source_target_pairs={{0,1},{1,0},{2,3},{3,2},{4,5},{5,4},{6,7},{7,6},{8,9},{9,8},{10,11... | collective-permute-start | bytes 1572872 | tf_op jit(solution)/shard_map/ppermute | solution.py:288
  4.3 30.7 %collective-permute-start = (bf16[2,512,256]{2,1,0:T(8,128)(2,1)}, bf16[2,512,256]{2,1,0:T(8,128)(2,1)}, u32[]{:S(2)}, u32[]{:S(2)}) collective-permute-start(bf16[2,512,256]{2,1,0:T(8,128)(2,1)} %pad_maximum_fusion), channel_id=1, source_target_pairs={{0,1},{1,0},{2,3},{3,2},{4,5},{5,4},{6,7},{7,6},{8,9},{9,8},{10,11... | collective-permute-start | bytes 1572872 | tf_op jit(solution)/shard_map/ppermute | solution.py:288
  18.5 9.6 %copy-start.51 = (s32[16384]{0:T(1024)S(1)}, s32[16384]{0:T(1024)}, u32[]{:S(2)}) copy-start(s32[16384]{0:T(1024)} %param.12) | copy-start | bytes 196612
  20.6 22.4 %collective-permute-start.3 = (bf16[2,512,256]{2,1,0:T(8,128)(2,1)}, bf16[2,512,256]{2,1,0:T(8,128)(2,1)}, u32[]{:S(2)}, u32[]{:S(2)}) collective-permute-start(bf16[2,512,256]{2,1,0:T(8,128)(2,1)} %get-tuple-element.131), channel_id=1, source_target_pairs={{2,0},{4,2},{6,4},{8,6},{10,8},{12,10},{14,12},{16,14},{18,16},{20... | collective-permute-start | bytes 1572872 | tf_op jit(solution)/shard_map/ppermute | solution.py:292
  23.8 19.3 %collective-permute-start.2 = (bf16[2,512,256]{2,1,0:T(8,128)(2,1)}, bf16[2,512,256]{2,1,0:T(8,128)(2,1)}, u32[]{:S(2)}, u32[]{:S(2)}) collective-permute-start(bf16[2,512,256]{2,1,0:T(8,128)(2,1)} %get-tuple-element.132), channel_id=1, source_target_pairs={{0,2},{2,4},{4,6},{6,8},{8,10},{10,12},{12,14},{14,16},{16,18},{18... | collective-permute-start | bytes 1572872 | tf_op jit(solution)/shard_map/ppermute | solution.py:292
  35.0 10.2 %copy-start.8 = (bf16[4,1024,128]{2,1,0:T(8,128)(2,1)}, bf16[4,1024,128]{2,1,0:T(8,128)(2,1)S(1)}, u32[]{:S(2)}) copy-start(bf16[4,1024,128]{2,1,0:T(8,128)(2,1)S(1)} %get-tuple-element.63.do_ref) | copy-start | bytes 3145732
  35.0 10.2 %copy-start.10 = (bf16[4,512,128]{2,1,0:T(8,128)(2,1)}, bf16[4,512,128]{2,1,0:T(8,128)(2,1)S(1)}, u32[]{:S(2)}) copy-start(bf16[4,512,128]{2,1,0:T(8,128)(2,1)S(1)} %get-tuple-element.65.k_ref) | copy-start | bytes 1572868
  35.0 10.2 %copy-start.12 = (bf16[4,128,512]{2,1,0:T(8,128)(2,1)}, bf16[4,128,512]{2,1,0:T(8,128)(2,1)S(1)}, u32[]{:S(2)}) copy-start(bf16[4,128,512]{2,1,0:T(8,128)(2,1)S(1)} %get-tuple-element.66.k_turned_ref) | copy-start | bytes 1572868
  35.0 10.2 %copy-start.14 = (bf16[4,512,128]{2,1,0:T(8,128)(2,1)}, bf16[4,512,128]{2,1,0:T(8,128)(2,1)S(1)}, u32[]{:S(2)}) copy-start(bf16[4,512,128]{2,1,0:T(8,128)(2,1)S(1)} %get-tuple-element.67.v_ref) | copy-start | bytes 1572868
  35.0 10.5 %copy-start.19 = (bf16[4,1024,128]{2,1,0:T(8,128)(2,1)S(1)}, bf16[4,1024,128]{2,1,0:T(8,128)(2,1)}, u32[]{:S(2)}) copy-start(bf16[4,1024,128]{2,1,0:T(8,128)(2,1)} %copy-done.18) | copy-start | bytes 3145732
  35.0 10.5 %copy-start.22 = (bf16[4,1024,128]{2,1,0:T(8,128)(2,1)S(1)}, bf16[4,1024,128]{2,1,0:T(8,128)(2,1)}, u32[]{:S(2)}) copy-start(bf16[4,1024,128]{2,1,0:T(8,128)(2,1)} %copy-done.21) | copy-start | bytes 3145732
  35.0 10.5 %copy-start.25 = (bf16[4,512,128]{2,1,0:T(8,128)(2,1)S(1)}, bf16[4,512,128]{2,1,0:T(8,128)(2,1)}, u32[]{:S(2)}) copy-start(bf16[4,512,128]{2,1,0:T(8,128)(2,1)} %copy-done.24) | copy-start | bytes 1572868
  35.0 10.5 %copy-start.28 = (bf16[4,128,512]{2,1,0:T(8,128)(2,1)S(1)}, bf16[4,128,512]{2,1,0:T(8,128)(2,1)}, u32[]{:S(2)}) copy-start(bf16[4,128,512]{2,1,0:T(8,128)(2,1)} %copy-done.27) | copy-start | bytes 1572868
  35.1 10.5 %copy-start.31 = (bf16[4,512,128]{2,1,0:T(8,128)(2,1)S(1)}, bf16[4,512,128]{2,1,0:T(8,128)(2,1)}, u32[]{:S(2)}) copy-start(bf16[4,512,128]{2,1,0:T(8,128)(2,1)} %copy-done.30) | copy-start | bytes 1572868
  36.8 16.6 %collective-permute-start.5 = (bf16[2,512,256]{2,1,0:T(8,128)(2,1)S(1)}, bf16[2,512,256]{2,1,0:T(8,128)(2,1)S(1)}, u32[]{:S(2)}, u32[]{:S(2)}) collective-permute-start(bf16[2,512,256]{2,1,0:T(8,128)(2,1)S(1)} %get-tuple-element.121), channel_id=1, source_target_pairs={{2,0},{4,2},{6,4},{8,6},{10,8},{12,10},{14,12},{16,14},{18,16},{20... | collective-permute-start | bytes 1572872 | tf_op jit(solution)/shard_map/ppermute | solution.py:292
  38.9 14.7 %collective-permute-start.4 = (bf16[2,512,256]{2,1,0:T(8,128)(2,1)S(1)}, bf16[2,512,256]{2,1,0:T(8,128)(2,1)S(1)}, u32[]{:S(2)}, u32[]{:S(2)}) collective-permute-start(bf16[2,512,256]{2,1,0:T(8,128)(2,1)S(1)} %get-tuple-element.122), channel_id=1, source_target_pairs={{0,2},{2,4},{4,6},{6,8},{8,10},{10,12},{12,14},{14,16},{16,18},{18... | collective-permute-start | bytes 1572872 | tf_op jit(solution)/shard_map/ppermute | solution.py:292
  45.2 20.3 %collective-permute-start.7 = (bf16[2,512,256]{2,1,0:T(8,128)(2,1)}, bf16[2,512,256]{2,1,0:T(8,128)(2,1)}, u32[]{:S(2)}, u32[]{:S(2)}) collective-permute-start(bf16[2,512,256]{2,1,0:T(8,128)(2,1)} %get-tuple-element.115), channel_id=1, source_target_pairs={{0,1},{1,0},{2,3},{3,2},{4,5},{5,4},{6,7},{7,6},{8,9},{9,8},{10,11... | collective-permute-start | bytes 1572872 | tf_op jit(solution)/shard_map/ppermute | solution.py:288
  52.9 2.3 %copy-start.9 = (bf16[4,1024,128]{2,1,0:T(8,128)(2,1)S(1)}, bf16[4,1024,128]{2,1,0:T(8,128)(2,1)}, u32[]{:S(2)}) copy-start(bf16[4,1024,128]{2,1,0:T(8,128)(2,1)} %copy-done.8) | copy-start | bytes 3145732
  52.9 2.3 %copy-start.11 = (bf16[4,512,128]{2,1,0:T(8,128)(2,1)S(1)}, bf16[4,512,128]{2,1,0:T(8,128)(2,1)}, u32[]{:S(2)}) copy-start(bf16[4,512,128]{2,1,0:T(8,128)(2,1)} %copy-done.10) | copy-start | bytes 1572868
  52.9 2.3 %copy-start.13 = (bf16[4,128,512]{2,1,0:T(8,128)(2,1)S(1)}, bf16[4,128,512]{2,1,0:T(8,128)(2,1)}, u32[]{:S(2)}) copy-start(bf16[4,128,512]{2,1,0:T(8,128)(2,1)} %copy-done.12) | copy-start | bytes 1572868
  54.7 18.5 %collective-permute-start.6 = (bf16[2,512,256]{2,1,0:T(8,128)(2,1)}, bf16[2,512,256]{2,1,0:T(8,128)(2,1)}, u32[]{:S(2)}, u32[]{:S(2)}) collective-permute-start(bf16[2,512,256]{2,1,0:T(8,128)(2,1)} %get-tuple-element.114), channel_id=1, source_target_pairs={{0,1},{1,0},{2,3},{3,2},{4,5},{5,4},{6,7},{7,6},{8,9},{9,8},{10,11... | collective-permute-start | bytes 1572872 | tf_op jit(solution)/shard_map/ppermute | solution.py:288
  57.3 8.1 %copy-start.20 = (bf16[4,1024,128]{2,1,0:T(8,128)(2,1)S(1)}, bf16[4,1024,128]{2,1,0:T(8,128)(2,1)}, u32[]{:S(2)}) copy-start(bf16[4,1024,128]{2,1,0:T(8,128)(2,1)} %copy-done.18) | copy-start | bytes 3145732
  57.4 8.1 %copy-start.23 = (bf16[4,1024,128]{2,1,0:T(8,128)(2,1)S(1)}, bf16[4,1024,128]{2,1,0:T(8,128)(2,1)}, u32[]{:S(2)}) copy-start(bf16[4,1024,128]{2,1,0:T(8,128)(2,1)} %copy-done.21) | copy-start | bytes 3145732
  57.4 8.1 %copy-start.26 = (bf16[4,512,128]{2,1,0:T(8,128)(2,1)S(1)}, bf16[4,512,128]{2,1,0:T(8,128)(2,1)}, u32[]{:S(2)}) copy-start(bf16[4,512,128]{2,1,0:T(8,128)(2,1)} %copy-done.24) | copy-start | bytes 1572868
  57.4 8.1 %copy-start.29 = (bf16[4,128,512]{2,1,0:T(8,128)(2,1)S(1)}, bf16[4,128,512]{2,1,0:T(8,128)(2,1)}, u32[]{:S(2)}) copy-start(bf16[4,128,512]{2,1,0:T(8,128)(2,1)} %copy-done.27) | copy-start | bytes 1572868
  57.4 8.1 %copy-start.32 = (bf16[4,512,128]{2,1,0:T(8,128)(2,1)S(1)}, bf16[4,512,128]{2,1,0:T(8,128)(2,1)}, u32[]{:S(2)}) copy-start(bf16[4,512,128]{2,1,0:T(8,128)(2,1)} %copy-done.30) | copy-start | bytes 1572868
  65.5 7.7 %copy-start.16 = (bf16[4,512,128]{2,1,0:T(8,128)(2,1)S(1)}, bf16[4,512,128]{2,1,0:T(8,128)(2,1)}, u32[]{:S(2)}) copy-start(bf16[4,512,128]{2,1,0:T(8,128)(2,1)} %copy-done.14) | copy-start | bytes 1572868
  72.2 7.6 %copy-start.46 = (bf16[2,512,128]{2,1,0:T(8,128)(2,1)}, bf16[2,512,128]{2,1,0:T(8,128)(2,1)S(1)}, u32[]{:S(2)}) copy-start(bf16[2,512,128]{2,1,0:T(8,128)(2,1)S(1)} %get-tuple-element.95.dk_ref) | copy-start | bytes 786436
  72.2 7.6 %copy-start.48 = (bf16[2,512,128]{2,1,0:T(8,128)(2,1)}, bf16[2,512,128]{2,1,0:T(8,128)(2,1)S(1)}, u32[]{:S(2)}) copy-start(bf16[2,512,128]{2,1,0:T(8,128)(2,1)S(1)} %get-tuple-element.96.dv_ref) | copy-start | bytes 786436
  72.2 13.2 %collective-permute-start.12 = (bf16[2,512,256]{2,1,0:T(8,128)(2,1)}, bf16[2,512,256]{2,1,0:T(8,128)(2,1)}, u32[]{:S(2)}, u32[]{:S(2)}) collective-permute-start(bf16[2,512,256]{2,1,0:T(8,128)(2,1)} %get-tuple-element.98), channel_id=1, source_target_pairs={{0,1},{1,0},{2,3},{3,2},{4,5},{5,4},{6,7},{7,6},{8,9},{9,8},{10,11... | collective-permute-start | bytes 1572872 | tf_op jit(solution)/shard_map/ppermute | solution.py:288
  81.2 15.4 %copy-start.35 = (bf16[2,512,256]{2,1,0:T(8,128)(2,1)S(1)}, bf16[2,512,256]{2,1,0:T(8,128)(2,1)}, u32[]{:S(2)}) copy-start(bf16[2,512,256]{2,1,0:T(8,128)(2,1)} %copy-done.34) | copy-start | bytes 1572868
  81.2 15.4 %collective-permute-start.8 = (bf16[2,512,256]{2,1,0:T(8,128)(2,1)}, bf16[2,512,256]{2,1,0:T(8,128)(2,1)S(1)}, u32[]{:S(2)}, u32[]{:S(2)}) collective-permute-start(bf16[2,512,256]{2,1,0:T(8,128)(2,1)} %get-tuple-element.92), channel_id=1, source_target_pairs={{0,1},{1,0},{2,3},{3,2},{4,5},{5,4},{6,7},{7,6},{8,9},{9,8},{10,11... | collective-permute-start | bytes 1572872 | tf_op jit(solution)/shard_map/ppermute | solution.py:288
  86.7 18.7 %collective-permute-start.13 = (bf16[2,512,256]{2,1,0:T(8,128)(2,1)S(1)}, bf16[2,512,256]{2,1,0:T(8,128)(2,1)S(1)}, u32[]{:S(2)}, u32[]{:S(2)}) collective-permute-start(bf16[2,512,256]{2,1,0:T(8,128)(2,1)S(1)} %get-tuple-element.117), channel_id=1, source_target_pairs={{2,0},{4,2},{6,4},{8,6},{10,8},{12,10},{14,12},{16,14},{18,16},{20... | collective-permute-start | bytes 1572872 | tf_op jit(solution)/shard_map/ppermute | solution.py:292
  91.2 14.2 %collective-permute-start.14 = (bf16[2,512,256]{2,1,0:T(8,128)(2,1)S(1)}, bf16[2,512,256]{2,1,0:T(8,128)(2,1)}, u32[]{:S(2)}, u32[]{:S(2)}) collective-permute-start(bf16[2,512,256]{2,1,0:T(8,128)(2,1)S(1)} %get-tuple-element.118), channel_id=1, source_target_pairs={{0,2},{2,4},{4,6},{6,8},{8,10},{10,12},{12,14},{14,16},{16,18},{18... | collective-permute-start | bytes 1572872 | tf_op jit(solution)/shard_map/ppermute | solution.py:292
  97.5 19.5 %collective-permute-start.9 = (bf16[2,512,256]{2,1,0:T(8,128)(2,1)}, bf16[2,512,256]{2,1,0:T(8,128)(2,1)S(1)}, u32[]{:S(2)}, u32[]{:S(2)}) collective-permute-start(bf16[2,512,256]{2,1,0:T(8,128)(2,1)} %get-tuple-element.119), channel_id=1, source_target_pairs={{2,0},{4,2},{6,4},{8,6},{10,8},{12,10},{14,12},{16,14},{18,16},{20... | collective-permute-start | bytes 1572872 | tf_op jit(solution)/shard_map/ppermute | solution.py:292
  100.9 16.1 %collective-permute-start.10 = (bf16[2,512,256]{2,1,0:T(8,128)(2,1)S(1)}, bf16[2,512,256]{2,1,0:T(8,128)(2,1)}, u32[]{:S(2)}, u32[]{:S(2)}) collective-permute-start(bf16[2,512,256]{2,1,0:T(8,128)(2,1)S(1)} %get-tuple-element.120), channel_id=1, source_target_pairs={{0,2},{2,4},{4,6},{6,8},{8,10},{10,12},{12,14},{14,16},{16,18},{18... | collective-permute-start | bytes 1572872 | tf_op jit(solution)/shard_map/ppermute | solution.py:292
  105.1 14.3 %copy-start.37 = (bf16[2,512,128]{2,1,0:T(8,128)(2,1)S(1)}, bf16[2,512,128]{2,1,0:T(8,128)(2,1)}, u32[]{:S(2)}) copy-start(bf16[2,512,128]{2,1,0:T(8,128)(2,1)} %copy-done.36) | copy-start | bytes 786436
  106.6 14.0 %copy-start.47 = (bf16[2,512,128]{2,1,0:T(8,128)(2,1)S(1)}, bf16[2,512,128]{2,1,0:T(8,128)(2,1)}, u32[]{:S(2)}) copy-start(bf16[2,512,128]{2,1,0:T(8,128)(2,1)} %copy-done.46) | copy-start | bytes 786436
  106.6 14.0 %copy-start.49 = (bf16[2,512,128]{2,1,0:T(8,128)(2,1)S(1)}, bf16[2,512,128]{2,1,0:T(8,128)(2,1)}, u32[]{:S(2)}) copy-start(bf16[2,512,128]{2,1,0:T(8,128)(2,1)} %copy-done.48) | copy-start | bytes 786436
  106.6 14.0 %collective-permute-start.15 = (bf16[2,512,256]{2,1,0:T(8,128)(2,1)S(1)}, bf16[2,512,256]{2,1,0:T(8,128)(2,1)S(1)}, u32[]{:S(2)}, u32[]{:S(2)}) collective-permute-start(bf16[2,512,256]{2,1,0:T(8,128)(2,1)S(1)} %get-tuple-element.110), channel_id=1, source_target_pairs={{0,1},{1,0},{2,3},{3,2},{4,5},{5,4},{6,7},{7,6},{8,9},{9,8},{10,11... | collective-permute-start | bytes 1572872 | tf_op jit(solution)/shard_map/ppermute | solution.py:288
  118.1 13.2 %collective-permute-start.11 = (bf16[2,512,256]{2,1,0:T(8,128)(2,1)S(1)}, bf16[2,512,256]{2,1,0:T(8,128)(2,1)S(1)}, u32[]{:S(2)}, u32[]{:S(2)}) collective-permute-start(bf16[2,512,256]{2,1,0:T(8,128)(2,1)S(1)} %get-tuple-element.112), channel_id=1, source_target_pairs={{0,1},{1,0},{2,3},{3,2},{4,5},{5,4},{6,7},{7,6},{8,9},{9,8},{10,11... | collective-permute-start | bytes 1572872 | tf_op jit(solution)/shard_map/ppermute | solution.py:288
  119.4 2.1 %copy-start.39 = (bf16[2,512,128]{2,1,0:T(8,128)(2,1)S(1)}, bf16[2,512,128]{2,1,0:T(8,128)(2,1)}, u32[]{:S(2)}) copy-start(bf16[2,512,128]{2,1,0:T(8,128)(2,1)} %copy-done.38) | copy-start | bytes 786436
  119.4 2.1 %copy-start.41 = (bf16[2,512,128]{2,1,0:T(8,128)(2,1)S(1)}, bf16[2,512,128]{2,1,0:T(8,128)(2,1)}, u32[]{:S(2)}) copy-start(bf16[2,512,128]{2,1,0:T(8,128)(2,1)} %copy-done.40) | copy-start | bytes 786436
  121.6 9.7 %copy-start.43 = (bf16[2,512,128]{2,1,0:T(8,128)(2,1)S(1)}, bf16[2,512,128]{2,1,0:T(8,128)(2,1)}, u32[]{:S(2)}) copy-start(bf16[2,512,128]{2,1,0:T(8,128)(2,1)} %copy-done.42) | copy-start | bytes 786436
  121.6 9.7 %copy-start.45 = (bf16[2,512,128]{2,1,0:T(8,128)(2,1)S(1)}, bf16[2,512,128]{2,1,0:T(8,128)(2,1)}, u32[]{:S(2)}) copy-start(bf16[2,512,128]{2,1,0:T(8,128)(2,1)} %copy-done.44) | copy-start | bytes 786436
  (21 other events, 23.1 us)

commit v12 on v11

--- a/solution.py
+++ b/solution.py
@@ -13,7 +13,8 @@
 CHUNKS = 2
 TILE = 128
 STRIP = 64
-VMEM_BYTES = 24 * 1024 * 1024
+VMEM_BYTES = 16 * 1024 * 1024
+SMALL_VMEM_BYTES = 6 * 1024 * 1024
 
 
 def dot(left, right, left_dim, right_dim):
@@ -47,17 +48,16 @@
     v_out[0] = v_ref[...]
 
 
-def arrange(row_arrays, first_head, heads_per_group, per_piece):
+def arrange(row_arrays):
     queries, keys, values, outputs, grads = row_arrays
     rows, members = keys.shape[0], queries.shape[1] // keys.shape[1]
-    groups = keys.shape[1] // HEAD_SIZE // heads_per_group
-    count = groups * per_piece
-
-    def column(group, step):
-        return (0, group * heads_per_group + first_head + step)
-
-    def leading(group, step):
-        return (group * per_piece + step, 0, 0)
+    count = keys.shape[1] // HEAD_SIZE
+
+    def column(step):
+        return (0, step)
+
+    def leading(step):
+        return (step, 0, 0)
 
     query_spec = pl.BlockSpec((rows, members * HEAD_SIZE), column)
     key_spec = pl.BlockSpec((rows, HEAD_SIZE), column)
@@ -71,11 +71,11 @@
     ]
     return pl.pallas_call(
         arrange_body,
-        grid=(groups, per_piece),
+        grid=(count,),
         in_specs=[query_spec, key_spec, key_spec, query_spec, query_spec],
         out_specs=[pl.BlockSpec((1, *shape), leading) for shape, _ in shapes],
         out_shape=[jax.ShapeDtypeStruct((count, *shape), dtype) for shape, dtype in shapes],
-        compiler_params=pltpu.CompilerParams(vmem_limit_bytes=VMEM_BYTES),
+        compiler_params=pltpu.CompilerParams(vmem_limit_bytes=SMALL_VMEM_BYTES),
         cost_estimate=pl.CostEstimate(
             flops=count * rows * 1024, bytes_accessed=count * rows * 4096, transcendentals=0
         ),
@@ -169,7 +169,7 @@
     members = arranged[0].shape[1] // rows
 
     def leading(step, group_ref):
-        return (group_ref[0] * count + step, 0, 0)
+        return (group_ref[0] * heads_per_group + first_head + step, 0, 0)
 
     def column(step, group_ref):
         return (0, group_ref[0] * heads_per_group + first_head + step)
@@ -247,7 +247,7 @@
         ),
         out_shape=[jax.ShapeDtypeStruct((rows, heads * HEAD_SIZE), jnp.bfloat16)] * 2,
         input_output_aliases={4 + i: i for i in range(len(carried))},
-        compiler_params=pltpu.CompilerParams(vmem_limit_bytes=VMEM_BYTES),
+        compiler_params=pltpu.CompilerParams(vmem_limit_bytes=SMALL_VMEM_BYTES),
         cost_estimate=pl.CostEstimate(
             flops=count * rows * 512, bytes_accessed=count * rows * 2048, transcendentals=0
         ),
@@ -330,19 +330,18 @@
             for slot in (early_slot, 1 - early_slot)
         ]
 
-    arranged, halves = [], []
+    arranged, halves = arrange(row_arrays), []
     for chunk in range(chunks):
         pieces = [piece_of(place, chunk)]
         pieces += [turned(piece_of(other(turn), chunk), turn) for turn in range(1, sharers)]
-        arrays = arrange(row_arrays, chunk * per_piece, heads_per_group, per_piece)
-        *arrays, pieces[-1] = together(*arrays, pieces[-1])
-        arranged.append(arrays)
+        if not halves:
+            *arranged, pieces[-1] = together(*arranged, pieces[-1])
         halves.append(halves_of(pieces))
     before = [(shifted(early, 1), shifted(late, -1)) for early, late in halves]
 
     def run(turn, chunk, past, carried):
         query_grads, *own[chunk, turn], back = attention(
-            groups[turn].reshape(1), low, arranged[chunk], past,
+            groups[turn].reshape(1), low, arranged, past,
             chunk * per_piece, heads_per_group, key_heads, carried,
         )
         return (query_grads,), back

time: 134 us -> 141 us (1.052)
  waiting for transfers between devices: 24.2 us -> 33.1 us
  starting transfers between devices: 34.5 us -> 32.3 us
    ppermute x8, waiting for transfers between devices: 9.95 us -> 21.7 us  [shifted(): lax.ppermute(value, 'blk', [(source, source + step) for source in range(f...]
    ppermute x8, waiting for transfers between devices: 14.2 us -> 11.4 us  [turned(): return lax.ppermute(value, 'head', pairs)]
    ppermute x8, starting transfers between devices: 6.66 us -> 4.55 us  [turned(): return lax.ppermute(value, 'head', pairs)]
    unnamed x106 -> x72, local copies, waits for them, and re-layouts: 21.2 us -> 22.1 us
    pallas_call x2 -> x1, Pallas kernels: 3.88 us -> 3.78 us  [arrange(): pl.pallas_call(arrange_body, grid=(count,), in_specs=[query_spec, key_spe...]
  transfers between devices with their start and end apart: 16 -> 16, of which waited for: 8 -> 7; matrix products, arithmetic and copies ran while one was open for 10% -> 9% of each run, Pallas kernels for 24% -> 23%
where the time goes in v12:
time: 141 us; the launch traced here: 140 us
  waiting for transfers between devices  33.1 us (23%)
  Pallas kernels  32.7 us (23%)
  starting transfers between devices  32.3 us (23%)
  local copies, waits for them, and re-layouts  22.9 us (16%)
  other arithmetic  15.6 us (11%)
  between operations  3.35 us (2%)
    ppermute x8, starting transfers between devices, shifted(): lax.ppermute(value, 'blk', [(source, source + step) for source in range(f...  27.8 us
    pallas_call x4, Pallas kernels, attention(): pl.pallas_call(functools.partial(attention_body, len(carried)), grid_spec...  25 us
    unnamed x72, local copies, waits for them, and re-layouts  22.1 us
    ppermute x8, waiting for transfers between devices, shifted(): lax.ppermute(value, 'blk', [(source, source + step) for source in range(f...  21.7 us
    ppermute x8, waiting for transfers between devices, turned(): return lax.ppermute(value, 'head', pairs)  11.4 us
    select_n x4, other arithmetic, pick(): result = jnp.where(index == place, items[place], result)  5.59 us
    ppermute x8, starting transfers between devices, turned(): return lax.ppermute(value, 'head', pairs)  4.55 us
    another operation x3, other arithmetic, piece_of(): jnp.stack([columns(keys, group, chunk), columns(values, group, chunk)])  4.2 us
  transfers between devices with their start and end apart: 16, of which 7 were waited for; matrix products, arithmetic and copies ran while one was open for 9% of the time, Pallas kernels for 23%

profile of v12, /device:TPU:11, one launch (start us, length us, event | category | flops | bytes accessed | tf_op | source)
XLA Modules:
  0.0 140.0 jit_solution(17448911485483318327)
XLA Ops:
  0.6 2.5 %select_bitcast_fusion.2 = (bf16[1,512,256]{2,1,0:T(8,128)(2,1)S(1)}, bf16[1,512,256]{2,1,0:T(8,128)(2,1)S(1)}, bf16[1,512,256]{2,1,0:T(8,128)(2,1)S(1)}, bf16[1...) fusion(pred[]{:T(512)S(6)} %eq.22, ...), kind=kLoop, calls=%fused_computation.27 | loop fusion | flops 1048576 | bytes 4194306 | tf_op jit(solution)/shard_map/stack | solution.py:302
  5.1 1.2 collective-permute-start.3
  8.2 1.2 copy-done.9
  9.5 1.2 copy-done.10
  10.7 1.6 %copy-done.12 = bf16[512,2048]{1,0:T(8,128)(2,1)S(1)} copy-done((bf16[512,2048]{1,0:T(8,128)(2,1)S(1)}, bf16[512,2048]{1,0:T(8,128)(2,1)}, u32[]{:S(2)}) %copy-start.12) | copy-done | bytes 2097176
  12.3 1.6 %copy-done.13 = bf16[512,2048]{1,0:T(8,128)(2,1)S(1)} copy-done((bf16[512,2048]{1,0:T(8,128)(2,1)S(1)}, bf16[512,2048]{1,0:T(8,128)(2,1)}, u32[]{:S(2)}) %copy-start.13) | copy-done | bytes 2097176
  13.9 1.6 %copy-done.14 = bf16[512,2048]{1,0:T(8,128)(2,1)S(1)} copy-done((bf16[512,2048]{1,0:T(8,128)(2,1)S(1)}, bf16[512,2048]{1,0:T(8,128)(2,1)}, u32[]{:S(2)}) %copy-start.14) | copy-done | bytes 2097176
  15.5 3.8 %arrange.1 = (bf16[8,1024,128]{2,1,0:T(8,128)(2,1)S(1)}, bf16[8,1024,128]{2,1,0:T(8,128)(2,1)S(1)}, f32[8,1,1024]{2,1,0:T(1,128)S(1)}, bf16[8,512,128]{2,1,0:T(8...) custom-call(bf16[512,2048]{1,0:T(8,128)(2,1)S(1)} %copy-done.12, ...), custom_call_target="tpu_custom_call" | custom-call | flops 4194304 | bytes 16777216 | tf_op jit(solution)/shard_map/arrange/pallas_call | solution.py:72
  19.3 1.3 copy-done
  20.6 1.0 copy-done.3
  21.6 1.0 copy-done.6
  22.5 2.1 %broadcast_select_fusion.7 = (bf16[2,512,256]{2,1,0:T(8,128)(2,1)}, bf16[2,512,256]{2,1,0:T(8,128)(2,1)}) fusion(bf16[2,512,256]{2,1,0:T(8,128)(2,1)} %collective-permute-done, pred[]{:T(512)S(6)} %eq.54, bf16[1,512,256]{2,1,0:T(8,128)(2,1)S(1)} %copy-done.32, bf16[1,512,256]{2,1,0:T(8,128)(2,1)S(1)} %copy-done.33, pred[]{:T(512)S(6)} %eq.26), kind=kLoop, calls=%fused_computation.12 | loop fusion | flops 786432 | bytes 2097154 | tf_op jit(solution)/shard_map/jit(_where)/select_n | solution.py:265
  24.7 3.1 %collective-permute-start.2 = (bf16[2,512,256]{2,1,0:T(8,128)(2,1)}, bf16[2,512,256]{2,1,0:T(8,128)(2,1)}, u32[]{:S(2)}, u32[]{:S(2)}) collective-permute-start(bf16[2,512,256]{2,1,0:T(8,128)(2,1)} %get-tuple-element.105), channel_id=1, source_target_pairs={{2,0},{4,2},{6,4},{8,6},{10,8},{12,10},{14,12},{16,14},{18,16},{20... | collective-permute-start | bytes 1572872 | tf_op jit(solution)/shard_map/ppermute | solution.py:292
  27.8 3.0 %collective-permute-start.1 = (bf16[2,512,256]{2,1,0:T(8,128)(2,1)}, bf16[2,512,256]{2,1,0:T(8,128)(2,1)}, u32[]{:S(2)}, u32[]{:S(2)}) collective-permute-start(bf16[2,512,256]{2,1,0:T(8,128)(2,1)} %get-tuple-element.106), channel_id=1, source_target_pairs={{0,2},{2,4},{4,6},{6,8},{8,10},{10,12},{12,14},{14,16},{16,18},{18... | collective-permute-start | bytes 1572872 | tf_op jit(solution)/shard_map/ppermute | solution.py:292
  32.2 1.3 broadcast_select_fusion.6
  33.5 2.1 %collective-permute-start.5 = (bf16[2,512,256]{2,1,0:T(8,128)(2,1)S(1)}, bf16[2,512,256]{2,1,0:T(8,128)(2,1)S(1)}, u32[]{:S(2)}, u32[]{:S(2)}) collective-permute-start(bf16[2,512,256]{2,1,0:T(8,128)(2,1)S(1)} %get-tuple-element.95), channel_id=1, source_target_pairs={{2,0},{4,2},{6,4},{8,6},{10,8},{12,10},{14,12},{16,14},{18,16},{20... | collective-permute-start | bytes 1572872 | tf_op jit(solution)/shard_map/ppermute | solution.py:292
  35.6 3.6 %collective-permute-start.4 = (bf16[2,512,256]{2,1,0:T(8,128)(2,1)S(1)}, bf16[2,512,256]{2,1,0:T(8,128)(2,1)S(1)}, u32[]{:S(2)}, u32[]{:S(2)}) collective-permute-start(bf16[2,512,256]{2,1,0:T(8,128)(2,1)S(1)} %get-tuple-element.96), channel_id=1, source_target_pairs={{0,2},{2,4},{4,6},{6,8},{8,10},{10,12},{12,14},{14,16},{16,18},{18... | collective-permute-start | bytes 1572872 | tf_op jit(solution)/shard_map/ppermute | solution.py:292
  39.6 2.1 %collective-permute-done.2 = bf16[2,512,256]{2,1,0:T(8,128)(2,1)} collective-permute-done((bf16[2,512,256]{2,1,0:T(8,128)(2,1)}, bf16[2,512,256]{2,1,0:T(8,128)(2,1)}, u32[]{:S(2)}, u32[]{:S(2)}) %collective-permute-start.2) | collective-permute-done | bytes 524320 | tf_op jit(solution)/shard_map/ppermute | solution.py:292
  41.7 5.2 %collective-permute-done.1 = bf16[2,512,256]{2,1,0:T(8,128)(2,1)} collective-permute-done((bf16[2,512,256]{2,1,0:T(8,128)(2,1)}, bf16[2,512,256]{2,1,0:T(8,128)(2,1)}, u32[]{:S(2)}, u32[]{:S(2)}) %collective-permute-start.1) | collective-permute-done | bytes 524320 | tf_op jit(solution)/shard_map/ppermute | solution.py:292
  46.9 2.1 %broadcast_select_fusion.18 = (bf16[2,512,256]{2,1,0:T(8,128)(2,1)}, bf16[2,512,256]{2,1,0:T(8,128)(2,1)S(1)}) fusion(bf16[2,512,256]{2,1,0:T(8,128)(2,1)} %collective-permute-done.1, pred[]{:T(512)S(6)} %eq.24, bf16[2,512,256]{2,1,0:T(8,128)(2,1)} %get-tuple-element.106, bf16[2,512,256]{2,1,0:T(8,128)(2,1)} %collective-permute-done.2, pred[]{:T(512)S(6)} %eq.27, ...), kind=kLoop, calls=%fused_computation.23 | loop fusion | flops 786432 | bytes 2621443 | tf_op jit(solution)/shard_map/jit(_where)/select_n | solution.py:357
  49.3 5.9 %attention.4 = (bf16[512,2048]{1,0:T(8,128)(2,1)}, bf16[2,512,128]{2,1,0:T(8,128)(2,1)S(1)}, bf16[2,512,128]{2,1,0:T(8,128)(2,1)S(1)}, bf16[2,512,256]{2,1,0:T(8,128)(2,1)S(1)}) custom-call(s32[1]{0:T(128)} %bitcast.6.group_ref, s32[1,512]{1,0:T(1,128)S(1)} %bitcast.21, bf16[8,1024,128]{2,1,0:T(8,128)(2,1)S(1)} %get-tuple-element.49.q_ref, ...), custom_call_target="tpu_custom_call" | custom-call | flops 1677721600 | bytes 2457600 | tf_op jit(solution)/shard_map/attention/pallas_call | solution.py:183
  56.6 1.1 broadcast_select_fusion.14
  57.7 1.2 collective-permute-start.6
  59.0 1.6 %copy-done.2 = bf16[8,1024,128]{2,1,0:T(8,128)(2,1)S(1)} copy-done((bf16[8,1024,128]{2,1,0:T(8,128)(2,1)S(1)}, bf16[8,1024,128]{2,1,0:T(8,128)(2,1)}, u32[]{:S(2)}) %copy-start.2) | copy-done | bytes 2097176
  60.5 1.2 copy-done.5
  61.8 1.2 copy-done.8
  63.0 1.0 copy-done.11
  64.0 5.9 %attention.5 = (bf16[512,2048]{1,0:T(8,128)(2,1)}, bf16[2,512,128]{2,1,0:T(8,128)(2,1)S(1)}, bf16[2,512,128]{2,1,0:T(8,128)(2,1)S(1)}, bf16[2,512,256]{2,1,0:T(8,128)(2,1)S(1)}) custom-call(s32[1]{0:T(128)} %bitcast.6.group_ref, s32[1,512]{1,0:T(1,128)S(1)} %bitcast.22, ...), custom_call_target="tpu_custom_call", output_to_operand_aliasing={{0}: (9, {})} | custom-call | flops 1677721600 | bytes 2457600 | tf_op jit(solution)/shard_map/attention/pallas_call | solution.py:183
  72.1 6.7 %attention.6 = (bf16[512,2048]{1,0:T(8,128)(2,1)}, bf16[2,512,128]{2,1,0:T(8,128)(2,1)S(1)}, bf16[2,512,128]{2,1,0:T(8,128)(2,1)S(1)}, bf16[2,512,256]{2,1,0:T(8,128)(2,1)}) custom-call(s32[1]{0:T(128)} %bitcast.group_ref, s32[1,512]{1,0:T(1,128)S(1)} %bitcast.23, ...), custom_call_target="tpu_custom_call", output_to_operand_aliasing={{0}: (9, {})} | custom-call | flops 1677721600 | bytes 2457600 | tf_op jit(solution)/shard_map/attention/pallas_call | solution.py:183
  80.4 6.7 %attention.7 = (bf16[512,2048]{1,0:T(8,128)(2,1)}, bf16[2,512,128]{2,1,0:T(8,128)(2,1)S(1)}, bf16[2,512,128]{2,1,0:T(8,128)(2,1)S(1)}, bf16[2,512,256]{2,1,0:T(8,128)(2,1)}) custom-call(s32[1]{0:T(128)} %bitcast.group_ref, s32[1,512]{1,0:T(1,128)S(1)} %bitcast.24, ...), custom_call_target="tpu_custom_call", output_to_operand_aliasing={{0}: (9, {})} | custom-call | flops 1677721600 | bytes 2457600 | tf_op jit(solution)/shard_map/attention/pallas_call | solution.py:183
  88.5 1.2 collective-permute-start.8
  89.7 1.9 %collective-permute-done.12 = bf16[2,512,256]{2,1,0:T(8,128)(2,1)} collective-permute-done((bf16[2,512,256]{2,1,0:T(8,128)(2,1)}, bf16[2,512,256]{2,1,0:T(8,128)(2,1)}, u32[]{:S(2)}, u32[]{:S(2)}) %collective-permute-start.12) | collective-permute-done | bytes 524320 | tf_op jit(solution)/shard_map/ppermute | solution.py:288
  91.7 1.3 broadcast_select_fusion.2
  92.9 1.9 %collective-permute-start.13 = (bf16[2,512,256]{2,1,0:T(8,128)(2,1)S(1)}, bf16[2,512,256]{2,1,0:T(8,128)(2,1)S(1)}, u32[]{:S(2)}, u32[]{:S(2)}) collective-permute-start(bf16[2,512,256]{2,1,0:T(8,128)(2,1)S(1)} %get-tuple-element.91), channel_id=1, source_target_pairs={{2,0},{4,2},{6,4},{8,6},{10,8},{12,10},{14,12},{16,14},{18,16},{20... | collective-permute-start | bytes 1572872 | tf_op jit(solution)/shard_map/ppermute | solution.py:292
  94.9 8.4 %collective-permute-start.14 = (bf16[2,512,256]{2,1,0:T(8,128)(2,1)S(1)}, bf16[2,512,256]{2,1,0:T(8,128)(2,1)}, u32[]{:S(2)}, u32[]{:S(2)}) collective-permute-start(bf16[2,512,256]{2,1,0:T(8,128)(2,1)S(1)} %get-tuple-element.92), channel_id=1, source_target_pairs={{0,2},{2,4},{4,6},{6,8},{8,10},{10,12},{12,14},{14,16},{16,18},{18... | collective-permute-start | bytes 1572872 | tf_op jit(solution)/shard_map/ppermute | solution.py:292
  103.3 0.9 broadcast_select_fusion.3
  104.2 1.9 %collective-permute-start.9 = (bf16[2,512,256]{2,1,0:T(8,128)(2,1)}, bf16[2,512,256]{2,1,0:T(8,128)(2,1)S(1)}, u32[]{:S(2)}, u32[]{:S(2)}) collective-permute-start(bf16[2,512,256]{2,1,0:T(8,128)(2,1)} %get-tuple-element.93), channel_id=1, source_target_pairs={{2,0},{4,2},{6,4},{8,6},{10,8},{12,10},{14,12},{16,14},{18,16},{20... | collective-permute-start | bytes 1572872 | tf_op jit(solution)/shard_map/ppermute | solution.py:292
  106.1 3.6 %collective-permute-start.10 = (bf16[2,512,256]{2,1,0:T(8,128)(2,1)S(1)}, bf16[2,512,256]{2,1,0:T(8,128)(2,1)}, u32[]{:S(2)}, u32[]{:S(2)}) collective-permute-start(bf16[2,512,256]{2,1,0:T(8,128)(2,1)S(1)} %get-tuple-element.94), channel_id=1, source_target_pairs={{0,2},{2,4},{4,6},{6,8},{8,10},{10,12},{12,14},{14,16},{16,18},{18... | collective-permute-start | bytes 1572872 | tf_op jit(solution)/shard_map/ppermute | solution.py:292
  109.8 10.0 %collective-permute-done.13 = bf16[2,512,256]{2,1,0:T(8,128)(2,1)S(1)} collective-permute-done((bf16[2,512,256]{2,1,0:T(8,128)(2,1)S(1)}, bf16[2,512,256]{2,1,0:T(8,128)(2,1)S(1)}, u32[]{:S(2)}, u32[]{:S(2)}) %collective-permute-start.13) | collective-permute-done | bytes 524320 | tf_op jit(solution)/shard_map/ppermute | solution.py:292
  119.8 1.1 broadcast_select_fusion
  121.0 4.4 %collective-permute-done.9 = bf16[2,512,256]{2,1,0:T(8,128)(2,1)S(1)} collective-permute-done((bf16[2,512,256]{2,1,0:T(8,128)(2,1)}, bf16[2,512,256]{2,1,0:T(8,128)(2,1)S(1)}, u32[]{:S(2)}, u32[]{:S(2)}) %collective-permute-start.9) | collective-permute-done | bytes 524320 | tf_op jit(solution)/shard_map/ppermute | solution.py:292
  125.4 1.1 broadcast_select_fusion.1
  126.6 1.0 finish.4
  127.6 5.8 %collective-permute-done.15.back_ref = bf16[2,512,256]{2,1,0:T(8,128)(2,1)S(1)} collective-permute-done((bf16[2,512,256]{2,1,0:T(8,128)(2,1)S(1)}, bf16[2,512,256]{2,1,0:T(8,128)(2,1)S(1)}, u32[]{:S(2)}, u32[]{:S(2)}) %collective-permute-start.15) | collective-permute-done | bytes 524320 | tf_op jit(solution)/shard_map/ppermute | solution.py:288
  133.4 1.0 finish.5
  134.4 1.0 finish.6
  135.4 3.6 %collective-permute-done.11.back_ref = bf16[2,512,256]{2,1,0:T(8,128)(2,1)S(1)} collective-permute-done((bf16[2,512,256]{2,1,0:T(8,128)(2,1)S(1)}, bf16[2,512,256]{2,1,0:T(8,128)(2,1)S(1)}, u32[]{:S(2)}, u32[]{:S(2)}) %collective-permute-start.11) | collective-permute-done | bytes 524320 | tf_op jit(solution)/shard_map/ppermute | solution.py:288
  139.0 1.0 finish.7
  (81 shorter events, 10.4 us)
Async XLA Ops:
  3.1 3.2 %copy-start.35 = (s32[32]{0:T(128)S(1)}, s32[32]{0:T(128)}, u32[]{:S(2)}) copy-start(s32[32]{0:T(128)} %param.13) | copy-start | bytes 388
  4.0 18.5 %collective-permute-start = (bf16[2,512,256]{2,1,0:T(8,128)(2,1)}, bf16[2,512,256]{2,1,0:T(8,128)(2,1)}, u32[]{:S(2)}, u32[]{:S(2)}) collective-permute-start(bf16[2,512,256]{2,1,0:T(8,128)(2,1)} %pad_maximum_fusion), channel_id=1, source_target_pairs={{0,1},{1,0},{2,3},{3,2},{4,5},{5,4},{6,7},{7,6},{8,9},{9,8},{10,11... | collective-permute-start | bytes 1572872 | tf_op jit(solution)/shard_map/ppermute | solution.py:288
  5.1 27.1 %collective-permute-start.3 = (bf16[2,512,256]{2,1,0:T(8,128)(2,1)}, bf16[2,512,256]{2,1,0:T(8,128)(2,1)}, u32[]{:S(2)}, u32[]{:S(2)}) collective-permute-start(bf16[2,512,256]{2,1,0:T(8,128)(2,1)} %pad_maximum_fusion.3), channel_id=1, source_target_pairs={{0,1},{1,0},{2,3},{3,2},{4,5},{5,4},{6,7},{7,6},{8,9},{9,8},{10,11... | collective-permute-start | bytes 1572872 | tf_op jit(solution)/shard_map/ppermute | solution.py:288
  8.2 1.2 copy-start.9
  9.5 1.2 copy-start.10
  10.7 1.6 %copy-start.12 = (bf16[512,2048]{1,0:T(8,128)(2,1)S(1)}, bf16[512,2048]{1,0:T(8,128)(2,1)}, u32[]{:S(2)}) copy-start(bf16[512,2048]{1,0:T(8,128)(2,1)} %q_ref.1) | copy-start | bytes 6291460
  12.3 1.6 %copy-start.13 = (bf16[512,2048]{1,0:T(8,128)(2,1)S(1)}, bf16[512,2048]{1,0:T(8,128)(2,1)}, u32[]{:S(2)}) copy-start(bf16[512,2048]{1,0:T(8,128)(2,1)} %o_ref.1) | copy-start | bytes 6291460
  13.9 1.6 %copy-start.14 = (bf16[512,2048]{1,0:T(8,128)(2,1)S(1)}, bf16[512,2048]{1,0:T(8,128)(2,1)}, u32[]{:S(2)}) copy-start(bf16[512,2048]{1,0:T(8,128)(2,1)} %do_ref.1) | copy-start | bytes 6291460
  15.5 7.1 %copy-start.32 = (bf16[1,512,256]{2,1,0:T(8,128)(2,1)S(1)}, bf16[1,512,256]{2,1,0:T(8,128)(2,1)}, u32[]{:S(2)}) copy-start(bf16[1,512,256]{2,1,0:T(8,128)(2,1)} %get-tuple-element.104) | copy-start | bytes 786436
  15.5 7.1 %copy-start.33 = (bf16[1,512,256]{2,1,0:T(8,128)(2,1)S(1)}, bf16[1,512,256]{2,1,0:T(8,128)(2,1)}, u32[]{:S(2)}) copy-start(bf16[1,512,256]{2,1,0:T(8,128)(2,1)} %get-tuple-element.109) | copy-start | bytes 786436
  19.3 1.3 copy-start
  20.6 1.0 copy-start.3
  21.6 1.0 copy-start.6
  22.5 9.5 %copy-start.34 = (s32[16384]{0:T(1024)S(1)}, s32[16384]{0:T(1024)}, u32[]{:S(2)}) copy-start(s32[16384]{0:T(1024)} %param.12) | copy-start | bytes 196612
  24.7 17.0 %collective-permute-start.2 = (bf16[2,512,256]{2,1,0:T(8,128)(2,1)}, bf16[2,512,256]{2,1,0:T(8,128)(2,1)}, u32[]{:S(2)}, u32[]{:S(2)}) collective-permute-start(bf16[2,512,256]{2,1,0:T(8,128)(2,1)} %get-tuple-element.105), channel_id=1, source_target_pairs={{2,0},{4,2},{6,4},{8,6},{10,8},{12,10},{14,12},{16,14},{18,16},{20... | collective-permute-start | bytes 1572872 | tf_op jit(solution)/shard_map/ppermute | solution.py:292
  27.8 19.1 %collective-permute-start.1 = (bf16[2,512,256]{2,1,0:T(8,128)(2,1)}, bf16[2,512,256]{2,1,0:T(8,128)(2,1)}, u32[]{:S(2)}, u32[]{:S(2)}) collective-permute-start(bf16[2,512,256]{2,1,0:T(8,128)(2,1)} %get-tuple-element.106), channel_id=1, source_target_pairs={{0,2},{2,4},{4,6},{6,8},{8,10},{10,12},{12,14},{14,16},{16,18},{18... | collective-permute-start | bytes 1572872 | tf_op jit(solution)/shard_map/ppermute | solution.py:292
  32.2 17.1 %copy-start.1 = (bf16[8,1024,128]{2,1,0:T(8,128)(2,1)S(1)}, bf16[8,1024,128]{2,1,0:T(8,128)(2,1)}, u32[]{:S(2)}) copy-start(bf16[8,1024,128]{2,1,0:T(8,128)(2,1)} %copy-done) | copy-start | bytes 6291460
  32.2 17.1 %copy-start.4 = (bf16[8,128,512]{2,1,0:T(8,128)(2,1)S(1)}, bf16[8,128,512]{2,1,0:T(8,128)(2,1)}, u32[]{:S(2)}) copy-start(bf16[8,128,512]{2,1,0:T(8,128)(2,1)} %copy-done.3) | copy-start | bytes 3145732
  32.2 17.1 %copy-start.7 = (bf16[8,512,128]{2,1,0:T(8,128)(2,1)S(1)}, bf16[8,512,128]{2,1,0:T(8,128)(2,1)}, u32[]{:S(2)}) copy-start(bf16[8,512,128]{2,1,0:T(8,128)(2,1)} %copy-done.6) | copy-start | bytes 3145732
  33.5 23.1 %collective-permute-start.5 = (bf16[2,512,256]{2,1,0:T(8,128)(2,1)S(1)}, bf16[2,512,256]{2,1,0:T(8,128)(2,1)S(1)}, u32[]{:S(2)}, u32[]{:S(2)}) collective-permute-start(bf16[2,512,256]{2,1,0:T(8,128)(2,1)S(1)} %get-tuple-element.95), channel_id=1, source_target_pairs={{2,0},{4,2},{6,4},{8,6},{10,8},{12,10},{14,12},{16,14},{18,16},{20... | collective-permute-start | bytes 1572872 | tf_op jit(solution)/shard_map/ppermute | solution.py:292
  35.6 21.0 %collective-permute-start.4 = (bf16[2,512,256]{2,1,0:T(8,128)(2,1)S(1)}, bf16[2,512,256]{2,1,0:T(8,128)(2,1)S(1)}, u32[]{:S(2)}, u32[]{:S(2)}) collective-permute-start(bf16[2,512,256]{2,1,0:T(8,128)(2,1)S(1)} %get-tuple-element.96), channel_id=1, source_target_pairs={{0,2},{2,4},{4,6},{6,8},{8,10},{10,12},{12,14},{14,16},{16,18},{18... | collective-permute-start | bytes 1572872 | tf_op jit(solution)/shard_map/ppermute | solution.py:292
  49.0 23.1 %collective-permute-start.7 = (bf16[2,512,256]{2,1,0:T(8,128)(2,1)}, bf16[2,512,256]{2,1,0:T(8,128)(2,1)}, u32[]{:S(2)}, u32[]{:S(2)}) collective-permute-start(bf16[2,512,256]{2,1,0:T(8,128)(2,1)} %get-tuple-element.89), channel_id=1, source_target_pairs={{0,1},{1,0},{2,3},{3,2},{4,5},{5,4},{6,7},{7,6},{8,9},{9,8},{10,11... | collective-permute-start | bytes 1572872 | tf_op jit(solution)/shard_map/ppermute | solution.py:288
  55.1 0.8 copy-start.15
  57.7 22.7 %collective-permute-start.6 = (bf16[2,512,256]{2,1,0:T(8,128)(2,1)}, bf16[2,512,256]{2,1,0:T(8,128)(2,1)}, u32[]{:S(2)}, u32[]{:S(2)}) collective-permute-start(bf16[2,512,256]{2,1,0:T(8,128)(2,1)} %get-tuple-element.88), channel_id=1, source_target_pairs={{0,1},{1,0},{2,3},{3,2},{4,5},{5,4},{6,7},{7,6},{8,9},{9,8},{10,11... | collective-permute-start | bytes 1572872 | tf_op jit(solution)/shard_map/ppermute | solution.py:288
  59.0 1.6 %copy-start.2 = (bf16[8,1024,128]{2,1,0:T(8,128)(2,1)S(1)}, bf16[8,1024,128]{2,1,0:T(8,128)(2,1)}, u32[]{:S(2)}) copy-start(bf16[8,1024,128]{2,1,0:T(8,128)(2,1)} %copy-done) | copy-start | bytes 6291460
  60.5 1.2 copy-start.5
  61.8 1.2 copy-start.8
  63.0 1.0 copy-start.11
  69.9 0.8 copy-start.16
  71.4 0.7 copy-start.22
  79.5 0.7 copy-start.30
  80.2 11.5 %collective-permute-start.12 = (bf16[2,512,256]{2,1,0:T(8,128)(2,1)}, bf16[2,512,256]{2,1,0:T(8,128)(2,1)}, u32[]{:S(2)}, u32[]{:S(2)}) collective-permute-start(bf16[2,512,256]{2,1,0:T(8,128)(2,1)} %get-tuple-element.72), channel_id=1, source_target_pairs={{0,1},{1,0},{2,3},{3,2},{4,5},{5,4},{6,7},{7,6},{8,9},{9,8},{10,11... | collective-permute-start | bytes 1572872 | tf_op jit(solution)/shard_map/ppermute | solution.py:288
  87.1 0.7 copy-start.24
  88.5 14.8 %copy-start.17 = (bf16[2,512,256]{2,1,0:T(8,128)(2,1)S(1)}, bf16[2,512,256]{2,1,0:T(8,128)(2,1)}, u32[]{:S(2)}) copy-start(bf16[2,512,256]{2,1,0:T(8,128)(2,1)} %copy-done.16) | copy-start | bytes 1572868
  88.5 14.8 %collective-permute-start.8 = (bf16[2,512,256]{2,1,0:T(8,128)(2,1)}, bf16[2,512,256]{2,1,0:T(8,128)(2,1)S(1)}, u32[]{:S(2)}, u32[]{:S(2)}) collective-permute-start(bf16[2,512,256]{2,1,0:T(8,128)(2,1)} %get-tuple-element.66), channel_id=1, source_target_pairs={{0,1},{1,0},{2,3},{3,2},{4,5},{5,4},{6,7},{7,6},{8,9},{9,8},{10,11... | collective-permute-start | bytes 1572872 | tf_op jit(solution)/shard_map/ppermute | solution.py:288
  92.9 26.8 %collective-permute-start.13 = (bf16[2,512,256]{2,1,0:T(8,128)(2,1)S(1)}, bf16[2,512,256]{2,1,0:T(8,128)(2,1)S(1)}, u32[]{:S(2)}, u32[]{:S(2)}) collective-permute-start(bf16[2,512,256]{2,1,0:T(8,128)(2,1)S(1)} %get-tuple-element.91), channel_id=1, source_target_pairs={{2,0},{4,2},{6,4},{8,6},{10,8},{12,10},{14,12},{16,14},{18,16},{20... | collective-permute-start | bytes 1572872 | tf_op jit(solution)/shard_map/ppermute | solution.py:292
  94.9 24.9 %collective-permute-start.14 = (bf16[2,512,256]{2,1,0:T(8,128)(2,1)S(1)}, bf16[2,512,256]{2,1,0:T(8,128)(2,1)}, u32[]{:S(2)}, u32[]{:S(2)}) collective-permute-start(bf16[2,512,256]{2,1,0:T(8,128)(2,1)S(1)} %get-tuple-element.92), channel_id=1, source_target_pairs={{0,2},{2,4},{4,6},{6,8},{8,10},{10,12},{12,14},{14,16},{16,18},{18... | collective-permute-start | bytes 1572872 | tf_op jit(solution)/shard_map/ppermute | solution.py:292
  104.2 21.2 %collective-permute-start.9 = (bf16[2,512,256]{2,1,0:T(8,128)(2,1)}, bf16[2,512,256]{2,1,0:T(8,128)(2,1)S(1)}, u32[]{:S(2)}, u32[]{:S(2)}) collective-permute-start(bf16[2,512,256]{2,1,0:T(8,128)(2,1)} %get-tuple-element.93), channel_id=1, source_target_pairs={{2,0},{4,2},{6,4},{8,6},{10,8},{12,10},{14,12},{16,14},{18,16},{20... | collective-permute-start | bytes 1572872 | tf_op jit(solution)/shard_map/ppermute | solution.py:292
  106.1 19.3 %collective-permute-start.10 = (bf16[2,512,256]{2,1,0:T(8,128)(2,1)S(1)}, bf16[2,512,256]{2,1,0:T(8,128)(2,1)}, u32[]{:S(2)}, u32[]{:S(2)}) collective-permute-start(bf16[2,512,256]{2,1,0:T(8,128)(2,1)S(1)} %get-tuple-element.94), channel_id=1, source_target_pairs={{0,2},{2,4},{4,6},{6,8},{8,10},{10,12},{12,14},{14,16},{16,18},{18... | collective-permute-start | bytes 1572872 | tf_op jit(solution)/shard_map/ppermute | solution.py:292
  109.8 16.8 %copy-start.19 = (bf16[2,512,128]{2,1,0:T(8,128)(2,1)S(1)}, bf16[2,512,128]{2,1,0:T(8,128)(2,1)}, u32[]{:S(2)}) copy-start(bf16[2,512,128]{2,1,0:T(8,128)(2,1)} %copy-done.18) | copy-start | bytes 786436
  120.9 12.5 %copy-start.29 = (bf16[2,512,128]{2,1,0:T(8,128)(2,1)S(1)}, bf16[2,512,128]{2,1,0:T(8,128)(2,1)}, u32[]{:S(2)}) copy-start(bf16[2,512,128]{2,1,0:T(8,128)(2,1)} %copy-done.28) | copy-start | bytes 786436
  120.9 12.5 %copy-start.31 = (bf16[2,512,128]{2,1,0:T(8,128)(2,1)S(1)}, bf16[2,512,128]{2,1,0:T(8,128)(2,1)}, u32[]{:S(2)}) copy-start(bf16[2,512,128]{2,1,0:T(8,128)(2,1)} %copy-done.30) | copy-start | bytes 786436
  120.9 12.5 %collective-permute-start.15 = (bf16[2,512,256]{2,1,0:T(8,128)(2,1)S(1)}, bf16[2,512,256]{2,1,0:T(8,128)(2,1)S(1)}, u32[]{:S(2)}, u32[]{:S(2)}) collective-permute-start(bf16[2,512,256]{2,1,0:T(8,128)(2,1)S(1)} %get-tuple-element.84), channel_id=1, source_target_pairs={{0,1},{1,0},{2,3},{3,2},{4,5},{5,4},{6,7},{7,6},{8,9},{9,8},{10,11... | collective-permute-start | bytes 1572872 | tf_op jit(solution)/shard_map/ppermute | solution.py:288
  126.5 12.5 %collective-permute-start.11 = (bf16[2,512,256]{2,1,0:T(8,128)(2,1)S(1)}, bf16[2,512,256]{2,1,0:T(8,128)(2,1)S(1)}, u32[]{:S(2)}, u32[]{:S(2)}) collective-permute-start(bf16[2,512,256]{2,1,0:T(8,128)(2,1)S(1)} %get-tuple-element.86), channel_id=1, source_target_pairs={{0,1},{1,0},{2,3},{3,2},{4,5},{5,4},{6,7},{7,6},{8,9},{9,8},{10,11... | collective-permute-start | bytes 1572872 | tf_op jit(solution)/shard_map/ppermute | solution.py:288
  126.6 7.8 %copy-start.21 = (bf16[2,512,128]{2,1,0:T(8,128)(2,1)S(1)}, bf16[2,512,128]{2,1,0:T(8,128)(2,1)}, u32[]{:S(2)}) copy-start(bf16[2,512,128]{2,1,0:T(8,128)(2,1)} %copy-done.20) | copy-start | bytes 786436
  126.6 7.8 %copy-start.23 = (bf16[2,512,128]{2,1,0:T(8,128)(2,1)S(1)}, bf16[2,512,128]{2,1,0:T(8,128)(2,1)}, u32[]{:S(2)}) copy-start(bf16[2,512,128]{2,1,0:T(8,128)(2,1)} %copy-done.22) | copy-start | bytes 786436
  134.4 4.6 %copy-start.25 = (bf16[2,512,128]{2,1,0:T(8,128)(2,1)S(1)}, bf16[2,512,128]{2,1,0:T(8,128)(2,1)}, u32[]{:S(2)}) copy-start(bf16[2,512,128]{2,1,0:T(8,128)(2,1)} %copy-done.24) | copy-start | bytes 786436
  134.4 4.6 %copy-start.27 = (bf16[2,512,128]{2,1,0:T(8,128)(2,1)S(1)}, bf16[2,512,128]{2,1,0:T(8,128)(2,1)}, u32[]{:S(2)}) copy-start(bf16[2,512,128]{2,1,0:T(8,128)(2,1)} %copy-done.26) | copy-start | bytes 786436
  (4 other events, 2.8 us)

commit v13 on v6

--- a/solution.py
+++ b/solution.py
@@ -14,6 +14,7 @@
 TILE = 128
 STRIP = 64
 VMEM_BYTES = 60 * 1024 * 1024
+FINISH_VMEM_BYTES = 6 * 1024 * 1024
 
 
 def dot(left, right, left_dim, right_dim):
@@ -247,7 +248,7 @@
         ),
         out_shape=[jax.ShapeDtypeStruct((rows, heads * HEAD_SIZE), jnp.bfloat16)] * 2,
         input_output_aliases={4 + i: i for i in range(len(carried))},
-        compiler_params=pltpu.CompilerParams(vmem_limit_bytes=VMEM_BYTES),
+        compiler_params=pltpu.CompilerParams(vmem_limit_bytes=FINISH_VMEM_BYTES),
         cost_estimate=pl.CostEstimate(
             flops=count * rows * 512, bytes_accessed=count * rows * 2048, transcendentals=0
         ),

time: 126 us -> 123 us (0.976)
  waiting for transfers between devices: 30 us -> 35.6 us
  Pallas kernels: 46.1 us -> 42.1 us
  other arithmetic: 11.1 us -> 8.41 us
  local copies, waits for them, and re-layouts: 3.97 us -> 2.42 us
    ppermute x8, waiting for transfers between devices: 18.4 us -> 23.2 us  [turned(): return lax.ppermute(value, 'head', pairs)]
    pallas_call x4, Pallas kernels: 7.96 us -> 3.9 us  [finish(): pl.pallas_call(functools.partial(finish_body, len(carried)), grid_spec=pl...]
    select_n x2, other arithmetic: 3.87 us -> 1.23 us  [rows_of(): jnp.where(is_early(device), sums[0], sums[1])]
    unnamed x16 -> x28, local copies, waits for them, and re-layouts: 3.22 us -> 1.67 us
  transfers between devices with their start and end apart: 16 -> 16, of which waited for: 8 -> 8; matrix products, arithmetic and copies ran while one was open for 8% -> 6% of each run, Pallas kernels for 35% -> 34%
where the time goes in v13:
time: 123 us; the launch traced here: 122 us
  Pallas kernels  42.1 us (34%)
  waiting for transfers between devices  35.6 us (29%)
  starting transfers between devices  30.2 us (25%)
  other arithmetic  8.41 us (7%)
  between operations  3.51 us (3%)
  local copies, waits for them, and re-layouts  2.42 us (2%)
    pallas_call x4, Pallas kernels, attention(): pl.pallas_call(functools.partial(attention_body, len(carried)), grid_spec...  28.4 us
    ppermute x8, starting transfers between devices, shifted(): lax.ppermute(value, 'blk', [(source, source + step) for source in range(f...  26.2 us
    ppermute x8, waiting for transfers between devices, turned(): return lax.ppermute(value, 'head', pairs)  23.2 us
    ppermute x8, waiting for transfers between devices, shifted(): lax.ppermute(value, 'blk', [(source, source + step) for source in range(f...  12.4 us
    pallas_call x2, Pallas kernels, arrange(): pl.pallas_call(arrange_body, grid=(groups, per_piece), in_specs=[query_sp...  9.75 us
    ppermute x8, starting transfers between devices, turned(): return lax.ppermute(value, 'head', pairs)  4.02 us
    pallas_call x4, Pallas kernels, finish(): pl.pallas_call(functools.partial(finish_body, len(carried)), grid_spec=pl...  3.9 us
    select_n x4, other arithmetic, pick(): result = jnp.where(index == place, items[place], result)  2.68 us
  transfers between devices with their start and end apart: 16, of which 8 were waited for; matrix products, arithmetic and copies ran while one was open for 6% of the time, Pallas kernels for 34%

profile of v13, /device:TPU:11, one launch (start us, length us, event | category | flops | bytes accessed | tf_op | source)
XLA Modules:
  0.0 122.3 jit_solution(8324310962282073400)
XLA Ops:
  0.6 1.7 %select_bitcast_fusion = (bf16[1,512,256]{2,1,0:T(8,128)(2,1)S(1)}, bf16[1,512,256]{2,1,0:T(8,128)(2,1)S(1)}, bf16[1,512,256]{2,1,0:T(8,128)(2,1)S(1)}, bf16[1,5...) fusion(pred[]{:T(512)S(6)} %eq.22, ...), kind=kLoop, calls=%fused_computation.25 | loop fusion | flops 1048576 | bytes 4194306 | tf_op jit(solution)/shard_map/stack | solution.py:303
  2.4 0.3 collective-permute-start.1
  2.8 1.3 %collective-permute-start = (bf16[2,512,256]{2,1,0:T(8,128)(2,1)S(1)}, bf16[2,512,256]{2,1,0:T(8,128)(2,1)S(1)}, u32[]{:S(2)}, u32[]{:S(2)}) collective-permute-start(bf16[2,512,256]{2,1,0:T(8,128)(2,1)S(1)} %pad_maximum_fusion), channel_id=1, source_target_pairs={{0,1},{1,0},{2,3},{3,2},{4,5},{5,4},{6,7},{7,6},{8,9},{9,8},{10,11... | collective-permute-start | bytes 1572872 | tf_op jit(solution)/shard_map/ppermute | solution.py:289
  4.1 0.1 dynamic_slice.6
  4.1 0.6 fusion
  6.0 4.9 %arrange.3 = (bf16[4,1024,128]{2,1,0:T(8,128)(2,1)}, bf16[4,1024,128]{2,1,0:T(8,128)(2,1)}, f32[4,1,1024]{2,1,0:T(1,128)}, bf16[4,512,128]{2,1,0:T(8,128)(2,1)},...) custom-call(bf16[512,2048]{1,0:T(8,128)(2,1)} %q_ref.3, bf16[512,1024]{1,0:T(8,128)(2,1)} %k_ref.3, ...), custom_call_target="tpu_custom_call" | custom-call | flops 2097152 | bytes 8388608 | tf_op jit(solution)/shard_map/arrange/pallas_call | solution.py:73
  10.9 4.3 %collective-permute-done.1 = bf16[2,512,256]{2,1,0:T(8,128)(2,1)S(1)} collective-permute-done((bf16[2,512,256]{2,1,0:T(8,128)(2,1)S(1)}, bf16[2,512,256]{2,1,0:T(8,128)(2,1)S(1)}, u32[]{:S(2)}, u32[]{:S(2)}) %collective-permute-start.1) | collective-permute-done | bytes 524320 | tf_op jit(solution)/shard_map/ppermute | solution.py:289
  15.3 0.9 broadcast_select_fusion.7
  16.1 4.6 %collective-permute-start.3 = (bf16[2,512,256]{2,1,0:T(8,128)(2,1)}, bf16[2,512,256]{2,1,0:T(8,128)(2,1)S(1)}, u32[]{:S(2)}, u32[]{:S(2)}) collective-permute-start(bf16[2,512,256]{2,1,0:T(8,128)(2,1)} %get-tuple-element.131), channel_id=1, source_target_pairs={{2,0},{4,2},{6,4},{8,6},{10,8},{12,10},{14,12},{16,14},{18,16},{20... | collective-permute-start | bytes 1572872 | tf_op jit(solution)/shard_map/ppermute | solution.py:293
  20.7 3.0 %collective-permute-start.2 = (bf16[2,512,256]{2,1,0:T(8,128)(2,1)S(1)}, bf16[2,512,256]{2,1,0:T(8,128)(2,1)S(1)}, u32[]{:S(2)}, u32[]{:S(2)}) collective-permute-start(bf16[2,512,256]{2,1,0:T(8,128)(2,1)S(1)} %get-tuple-element.132), channel_id=1, source_target_pairs={{0,2},{2,4},{4,6},{6,8},{8,10},{10,12},{12,14},{14,16},{16,18},{18... | collective-permute-start | bytes 1572872 | tf_op jit(solution)/shard_map/ppermute | solution.py:293
  25.1 0.1 pad_dynamic-slice_fusion
  25.2 4.9 %arrange.2 = (bf16[4,1024,128]{2,1,0:T(8,128)(2,1)}, bf16[4,1024,128]{2,1,0:T(8,128)(2,1)}, f32[4,1,1024]{2,1,0:T(1,128)}, bf16[4,512,128]{2,1,0:T(8,128)(2,1)},...) custom-call(bf16[512,2048]{1,0:T(8,128)(2,1)} %q_ref.3, bf16[512,1024]{1,0:T(8,128)(2,1)} %k_ref.3, ...), custom_call_target="tpu_custom_call" | custom-call | flops 2097152 | bytes 8388608 | tf_op jit(solution)/shard_map/arrange/pallas_call | solution.py:73
  30.1 0.9 broadcast_select_fusion.6
  30.9 1.9 %collective-permute-start.5 = (bf16[2,512,256]{2,1,0:T(8,128)(2,1)}, bf16[2,512,256]{2,1,0:T(8,128)(2,1)S(1)}, u32[]{:S(2)}, u32[]{:S(2)}) collective-permute-start(bf16[2,512,256]{2,1,0:T(8,128)(2,1)} %get-tuple-element.121), channel_id=1, source_target_pairs={{2,0},{4,2},{6,4},{8,6},{10,8},{12,10},{14,12},{16,14},{18,16},{20... | collective-permute-start | bytes 1572872 | tf_op jit(solution)/shard_map/ppermute | solution.py:293
  32.9 3.6 %collective-permute-start.4 = (bf16[2,512,256]{2,1,0:T(8,128)(2,1)S(1)}, bf16[2,512,256]{2,1,0:T(8,128)(2,1)S(1)}, u32[]{:S(2)}, u32[]{:S(2)}) collective-permute-start(bf16[2,512,256]{2,1,0:T(8,128)(2,1)S(1)} %get-tuple-element.122), channel_id=1, source_target_pairs={{0,2},{2,4},{4,6},{6,8},{8,10},{10,12},{12,14},{14,16},{16,18},{18... | collective-permute-start | bytes 1572872 | tf_op jit(solution)/shard_map/ppermute | solution.py:293
  36.5 0.9 convert_reduce_fusion
  37.5 0.9 broadcast_select_fusion.18
  38.3 0.3 collective-permute-start.7
  38.6 7.1 %attention.4 = (bf16[512,2048]{1,0:T(8,128)(2,1)}, bf16[2,512,128]{2,1,0:T(8,128)(2,1)}, bf16[2,512,128]{2,1,0:T(8,128)(2,1)}, bf16[2,512,256]{2,1,0:T(8,128)(2,1)}) custom-call(s32[1]{0:T(128)} %bitcast.6.group_ref, s32[1,512]{1,0:T(1,128)} %bitcast.21, bf16[4,1024,128]{2,1,0:T(8,128)(2,1)} %get-tuple-element.74.q_ref, ...), custom_call_target="tpu_custom_call" | custom-call | flops 1677721600 | bytes 2457600 | tf_op jit(solution)/shard_map/attention/pallas_call | solution.py:184
  45.7 1.9 %collective-permute-done.5 = bf16[2,512,256]{2,1,0:T(8,128)(2,1)S(1)} collective-permute-done((bf16[2,512,256]{2,1,0:T(8,128)(2,1)}, bf16[2,512,256]{2,1,0:T(8,128)(2,1)S(1)}, u32[]{:S(2)}, u32[]{:S(2)}) %collective-permute-start.5) | collective-permute-done | bytes 524320 | tf_op jit(solution)/shard_map/ppermute | solution.py:293
  47.6 0.9 broadcast_select_fusion.14
  48.4 0.3 collective-permute-start.6
  48.7 7.1 %attention.5 = (bf16[512,2048]{1,0:T(8,128)(2,1)}, bf16[2,512,128]{2,1,0:T(8,128)(2,1)}, bf16[2,512,128]{2,1,0:T(8,128)(2,1)}, bf16[2,512,256]{2,1,0:T(8,128)(2,1)}) custom-call(s32[1]{0:T(128)} %bitcast.6.group_ref, s32[1,512]{1,0:T(1,128)} %bitcast.22, bf16[4,1024,128]{2,1,0:T(8,128)(2,1)} %get-tuple-element.62.q_ref, ...), custom_call_target="tpu_custom_call", output_to_operand_aliasing={{0}: (9, {})} | custom-call | flops 1677721600 | bytes 2457600 | tf_op jit(solution)/shard_map/attention/pallas_call | solution.py:184
  55.8 0.8 copy-done.8
  56.6 7.1 %attention.6 = (bf16[512,2048]{1,0:T(8,128)(2,1)}, bf16[2,512,128]{2,1,0:T(8,128)(2,1)}, bf16[2,512,128]{2,1,0:T(8,128)(2,1)}, bf16[2,512,256]{2,1,0:T(8,128)(2,1)}) custom-call(s32[1]{0:T(128)} %bitcast.group_ref, s32[1,512]{1,0:T(1,128)} %bitcast.23, bf16[4,1024,128]{2,1,0:T(8,128)(2,1)} %get-tuple-element.74.q_ref, ...), custom_call_target="tpu_custom_call", output_to_operand_aliasing={{0}: (9, {})} | custom-call | flops 1677721600 | bytes 2457600 | tf_op jit(solution)/shard_map/attention/pallas_call | solution.py:184
  63.7 1.3 %collective-permute-start.12 = (bf16[2,512,256]{2,1,0:T(8,128)(2,1)}, bf16[2,512,256]{2,1,0:T(8,128)(2,1)S(1)}, u32[]{:S(2)}, u32[]{:S(2)}) collective-permute-start(bf16[2,512,256]{2,1,0:T(8,128)(2,1)} %get-tuple-element.98), channel_id=1, source_target_pairs={{0,1},{1,0},{2,3},{3,2},{4,5},{5,4},{6,7},{7,6},{8,9},{9,8},{10,11... | collective-permute-start | bytes 1572872 | tf_op jit(solution)/shard_map/ppermute | solution.py:289
  65.0 0.8 copy-done.9
  65.8 7.1 %attention.7 = (bf16[512,2048]{1,0:T(8,128)(2,1)}, bf16[2,512,128]{2,1,0:T(8,128)(2,1)}, bf16[2,512,128]{2,1,0:T(8,128)(2,1)}, bf16[2,512,256]{2,1,0:T(8,128)(2,1)}) custom-call(s32[1]{0:T(128)} %bitcast.group_ref, s32[1,512]{1,0:T(1,128)} %bitcast.24, bf16[4,1024,128]{2,1,0:T(8,128)(2,1)} %get-tuple-element.62.q_ref, ...), custom_call_target="tpu_custom_call", output_to_operand_aliasing={{0}: (9, {})} | custom-call | flops 1677721600 | bytes 2457600 | tf_op jit(solution)/shard_map/attention/pallas_call | solution.py:184
  73.0 0.3 collective-permute-start.8
  73.3 4.6 %collective-permute-done.12 = bf16[2,512,256]{2,1,0:T(8,128)(2,1)S(1)} collective-permute-done((bf16[2,512,256]{2,1,0:T(8,128)(2,1)}, bf16[2,512,256]{2,1,0:T(8,128)(2,1)S(1)}, u32[]{:S(2)}, u32[]{:S(2)}) %collective-permute-start.12) | collective-permute-done | bytes 524320 | tf_op jit(solution)/shard_map/ppermute | solution.py:289
  78.0 2.2 %collective-permute-start.13 = (bf16[2,512,256]{2,1,0:T(8,128)(2,1)S(1)}, bf16[2,512,256]{2,1,0:T(8,128)(2,1)S(1)}, u32[]{:S(2)}, u32[]{:S(2)}) collective-permute-start(bf16[2,512,256]{2,1,0:T(8,128)(2,1)S(1)} %get-tuple-element.117), channel_id=1, source_target_pairs={{2,0},{4,2},{6,4},{8,6},{10,8},{12,10},{14,12},{16,14},{18,16},{20... | collective-permute-start | bytes 1572872 | tf_op jit(solution)/shard_map/ppermute | solution.py:293
  80.2 5.3 %collective-permute-start.14 = (bf16[2,512,256]{2,1,0:T(8,128)(2,1)S(1)}, bf16[2,512,256]{2,1,0:T(8,128)(2,1)}, u32[]{:S(2)}, u32[]{:S(2)}) collective-permute-start(bf16[2,512,256]{2,1,0:T(8,128)(2,1)S(1)} %get-tuple-element.118), channel_id=1, source_target_pairs={{0,2},{2,4},{4,6},{6,8},{8,10},{10,12},{12,14},{14,16},{16,18},{18... | collective-permute-start | bytes 1572872 | tf_op jit(solution)/shard_map/ppermute | solution.py:293
  85.5 3.7 %collective-permute-done.8 = bf16[2,512,256]{2,1,0:T(8,128)(2,1)S(1)} collective-permute-done((bf16[2,512,256]{2,1,0:T(8,128)(2,1)}, bf16[2,512,256]{2,1,0:T(8,128)(2,1)S(1)}, u32[]{:S(2)}, u32[]{:S(2)}) %collective-permute-start.8) | collective-permute-done | bytes 524320 | tf_op jit(solution)/shard_map/ppermute | solution.py:289
  89.2 0.9 broadcast_select_fusion.3
  90.1 2.1 %collective-permute-start.9 = (bf16[2,512,256]{2,1,0:T(8,128)(2,1)}, bf16[2,512,256]{2,1,0:T(8,128)(2,1)S(1)}, u32[]{:S(2)}, u32[]{:S(2)}) collective-permute-start(bf16[2,512,256]{2,1,0:T(8,128)(2,1)} %get-tuple-element.119), channel_id=1, source_target_pairs={{2,0},{4,2},{6,4},{8,6},{10,8},{12,10},{14,12},{16,14},{18,16},{20... | collective-permute-start | bytes 1572872 | tf_op jit(solution)/shard_map/ppermute | solution.py:293
  92.2 3.4 %collective-permute-start.10 = (bf16[2,512,256]{2,1,0:T(8,128)(2,1)S(1)}, bf16[2,512,256]{2,1,0:T(8,128)(2,1)S(1)}, u32[]{:S(2)}, u32[]{:S(2)}) collective-permute-start(bf16[2,512,256]{2,1,0:T(8,128)(2,1)S(1)} %get-tuple-element.120), channel_id=1, source_target_pairs={{0,2},{2,4},{4,6},{6,8},{8,10},{10,12},{12,14},{14,16},{16,18},{18... | collective-permute-start | bytes 1572872 | tf_op jit(solution)/shard_map/ppermute | solution.py:293
  95.7 0.3 collective-permute-done.13
  96.0 1.1 broadcast_select_fusion
  97.2 0.2 collective-permute-start.15
  97.4 10.2 %collective-permute-done.9 = bf16[2,512,256]{2,1,0:T(8,128)(2,1)S(1)} collective-permute-done((bf16[2,512,256]{2,1,0:T(8,128)(2,1)}, bf16[2,512,256]{2,1,0:T(8,128)(2,1)S(1)}, u32[]{:S(2)}, u32[]{:S(2)}) %collective-permute-start.9) | collective-permute-done | bytes 524320 | tf_op jit(solution)/shard_map/ppermute | solution.py:293
  107.5 0.1 broadcast_select_fusion.1
  107.6 0.1 collective-permute-start.11
  107.8 1.0 finish.4
  108.8 2.4 %collective-permute-done.15.back_ref = bf16[2,512,256]{2,1,0:T(8,128)(2,1)S(1)} collective-permute-done((bf16[2,512,256]{2,1,0:T(8,128)(2,1)S(1)}, bf16[2,512,256]{2,1,0:T(8,128)(2,1)S(1)}, u32[]{:S(2)}, u32[]{:S(2)}) %collective-permute-start.15) | collective-permute-done | bytes 524320 | tf_op jit(solution)/shard_map/ppermute | solution.py:289
  111.2 1.0 finish.5
  112.2 1.0 finish.6
  113.1 8.2 %collective-permute-done.11.back_ref = bf16[2,512,256]{2,1,0:T(8,128)(2,1)S(1)} collective-permute-done((bf16[2,512,256]{2,1,0:T(8,128)(2,1)S(1)}, bf16[2,512,256]{2,1,0:T(8,128)(2,1)S(1)}, u32[]{:S(2)}, u32[]{:S(2)}) %collective-permute-start.11) | collective-permute-done | bytes 524320 | tf_op jit(solution)/shard_map/ppermute | solution.py:289
  121.3 1.0 finish.7
  (38 shorter events, 0.3 us)
Async XLA Ops:
  2.3 1.7 %copy-start.13 = (s32[32]{0:T(128)S(1)}, s32[32]{0:T(128)}, u32[]{:S(2)}) copy-start(s32[32]{0:T(128)} %param.13) | copy-start | bytes 388
  2.4 12.9 %collective-permute-start.1 = (bf16[2,512,256]{2,1,0:T(8,128)(2,1)S(1)}, bf16[2,512,256]{2,1,0:T(8,128)(2,1)S(1)}, u32[]{:S(2)}, u32[]{:S(2)}) collective-permute-start(bf16[2,512,256]{2,1,0:T(8,128)(2,1)S(1)} %pad_maximum_fusion.1), channel_id=1, source_target_pairs={{0,1},{1,0},{2,3},{3,2},{4,5},{5,4},{6,7},{7,6},{8,9},{9,8},{10,11... | collective-permute-start | bytes 1572872 | tf_op jit(solution)/shard_map/ppermute | solution.py:289
  2.8 27.3 %collective-permute-start = (bf16[2,512,256]{2,1,0:T(8,128)(2,1)S(1)}, bf16[2,512,256]{2,1,0:T(8,128)(2,1)S(1)}, u32[]{:S(2)}, u32[]{:S(2)}) collective-permute-start(bf16[2,512,256]{2,1,0:T(8,128)(2,1)S(1)} %pad_maximum_fusion), channel_id=1, source_target_pairs={{0,1},{1,0},{2,3},{3,2},{4,5},{5,4},{6,7},{7,6},{8,9},{9,8},{10,11... | collective-permute-start | bytes 1572872 | tf_op jit(solution)/shard_map/ppermute | solution.py:289
  10.9 14.2 %copy-start.12 = (s32[16384]{0:T(1024)S(1)}, s32[16384]{0:T(1024)}, u32[]{:S(2)}) copy-start(s32[16384]{0:T(1024)} %param.12) | copy-start | bytes 196612
  16.1 21.3 %collective-permute-start.3 = (bf16[2,512,256]{2,1,0:T(8,128)(2,1)}, bf16[2,512,256]{2,1,0:T(8,128)(2,1)S(1)}, u32[]{:S(2)}, u32[]{:S(2)}) collective-permute-start(bf16[2,512,256]{2,1,0:T(8,128)(2,1)} %get-tuple-element.131), channel_id=1, source_target_pairs={{2,0},{4,2},{6,4},{8,6},{10,8},{12,10},{14,12},{16,14},{18,16},{20... | collective-permute-start | bytes 1572872 | tf_op jit(solution)/shard_map/ppermute | solution.py:293
  20.7 16.7 %collective-permute-start.2 = (bf16[2,512,256]{2,1,0:T(8,128)(2,1)S(1)}, bf16[2,512,256]{2,1,0:T(8,128)(2,1)S(1)}, u32[]{:S(2)}, u32[]{:S(2)}) collective-permute-start(bf16[2,512,256]{2,1,0:T(8,128)(2,1)S(1)} %get-tuple-element.132), channel_id=1, source_target_pairs={{0,2},{2,4},{4,6},{6,8},{8,10},{10,12},{12,14},{14,16},{16,18},{18... | collective-permute-start | bytes 1572872 | tf_op jit(solution)/shard_map/ppermute | solution.py:293
  30.9 16.6 %collective-permute-start.5 = (bf16[2,512,256]{2,1,0:T(8,128)(2,1)}, bf16[2,512,256]{2,1,0:T(8,128)(2,1)S(1)}, u32[]{:S(2)}, u32[]{:S(2)}) collective-permute-start(bf16[2,512,256]{2,1,0:T(8,128)(2,1)} %get-tuple-element.121), channel_id=1, source_target_pairs={{2,0},{4,2},{6,4},{8,6},{10,8},{12,10},{14,12},{16,14},{18,16},{20... | collective-permute-start | bytes 1572872 | tf_op jit(solution)/shard_map/ppermute | solution.py:293
  32.9 14.7 %collective-permute-start.4 = (bf16[2,512,256]{2,1,0:T(8,128)(2,1)S(1)}, bf16[2,512,256]{2,1,0:T(8,128)(2,1)S(1)}, u32[]{:S(2)}, u32[]{:S(2)}) collective-permute-start(bf16[2,512,256]{2,1,0:T(8,128)(2,1)S(1)} %get-tuple-element.122), channel_id=1, source_target_pairs={{0,2},{2,4},{4,6},{6,8},{8,10},{10,12},{12,14},{14,16},{16,18},{18... | collective-permute-start | bytes 1572872 | tf_op jit(solution)/shard_map/ppermute | solution.py:293
  38.3 17.5 %collective-permute-start.7 = (bf16[2,512,256]{2,1,0:T(8,128)(2,1)S(1)}, bf16[2,512,256]{2,1,0:T(8,128)(2,1)S(1)}, u32[]{:S(2)}, u32[]{:S(2)}) collective-permute-start(bf16[2,512,256]{2,1,0:T(8,128)(2,1)S(1)} %get-tuple-element.115), channel_id=1, source_target_pairs={{0,1},{1,0},{2,3},{3,2},{4,5},{5,4},{6,7},{7,6},{8,9},{9,8},{10,11... | collective-permute-start | bytes 1572872 | tf_op jit(solution)/shard_map/ppermute | solution.py:289
  48.4 16.6 %collective-permute-start.6 = (bf16[2,512,256]{2,1,0:T(8,128)(2,1)S(1)}, bf16[2,512,256]{2,1,0:T(8,128)(2,1)S(1)}, u32[]{:S(2)}, u32[]{:S(2)}) collective-permute-start(bf16[2,512,256]{2,1,0:T(8,128)(2,1)S(1)} %get-tuple-element.114), channel_id=1, source_target_pairs={{0,1},{1,0},{2,3},{3,2},{4,5},{5,4},{6,7},{7,6},{8,9},{9,8},{10,11... | collective-permute-start | bytes 1572872 | tf_op jit(solution)/shard_map/ppermute | solution.py:289
  55.8 0.8 copy-start.8
  63.7 14.2 %collective-permute-start.12 = (bf16[2,512,256]{2,1,0:T(8,128)(2,1)}, bf16[2,512,256]{2,1,0:T(8,128)(2,1)S(1)}, u32[]{:S(2)}, u32[]{:S(2)}) collective-permute-start(bf16[2,512,256]{2,1,0:T(8,128)(2,1)} %get-tuple-element.98), channel_id=1, source_target_pairs={{0,1},{1,0},{2,3},{3,2},{4,5},{5,4},{6,7},{7,6},{8,9},{9,8},{10,11... | collective-permute-start | bytes 1572872 | tf_op jit(solution)/shard_map/ppermute | solution.py:289
  65.0 0.8 copy-start.9
  65.8 12.1 %copy-start.10 = (bf16[2,512,256]{2,1,0:T(8,128)(2,1)S(1)}, bf16[2,512,256]{2,1,0:T(8,128)(2,1)}, u32[]{:S(2)}) copy-start(bf16[2,512,256]{2,1,0:T(8,128)(2,1)} %get-tuple-element.97) | copy-start | bytes 1572868
  73.0 16.2 %copy-start.11 = (bf16[2,512,256]{2,1,0:T(8,128)(2,1)S(1)}, bf16[2,512,256]{2,1,0:T(8,128)(2,1)}, u32[]{:S(2)}) copy-start(bf16[2,512,256]{2,1,0:T(8,128)(2,1)} %get-tuple-element.91) | copy-start | bytes 1572868
  73.0 16.2 %collective-permute-start.8 = (bf16[2,512,256]{2,1,0:T(8,128)(2,1)}, bf16[2,512,256]{2,1,0:T(8,128)(2,1)S(1)}, u32[]{:S(2)}, u32[]{:S(2)}) collective-permute-start(bf16[2,512,256]{2,1,0:T(8,128)(2,1)} %get-tuple-element.92), channel_id=1, source_target_pairs={{0,1},{1,0},{2,3},{3,2},{4,5},{5,4},{6,7},{7,6},{8,9},{9,8},{10,11... | collective-permute-start | bytes 1572872 | tf_op jit(solution)/shard_map/ppermute | solution.py:289
  78.0 18.0 %collective-permute-start.13 = (bf16[2,512,256]{2,1,0:T(8,128)(2,1)S(1)}, bf16[2,512,256]{2,1,0:T(8,128)(2,1)S(1)}, u32[]{:S(2)}, u32[]{:S(2)}) collective-permute-start(bf16[2,512,256]{2,1,0:T(8,128)(2,1)S(1)} %get-tuple-element.117), channel_id=1, source_target_pairs={{2,0},{4,2},{6,4},{8,6},{10,8},{12,10},{14,12},{16,14},{18,16},{20... | collective-permute-start | bytes 1572872 | tf_op jit(solution)/shard_map/ppermute | solution.py:293
  80.2 15.8 %collective-permute-start.14 = (bf16[2,512,256]{2,1,0:T(8,128)(2,1)S(1)}, bf16[2,512,256]{2,1,0:T(8,128)(2,1)}, u32[]{:S(2)}, u32[]{:S(2)}) collective-permute-start(bf16[2,512,256]{2,1,0:T(8,128)(2,1)S(1)} %get-tuple-element.118), channel_id=1, source_target_pairs={{0,2},{2,4},{4,6},{6,8},{8,10},{10,12},{12,14},{14,16},{16,18},{18... | collective-permute-start | bytes 1572872 | tf_op jit(solution)/shard_map/ppermute | solution.py:293
  90.1 17.5 %collective-permute-start.9 = (bf16[2,512,256]{2,1,0:T(8,128)(2,1)}, bf16[2,512,256]{2,1,0:T(8,128)(2,1)S(1)}, u32[]{:S(2)}, u32[]{:S(2)}) collective-permute-start(bf16[2,512,256]{2,1,0:T(8,128)(2,1)} %get-tuple-element.119), channel_id=1, source_target_pairs={{2,0},{4,2},{6,4},{8,6},{10,8},{12,10},{14,12},{16,14},{18,16},{20... | collective-permute-start | bytes 1572872 | tf_op jit(solution)/shard_map/ppermute | solution.py:293
  92.2 15.3 %collective-permute-start.10 = (bf16[2,512,256]{2,1,0:T(8,128)(2,1)S(1)}, bf16[2,512,256]{2,1,0:T(8,128)(2,1)S(1)}, u32[]{:S(2)}, u32[]{:S(2)}) collective-permute-start(bf16[2,512,256]{2,1,0:T(8,128)(2,1)S(1)} %get-tuple-element.120), channel_id=1, source_target_pairs={{0,2},{2,4},{4,6},{6,8},{8,10},{10,12},{12,14},{14,16},{16,18},{18... | collective-permute-start | bytes 1572872 | tf_op jit(solution)/shard_map/ppermute | solution.py:293
  95.7 12.1 %copy-start = (bf16[2,512,128]{2,1,0:T(8,128)(2,1)S(1)}, bf16[2,512,128]{2,1,0:T(8,128)(2,1)}, u32[]{:S(2)}) copy-start(bf16[2,512,128]{2,1,0:T(8,128)(2,1)} %get-tuple-element.99.dk_ref) | copy-start | bytes 786436
  95.7 12.1 %copy-start.1 = (bf16[2,512,128]{2,1,0:T(8,128)(2,1)S(1)}, bf16[2,512,128]{2,1,0:T(8,128)(2,1)}, u32[]{:S(2)}) copy-start(bf16[2,512,128]{2,1,0:T(8,128)(2,1)} %get-tuple-element.100.dv_ref) | copy-start | bytes 786436
  97.2 14.0 %copy-start.6 = (bf16[2,512,128]{2,1,0:T(8,128)(2,1)S(1)}, bf16[2,512,128]{2,1,0:T(8,128)(2,1)}, u32[]{:S(2)}) copy-start(bf16[2,512,128]{2,1,0:T(8,128)(2,1)} %get-tuple-element.95.dk_ref) | copy-start | bytes 786436
  97.2 14.0 %copy-start.7 = (bf16[2,512,128]{2,1,0:T(8,128)(2,1)S(1)}, bf16[2,512,128]{2,1,0:T(8,128)(2,1)}, u32[]{:S(2)}) copy-start(bf16[2,512,128]{2,1,0:T(8,128)(2,1)} %get-tuple-element.96.dv_ref) | copy-start | bytes 786436
  97.2 14.0 %collective-permute-start.15 = (bf16[2,512,256]{2,1,0:T(8,128)(2,1)S(1)}, bf16[2,512,256]{2,1,0:T(8,128)(2,1)S(1)}, u32[]{:S(2)}, u32[]{:S(2)}) collective-permute-start(bf16[2,512,256]{2,1,0:T(8,128)(2,1)S(1)} %get-tuple-element.110), channel_id=1, source_target_pairs={{0,1},{1,0},{2,3},{3,2},{4,5},{5,4},{6,7},{7,6},{8,9},{9,8},{10,11... | collective-permute-start | bytes 1572872 | tf_op jit(solution)/shard_map/ppermute | solution.py:289
  107.6 13.7 %collective-permute-start.11 = (bf16[2,512,256]{2,1,0:T(8,128)(2,1)S(1)}, bf16[2,512,256]{2,1,0:T(8,128)(2,1)S(1)}, u32[]{:S(2)}, u32[]{:S(2)}) collective-permute-start(bf16[2,512,256]{2,1,0:T(8,128)(2,1)S(1)} %get-tuple-element.112), channel_id=1, source_target_pairs={{0,1},{1,0},{2,3},{3,2},{4,5},{5,4},{6,7},{7,6},{8,9},{9,8},{10,11... | collective-permute-start | bytes 1572872 | tf_op jit(solution)/shard_map/ppermute | solution.py:289
  107.8 4.4 %copy-start.2 = (bf16[2,512,128]{2,1,0:T(8,128)(2,1)S(1)}, bf16[2,512,128]{2,1,0:T(8,128)(2,1)}, u32[]{:S(2)}) copy-start(bf16[2,512,128]{2,1,0:T(8,128)(2,1)} %get-tuple-element.93.dk_ref) | copy-start | bytes 786436
  107.8 4.4 %copy-start.3 = (bf16[2,512,128]{2,1,0:T(8,128)(2,1)S(1)}, bf16[2,512,128]{2,1,0:T(8,128)(2,1)}, u32[]{:S(2)}) copy-start(bf16[2,512,128]{2,1,0:T(8,128)(2,1)} %get-tuple-element.94.dv_ref) | copy-start | bytes 786436
  112.1 9.2 %copy-start.4 = (bf16[2,512,128]{2,1,0:T(8,128)(2,1)S(1)}, bf16[2,512,128]{2,1,0:T(8,128)(2,1)}, u32[]{:S(2)}) copy-start(bf16[2,512,128]{2,1,0:T(8,128)(2,1)} %get-tuple-element.89.dk_ref) | copy-start | bytes 786436
  112.1 9.2 %copy-start.5 = (bf16[2,512,128]{2,1,0:T(8,128)(2,1)S(1)}, bf16[2,512,128]{2,1,0:T(8,128)(2,1)}, u32[]{:S(2)}) copy-start(bf16[2,512,128]{2,1,0:T(8,128)(2,1)} %get-tuple-element.90.dv_ref) | copy-start | bytes 786436

commit v14 on v13

--- a/solution.py
+++ b/solution.py
@@ -362,14 +362,24 @@
             own = jnp.where(is_early(device), early, late)
             return part_rows(jnp.concatenate([before, own], axis=1), device, window)
 
-        pasts.append([turned(past_of(other(turn)), turn) for turn in range(1, sharers)])
-        carried, back = run(0, chunk, past_of(place), carried)
-        terms.append([back])
-
+        pasts.append(
+            [past_of(place)] + [turned(past_of(other(turn)), turn) for turn in range(1, sharers)]
+        )
+        if chunk == 0:
+            carried, back = run(0, 0, pasts[0][0], carried)
+            terms.append([back])
+
+    if chunks > 1:
+        pasts[0][1], _ = together(pasts[0][1], pasts[1][0])
     for chunk in range(chunks):
+        swapped = []
         for turn in range(1, sharers):
-            carried, back = run(turn, chunk, pasts[chunk][turn - 1], carried)
-            terms[chunk].append(turned(back, -turn))
+            carried, back = run(turn, chunk, pasts[chunk][turn], carried)
+            swapped.append(turned(back, -turn))
+        if chunk:
+            carried, back = run(0, chunk, pasts[chunk][0], carried)
+            terms.append([back])
+        terms[chunk] += swapped
 
     (query_grads,) = carried
     results = ()

time: 123 us -> 123 us (level)
  starting transfers between devices: 30.2 us -> 28.4 us
  transfers between devices with their start and end apart: 16 -> 16, of which waited for: 8 -> 8; matrix products, arithmetic and copies ran while one was open for 6% -> 7% of each run, Pallas kernels for 34% -> 34%
where the time goes in v14:
time: 123 us; the launch traced here: 121 us
  Pallas kernels  42.1 us (34%)
  waiting for transfers between devices  35.3 us (29%)
  starting transfers between devices  28.4 us (23%)
  other arithmetic  9.43 us (8%)
  between operations  3.51 us (3%)
  local copies, waits for them, and re-layouts  2.43 us (2%)
    pallas_call x4, Pallas kernels, attention(): pl.pallas_call(functools.partial(attention_body, len(carried)), grid_spec...  28.5 us
    ppermute x8, starting transfers between devices, shifted(): lax.ppermute(value, 'blk', [(source, source + step) for source in range(f...  25 us
    ppermute x8, waiting for transfers between devices, turned(): return lax.ppermute(value, 'head', pairs)  22.4 us
    ppermute x8, waiting for transfers between devices, shifted(): lax.ppermute(value, 'blk', [(source, source + step) for source in range(f...  12.9 us
    pallas_call x2, Pallas kernels, arrange(): pl.pallas_call(arrange_body, grid=(groups, per_piece), in_specs=[query_sp...  9.76 us
    pallas_call x4, Pallas kernels, finish(): pl.pallas_call(functools.partial(finish_body, len(carried)), grid_spec=pl...  3.92 us
    select_n x4, other arithmetic, pick(): result = jnp.where(index == place, items[place], result)  3.72 us
    ppermute x8, starting transfers between devices, turned(): return lax.ppermute(value, 'head', pairs)  3.39 us
  transfers between devices with their start and end apart: 16, of which 8 were waited for; matrix products, arithmetic and copies ran while one was open for 7% of the time, Pallas kernels for 34%

profile of v14, /device:TPU:11, one launch (start us, length us, event | category | flops | bytes accessed | tf_op | source)
XLA Modules:
  0.0 121.2 jit_solution(7258094537625988161)
XLA Ops:
  0.6 1.7 %select_bitcast_fusion = (bf16[1,512,256]{2,1,0:T(8,128)(2,1)S(1)}, bf16[1,512,256]{2,1,0:T(8,128)(2,1)S(1)}, bf16[1,512,256]{2,1,0:T(8,128)(2,1)S(1)}, bf16[1,5...) fusion(pred[]{:T(512)S(6)} %eq.22, ...), kind=kLoop, calls=%fused_computation.25 | loop fusion | flops 1048576 | bytes 4194306 | tf_op jit(solution)/shard_map/stack | solution.py:303
  2.4 0.3 collective-permute-start.1
  2.8 1.3 %collective-permute-start = (bf16[2,512,256]{2,1,0:T(8,128)(2,1)S(1)}, bf16[2,512,256]{2,1,0:T(8,128)(2,1)S(1)}, u32[]{:S(2)}, u32[]{:S(2)}) collective-permute-start(bf16[2,512,256]{2,1,0:T(8,128)(2,1)S(1)} %pad_maximum_fusion), channel_id=1, source_target_pairs={{0,1},{1,0},{2,3},{3,2},{4,5},{5,4},{6,7},{7,6},{8,9},{9,8},{10,11... | collective-permute-start | bytes 1572872 | tf_op jit(solution)/shard_map/ppermute | solution.py:289
  4.1 0.1 dynamic_slice.6
  4.1 0.6 fusion
  6.0 4.9 %arrange.3 = (bf16[4,1024,128]{2,1,0:T(8,128)(2,1)}, bf16[4,1024,128]{2,1,0:T(8,128)(2,1)}, f32[4,1,1024]{2,1,0:T(1,128)}, bf16[4,512,128]{2,1,0:T(8,128)(2,1)},...) custom-call(bf16[512,2048]{1,0:T(8,128)(2,1)} %q_ref.3, bf16[512,1024]{1,0:T(8,128)(2,1)} %k_ref.3, ...), custom_call_target="tpu_custom_call" | custom-call | flops 2097152 | bytes 8388608 | tf_op jit(solution)/shard_map/arrange/pallas_call | solution.py:73
  10.9 4.3 %collective-permute-done.1 = bf16[2,512,256]{2,1,0:T(8,128)(2,1)S(1)} collective-permute-done((bf16[2,512,256]{2,1,0:T(8,128)(2,1)S(1)}, bf16[2,512,256]{2,1,0:T(8,128)(2,1)S(1)}, u32[]{:S(2)}, u32[]{:S(2)}) %collective-permute-start.1) | collective-permute-done | bytes 524320 | tf_op jit(solution)/shard_map/ppermute | solution.py:289
  15.3 0.9 broadcast_select_fusion.11
  16.1 4.6 %collective-permute-start.3 = (bf16[2,512,256]{2,1,0:T(8,128)(2,1)}, bf16[2,512,256]{2,1,0:T(8,128)(2,1)S(1)}, u32[]{:S(2)}, u32[]{:S(2)}) collective-permute-start(bf16[2,512,256]{2,1,0:T(8,128)(2,1)} %get-tuple-element.133), channel_id=1, source_target_pairs={{2,0},{4,2},{6,4},{8,6},{10,8},{12,10},{14,12},{16,14},{18,16},{20... | collective-permute-start | bytes 1572872 | tf_op jit(solution)/shard_map/ppermute | solution.py:293
  20.7 3.0 %collective-permute-start.2 = (bf16[2,512,256]{2,1,0:T(8,128)(2,1)S(1)}, bf16[2,512,256]{2,1,0:T(8,128)(2,1)S(1)}, u32[]{:S(2)}, u32[]{:S(2)}) collective-permute-start(bf16[2,512,256]{2,1,0:T(8,128)(2,1)S(1)} %get-tuple-element.134), channel_id=1, source_target_pairs={{0,2},{2,4},{4,6},{6,8},{8,10},{10,12},{12,14},{14,16},{16,18},{18... | collective-permute-start | bytes 1572872 | tf_op jit(solution)/shard_map/ppermute | solution.py:293
  25.1 0.1 pad_dynamic-slice_fusion
  25.2 4.9 %arrange.2 = (bf16[4,1024,128]{2,1,0:T(8,128)(2,1)}, bf16[4,1024,128]{2,1,0:T(8,128)(2,1)}, f32[4,1,1024]{2,1,0:T(1,128)}, bf16[4,512,128]{2,1,0:T(8,128)(2,1)},...) custom-call(bf16[512,2048]{1,0:T(8,128)(2,1)} %q_ref.3, bf16[512,1024]{1,0:T(8,128)(2,1)} %k_ref.3, ...), custom_call_target="tpu_custom_call" | custom-call | flops 2097152 | bytes 8388608 | tf_op jit(solution)/shard_map/arrange/pallas_call | solution.py:73
  30.1 0.9 broadcast_select_fusion.10
  30.9 1.9 %collective-permute-start.5 = (bf16[2,512,256]{2,1,0:T(8,128)(2,1)}, bf16[2,512,256]{2,1,0:T(8,128)(2,1)S(1)}, u32[]{:S(2)}, u32[]{:S(2)}) collective-permute-start(bf16[2,512,256]{2,1,0:T(8,128)(2,1)} %get-tuple-element.123), channel_id=1, source_target_pairs={{2,0},{4,2},{6,4},{8,6},{10,8},{12,10},{14,12},{16,14},{18,16},{20... | collective-permute-start | bytes 1572872 | tf_op jit(solution)/shard_map/ppermute | solution.py:293
  32.9 3.6 %collective-permute-start.4 = (bf16[2,512,256]{2,1,0:T(8,128)(2,1)S(1)}, bf16[2,512,256]{2,1,0:T(8,128)(2,1)S(1)}, u32[]{:S(2)}, u32[]{:S(2)}) collective-permute-start(bf16[2,512,256]{2,1,0:T(8,128)(2,1)S(1)} %get-tuple-element.124), channel_id=1, source_target_pairs={{0,2},{2,4},{4,6},{6,8},{8,10},{10,12},{12,14},{14,16},{16,18},{18... | collective-permute-start | bytes 1572872 | tf_op jit(solution)/shard_map/ppermute | solution.py:293
  36.5 0.9 convert_reduce_fusion
  37.4 0.9 broadcast_select_fusion.8
  38.3 0.3 collective-permute-start.7
  38.6 7.1 %attention.4 = (bf16[512,2048]{1,0:T(8,128)(2,1)}, bf16[2,512,128]{2,1,0:T(8,128)(2,1)}, bf16[2,512,128]{2,1,0:T(8,128)(2,1)}, bf16[2,512,256]{2,1,0:T(8,128)(2,1)}) custom-call(s32[1]{0:T(128)} %bitcast.group_ref, s32[1,512]{1,0:T(1,128)} %bitcast.21, bf16[4,1024,128]{2,1,0:T(8,128)(2,1)} %get-tuple-element.75.q_ref, ...), custom_call_target="tpu_custom_call" | custom-call | flops 1677721600 | bytes 2457600 | tf_op jit(solution)/shard_map/attention/pallas_call | solution.py:184
  45.7 1.9 %collective-permute-done.5 = bf16[2,512,256]{2,1,0:T(8,128)(2,1)S(1)} collective-permute-done((bf16[2,512,256]{2,1,0:T(8,128)(2,1)}, bf16[2,512,256]{2,1,0:T(8,128)(2,1)S(1)}, u32[]{:S(2)}, u32[]{:S(2)}) %collective-permute-start.5) | collective-permute-done | bytes 524320 | tf_op jit(solution)/shard_map/ppermute | solution.py:293
  47.6 0.9 broadcast_select_fusion.9
  48.5 0.3 collective-permute-start.6
  48.7 3.3 %collective-permute-done.7.past_ref = bf16[2,512,256]{2,1,0:T(8,128)(2,1)S(1)} collective-permute-done((bf16[2,512,256]{2,1,0:T(8,128)(2,1)S(1)}, bf16[2,512,256]{2,1,0:T(8,128)(2,1)S(1)}, u32[]{:S(2)}, u32[]{:S(2)}) %collective-permute-start.7) | collective-permute-done | bytes 524320 | tf_op jit(solution)/shard_map/ppermute | solution.py:289
  52.0 0.8 copy-done.8
  52.8 7.1 %attention.5 = (bf16[512,2048]{1,0:T(8,128)(2,1)}, bf16[2,512,128]{2,1,0:T(8,128)(2,1)}, bf16[2,512,128]{2,1,0:T(8,128)(2,1)}, bf16[2,512,256]{2,1,0:T(8,128)(2,1)}) custom-call(s32[1]{0:T(128)} %bitcast.12.group_ref, s32[1,512]{1,0:T(1,128)} %bitcast.22, bf16[4,1024,128]{2,1,0:T(8,128)(2,1)} %get-tuple-element.75.q_ref, ...), custom_call_target="tpu_custom_call", output_to_operand_aliasing={{0}: (9, {})} | custom-call | flops 1677721600 | bytes 2457600 | tf_op jit(solution)/shard_map/attention/pallas_call | solution.py:184
  59.9 0.3 collective-permute-start.12
  60.2 3.0 %collective-permute-done.6.past_ref = bf16[2,512,256]{2,1,0:T(8,128)(2,1)S(1)} collective-permute-done((bf16[2,512,256]{2,1,0:T(8,128)(2,1)S(1)}, bf16[2,512,256]{2,1,0:T(8,128)(2,1)S(1)}, u32[]{:S(2)}, u32[]{:S(2)}) %collective-permute-start.6) | collective-permute-done | bytes 524320 | tf_op jit(solution)/shard_map/ppermute | solution.py:289
  63.2 0.8 copy-done.9
  64.1 7.1 %attention.6 = (bf16[512,2048]{1,0:T(8,128)(2,1)}, bf16[2,512,128]{2,1,0:T(8,128)(2,1)}, bf16[2,512,128]{2,1,0:T(8,128)(2,1)}, bf16[2,512,256]{2,1,0:T(8,128)(2,1)}) custom-call(s32[1]{0:T(128)} %bitcast.12.group_ref, s32[1,512]{1,0:T(1,128)} %bitcast.23, bf16[4,1024,128]{2,1,0:T(8,128)(2,1)} %get-tuple-element.63.q_ref, ...), custom_call_target="tpu_custom_call", output_to_operand_aliasing={{0}: (9, {})} | custom-call | flops 1677721600 | bytes 2457600 | tf_op jit(solution)/shard_map/attention/pallas_call | solution.py:184
  71.2 0.3 collective-permute-start.8
  71.5 2.4 %collective-permute-done.12 = bf16[2,512,256]{2,1,0:T(8,128)(2,1)S(1)} collective-permute-done((bf16[2,512,256]{2,1,0:T(8,128)(2,1)}, bf16[2,512,256]{2,1,0:T(8,128)(2,1)S(1)}, u32[]{:S(2)}, u32[]{:S(2)}) %collective-permute-start.12) | collective-permute-done | bytes 524320 | tf_op jit(solution)/shard_map/ppermute | solution.py:289
  74.0 3.6 %collective-permute-start.13 = (bf16[2,512,256]{2,1,0:T(8,128)(2,1)S(1)}, bf16[2,512,256]{2,1,0:T(8,128)(2,1)S(1)}, u32[]{:S(2)}, u32[]{:S(2)}) collective-permute-start(bf16[2,512,256]{2,1,0:T(8,128)(2,1)S(1)} %get-tuple-element.119), channel_id=1, source_target_pairs={{2,0},{4,2},{6,4},{8,6},{10,8},{12,10},{14,12},{16,14},{18,16},{20... | collective-permute-start | bytes 1572872 | tf_op jit(solution)/shard_map/ppermute | solution.py:293
  77.6 2.7 %collective-permute-start.14 = (bf16[2,512,256]{2,1,0:T(8,128)(2,1)S(1)}, bf16[2,512,256]{2,1,0:T(8,128)(2,1)S(1)}, u32[]{:S(2)}, u32[]{:S(2)}) collective-permute-start(bf16[2,512,256]{2,1,0:T(8,128)(2,1)S(1)} %get-tuple-element.120), channel_id=1, source_target_pairs={{0,2},{2,4},{4,6},{6,8},{8,10},{10,12},{12,14},{14,16},{16,18},{18... | collective-permute-start | bytes 1572872 | tf_op jit(solution)/shard_map/ppermute | solution.py:293
  80.3 7.1 %attention.7 = (bf16[512,2048]{1,0:T(8,128)(2,1)}, bf16[2,512,128]{2,1,0:T(8,128)(2,1)}, bf16[2,512,128]{2,1,0:T(8,128)(2,1)}, bf16[2,512,256]{2,1,0:T(8,128)(2,1)}) custom-call(s32[1]{0:T(128)} %bitcast.group_ref, s32[1,512]{1,0:T(1,128)} %bitcast.24, bf16[4,1024,128]{2,1,0:T(8,128)(2,1)} %get-tuple-element.63.q_ref, ...), custom_call_target="tpu_custom_call", output_to_operand_aliasing={{0}: (9, {})} | custom-call | flops 1677721600 | bytes 2457600 | tf_op jit(solution)/shard_map/attention/pallas_call | solution.py:184
  87.4 1.9 %broadcast_select_fusion.3 = (bf16[2,512,256]{2,1,0:T(8,128)(2,1)}, bf16[2,512,256]{2,1,0:T(8,128)(2,1)S(1)}) fusion(bf16[2,512,256]{2,1,0:T(8,128)(2,1)} %get-tuple-element.93, bf16[2,512,256]{2,1,0:T(8,128)(2,1)S(1)} %collective-permute-done.8, pred[]{:T(512)S(6)} %eq.56, pred[]{:T(512)S(6)} %eq.55), kind=kLoop, calls=%fused_computation.8 | loop fusion | flops 524288 | bytes 2097154 | tf_op jit(solution)/shard_map/jit(_where)/select_n | solution.py:266
  89.3 1.9 %collective-permute-start.9 = (bf16[2,512,256]{2,1,0:T(8,128)(2,1)}, bf16[2,512,256]{2,1,0:T(8,128)(2,1)S(1)}, u32[]{:S(2)}, u32[]{:S(2)}) collective-permute-start(bf16[2,512,256]{2,1,0:T(8,128)(2,1)} %get-tuple-element.121), channel_id=1, source_target_pairs={{2,0},{4,2},{6,4},{8,6},{10,8},{12,10},{14,12},{16,14},{18,16},{20... | collective-permute-start | bytes 1572872 | tf_op jit(solution)/shard_map/ppermute | solution.py:293
  91.2 3.6 %collective-permute-start.10 = (bf16[2,512,256]{2,1,0:T(8,128)(2,1)S(1)}, bf16[2,512,256]{2,1,0:T(8,128)(2,1)}, u32[]{:S(2)}, u32[]{:S(2)}) collective-permute-start(bf16[2,512,256]{2,1,0:T(8,128)(2,1)S(1)} %get-tuple-element.122), channel_id=1, source_target_pairs={{0,2},{2,4},{4,6},{6,8},{8,10},{10,12},{12,14},{14,16},{16,18},{18... | collective-permute-start | bytes 1572872 | tf_op jit(solution)/shard_map/ppermute | solution.py:293
  94.9 0.1 broadcast_select_fusion
  95.0 0.3 collective-permute-start.15
  95.4 10.6 %collective-permute-done.9 = bf16[2,512,256]{2,1,0:T(8,128)(2,1)S(1)} collective-permute-done((bf16[2,512,256]{2,1,0:T(8,128)(2,1)}, bf16[2,512,256]{2,1,0:T(8,128)(2,1)S(1)}, u32[]{:S(2)}, u32[]{:S(2)}) %collective-permute-start.9) | collective-permute-done | bytes 524320 | tf_op jit(solution)/shard_map/ppermute | solution.py:293
  105.9 0.5 collective-permute-done.10
  106.4 1.1 broadcast_select_fusion.1
  107.5 0.3 collective-permute-start.11
  107.9 1.0 finish.4
  108.9 1.0 finish.5
  109.9 1.0 finish.6
  110.8 9.3 %collective-permute-done.11.back_ref = bf16[2,512,256]{2,1,0:T(8,128)(2,1)S(1)} collective-permute-done((bf16[2,512,256]{2,1,0:T(8,128)(2,1)S(1)}, bf16[2,512,256]{2,1,0:T(8,128)(2,1)S(1)}, u32[]{:S(2)}, u32[]{:S(2)}) %collective-permute-start.11) | collective-permute-done | bytes 524320 | tf_op jit(solution)/shard_map/ppermute | solution.py:289
  120.2 1.0 finish.7
  (36 shorter events, 0.3 us)
Async XLA Ops:
  2.3 1.7 %copy-start.12 = (s32[32]{0:T(128)S(1)}, s32[32]{0:T(128)}, u32[]{:S(2)}) copy-start(s32[32]{0:T(128)} %param.13) | copy-start | bytes 388
  2.4 12.9 %collective-permute-start.1 = (bf16[2,512,256]{2,1,0:T(8,128)(2,1)S(1)}, bf16[2,512,256]{2,1,0:T(8,128)(2,1)S(1)}, u32[]{:S(2)}, u32[]{:S(2)}) collective-permute-start(bf16[2,512,256]{2,1,0:T(8,128)(2,1)S(1)} %pad_maximum_fusion.1), channel_id=1, source_target_pairs={{0,1},{1,0},{2,3},{3,2},{4,5},{5,4},{6,7},{7,6},{8,9},{9,8},{10,11... | collective-permute-start | bytes 1572872 | tf_op jit(solution)/shard_map/ppermute | solution.py:289
  2.8 27.3 %collective-permute-start = (bf16[2,512,256]{2,1,0:T(8,128)(2,1)S(1)}, bf16[2,512,256]{2,1,0:T(8,128)(2,1)S(1)}, u32[]{:S(2)}, u32[]{:S(2)}) collective-permute-start(bf16[2,512,256]{2,1,0:T(8,128)(2,1)S(1)} %pad_maximum_fusion), channel_id=1, source_target_pairs={{0,1},{1,0},{2,3},{3,2},{4,5},{5,4},{6,7},{7,6},{8,9},{9,8},{10,11... | collective-permute-start | bytes 1572872 | tf_op jit(solution)/shard_map/ppermute | solution.py:289
  10.9 14.2 %copy-start.11 = (s32[16384]{0:T(1024)S(1)}, s32[16384]{0:T(1024)}, u32[]{:S(2)}) copy-start(s32[16384]{0:T(1024)} %param.12) | copy-start | bytes 196612
  16.1 21.3 %collective-permute-start.3 = (bf16[2,512,256]{2,1,0:T(8,128)(2,1)}, bf16[2,512,256]{2,1,0:T(8,128)(2,1)S(1)}, u32[]{:S(2)}, u32[]{:S(2)}) collective-permute-start(bf16[2,512,256]{2,1,0:T(8,128)(2,1)} %get-tuple-element.133), channel_id=1, source_target_pairs={{2,0},{4,2},{6,4},{8,6},{10,8},{12,10},{14,12},{16,14},{18,16},{20... | collective-permute-start | bytes 1572872 | tf_op jit(solution)/shard_map/ppermute | solution.py:293
  20.7 16.7 %collective-permute-start.2 = (bf16[2,512,256]{2,1,0:T(8,128)(2,1)S(1)}, bf16[2,512,256]{2,1,0:T(8,128)(2,1)S(1)}, u32[]{:S(2)}, u32[]{:S(2)}) collective-permute-start(bf16[2,512,256]{2,1,0:T(8,128)(2,1)S(1)} %get-tuple-element.134), channel_id=1, source_target_pairs={{0,2},{2,4},{4,6},{6,8},{8,10},{10,12},{12,14},{14,16},{16,18},{18... | collective-permute-start | bytes 1572872 | tf_op jit(solution)/shard_map/ppermute | solution.py:293
  30.9 16.6 %collective-permute-start.5 = (bf16[2,512,256]{2,1,0:T(8,128)(2,1)}, bf16[2,512,256]{2,1,0:T(8,128)(2,1)S(1)}, u32[]{:S(2)}, u32[]{:S(2)}) collective-permute-start(bf16[2,512,256]{2,1,0:T(8,128)(2,1)} %get-tuple-element.123), channel_id=1, source_target_pairs={{2,0},{4,2},{6,4},{8,6},{10,8},{12,10},{14,12},{16,14},{18,16},{20... | collective-permute-start | bytes 1572872 | tf_op jit(solution)/shard_map/ppermute | solution.py:293
  32.9 14.7 %collective-permute-start.4 = (bf16[2,512,256]{2,1,0:T(8,128)(2,1)S(1)}, bf16[2,512,256]{2,1,0:T(8,128)(2,1)S(1)}, u32[]{:S(2)}, u32[]{:S(2)}) collective-permute-start(bf16[2,512,256]{2,1,0:T(8,128)(2,1)S(1)} %get-tuple-element.124), channel_id=1, source_target_pairs={{0,2},{2,4},{4,6},{6,8},{8,10},{10,12},{12,14},{14,16},{16,18},{18... | collective-permute-start | bytes 1572872 | tf_op jit(solution)/shard_map/ppermute | solution.py:293
  38.3 13.7 %collective-permute-start.7 = (bf16[2,512,256]{2,1,0:T(8,128)(2,1)S(1)}, bf16[2,512,256]{2,1,0:T(8,128)(2,1)S(1)}, u32[]{:S(2)}, u32[]{:S(2)}) collective-permute-start(bf16[2,512,256]{2,1,0:T(8,128)(2,1)S(1)} %get-tuple-element.115), channel_id=1, source_target_pairs={{0,1},{1,0},{2,3},{3,2},{4,5},{5,4},{6,7},{7,6},{8,9},{9,8},{10,11... | collective-permute-start | bytes 1572872 | tf_op jit(solution)/shard_map/ppermute | solution.py:289
  48.5 14.8 %collective-permute-start.6 = (bf16[2,512,256]{2,1,0:T(8,128)(2,1)S(1)}, bf16[2,512,256]{2,1,0:T(8,128)(2,1)S(1)}, u32[]{:S(2)}, u32[]{:S(2)}) collective-permute-start(bf16[2,512,256]{2,1,0:T(8,128)(2,1)S(1)} %get-tuple-element.117), channel_id=1, source_target_pairs={{0,1},{1,0},{2,3},{3,2},{4,5},{5,4},{6,7},{7,6},{8,9},{9,8},{10,11... | collective-permute-start | bytes 1572872 | tf_op jit(solution)/shard_map/ppermute | solution.py:289
  52.0 0.8 copy-start.8
  59.9 14.0 %collective-permute-start.12 = (bf16[2,512,256]{2,1,0:T(8,128)(2,1)}, bf16[2,512,256]{2,1,0:T(8,128)(2,1)S(1)}, u32[]{:S(2)}, u32[]{:S(2)}) collective-permute-start(bf16[2,512,256]{2,1,0:T(8,128)(2,1)} %get-tuple-element.100), channel_id=1, source_target_pairs={{0,1},{1,0},{2,3},{3,2},{4,5},{5,4},{6,7},{7,6},{8,9},{9,8},{10,11... | collective-permute-start | bytes 1572872 | tf_op jit(solution)/shard_map/ppermute | solution.py:289
  63.2 0.8 copy-start.9
  64.1 9.8 %copy-start.10 = (bf16[2,512,256]{2,1,0:T(8,128)(2,1)S(1)}, bf16[2,512,256]{2,1,0:T(8,128)(2,1)}, u32[]{:S(2)}) copy-start(bf16[2,512,256]{2,1,0:T(8,128)(2,1)} %get-tuple-element.99) | copy-start | bytes 1572868
  71.2 16.2 %collective-permute-start.8 = (bf16[2,512,256]{2,1,0:T(8,128)(2,1)}, bf16[2,512,256]{2,1,0:T(8,128)(2,1)S(1)}, u32[]{:S(2)}, u32[]{:S(2)}) collective-permute-start(bf16[2,512,256]{2,1,0:T(8,128)(2,1)} %get-tuple-element.94), channel_id=1, source_target_pairs={{0,1},{1,0},{2,3},{3,2},{4,5},{5,4},{6,7},{7,6},{8,9},{9,8},{10,11... | collective-permute-start | bytes 1572872 | tf_op jit(solution)/shard_map/ppermute | solution.py:289
  74.0 20.9 %collective-permute-start.13 = (bf16[2,512,256]{2,1,0:T(8,128)(2,1)S(1)}, bf16[2,512,256]{2,1,0:T(8,128)(2,1)S(1)}, u32[]{:S(2)}, u32[]{:S(2)}) collective-permute-start(bf16[2,512,256]{2,1,0:T(8,128)(2,1)S(1)} %get-tuple-element.119), channel_id=1, source_target_pairs={{2,0},{4,2},{6,4},{8,6},{10,8},{12,10},{14,12},{16,14},{18,16},{20... | collective-permute-start | bytes 1572872 | tf_op jit(solution)/shard_map/ppermute | solution.py:293
  77.6 17.4 %collective-permute-start.14 = (bf16[2,512,256]{2,1,0:T(8,128)(2,1)S(1)}, bf16[2,512,256]{2,1,0:T(8,128)(2,1)S(1)}, u32[]{:S(2)}, u32[]{:S(2)}) collective-permute-start(bf16[2,512,256]{2,1,0:T(8,128)(2,1)S(1)} %get-tuple-element.120), channel_id=1, source_target_pairs={{0,2},{2,4},{4,6},{6,8},{8,10},{10,12},{12,14},{14,16},{16,18},{18... | collective-permute-start | bytes 1572872 | tf_op jit(solution)/shard_map/ppermute | solution.py:293
  89.3 16.6 %collective-permute-start.9 = (bf16[2,512,256]{2,1,0:T(8,128)(2,1)}, bf16[2,512,256]{2,1,0:T(8,128)(2,1)S(1)}, u32[]{:S(2)}, u32[]{:S(2)}) collective-permute-start(bf16[2,512,256]{2,1,0:T(8,128)(2,1)} %get-tuple-element.121), channel_id=1, source_target_pairs={{2,0},{4,2},{6,4},{8,6},{10,8},{12,10},{14,12},{16,14},{18,16},{20... | collective-permute-start | bytes 1572872 | tf_op jit(solution)/shard_map/ppermute | solution.py:293
  91.2 15.2 %collective-permute-start.10 = (bf16[2,512,256]{2,1,0:T(8,128)(2,1)S(1)}, bf16[2,512,256]{2,1,0:T(8,128)(2,1)}, u32[]{:S(2)}, u32[]{:S(2)}) collective-permute-start(bf16[2,512,256]{2,1,0:T(8,128)(2,1)S(1)} %get-tuple-element.122), channel_id=1, source_target_pairs={{0,2},{2,4},{4,6},{6,8},{8,10},{10,12},{12,14},{14,16},{16,18},{18... | collective-permute-start | bytes 1572872 | tf_op jit(solution)/shard_map/ppermute | solution.py:293
  94.9 13.0 %copy-start = (bf16[2,512,128]{2,1,0:T(8,128)(2,1)S(1)}, bf16[2,512,128]{2,1,0:T(8,128)(2,1)}, u32[]{:S(2)}) copy-start(bf16[2,512,128]{2,1,0:T(8,128)(2,1)} %get-tuple-element.101.dk_ref) | copy-start | bytes 786436
  94.9 13.0 %copy-start.1 = (bf16[2,512,128]{2,1,0:T(8,128)(2,1)S(1)}, bf16[2,512,128]{2,1,0:T(8,128)(2,1)}, u32[]{:S(2)}) copy-start(bf16[2,512,128]{2,1,0:T(8,128)(2,1)} %get-tuple-element.102.dv_ref) | copy-start | bytes 786436
  95.0 13.8 %copy-start.4 = (bf16[2,512,128]{2,1,0:T(8,128)(2,1)S(1)}, bf16[2,512,128]{2,1,0:T(8,128)(2,1)}, u32[]{:S(2)}) copy-start(bf16[2,512,128]{2,1,0:T(8,128)(2,1)} %get-tuple-element.97.dk_ref) | copy-start | bytes 786436
  95.0 13.8 %copy-start.5 = (bf16[2,512,128]{2,1,0:T(8,128)(2,1)S(1)}, bf16[2,512,128]{2,1,0:T(8,128)(2,1)}, u32[]{:S(2)}) copy-start(bf16[2,512,128]{2,1,0:T(8,128)(2,1)} %get-tuple-element.98.dv_ref) | copy-start | bytes 786436
  95.0 13.8 %collective-permute-start.15 = (bf16[2,512,256]{2,1,0:T(8,128)(2,1)S(1)}, bf16[2,512,256]{2,1,0:T(8,128)(2,1)S(1)}, u32[]{:S(2)}, u32[]{:S(2)}) collective-permute-start(bf16[2,512,256]{2,1,0:T(8,128)(2,1)S(1)} %get-tuple-element.112), channel_id=1, source_target_pairs={{0,1},{1,0},{2,3},{3,2},{4,5},{5,4},{6,7},{7,6},{8,9},{9,8},{10,11... | collective-permute-start | bytes 1572872 | tf_op jit(solution)/shard_map/ppermute | solution.py:289
  107.5 12.7 %collective-permute-start.11 = (bf16[2,512,256]{2,1,0:T(8,128)(2,1)S(1)}, bf16[2,512,256]{2,1,0:T(8,128)(2,1)S(1)}, u32[]{:S(2)}, u32[]{:S(2)}) collective-permute-start(bf16[2,512,256]{2,1,0:T(8,128)(2,1)S(1)} %get-tuple-element.114), channel_id=1, source_target_pairs={{0,1},{1,0},{2,3},{3,2},{4,5},{5,4},{6,7},{7,6},{8,9},{9,8},{10,11... | collective-permute-start | bytes 1572872 | tf_op jit(solution)/shard_map/ppermute | solution.py:289
  107.9 2.0 %copy-start.6 = (bf16[2,512,128]{2,1,0:T(8,128)(2,1)S(1)}, bf16[2,512,128]{2,1,0:T(8,128)(2,1)}, u32[]{:S(2)}) copy-start(bf16[2,512,128]{2,1,0:T(8,128)(2,1)} %get-tuple-element.95.dk_ref) | copy-start | bytes 786436
  107.9 2.0 %copy-start.7 = (bf16[2,512,128]{2,1,0:T(8,128)(2,1)S(1)}, bf16[2,512,128]{2,1,0:T(8,128)(2,1)}, u32[]{:S(2)}) copy-start(bf16[2,512,128]{2,1,0:T(8,128)(2,1)} %get-tuple-element.96.dv_ref) | copy-start | bytes 786436
  109.8 10.4 %copy-start.2 = (bf16[2,512,128]{2,1,0:T(8,128)(2,1)S(1)}, bf16[2,512,128]{2,1,0:T(8,128)(2,1)}, u32[]{:S(2)}) copy-start(bf16[2,512,128]{2,1,0:T(8,128)(2,1)} %get-tuple-element.91.dk_ref) | copy-start | bytes 786436
  109.8 10.4 %copy-start.3 = (bf16[2,512,128]{2,1,0:T(8,128)(2,1)S(1)}, bf16[2,512,128]{2,1,0:T(8,128)(2,1)}, u32[]{:S(2)}) copy-start(bf16[2,512,128]{2,1,0:T(8,128)(2,1)} %get-tuple-element.92.dv_ref) | copy-start | bytes 786436

commit v15 on v14

--- a/solution.py
+++ b/solution.py
@@ -336,6 +336,8 @@
         pieces = [piece_of(place, chunk)]
         pieces += [turned(piece_of(other(turn), chunk), turn) for turn in range(1, sharers)]
         arrays = arrange(row_arrays, chunk * per_piece, heads_per_group, per_piece)
+        if not halves:
+            low, pieces[-1] = together(low, pieces[-1])
         *arrays, pieces[-1] = together(*arrays, pieces[-1])
         arranged.append(arrays)
         halves.append(halves_of(pieces))

time: 123 us -> 123 us (level)
  waiting for transfers between devices: 35.3 us -> 33.1 us
  starting transfers between devices: 28.4 us -> 29.7 us
    ppermute x8, waiting for transfers between devices: 22.4 us -> 20.2 us  [turned(): return lax.ppermute(value, 'head', pairs)]
    ppermute x8, starting transfers between devices: 25 us -> 26.3 us  [shifted(): lax.ppermute(value, 'blk', [(source, source + step) for source in range(f...]
  transfers between devices with their start and end apart: 16 -> 16, of which waited for: 8 -> 9; matrix products, arithmetic and copies ran while one was open for 7% -> 7% of each run, Pallas kernels for 34% -> 34%
where the time goes in v15:
time: 123 us; the launch traced here: 121 us
  Pallas kernels  42.1 us (34%)
  waiting for transfers between devices  33.1 us (27%)
  starting transfers between devices  29.7 us (24%)
  other arithmetic  9.85 us (8%)
  between operations  3.52 us (3%)
  local copies, waits for them, and re-layouts  2.43 us (2%)
    pallas_call x4, Pallas kernels, attention(): pl.pallas_call(functools.partial(attention_body, len(carried)), grid_spec...  28.5 us
    ppermute x8, starting transfers between devices, shifted(): lax.ppermute(value, 'blk', [(source, source + step) for source in range(f...  26.3 us
    ppermute x8, waiting for transfers between devices, turned(): return lax.ppermute(value, 'head', pairs)  20.2 us
    ppermute x8, waiting for transfers between devices, shifted(): lax.ppermute(value, 'blk', [(source, source + step) for source in range(f...  12.8 us
    pallas_call x2, Pallas kernels, arrange(): pl.pallas_call(arrange_body, grid=(groups, per_piece), in_specs=[query_sp...  9.76 us
    pallas_call x4, Pallas kernels, finish(): pl.pallas_call(functools.partial(finish_body, len(carried)), grid_spec=pl...  3.9 us
    ppermute x8, starting transfers between devices, turned(): return lax.ppermute(value, 'head', pairs)  3.37 us
    select_n x2, other arithmetic, past_of(): before = jnp.where(is_early(device), before_early, before_late)  3 us
  transfers between devices with their start and end apart: 16, of which 9 were waited for; matrix products, arithmetic and copies ran while one was open for 7% of the time, Pallas kernels for 34%

profile of v15, /device:TPU:11, one launch (start us, length us, event | category | flops | bytes accessed | tf_op | source)
XLA Modules:
  0.0 120.7 jit_solution(14095759111678303300)
XLA Ops:
  0.6 1.7 %select_bitcast_fusion = (bf16[1,512,256]{2,1,0:T(8,128)(2,1)S(1)}, bf16[1,512,256]{2,1,0:T(8,128)(2,1)S(1)}, bf16[1,512,256]{2,1,0:T(8,128)(2,1)S(1)}, bf16[1,5...) fusion(pred[]{:T(512)S(6)} %eq.22, ...), kind=kLoop, calls=%fused_computation.25 | loop fusion | flops 1048576 | bytes 4194306 | tf_op jit(solution)/shard_map/stack | solution.py:303
  2.4 0.3 collective-permute-start
  2.8 1.3 %collective-permute-start.1 = (bf16[2,512,256]{2,1,0:T(8,128)(2,1)S(1)}, bf16[2,512,256]{2,1,0:T(8,128)(2,1)S(1)}, u32[]{:S(2)}, u32[]{:S(2)}) collective-permute-start(bf16[2,512,256]{2,1,0:T(8,128)(2,1)S(1)} %pad_maximum_fusion.1), channel_id=1, source_target_pairs={{0,1},{1,0},{2,3},{3,2},{4,5},{5,4},{6,7},{7,6},{8,9},{9,8},{10,11... | collective-permute-start | bytes 1572872 | tf_op jit(solution)/shard_map/ppermute | solution.py:289
  4.1 0.6 fusion
  7.4 0.1 pad_dynamic-slice_fusion
  7.4 4.9 %arrange.3 = (bf16[4,1024,128]{2,1,0:T(8,128)(2,1)}, bf16[4,1024,128]{2,1,0:T(8,128)(2,1)}, f32[4,1,1024]{2,1,0:T(1,128)}, bf16[4,512,128]{2,1,0:T(8,128)(2,1)},...) custom-call(bf16[512,2048]{1,0:T(8,128)(2,1)} %q_ref.3, bf16[512,1024]{1,0:T(8,128)(2,1)} %k_ref.3, ...), custom_call_target="tpu_custom_call" | custom-call | flops 2097152 | bytes 8388608 | tf_op jit(solution)/shard_map/arrange/pallas_call | solution.py:73
  12.3 0.9 convert_reduce_fusion
  13.2 2.1 %collective-permute-done = bf16[2,512,256]{2,1,0:T(8,128)(2,1)S(1)} collective-permute-done((bf16[2,512,256]{2,1,0:T(8,128)(2,1)S(1)}, bf16[2,512,256]{2,1,0:T(8,128)(2,1)S(1)}, u32[]{:S(2)}, u32[]{:S(2)}) %collective-permute-start) | collective-permute-done | bytes 524320 | tf_op jit(solution)/shard_map/ppermute | solution.py:289
  15.3 0.9 broadcast_select_fusion.11
  16.1 4.6 %collective-permute-start.3 = (bf16[2,512,256]{2,1,0:T(8,128)(2,1)}, bf16[2,512,256]{2,1,0:T(8,128)(2,1)S(1)}, u32[]{:S(2)}, u32[]{:S(2)}) collective-permute-start(bf16[2,512,256]{2,1,0:T(8,128)(2,1)} %get-tuple-element.137), channel_id=1, source_target_pairs={{2,0},{4,2},{6,4},{8,6},{10,8},{12,10},{14,12},{16,14},{18,16},{20... | collective-permute-start | bytes 1572872 | tf_op jit(solution)/shard_map/ppermute | solution.py:293
  20.7 3.0 %collective-permute-start.2 = (bf16[2,512,256]{2,1,0:T(8,128)(2,1)S(1)}, bf16[2,512,256]{2,1,0:T(8,128)(2,1)}, u32[]{:S(2)}, u32[]{:S(2)}) collective-permute-start(bf16[2,512,256]{2,1,0:T(8,128)(2,1)S(1)} %get-tuple-element.138), channel_id=1, source_target_pairs={{0,2},{2,4},{4,6},{6,8},{8,10},{10,12},{12,14},{14,16},{16,18},{18... | collective-permute-start | bytes 1572872 | tf_op jit(solution)/shard_map/ppermute | solution.py:293
  23.8 4.9 %arrange.2 = (bf16[4,1024,128]{2,1,0:T(8,128)(2,1)}, bf16[4,1024,128]{2,1,0:T(8,128)(2,1)}, f32[4,1,1024]{2,1,0:T(1,128)}, bf16[4,512,128]{2,1,0:T(8,128)(2,1)},...) custom-call(bf16[512,2048]{1,0:T(8,128)(2,1)} %q_ref.3, bf16[512,1024]{1,0:T(8,128)(2,1)} %k_ref.3, ...), custom_call_target="tpu_custom_call" | custom-call | flops 2097152 | bytes 8388608 | tf_op jit(solution)/shard_map/arrange/pallas_call | solution.py:73
  28.7 0.1 broadcast_select_fusion.10
  28.8 1.9 %collective-permute-start.5 = (bf16[2,512,256]{2,1,0:T(8,128)(2,1)S(1)}, bf16[2,512,256]{2,1,0:T(8,128)(2,1)S(1)}, u32[]{:S(2)}, u32[]{:S(2)}) collective-permute-start(bf16[2,512,256]{2,1,0:T(8,128)(2,1)S(1)} %get-tuple-element.127), channel_id=1, source_target_pairs={{2,0},{4,2},{6,4},{8,6},{10,8},{12,10},{14,12},{16,14},{18,16},{20... | collective-permute-start | bytes 1572872 | tf_op jit(solution)/shard_map/ppermute | solution.py:293
  30.7 3.6 %collective-permute-start.4 = (bf16[2,512,256]{2,1,0:T(8,128)(2,1)S(1)}, bf16[2,512,256]{2,1,0:T(8,128)(2,1)S(1)}, u32[]{:S(2)}, u32[]{:S(2)}) collective-permute-start(bf16[2,512,256]{2,1,0:T(8,128)(2,1)S(1)} %get-tuple-element.128), channel_id=1, source_target_pairs={{0,2},{2,4},{4,6},{6,8},{8,10},{10,12},{12,14},{14,16},{16,18},{18... | collective-permute-start | bytes 1572872 | tf_op jit(solution)/shard_map/ppermute | solution.py:293
  34.4 0.2 collective-permute-done.3
  34.5 2.1 %broadcast_select_fusion.8 = (bf16[2,512,256]{2,1,0:T(8,128)(2,1)}, bf16[2,512,256]{2,1,0:T(8,128)(2,1)}) fusion(bf16[2,512,256]{2,1,0:T(8,128)(2,1)} %collective-permute-done.2, pred[]{:T(512)S(6)} %eq.54, bf16[2,512,256]{2,1,0:T(8,128)(2,1)S(1)} %get-tuple-element.138, bf16[2,512,256]{2,1,0:T(8,128)(2,1)S(1)} %collective-permute-done.3, pred[]{:T(512)S(6)} %eq.26, ...), kind=kLoop, calls=%fused_computation.13 | loop fusion | flops 786432 | bytes 2621443 | tf_op jit(solution)/shard_map/jit(_where)/select_n | solution.py:361
  36.7 0.3 collective-permute-start.7
  36.9 7.1 %attention.4 = (bf16[512,2048]{1,0:T(8,128)(2,1)}, bf16[2,512,128]{2,1,0:T(8,128)(2,1)}, bf16[2,512,128]{2,1,0:T(8,128)(2,1)}, bf16[2,512,256]{2,1,0:T(8,128)(2,1)}) custom-call(s32[1]{0:T(128)} %bitcast.group_ref, s32[1,512]{1,0:T(1,128)} %bitcast.21, bf16[4,1024,128]{2,1,0:T(8,128)(2,1)} %get-tuple-element.79.q_ref, ...), custom_call_target="tpu_custom_call" | custom-call | flops 1677721600 | bytes 2457600 | tf_op jit(solution)/shard_map/attention/pallas_call | solution.py:184
  44.0 2.1 %collective-permute-done.5 = bf16[2,512,256]{2,1,0:T(8,128)(2,1)S(1)} collective-permute-done((bf16[2,512,256]{2,1,0:T(8,128)(2,1)S(1)}, bf16[2,512,256]{2,1,0:T(8,128)(2,1)S(1)}, u32[]{:S(2)}, u32[]{:S(2)}) %collective-permute-start.5) | collective-permute-done | bytes 524320 | tf_op jit(solution)/shard_map/ppermute | solution.py:293
  46.1 0.9 broadcast_select_fusion.9
  47.0 0.3 collective-permute-start.6
  47.2 3.5 %collective-permute-done.7.past_ref = bf16[2,512,256]{2,1,0:T(8,128)(2,1)S(1)} collective-permute-done((bf16[2,512,256]{2,1,0:T(8,128)(2,1)}, bf16[2,512,256]{2,1,0:T(8,128)(2,1)S(1)}, u32[]{:S(2)}, u32[]{:S(2)}) %collective-permute-start.7) | collective-permute-done | bytes 524320 | tf_op jit(solution)/shard_map/ppermute | solution.py:289
  50.7 0.8 copy-done.8
  51.5 7.1 %attention.5 = (bf16[512,2048]{1,0:T(8,128)(2,1)}, bf16[2,512,128]{2,1,0:T(8,128)(2,1)}, bf16[2,512,128]{2,1,0:T(8,128)(2,1)}, bf16[2,512,256]{2,1,0:T(8,128)(2,1)}) custom-call(s32[1]{0:T(128)} %bitcast.12.group_ref, s32[1,512]{1,0:T(1,128)} %bitcast.22, bf16[4,1024,128]{2,1,0:T(8,128)(2,1)} %get-tuple-element.79.q_ref, ...), custom_call_target="tpu_custom_call", output_to_operand_aliasing={{0}: (9, {})} | custom-call | flops 1677721600 | bytes 2457600 | tf_op jit(solution)/shard_map/attention/pallas_call | solution.py:184
  58.6 0.3 collective-permute-start.12
  58.9 3.0 %collective-permute-done.6.past_ref = bf16[2,512,256]{2,1,0:T(8,128)(2,1)S(1)} collective-permute-done((bf16[2,512,256]{2,1,0:T(8,128)(2,1)S(1)}, bf16[2,512,256]{2,1,0:T(8,128)(2,1)S(1)}, u32[]{:S(2)}, u32[]{:S(2)}) %collective-permute-start.6) | collective-permute-done | bytes 524320 | tf_op jit(solution)/shard_map/ppermute | solution.py:289
  62.0 0.8 copy-done.9
  62.8 7.1 %attention.6 = (bf16[512,2048]{1,0:T(8,128)(2,1)}, bf16[2,512,128]{2,1,0:T(8,128)(2,1)}, bf16[2,512,128]{2,1,0:T(8,128)(2,1)}, bf16[2,512,256]{2,1,0:T(8,128)(2,1)}) custom-call(s32[1]{0:T(128)} %bitcast.12.group_ref, s32[1,512]{1,0:T(1,128)} %bitcast.23, bf16[4,1024,128]{2,1,0:T(8,128)(2,1)} %get-tuple-element.66.q_ref, ...), custom_call_target="tpu_custom_call", output_to_operand_aliasing={{0}: (9, {})} | custom-call | flops 1677721600 | bytes 2457600 | tf_op jit(solution)/shard_map/attention/pallas_call | solution.py:184
  69.9 0.3 collective-permute-start.8
  70.3 2.4 %collective-permute-done.12 = bf16[2,512,256]{2,1,0:T(8,128)(2,1)S(1)} collective-permute-done((bf16[2,512,256]{2,1,0:T(8,128)(2,1)}, bf16[2,512,256]{2,1,0:T(8,128)(2,1)S(1)}, u32[]{:S(2)}, u32[]{:S(2)}) %collective-permute-start.12) | collective-permute-done | bytes 524320 | tf_op jit(solution)/shard_map/ppermute | solution.py:289
  72.7 3.3 %collective-permute-start.13 = (bf16[2,512,256]{2,1,0:T(8,128)(2,1)S(1)}, bf16[2,512,256]{2,1,0:T(8,128)(2,1)S(1)}, u32[]{:S(2)}, u32[]{:S(2)}) collective-permute-start(bf16[2,512,256]{2,1,0:T(8,128)(2,1)S(1)} %get-tuple-element.123), channel_id=1, source_target_pairs={{2,0},{4,2},{6,4},{8,6},{10,8},{12,10},{14,12},{16,14},{18,16},{20... | collective-permute-start | bytes 1572872 | tf_op jit(solution)/shard_map/ppermute | solution.py:293
  76.0 4.3 %collective-permute-start.14 = (bf16[2,512,256]{2,1,0:T(8,128)(2,1)S(1)}, bf16[2,512,256]{2,1,0:T(8,128)(2,1)S(1)}, u32[]{:S(2)}, u32[]{:S(2)}) collective-permute-start(bf16[2,512,256]{2,1,0:T(8,128)(2,1)S(1)} %get-tuple-element.124), channel_id=1, source_target_pairs={{0,2},{2,4},{4,6},{6,8},{8,10},{10,12},{12,14},{14,16},{16,18},{18... | collective-permute-start | bytes 1572872 | tf_op jit(solution)/shard_map/ppermute | solution.py:293
  80.3 7.1 %attention.7 = (bf16[512,2048]{1,0:T(8,128)(2,1)}, bf16[2,512,128]{2,1,0:T(8,128)(2,1)}, bf16[2,512,128]{2,1,0:T(8,128)(2,1)}, bf16[2,512,256]{2,1,0:T(8,128)(2,1)}) custom-call(s32[1]{0:T(128)} %bitcast.group_ref, s32[1,512]{1,0:T(1,128)} %bitcast.24, bf16[4,1024,128]{2,1,0:T(8,128)(2,1)} %get-tuple-element.66.q_ref, ...), custom_call_target="tpu_custom_call", output_to_operand_aliasing={{0}: (9, {})} | custom-call | flops 1677721600 | bytes 2457600 | tf_op jit(solution)/shard_map/attention/pallas_call | solution.py:184
  87.4 1.9 %broadcast_select_fusion.3 = (bf16[2,512,256]{2,1,0:T(8,128)(2,1)}, bf16[2,512,256]{2,1,0:T(8,128)(2,1)S(1)}) fusion(bf16[2,512,256]{2,1,0:T(8,128)(2,1)} %get-tuple-element.97, bf16[2,512,256]{2,1,0:T(8,128)(2,1)S(1)} %collective-permute-done.8, pred[]{:T(512)S(6)} %eq.56, pred[]{:T(512)S(6)} %eq.55), kind=kLoop, calls=%fused_computation.8 | loop fusion | flops 524288 | bytes 2097154 | tf_op jit(solution)/shard_map/jit(_where)/select_n | solution.py:266
  89.3 1.9 %collective-permute-start.9 = (bf16[2,512,256]{2,1,0:T(8,128)(2,1)}, bf16[2,512,256]{2,1,0:T(8,128)(2,1)S(1)}, u32[]{:S(2)}, u32[]{:S(2)}) collective-permute-start(bf16[2,512,256]{2,1,0:T(8,128)(2,1)} %get-tuple-element.125), channel_id=1, source_target_pairs={{2,0},{4,2},{6,4},{8,6},{10,8},{12,10},{14,12},{16,14},{18,16},{20... | collective-permute-start | bytes 1572872 | tf_op jit(solution)/shard_map/ppermute | solution.py:293
  91.2 3.6 %collective-permute-start.10 = (bf16[2,512,256]{2,1,0:T(8,128)(2,1)S(1)}, bf16[2,512,256]{2,1,0:T(8,128)(2,1)}, u32[]{:S(2)}, u32[]{:S(2)}) collective-permute-start(bf16[2,512,256]{2,1,0:T(8,128)(2,1)S(1)} %get-tuple-element.126), channel_id=1, source_target_pairs={{0,2},{2,4},{4,6},{6,8},{8,10},{10,12},{12,14},{14,16},{16,18},{18... | collective-permute-start | bytes 1572872 | tf_op jit(solution)/shard_map/ppermute | solution.py:293
  94.9 0.1 broadcast_select_fusion
  95.1 0.3 collective-permute-start.15
  95.4 10.6 %collective-permute-done.9 = bf16[2,512,256]{2,1,0:T(8,128)(2,1)S(1)} collective-permute-done((bf16[2,512,256]{2,1,0:T(8,128)(2,1)}, bf16[2,512,256]{2,1,0:T(8,128)(2,1)S(1)}, u32[]{:S(2)}, u32[]{:S(2)}) %collective-permute-start.9) | collective-permute-done | bytes 524320 | tf_op jit(solution)/shard_map/ppermute | solution.py:293
  105.9 1.1 broadcast_select_fusion.1
  107.1 0.3 collective-permute-start.11
  107.4 1.0 finish.4
  108.4 0.7 collective-permute-done.15.back_ref
  109.1 1.0 finish.5
  110.1 1.0 finish.6
  111.0 8.7 %collective-permute-done.11.back_ref = bf16[2,512,256]{2,1,0:T(8,128)(2,1)S(1)} collective-permute-done((bf16[2,512,256]{2,1,0:T(8,128)(2,1)S(1)}, bf16[2,512,256]{2,1,0:T(8,128)(2,1)S(1)}, u32[]{:S(2)}, u32[]{:S(2)}) %collective-permute-start.11) | collective-permute-done | bytes 524320 | tf_op jit(solution)/shard_map/ppermute | solution.py:289
  119.7 1.0 finish.7
  (36 shorter events, 0.3 us)
Async XLA Ops:
  2.3 1.7 %copy-start.12 = (s32[32]{0:T(128)S(1)}, s32[32]{0:T(128)}, u32[]{:S(2)}) copy-start(s32[32]{0:T(128)} %param.13) | copy-start | bytes 388
  2.4 5.0 %copy-start.11 = (s32[16384]{0:T(1024)S(1)}, s32[16384]{0:T(1024)}, u32[]{:S(2)}) copy-start(s32[16384]{0:T(1024)} %param.12) | copy-start | bytes 196612
  2.4 12.9 %collective-permute-start = (bf16[2,512,256]{2,1,0:T(8,128)(2,1)S(1)}, bf16[2,512,256]{2,1,0:T(8,128)(2,1)S(1)}, u32[]{:S(2)}, u32[]{:S(2)}) collective-permute-start(bf16[2,512,256]{2,1,0:T(8,128)(2,1)S(1)} %pad_maximum_fusion), channel_id=1, source_target_pairs={{0,1},{1,0},{2,3},{3,2},{4,5},{5,4},{6,7},{7,6},{8,9},{9,8},{10,11... | collective-permute-start | bytes 1572872 | tf_op jit(solution)/shard_map/ppermute | solution.py:289
  2.8 25.9 %collective-permute-start.1 = (bf16[2,512,256]{2,1,0:T(8,128)(2,1)S(1)}, bf16[2,512,256]{2,1,0:T(8,128)(2,1)S(1)}, u32[]{:S(2)}, u32[]{:S(2)}) collective-permute-start(bf16[2,512,256]{2,1,0:T(8,128)(2,1)S(1)} %pad_maximum_fusion.1), channel_id=1, source_target_pairs={{0,1},{1,0},{2,3},{3,2},{4,5},{5,4},{6,7},{7,6},{8,9},{9,8},{10,11... | collective-permute-start | bytes 1572872 | tf_op jit(solution)/shard_map/ppermute | solution.py:289
  16.1 18.4 %collective-permute-start.3 = (bf16[2,512,256]{2,1,0:T(8,128)(2,1)}, bf16[2,512,256]{2,1,0:T(8,128)(2,1)S(1)}, u32[]{:S(2)}, u32[]{:S(2)}) collective-permute-start(bf16[2,512,256]{2,1,0:T(8,128)(2,1)} %get-tuple-element.137), channel_id=1, source_target_pairs={{2,0},{4,2},{6,4},{8,6},{10,8},{12,10},{14,12},{16,14},{18,16},{20... | collective-permute-start | bytes 1572872 | tf_op jit(solution)/shard_map/ppermute | solution.py:293
  20.7 13.8 %collective-permute-start.2 = (bf16[2,512,256]{2,1,0:T(8,128)(2,1)S(1)}, bf16[2,512,256]{2,1,0:T(8,128)(2,1)}, u32[]{:S(2)}, u32[]{:S(2)}) collective-permute-start(bf16[2,512,256]{2,1,0:T(8,128)(2,1)S(1)} %get-tuple-element.138), channel_id=1, source_target_pairs={{0,2},{2,4},{4,6},{6,8},{8,10},{10,12},{12,14},{14,16},{16,18},{18... | collective-permute-start | bytes 1572872 | tf_op jit(solution)/shard_map/ppermute | solution.py:293
  28.8 17.3 %collective-permute-start.5 = (bf16[2,512,256]{2,1,0:T(8,128)(2,1)S(1)}, bf16[2,512,256]{2,1,0:T(8,128)(2,1)S(1)}, u32[]{:S(2)}, u32[]{:S(2)}) collective-permute-start(bf16[2,512,256]{2,1,0:T(8,128)(2,1)S(1)} %get-tuple-element.127), channel_id=1, source_target_pairs={{2,0},{4,2},{6,4},{8,6},{10,8},{12,10},{14,12},{16,14},{18,16},{20... | collective-permute-start | bytes 1572872 | tf_op jit(solution)/shard_map/ppermute | solution.py:293
  30.7 15.4 %collective-permute-start.4 = (bf16[2,512,256]{2,1,0:T(8,128)(2,1)S(1)}, bf16[2,512,256]{2,1,0:T(8,128)(2,1)S(1)}, u32[]{:S(2)}, u32[]{:S(2)}) collective-permute-start(bf16[2,512,256]{2,1,0:T(8,128)(2,1)S(1)} %get-tuple-element.128), channel_id=1, source_target_pairs={{0,2},{2,4},{4,6},{6,8},{8,10},{10,12},{12,14},{14,16},{16,18},{18... | collective-permute-start | bytes 1572872 | tf_op jit(solution)/shard_map/ppermute | solution.py:293
  36.7 14.1 %collective-permute-start.7 = (bf16[2,512,256]{2,1,0:T(8,128)(2,1)}, bf16[2,512,256]{2,1,0:T(8,128)(2,1)S(1)}, u32[]{:S(2)}, u32[]{:S(2)}) collective-permute-start(bf16[2,512,256]{2,1,0:T(8,128)(2,1)} %get-tuple-element.119), channel_id=1, source_target_pairs={{0,1},{1,0},{2,3},{3,2},{4,5},{5,4},{6,7},{7,6},{8,9},{9,8},{10,11... | collective-permute-start | bytes 1572872 | tf_op jit(solution)/shard_map/ppermute | solution.py:289
  47.0 15.0 %collective-permute-start.6 = (bf16[2,512,256]{2,1,0:T(8,128)(2,1)S(1)}, bf16[2,512,256]{2,1,0:T(8,128)(2,1)S(1)}, u32[]{:S(2)}, u32[]{:S(2)}) collective-permute-start(bf16[2,512,256]{2,1,0:T(8,128)(2,1)S(1)} %get-tuple-element.121), channel_id=1, source_target_pairs={{0,1},{1,0},{2,3},{3,2},{4,5},{5,4},{6,7},{7,6},{8,9},{9,8},{10,11... | collective-permute-start | bytes 1572872 | tf_op jit(solution)/shard_map/ppermute | solution.py:289
  50.7 0.8 copy-start.8
  58.6 14.0 %collective-permute-start.12 = (bf16[2,512,256]{2,1,0:T(8,128)(2,1)}, bf16[2,512,256]{2,1,0:T(8,128)(2,1)S(1)}, u32[]{:S(2)}, u32[]{:S(2)}) collective-permute-start(bf16[2,512,256]{2,1,0:T(8,128)(2,1)} %get-tuple-element.104), channel_id=1, source_target_pairs={{0,1},{1,0},{2,3},{3,2},{4,5},{5,4},{6,7},{7,6},{8,9},{9,8},{10,11... | collective-permute-start | bytes 1572872 | tf_op jit(solution)/shard_map/ppermute | solution.py:289
  62.0 0.8 copy-start.9
  62.8 9.8 %copy-start.10 = (bf16[2,512,256]{2,1,0:T(8,128)(2,1)S(1)}, bf16[2,512,256]{2,1,0:T(8,128)(2,1)}, u32[]{:S(2)}) copy-start(bf16[2,512,256]{2,1,0:T(8,128)(2,1)} %get-tuple-element.103) | copy-start | bytes 1572868
  69.9 17.5 %collective-permute-start.8 = (bf16[2,512,256]{2,1,0:T(8,128)(2,1)}, bf16[2,512,256]{2,1,0:T(8,128)(2,1)S(1)}, u32[]{:S(2)}, u32[]{:S(2)}) collective-permute-start(bf16[2,512,256]{2,1,0:T(8,128)(2,1)} %get-tuple-element.98), channel_id=1, source_target_pairs={{0,1},{1,0},{2,3},{3,2},{4,5},{5,4},{6,7},{7,6},{8,9},{9,8},{10,11... | collective-permute-start | bytes 1572872 | tf_op jit(solution)/shard_map/ppermute | solution.py:289
  72.7 22.2 %collective-permute-start.13 = (bf16[2,512,256]{2,1,0:T(8,128)(2,1)S(1)}, bf16[2,512,256]{2,1,0:T(8,128)(2,1)S(1)}, u32[]{:S(2)}, u32[]{:S(2)}) collective-permute-start(bf16[2,512,256]{2,1,0:T(8,128)(2,1)S(1)} %get-tuple-element.123), channel_id=1, source_target_pairs={{2,0},{4,2},{6,4},{8,6},{10,8},{12,10},{14,12},{16,14},{18,16},{20... | collective-permute-start | bytes 1572872 | tf_op jit(solution)/shard_map/ppermute | solution.py:293
  76.0 19.0 %collective-permute-start.14 = (bf16[2,512,256]{2,1,0:T(8,128)(2,1)S(1)}, bf16[2,512,256]{2,1,0:T(8,128)(2,1)S(1)}, u32[]{:S(2)}, u32[]{:S(2)}) collective-permute-start(bf16[2,512,256]{2,1,0:T(8,128)(2,1)S(1)} %get-tuple-element.124), channel_id=1, source_target_pairs={{0,2},{2,4},{4,6},{6,8},{8,10},{10,12},{12,14},{14,16},{16,18},{18... | collective-permute-start | bytes 1572872 | tf_op jit(solution)/shard_map/ppermute | solution.py:293
  89.3 16.6 %collective-permute-start.9 = (bf16[2,512,256]{2,1,0:T(8,128)(2,1)}, bf16[2,512,256]{2,1,0:T(8,128)(2,1)S(1)}, u32[]{:S(2)}, u32[]{:S(2)}) collective-permute-start(bf16[2,512,256]{2,1,0:T(8,128)(2,1)} %get-tuple-element.125), channel_id=1, source_target_pairs={{2,0},{4,2},{6,4},{8,6},{10,8},{12,10},{14,12},{16,14},{18,16},{20... | collective-permute-start | bytes 1572872 | tf_op jit(solution)/shard_map/ppermute | solution.py:293
  91.2 14.7 %collective-permute-start.10 = (bf16[2,512,256]{2,1,0:T(8,128)(2,1)S(1)}, bf16[2,512,256]{2,1,0:T(8,128)(2,1)}, u32[]{:S(2)}, u32[]{:S(2)}) collective-permute-start(bf16[2,512,256]{2,1,0:T(8,128)(2,1)S(1)} %get-tuple-element.126), channel_id=1, source_target_pairs={{0,2},{2,4},{4,6},{6,8},{8,10},{10,12},{12,14},{14,16},{16,18},{18... | collective-permute-start | bytes 1572872 | tf_op jit(solution)/shard_map/ppermute | solution.py:293
  94.9 12.5 %copy-start = (bf16[2,512,128]{2,1,0:T(8,128)(2,1)S(1)}, bf16[2,512,128]{2,1,0:T(8,128)(2,1)}, u32[]{:S(2)}) copy-start(bf16[2,512,128]{2,1,0:T(8,128)(2,1)} %get-tuple-element.105.dk_ref) | copy-start | bytes 786436
  94.9 12.5 %copy-start.1 = (bf16[2,512,128]{2,1,0:T(8,128)(2,1)S(1)}, bf16[2,512,128]{2,1,0:T(8,128)(2,1)}, u32[]{:S(2)}) copy-start(bf16[2,512,128]{2,1,0:T(8,128)(2,1)} %get-tuple-element.106.dv_ref) | copy-start | bytes 786436
  95.0 14.0 %copy-start.4 = (bf16[2,512,128]{2,1,0:T(8,128)(2,1)S(1)}, bf16[2,512,128]{2,1,0:T(8,128)(2,1)}, u32[]{:S(2)}) copy-start(bf16[2,512,128]{2,1,0:T(8,128)(2,1)} %get-tuple-element.101.dk_ref) | copy-start | bytes 786436
  95.1 14.0 %copy-start.5 = (bf16[2,512,128]{2,1,0:T(8,128)(2,1)S(1)}, bf16[2,512,128]{2,1,0:T(8,128)(2,1)}, u32[]{:S(2)}) copy-start(bf16[2,512,128]{2,1,0:T(8,128)(2,1)} %get-tuple-element.102.dv_ref) | copy-start | bytes 786436
  95.1 14.0 %collective-permute-start.15 = (bf16[2,512,256]{2,1,0:T(8,128)(2,1)S(1)}, bf16[2,512,256]{2,1,0:T(8,128)(2,1)S(1)}, u32[]{:S(2)}, u32[]{:S(2)}) collective-permute-start(bf16[2,512,256]{2,1,0:T(8,128)(2,1)S(1)} %get-tuple-element.116), channel_id=1, source_target_pairs={{0,1},{1,0},{2,3},{3,2},{4,5},{5,4},{6,7},{7,6},{8,9},{9,8},{10,11... | collective-permute-start | bytes 1572872 | tf_op jit(solution)/shard_map/ppermute | solution.py:289
  107.1 12.6 %collective-permute-start.11 = (bf16[2,512,256]{2,1,0:T(8,128)(2,1)S(1)}, bf16[2,512,256]{2,1,0:T(8,128)(2,1)S(1)}, u32[]{:S(2)}, u32[]{:S(2)}) collective-permute-start(bf16[2,512,256]{2,1,0:T(8,128)(2,1)S(1)} %get-tuple-element.118), channel_id=1, source_target_pairs={{0,1},{1,0},{2,3},{3,2},{4,5},{5,4},{6,7},{7,6},{8,9},{9,8},{10,11... | collective-permute-start | bytes 1572872 | tf_op jit(solution)/shard_map/ppermute | solution.py:289
  107.4 2.7 %copy-start.6 = (bf16[2,512,128]{2,1,0:T(8,128)(2,1)S(1)}, bf16[2,512,128]{2,1,0:T(8,128)(2,1)}, u32[]{:S(2)}) copy-start(bf16[2,512,128]{2,1,0:T(8,128)(2,1)} %get-tuple-element.99.dk_ref) | copy-start | bytes 786436
  107.4 2.7 %copy-start.7 = (bf16[2,512,128]{2,1,0:T(8,128)(2,1)S(1)}, bf16[2,512,128]{2,1,0:T(8,128)(2,1)}, u32[]{:S(2)}) copy-start(bf16[2,512,128]{2,1,0:T(8,128)(2,1)} %get-tuple-element.100.dv_ref) | copy-start | bytes 786436
  110.0 9.7 %copy-start.2 = (bf16[2,512,128]{2,1,0:T(8,128)(2,1)S(1)}, bf16[2,512,128]{2,1,0:T(8,128)(2,1)}, u32[]{:S(2)}) copy-start(bf16[2,512,128]{2,1,0:T(8,128)(2,1)} %get-tuple-element.95.dk_ref) | copy-start | bytes 786436
  110.0 9.7 %copy-start.3 = (bf16[2,512,128]{2,1,0:T(8,128)(2,1)S(1)}, bf16[2,512,128]{2,1,0:T(8,128)(2,1)}, u32[]{:S(2)}) copy-start(bf16[2,512,128]{2,1,0:T(8,128)(2,1)} %get-tuple-element.96.dv_ref) | copy-start | bytes 786436
